TPU v7x, 512 devices: a whole 4x4x16 slice. The times are simulated.
512 devices in a mesh: rel: 32 (over z, core), rep: 16 (over y, x).
Axes of the slice: x: 4, y: 4, z: 16, core: 2. Of those that a mesh axis runs over, the one named last changes fastest.
Arguments:
- core: bfloat16 [512, 128, 512], P('rel'), may hold values from -0.0234375 to 0.0234375
- rel_emb: bfloat16 [64, 128], replicated, may hold values from -0.5 to 0.5
- ents: bfloat16 [65536, 512], P(('rel', 'rep')), may hold values from -6 to 6
- pool: bfloat16 [256, 512], replicated, may hold values from -6 to 6
- owner_of: int32 [64], replicated, may hold values from 0 to 31, as said below
- rel_ids: int32 [524288], P(('rel', 'rep')), may hold values from 0 to 63, as said below
- head_ids: int32 [524288], P(('rel', 'rep')), may hold values from 0 to 127
- tail_ids: int32 [524288], P(('rel', 'rep')), may hold values from 0 to 127
- fill: int32 [512, 32], P(('rel', 'rep')), may hold values from 0 to 32, as said below
Outputs:
- core_grad: bfloat16 [512, 128, 512], P('rel')
- rel_grad: float32 [64, 128], replicated
- ent_grad: bfloat16 [65536, 512], P(('rel', 'rep'))
- pool_grad: bfloat16 [256, 512], replicated
Inputs may be any that keep to these rules, and one draw needn't show every extreme that they name: `owner_of`: every owner index names exactly 2 relations. `rel_ids`: every slot of a device's block o, used or not, names a relation whose owner is o. `fill`: some block is full in every draw.
All inputs are finite; a program needn't handle non-finite values.
Results may differ from a plain program's by a relative error of at most 0.019.
Values may be sent and summed in bfloat16 or wider, within the bound.
No kernel may reach another device: no remote copies, remote signals or barrier semaphores. Data moves between devices by JAX's collectives and lax.ppermute only.
A program may use at most 64 MiB of HBM per device.

v0:
```python
import jax
import jax.numpy as jnp
from jax import lax
from jax.sharding import PartitionSpec as P


def order_tables(owner_of, per_owner):
    count = owner_of.shape[0]
    index = jnp.arange(count, dtype=jnp.int32)
    same = owner_of[:, None] == owner_of[None, :]
    rank = jnp.sum((same & (index[None, :] < index[:, None])).astype(jnp.int32), axis=1)
    return (rank, owner_of * per_owner + rank)


def forward(rows, select, mats):
    query = jnp.zeros((rows.shape[0], mats.shape[2]), jnp.float32)
    for which in range(mats.shape[0]):
        query = query + select[:, which : which + 1].astype(jnp.float32) * jnp.dot(
            rows, mats[which], preferred_element_type=jnp.float32
        )
    return query.astype(jnp.bfloat16)


def backward(rows, select, dquery, mats):
    dhead = jnp.zeros((rows.shape[0], mats.shape[1]), jnp.float32)
    pieces = []
    for which in range(mats.shape[0]):
        mask = select[:, which : which + 1].astype(jnp.float32)
        dhead = dhead + mask * lax.dot_general(
            dquery, mats[which], (((1,), (1,)), ((), ())), preferred_element_type=jnp.float32
        )
        masked = (mask * dquery.astype(jnp.float32)).astype(jnp.bfloat16)
        pieces.append(
            lax.dot_general(
                rows, masked, (((0,), (0,)), ((), ())), preferred_element_type=jnp.float32
            ).astype(jnp.bfloat16)
        )
    return (dhead.astype(jnp.bfloat16), jnp.stack(pieces))


def score(query, tails, used, pool, scale):
    qfloat = query.astype(jnp.float32)
    positive = jnp.sum(qfloat * tails.astype(jnp.float32), axis=1)
    negative = lax.dot_general(
        query, pool, (((1,), (1,)), ((), ())), preferred_element_type=jnp.float32
    )
    gpos = -jax.nn.sigmoid(-positive) * used * scale
    gneg = (jax.nn.sigmoid(negative) * (used * scale / pool.shape[0])[:, None]).astype(jnp.bfloat16)
    dquery = (
        gpos[:, None] * tails.astype(jnp.float32)
        + jnp.dot(gneg, pool, preferred_element_type=jnp.float32)
    ).astype(jnp.bfloat16)
    dtail = (gpos[:, None] * qfloat).astype(jnp.bfloat16)
    dpool = lax.dot_general(
        gneg, query, (((0,), (0,)), ((), ())), preferred_element_type=jnp.float32
    )
    return (dquery, dtail, dpool)


def body(core, rel_emb, ents, pool, owner_of, rel_ids, head_ids, tail_ids, fill):
    nrel = lax.axis_size("rel")
    nrep = lax.axis_size("rep")
    rels = rel_emb.shape[0]
    per_owner = rels // nrel
    rows_dev = core.shape[0]
    feats = core.shape[2]
    cap = rel_ids.shape[0] // nrel
    slots = nrel * cap
    ent_rows = ents.shape[0]
    scale = 1.0 / nrep
    rank, slot_of = order_tables(owner_of, per_owner)
    qindex = jnp.arange(rels, dtype=jnp.int32)
    order_sel = (slot_of[None, :] == qindex[:, None]).astype(jnp.bfloat16)
    ordered = jnp.dot(order_sel, rel_emb, preferred_element_type=jnp.float32).astype(jnp.bfloat16)
    partial_mats = jnp.einsum(
        "qk,akb->qab", ordered, core, preferred_element_type=jnp.float32
    ).astype(jnp.bfloat16)
    own_mats = lax.all_to_all(
        partial_mats.reshape(nrel, per_owner, rows_dev, feats),
        "rel",
        split_axis=0,
        concat_axis=2,
        tiled=True,
    )
    own_mats = own_mats.reshape(per_owner, feats, feats)
    heads = jnp.take(ents, head_ids, axis=0)
    tails = jnp.take(ents, tail_ids, axis=0)
    slot_index = jnp.arange(slots, dtype=jnp.int32)
    limit = jnp.take(fill[0], slot_index // cap)
    used = (slot_index % cap < limit).astype(jnp.float32)
    rank_slot = jnp.take(rank, rel_ids)
    select = (
        used[:, None]
        * (rank_slot[:, None] == jnp.arange(per_owner, dtype=jnp.int32)[None, :]).astype(
            jnp.float32
        )
    ).astype(jnp.bfloat16)
    got_heads, got_select = (
        lax.all_to_all(
            heads.reshape(nrel, cap, feats), "rel", split_axis=0, concat_axis=0, tiled=True
        ),
        lax.all_to_all(
            select.reshape(nrel, cap, per_owner), "rel", split_axis=0, concat_axis=0, tiled=True
        ),
    )
    got_heads = got_heads.reshape(slots, feats)
    got_select = got_select.reshape(slots, per_owner)
    query = forward(got_heads, got_select, own_mats)
    home_query = lax.all_to_all(
        query.reshape(nrel, cap, feats), "rel", split_axis=0, concat_axis=0, tiled=True
    ).reshape(slots, feats)
    dquery, back_tail, pool_part = score(home_query, tails, used, pool, scale)
    owner_dquery = lax.all_to_all(
        dquery.reshape(nrel, cap, feats), "rel", split_axis=0, concat_axis=0, tiled=True
    ).reshape(slots, feats)
    dhead_owner, dmats = backward(got_heads, got_select, owner_dquery, own_mats)
    back_head = lax.all_to_all(
        dhead_owner.reshape(nrel, cap, feats), "rel", split_axis=0, concat_axis=0, tiled=True
    )
    back_head = back_head.reshape(slots, feats)
    entity_index = jnp.arange(ent_rows, dtype=jnp.int32)
    head_hot = (head_ids[:, None] == entity_index[None, :]).astype(jnp.bfloat16)
    tail_hot = (tail_ids[:, None] == entity_index[None, :]).astype(jnp.bfloat16)
    ent_total = lax.dot_general(
        head_hot, back_head, (((0,), (0,)), ((), ())), preferred_element_type=jnp.float32
    )
    ent_total = ent_total + lax.dot_general(
        tail_hot, back_tail, (((0,), (0,)), ((), ())), preferred_element_type=jnp.float32
    )
    ent_grad = ent_total.astype(jnp.bfloat16)
    grad_rows = lax.all_to_all(
        dmats.reshape(per_owner, nrel, rows_dev, feats),
        "rel",
        split_axis=1,
        concat_axis=0,
        tiled=True,
    )
    grad_rows = grad_rows.reshape(rels, rows_dev, feats)
    summed_rows = lax.psum(grad_rows, "rep").astype(jnp.float32)
    core_grad = jnp.einsum(
        "qk,qab->akb", ordered.astype(jnp.float32), summed_rows, precision=lax.Precision.HIGHEST
    ).astype(jnp.bfloat16)
    ordered_grad = jnp.einsum(
        "qab,akb->qk", summed_rows, core.astype(jnp.float32), precision=lax.Precision.HIGHEST
    )
    rel_part = lax.dot_general(
        order_sel.astype(jnp.float32),
        ordered_grad,
        (((0,), (0,)), ((), ())),
        precision=lax.Precision.HIGHEST,
    )
    rel_grad = lax.psum(rel_part.astype(jnp.bfloat16), "rel").astype(jnp.float32)
    pool_total = lax.psum(pool_part, ("rel", "rep"))
    return (core_grad, rel_grad, ent_grad, pool_total.astype(jnp.bfloat16))


def solution(mesh):
    return jax.shard_map(
        body,
        mesh=mesh,
        in_specs=(
            P("rel", None, None),
            P(),
            P(("rel", "rep"), None),
            P(),
            P(),
            P(("rel", "rep")),
            P(("rel", "rep")),
            P(("rel", "rep")),
            P(("rel", "rep"), None),
        ),
        out_specs=(P("rel", None, None), P(), P(("rel", "rep"), None), P()),
        check_vma=False,
    )
```

profile of v0, /device:TPU:1, one launch (start us, length us, event | category | flops | bytes accessed | tf_op | source)
XLA Modules:
  0.0 661.1 jit_solution(8998891396797893767)
XLA Ops:
  7.2 0.0 copy-start
  7.2 1.0 convert_reduce_fusion
  8.2 0.7 fusion.50
  8.9 0.7 fusion.51
  9.6 0.7 fusion.52
  10.3 0.7 fusion.53
  11.0 2.1 fusion.54
  13.1 1.8 fusion.55
  15.8 40.6 %select_select_fusion.1 = s32[1024]{0:T(1024)S(1)} fusion(s32[1024]{0:T(1024)} %param.16, s32[]{:T(128)} %bitcast.1, s32[]{:T(128)} %bitcast.2, s32[]{:T(128)} %bitcast.3, s32[]{:T(128)} %bitcast.4, s32[]{:T(128)} %bitcast.5, s32[]{:T(128)} %bitcast.6, s32[]{:T(128)} %bitcast.7, s32[]{:T(128)} %bitcast.8, s32[]{:T(128)} %bitcast.9, s32[]{:T(128)} %bitcast.10, ...), kind=kLoop, calls=%fused_computation.116 | loop fusion | flops 136192 | bytes 8448 | tf_op jit(solution)/shard_map/jit(_take)/select_n | solution.py:91
  56.4 0.1 eq.36
  56.5 4.4 compare_select_fusion.3
  60.9 15.7 %select_select_fusion = s32[1024]{0:T(1024)S(1)} fusion(pred[1024]{0:T(1024)(128)(4,1)S(1)} %compare_reduce_fusion, pred[1024]{0:T(1024)(128)(4,1)S(1)} %compare_reduce_fusion.1, pred[1024]{0:T(1024)(128)(4,1)S(1)} %compare_reduce_fusion.2, pred[1024]{0:T(1024)(128)(4,1)S(1)} %compare_reduce_fusion.3, pred[1024]{0:T(1024)(128)(4,1)S(1)} %compare_reduce_fusion.4, ...), kind=kLoop, calls=%fused_computation.115 | loop fusion | flops 25600 | bytes 33892 | tf_op jit(solution)/shard_map/jit(_take)/gather | solution.py:89
  76.6 0.1 gather.15
  76.7 0.6 fusion.24
  77.3 16.7 %all-to-all-start.1 = ((bf16[32,32,2]{1,2,0:T(2,128)(2,1)}), bf16[32,32,2]{1,2,0:T(2,128)(2,1)S(1)}, u32[]{:S(2)}, u32[]{:S(2)}) async-start(bf16[32,32,2]{1,2,0:T(2,128)(2,1)} %fusion.24), calls=%async_computation.1 | async-start | bytes 32768 | tf_op jit(solution)/shard_map/all_to_all | solution.py:102
  94.1 0.7 multiply_add_fusion.1
  94.7 0.8 fusion.14
  95.6 0.4 convolution_convert_fusion
  96.0 0.0 copy-start.8
  96.0 0.0 copy-start.1
  96.0 1.6 copy.38
  97.6 8.1 %all-to-all-done.1 = bf16[32,32,2]{1,2,0:T(2,128)(2,1)S(1)} async-done(((bf16[32,32,2]{1,2,0:T(2,128)(2,1)}), bf16[32,32,2]{1,2,0:T(2,128)(2,1)S(1)}, u32[]{:S(2)}, u32[]{:S(2)}) %all-to-all-start.1) | async-done | bytes 4128 | tf_op jit(solution)/shard_map/all_to_all | solution.py:102
  105.8 5.2 all-to-all-start.2
  111.0 4.0 gather_fusion
  115.0 1.2 broadcast_select_fusion.1
  116.1 50.7 %all-to-all-done.2 = bf16[32,2,16,512]{3,2,1,0:T(8,128)(2,1)} async-done(((bf16[32,2,16,512]{3,2,1,0:T(8,128)(2,1)}), bf16[32,2,16,512]{3,2,1,0:T(8,128)(2,1)}, u32[]{:S(2)}, u32[]{:S(2)}) %all-to-all-start.2) | async-done | bytes 1048608 | tf_op jit(solution)/shard_map/all_to_all | solution.py:78
  166.8 4.6 all-to-all-start
  171.5 0.1 reshape.184
  171.6 1.3 copy.41
  172.9 1.1 fusion.49
  174.0 53.3 %all-to-all-done = bf16[32,32,512]{2,1,0:T(8,128)(2,1)S(1)} async-done(((bf16[32,32,512]{2,1,0:T(8,128)(2,1)}), bf16[32,32,512]{2,1,0:T(8,128)(2,1)S(1)}, u32[]{:S(2)}, u32[]{:S(2)}) %all-to-all-start) | async-done | bytes 1048608 | tf_op jit(solution)/shard_map/all_to_all | solution.py:99
  227.3 1.8 fusion.56
  229.1 1.7 add_convert_fusion.1
  230.8 5.4 all-to-all-start.3
  236.2 5.1 gather_fusion.1
  241.3 50.8 %all-to-all-done.3 = bf16[32,32,512]{2,1,0:T(8,128)(2,1)} async-done(((bf16[32,32,512]{2,1,0:T(8,128)(2,1)}), bf16[32,32,512]{2,1,0:T(8,128)(2,1)}, u32[]{:S(2)}, u32[]{:S(2)}) %all-to-all-start.3) | async-done | bytes 1048608 | tf_op jit(solution)/shard_map/all_to_all | solution.py:109
  292.1 2.2 fusion.1
  294.3 1.8 fusion.12
  296.1 1.4 fusion.3
  297.6 5.3 all-to-all-start.4
  302.9 0.1 mul.108
  303.0 0.1 mul.127
  303.0 55.7 %all-to-all-done.4 = bf16[32,32,512]{2,1,0:T(8,128)(2,1)} async-done(((bf16[32,32,512]{2,1,0:T(8,128)(2,1)}), bf16[32,32,512]{2,1,0:T(8,128)(2,1)}, u32[]{:S(2)}, u32[]{:S(2)}) %all-to-all-start.4) | async-done | bytes 1048608 | tf_op jit(solution)/shard_map/all_to_all | solution.py:113
  358.7 2.0 fusion.10
  360.8 2.0 fusion.11
  362.8 1.1 pad_maximum_fusion
  363.9 5.3 all-to-all-start.5
  369.2 2.0 fusion.57
  371.2 3.0 add_convert_fusion
  374.2 50.8 %all-to-all-done.5 = bf16[2,32,16,512]{3,2,0,1:T(8,128)(2,1)} async-done(((bf16[2,32,16,512]{3,2,0,1:T(8,128)(2,1)}), bf16[2,32,16,512]{3,2,0,1:T(8,128)(2,1)}, u32[]{:S(2)}, u32[]{:S(2)}) %all-to-all-start.5) | async-done | bytes 1048608 | tf_op jit(solution)/shard_map/all_to_all | solution.py:131
  425.0 4.6 all-to-all-start.6
  429.7 0.0 all-reduce.3.cloned.1.call-start
  429.7 2.8 copy.39
  432.5 0.0 all-reduce.3.cloned.1.call-update
  432.5 2.6 fusion.58
  435.1 118.2 %all-reduce.4 = bf16[256,512]{1,0:T(8,128)(2,1)} all-reduce(f32[256,512]{1,0:T(8,128)} %fusion.58), channel_id=1, replica_groups=mesh['rel'=32,'rep'=16] {'rel','rep'}, use_global_device_ids=true, to_apply=%region_4.6 | all-reduce | flops 131072 | bytes 786432 | tf_op jit(solution)/shard_map/psum | solution.py:153
  553.4 0.6 fusion.21
  554.0 2.6 fusion.13
  556.6 3.3 convert_bitcast_fusion
  559.9 4.0 copy.37
  563.9 0.8 convolution_bitcast_fusion.2
  564.8 0.2 convolution_convert_fusion.1
  565.0 88.6 %psum.22 = bf16[64,128]{1,0:T(8,128)(2,1)S(1)} all-reduce(bf16[64,128]{1,0:T(8,128)(2,1)S(1)} %convolution_convert_fusion.1), channel_id=1, replica_groups=mesh['rel'=32,'rep'=16] {'rel'}, use_global_device_ids=true, to_apply=%region_3.5 | all-reduce | flops 8192 | bytes 32768 | tf_op jit(solution)/shard_map/psum | solution.py:152
  653.6 0.6 convert_element_type.116
  (56 shorter events, 1.0 us)
Async XLA Ops:
  7.2 88.4 %copy-start = (bf16[16,128,512]{2,1,0:T(8,128)(2,1)S(1)}, bf16[16,128,512]{2,1,0:T(8,128)(2,1)}, u32[]{:S(2)}) copy-start(bf16[16,128,512]{2,1,0:T(8,128)(2,1)} %param.11) | copy-start | bytes 6291460
  77.3 28.5 %all-to-all-start.1 = ((bf16[32,32,2]{1,2,0:T(2,128)(2,1)}), bf16[32,32,2]{1,2,0:T(2,128)(2,1)S(1)}, u32[]{:S(2)}, u32[]{:S(2)}) async-start(bf16[32,32,2]{1,2,0:T(2,128)(2,1)} %fusion.24), calls=%async_computation.1 | async-start | bytes 32768 | tf_op jit(solution)/shard_map/all_to_all | solution.py:102
  96.0 14.9 %copy-start.8 = (s32[1024]{0:T(1024)S(1)}, s32[1024]{0:T(1024)}, u32[]{:S(2)}) copy-start(s32[1024]{0:T(1024)} %param.17) | copy-start | bytes 12292
  96.0 14.9 %copy-start.1 = (bf16[128,512]{1,0:T(8,128)(2,1)S(1)}, bf16[128,512]{1,0:T(8,128)(2,1)}, u32[]{:S(2)}) copy-start(bf16[128,512]{1,0:T(8,128)(2,1)} %param.13) | copy-start | bytes 393220
  105.8 61.0 %all-to-all-start.2 = ((bf16[32,2,16,512]{3,2,1,0:T(8,128)(2,1)}), bf16[32,2,16,512]{3,2,1,0:T(8,128)(2,1)}, u32[]{:S(2)}, u32[]{:S(2)}) async-start(bf16[32,2,16,512]{3,2,1,0:T(8,128)(2,1)} %bitcast.101), calls=%async_computation.2 | async-start | bytes 2097152 | tf_op jit(solution)/shard_map/all_to_all | solution.py:78
  166.8 60.4 %all-to-all-start = ((bf16[32,32,512]{2,1,0:T(8,128)(2,1)}), bf16[32,32,512]{2,1,0:T(8,128)(2,1)S(1)}, u32[]{:S(2)}, u32[]{:S(2)}) async-start(bf16[32,32,512]{2,1,0:T(8,128)(2,1)} %bitcast.176), calls=%async_computation | async-start | bytes 2097152 | tf_op jit(solution)/shard_map/all_to_all | solution.py:99
  227.3 1.8 copy-start.2
  230.8 5.4 copy-start.9
  230.8 61.3 %all-to-all-start.3 = ((bf16[32,32,512]{2,1,0:T(8,128)(2,1)}), bf16[32,32,512]{2,1,0:T(8,128)(2,1)}, u32[]{:S(2)}, u32[]{:S(2)}) async-start(bf16[32,32,512]{2,1,0:T(8,128)(2,1)} %bitcast.178), calls=%async_computation.3 | async-start | bytes 2097152 | tf_op jit(solution)/shard_map/all_to_all | solution.py:109
  292.1 2.2 copy-start.10
  294.3 1.9 copy-start.6
  296.1 1.5 copy-start.7
  297.6 61.2 %all-to-all-start.4 = ((bf16[32,32,512]{2,1,0:T(8,128)(2,1)}), bf16[32,32,512]{2,1,0:T(8,128)(2,1)}, u32[]{:S(2)}, u32[]{:S(2)}) async-start(bf16[32,32,512]{2,1,0:T(8,128)(2,1)} %bitcast.179), calls=%async_computation.4 | async-start | bytes 2097152 | tf_op jit(solution)/shard_map/all_to_all | solution.py:113
  362.8 6.4 copy-start.4
  363.9 61.2 %all-to-all-start.5 = ((bf16[2,32,16,512]{3,2,0,1:T(8,128)(2,1)}), bf16[2,32,16,512]{3,2,0,1:T(8,128)(2,1)}, u32[]{:S(2)}, u32[]{:S(2)}) async-start(bf16[2,32,16,512]{3,2,0,1:T(8,128)(2,1)} %pad_maximum_fusion), calls=%async_computation.5 | async-start | bytes 2097152 | tf_op jit(solution)/shard_map/all_to_all | solution.py:131
  369.2 2.0 copy-start.3
  425.0 128.4 %all-to-all-start.6 = ((bf16[32,32,512]{2,1,0:T(8,128)(2,1)}), bf16[32,32,512]{2,1,0:T(8,128)(2,1)S(1)}, u32[]{:S(2)}, u32[]{:S(2)}) async-start(bf16[32,32,512]{2,1,0:T(8,128)(2,1)} %bitcast.177), calls=%async_computation.6 | async-start | bytes 2097152 | tf_op jit(solution)/shard_map/all_to_all | solution.py:117
  429.7 126.9 %all-reduce.3.cloned.1.call-start = ((), (), s32[]{:S(2)}) async-start(), calls=%async_computation.7 | async-start | bytes 2097152 | tf_op jit(solution)/shard_map/psum | solution.py:139
  559.9 4.0 copy-start.5
Sparse Core Ops, SparseCore 0:
  434.3 117.1 all-reduce.2
where the time goes:
time: 665 us; the launch traced here: 661 us
  waiting for transfers between devices  269 us (40%)
  blocking collectives  207 us (31%)
  other arithmetic  69 us (10%)
  starting transfers between devices  47.2 us (7%)
  matrix products  27.3 us (4%)
  local copies, waits for them, and re-layouts  27 us (4%)
  between operations  14.4 us (2%)
    psum x1, blocking collectives, body(): pool_total = lax.psum(pool_part, ('rel', 'rep'))  118 us
    psum x1, blocking collectives, body(): lax.psum(rel_part.astype(jnp.bfloat16), 'rel').astype(jnp.float32)  88.6 us
    all_to_all x1, waiting for transfers between devices, body(): lax.all_to_all(dquery.reshape(nrel, cap, feats), 'rel', split_axis=0, con...  55.7 us
    all_to_all x1, waiting for transfers between devices, body(): lax.all_to_all(heads.reshape(nrel, cap, feats), 'rel', split_axis=0, conc...  53.3 us
    all_to_all x1, waiting for transfers between devices, body(): lax.all_to_all(dmats.reshape(per_owner, nrel, rows_dev, feats), 'rel', sp...  50.8 us
    all_to_all x1, waiting for transfers between devices, body(): lax.all_to_all(query.reshape(nrel, cap, feats), 'rel', split_axis=0, conc...  50.8 us
    all_to_all x1, waiting for transfers between devices, body(): lax.all_to_all(partial_mats.reshape(nrel, per_owner, rows_dev, feats), 'r...  50.7 us
    select_n x1, other arithmetic, body(): rank_slot = jnp.take(rank, rel_ids)  40.6 us
  transfers between devices with their start and end apart: 8, of which 6 were waited for; matrix products, arithmetic and copies ran while one was open for 5% of the time, Pallas kernels for 0%

commit v1 on v0

v1 whole, which is shorter than its diff:
```python
import jax
import jax.numpy as jnp
from jax import lax
from jax.sharding import Mesh, PartitionSpec as P

ZH, ZL, CORES, REPS = 4, 4, 2, 16
Z = ZH * ZL
REL = ("zh", "zl", "core")
REP = ("y", "x")
LINE = ("zh", "zl")
NEAR = (1, 2, 3)
EXTRA = 16
F32 = jnp.float32
BF16 = jnp.bfloat16


def order_tables(owner_of, per_owner):
    count = owner_of.shape[0]
    index = jnp.arange(count, dtype=jnp.int32)
    same = owner_of[:, None] == owner_of[None, :]
    rank = jnp.sum((same & (index[None, :] < index[:, None])).astype(jnp.int32), axis=1)
    return (rank, owner_of * per_owner + rank)


def exchange(blocks, axis):
    return lax.all_to_all(blocks, axis, split_axis=0, concat_axis=0, tiled=True)


def spread(block, axis, count):
    return exchange(jnp.broadcast_to(block[None], (count,) + block.shape), axis)


def near_step(near):
    pairs = []
    for z in range(Z):
        for core in range(CORES):
            step = {1: 1, 2: 2 if core == 0 else -2, 3: -1}[near]
            pairs.append((z * CORES + core, (z + step) % Z * CORES + core))
    return pairs


def swap_core(block):
    return lax.ppermute(block, "core", [(0, 1), (1, 0)])


def body(core, rel_emb, ents, pool, owner_of, rel_ids, head_ids, tail_ids, fill):
    rels, feats_rel = rel_emb.shape
    rows_dev, _, feats = core.shape
    owners = fill.shape[1]
    cap = rel_ids.shape[0] // owners
    per_owner = rels // owners
    own = owners // REPS
    mine = own * per_owner
    seats = own * cap
    ent_rows = ents.shape[0]
    pool_rows = pool.shape[0]
    scale = 1.0 / REPS
    g = lax.axis_index(REP)
    zl = lax.axis_index("zl")
    c = lax.axis_index("core")

    rank, slot_of = order_tables(owner_of, per_owner)
    qindex = jnp.arange(rels, dtype=jnp.int32)
    order_sel = (slot_of[None, :] == qindex[:, None]).astype(BF16)
    ordered = jnp.dot(order_sel, rel_emb, preferred_element_type=F32).astype(BF16)

    own_rows = lax.dynamic_slice_in_dim(ordered, g * mine, mine, 0)
    part = jnp.einsum("wk,akb->wab", own_rows, core, preferred_element_type=F32).astype(BF16)
    far = spread(part, "zh", ZH)
    near = [far] + [lax.ppermute(far, REL, near_step(s)) for s in NEAR]
    half = jnp.stack(near)
    half = jnp.take(half, (zl - jnp.arange(ZL)) % ZL, axis=0)
    other = swap_core(half)
    both = jnp.where(c == 0, jnp.stack([half, other]), jnp.stack([other, half]))
    mats = jnp.transpose(both, (3, 2, 1, 0, 4, 5)).reshape(own, per_owner * feats, feats)

    relhot = rel_ids[None, :] == jnp.arange(rels, dtype=jnp.int32)[:, None]
    rank_slot = jnp.sum(jnp.where(relhot, rank[:, None], 0), axis=0)
    used = (jnp.arange(cap, dtype=jnp.int32)[None, :] < fill[0][:, None]).astype(jnp.int32)
    numbers = jnp.concatenate(
        [a.reshape(REPS, seats) for a in (head_ids, tail_ids, rank_slot, used)], axis=1
    ).astype(BF16)
    numbers = jnp.pad(numbers[:, None, :], ((0, 0), (0, EXTRA - 1), (0, feats - 4 * seats)))
    sent = jnp.concatenate(
        [jnp.broadcast_to(ents[None], (REPS, ent_rows, feats)), numbers], axis=1
    )
    got = exchange(sent, REP)
    table = got[:, :ent_rows]
    line = got[:, ent_rows].astype(jnp.int32)
    hot = (
        line[:, None, : 2 * seats] == jnp.arange(ent_rows, dtype=jnp.int32)[None, :, None]
    ).astype(BF16)
    rows = jnp.einsum("sen,sef->snf", hot, table, preferred_element_type=F32).astype(BF16)

    def by_owner(a):
        a = a.reshape((REPS, own, cap) + a.shape[2:])
        return jnp.swapaxes(a, 0, 1).reshape((own, REPS * cap) + a.shape[3:])

    def by_source(a):
        a = a.reshape((own, REPS, cap) + a.shape[2:])
        return jnp.swapaxes(a, 0, 1).reshape((REPS, seats) + a.shape[3:])

    heads = by_owner(rows[:, :seats])
    tails = by_owner(rows[:, seats:])
    rank_got = by_owner(line[:, 2 * seats : 3 * seats])
    live = by_owner(line[:, 3 * seats : 4 * seats]).astype(F32)
    mask = [live * (rank_got == w).astype(F32) for w in range(per_owner)]
    masks = [m[..., None].astype(BF16) for m in mask]
    heads_wide = jnp.concatenate([m * heads for m in masks], axis=-1)

    query = jnp.einsum("oni,oif->onf", heads_wide, mats, preferred_element_type=F32).astype(BF16)
    qfloat = query.astype(F32)
    positive = jnp.sum(qfloat * tails.astype(F32), axis=-1)
    negative = jnp.einsum("onf,pf->onp", query, pool, preferred_element_type=F32)
    gpos = -jax.nn.sigmoid(-positive) * live * scale
    gneg = (jax.nn.sigmoid(negative) * (live * scale / pool_rows)[..., None]).astype(BF16)
    dquery = (
        gpos[..., None] * tails.astype(F32)
        + jnp.einsum("onp,pf->onf", gneg, pool, preferred_element_type=F32)
    ).astype(BF16)
    dtail = (gpos[..., None] * qfloat).astype(BF16)
    dpool = jnp.einsum("onp,onf->pf", gneg, query, preferred_element_type=F32).astype(BF16)
    dmats = jnp.einsum("oni,onf->oif", heads_wide, dquery, preferred_element_type=F32)

    dm = dmats.reshape(mine, ZH, ZL, CORES, rows_dev, feats)
    dm = jnp.transpose(dm, (3, 2, 1, 0, 4, 5))
    kept = lax.dynamic_index_in_dim(dm, c, 0, keepdims=False)
    given = lax.dynamic_index_in_dim(dm, 1 - c, 0, keepdims=False).astype(BF16)
    pair = (kept + swap_core(given).astype(F32)).astype(BF16)
    pair = jnp.take(pair, (zl + jnp.arange(ZL)) % ZL, axis=0)
    total = pair[0].astype(F32)
    for s in NEAR:
        total = total + lax.ppermute(pair[s], REL, near_step(s)).astype(F32)
    total = exchange(total.astype(BF16), "zh")
    own_sum = jnp.sum(total.astype(F32), axis=0).astype(BF16)

    dwide = jnp.concatenate([m * dquery for m in masks], axis=-1)
    mats4 = mats.reshape(own, per_owner, feats, feats)
    dhead = jnp.einsum(
        "onwf,owif->oni",
        dwide.reshape(own, REPS * cap, per_owner, feats),
        mats4,
        preferred_element_type=F32,
    ).astype(BF16)
    grads = jnp.concatenate([by_source(dhead), by_source(dtail)], axis=1)
    ent_part = jnp.einsum("sen,snf->sef", hot, grads, preferred_element_type=F32).astype(BF16)
    back = exchange(
        jnp.concatenate([ent_part, dpool.reshape(REPS, pool_rows // REPS, feats)], axis=1), REP
    )
    back = jnp.sum(back.astype(F32), axis=0)
    ent_grad = back[:ent_rows].astype(BF16)
    pool_own = back[ent_rows:].astype(BF16)

    all_rows = spread(own_sum, REP, REPS).reshape(rels, rows_dev, feats)
    core_grad = jnp.einsum(
        "qk,qab->akb", ordered, all_rows, preferred_element_type=F32
    ).astype(BF16)

    own_rel = jnp.einsum("wab,akb->wk", own_sum, core, preferred_element_type=F32).astype(BF16)
    small = jnp.concatenate(
        [pool_own, jnp.pad(own_rel.reshape(1, feats), ((0, 15), (0, 0)))], axis=0
    )
    small = jnp.sum(spread(small, LINE, Z).astype(F32), axis=0)
    small = (small + swap_core(small)).astype(BF16)
    small = spread(small, REP, REPS)
    pool_grad = small[:, : pool_rows // REPS].reshape(pool_rows, feats)
    rel_ordered = small[:, pool_rows // REPS].reshape(rels, feats_rel)
    rel_grad = lax.dot_general(
        order_sel, rel_ordered, (((0,), (0,)), ((), ())), preferred_element_type=F32
    )
    return (core_grad, rel_grad, ent_grad, pool_grad)


def solution(mesh):
    cut = Mesh(mesh.devices.reshape(ZH, ZL, CORES, 4, 4), REL + REP)
    whole = REL + REP
    return jax.shard_map(
        body,
        mesh=cut,
        in_specs=(
            P(REL, None, None),
            P(),
            P(whole, None),
            P(),
            P(),
            P(whole),
            P(whole),
            P(whole),
            P(whole, None),
        ),
        out_specs=(P(REL, None, None), P(), P(whole, None), P()),
        check_vma=False,
    )
```

time: 665 us -> 266 us (0.40)
  the two profiles are of different devices: /device:TPU:1 before, /device:TPU:32 now
where the time goes in v1:
time: 266 us; the launch traced here: 264 us
  waiting for transfers between devices  127 us (48%)
  starting transfers between devices  68.2 us (26%)
  local copies, waits for them, and re-layouts  28.1 us (11%)
  other arithmetic  22.4 us (8%)
  matrix products  16.9 us (6%)
    all_to_all x7, waiting for transfers between devices, exchange(): return lax.all_to_all(blocks, axis, split_axis=0, concat_axis=0, tiled=True)  108 us
    all_to_all x7, starting transfers between devices, exchange(): return lax.all_to_all(blocks, axis, split_axis=0, concat_axis=0, tiled=True)  46.1 us
    unnamed x38, local copies, waits for them, and re-layouts  9.87 us
    ppermute x3, waiting for transfers between devices, body(): near = [far] + [lax.ppermute(far, REL, near_step(s)) for s in NEAR]  8.9 us
    ppermute x3, starting transfers between devices, body(): near = [far] + [lax.ppermute(far, REL, near_step(s)) for s in NEAR]  8.26 us
    ppermute x3, starting transfers between devices, body(): total = total + lax.ppermute(pair[s], REL, near_step(s)).astype(F32)  8.13 us
    ppermute x3, waiting for transfers between devices, body(): total = total + lax.ppermute(pair[s], REL, near_step(s)).astype(F32)  6.08 us
    ppermute x3, starting transfers between devices, swap_core(): return lax.ppermute(block, 'core', [(0, 1), (1, 0)])  5.74 us
  transfers between devices with their start and end apart: 16, of which 14 were waited for; matrix products, arithmetic and copies ran while one was open for 12% of the time, Pallas kernels for 0%

profile of v1, /device:TPU:32, one launch (start us, length us, event | category | flops | bytes accessed | tf_op | source)
XLA Modules:
  0.0 264.1 jit_solution(4912926398517703116)
XLA Ops:
  0.7 1.0 convert_reduce_fusion.1
  2.4 0.8 convolution_convert_fusion.2
  4.4 14.2 %all-to-all-start.1 = ((bf16[4,4,16,512]{3,2,1,0:T(8,128)(2,1)}), bf16[4,4,16,512]{3,2,1,0:T(8,128)(2,1)S(1)}, u32[]{:S(2)}, u32[]{:S(2)}) async-start(bf16[4,4,16,512]{3,2,1,0:T(8,128)(2,1)} %broadcast_in_dim.34), calls=%async_computation.1 | async-start | bytes 524288 | tf_op jit(solution)/shard_map/all_to_all | solution.py:26
  20.8 1.6 pad_maximum_fusion
  22.5 17.0 %all-to-all-done.1 = bf16[4,4,16,512]{3,2,1,0:T(8,128)(2,1)S(1)} async-done(((bf16[4,4,16,512]{3,2,1,0:T(8,128)(2,1)}), bf16[4,4,16,512]{3,2,1,0:T(8,128)(2,1)S(1)}, u32[]{:S(2)}, u32[]{:S(2)}) %all-to-all-start.1) | async-done | bytes 262176 | tf_op jit(solution)/shard_map/all_to_all | solution.py:26
  39.4 7.1 %all-to-all-start = ((bf16[16,144,512]{2,1,0:T(8,128)(2,1)}), bf16[16,144,512]{2,1,0:T(8,128)(2,1)}, u32[]{:S(2)}, u32[]{:S(2)}) async-start(bf16[16,144,512]{2,1,0:T(8,128)(2,1)} %pad_maximum_fusion), calls=%async_computation | async-start | bytes 4718592 | tf_op jit(solution)/shard_map/all_to_all | solution.py:26
  46.5 1.9 collective-permute-start.1
  48.5 4.4 %collective-permute-start.2 = (bf16[4,4,16,512]{3,2,1,0:T(8,128)(2,1)S(1)}, bf16[4,4,16,512]{3,2,1,0:T(8,128)(2,1)S(1)}, u32[]{:S(2)}, u32[]{:S(2)}) collective-permute-start(bf16[4,4,16,512]{3,2,1,0:T(8,128)(2,1)S(1)} %all-to-all-done.1), channel_id=1, source_target_pairs={{0,480},{16,496},{32,0},{48,16},{64,32},{80,48},{96,64},{112,80},{... | collective-permute-start | bytes 786440 | tf_op jit(solution)/shard_map/ppermute | solution.py:70
  52.9 1.9 collective-permute-start
  54.9 4.9 %collective-permute-done.1 = bf16[4,4,16,512]{3,2,1,0:T(8,128)(2,1)S(1)} collective-permute-done((bf16[4,4,16,512]{3,2,1,0:T(8,128)(2,1)S(1)}, bf16[4,4,16,512]{3,2,1,0:T(8,128)(2,1)S(1)}, u32[]{:S(2)}, u32[]{:S(2)}) %collective-permute-start.1) | collective-permute-done | bytes 262176 | tf_op jit(solution)/shard_map/ppermute | solution.py:70
  59.8 4.0 %collective-permute-done = bf16[4,4,16,512]{3,2,1,0:T(8,128)(2,1)S(1)} collective-permute-done((bf16[4,4,16,512]{3,2,1,0:T(8,128)(2,1)S(1)}, bf16[4,4,16,512]{3,2,1,0:T(8,128)(2,1)S(1)}, u32[]{:S(2)}, u32[]{:S(2)}) %collective-permute-start) | collective-permute-done | bytes 262176 | tf_op jit(solution)/shard_map/ppermute | solution.py:70
  63.8 1.1 pad_maximum_fusion.6
  64.9 1.8 gather_fusion
  66.7 1.1 broadcast_select_fusion.1
  67.9 1.9 collective-permute-start.3
  70.0 2.8 %collective-permute-done.3 = bf16[4,4,4,16,512]{4,3,2,1,0:T(8,128)(2,1)} collective-permute-done((bf16[4,4,4,16,512]{4,3,2,1,0:T(8,128)(2,1)}, bf16[4,4,4,16,512]{4,3,2,1,0:T(8,128)(2,1)}, u32[]{:S(2)}, u32[]{:S(2)}) %collective-permute-start.3) | collective-permute-done | bytes 1048608 | tf_op jit(solution)/shard_map/ppermute | solution.py:43
  72.7 1.9 fusion.7
  74.6 1.6 copy.133
  76.2 2.5 all-to-all-done
  78.6 0.9 slice_convert_fusion
  80.2 2.4 fusion.19
  83.8 1.2 copy-done.3
  85.0 1.3 fusion
  87.3 1.7 broadcast_multiply_fusion.1
  89.0 1.3 fusion.28
  90.3 1.9 copy-done.1
  92.2 1.2 fusion.33
  93.4 1.9 collective-permute-start.4
  95.3 3.0 %pad_maximum_fusion.3 = bf16[2,512,1024]{2,1,0:T(8,128)(2,1)} fusion(bf16[2,512,512]{2,1,0:T(8,128)(2,1)} %get-tuple-element.32, bf16[2,512,512]{2,1,0:T(8,128)(2,1)S(1)} %get-tuple-element.31), kind=kLoop, calls=%fused_computation.16 | loop fusion | flops 4194304 | bytes 4194304 | tf_op jit(solution)/shard_map/concatenate | solution.py:137
  98.3 1.7 fusion.13
  100.0 1.6 gather_fusion.1
  101.6 1.5 broadcast_select_fusion
  103.2 2.8 %collective-permute-start.5 = (bf16[4,4,16,512]{3,2,1,0:T(8,128)(2,1)S(1)}, bf16[4,4,16,512]{3,2,1,0:T(8,128)(2,1)S(1)}, u32[]{:S(2)}, u32[]{:S(2)}) collective-permute-start(bf16[4,4,16,512]{3,2,1,0:T(8,128)(2,1)S(1)} %get-tuple-element.33), channel_id=1, source_target_pairs={{0,32},{16,48},{32,64},{48,80},{64,96},{80,112},{96,128},{112,144}... | collective-permute-start | bytes 786440 | tf_op jit(solution)/shard_map/ppermute | solution.py:133
  106.1 1.9 collective-permute-start.6
  108.0 3.4 %collective-permute-start.7 = (bf16[4,4,16,512]{3,2,1,0:T(8,128)(2,1)S(1)}, bf16[4,4,16,512]{3,2,1,0:T(8,128)(2,1)S(1)}, u32[]{:S(2)}, u32[]{:S(2)}) collective-permute-start(bf16[4,4,16,512]{3,2,1,0:T(8,128)(2,1)S(1)} %get-tuple-element.34), channel_id=1, source_target_pairs={{0,480},{16,496},{32,0},{48,16},{64,32},{80,48},{96,64},{112,80},{... | collective-permute-start | bytes 786440 | tf_op jit(solution)/shard_map/ppermute | solution.py:133
  111.4 3.9 %bitcast_convert_fusion = bf16[2,512,512]{2,1,0:T(8,128)(2,1)} fusion(bf16[2,2,512,512]{3,2,1,0:T(8,128)(2,1)S(1)} %bitcast.135, bf16[2,64,2,8,512]{4,3,2,1,0:T(8,128)(2,1)} %bitcast.136), kind=kOutput, calls=%fused_computation.26 | convolution fusion | flops 1074266112 | bytes 5242880 | tf_op jit(solution)/shard_map/onwf,owif->oni/dot_general | solution.py:139
  115.9 3.4 %collective-permute-done.6 = bf16[4,4,16,512]{3,2,1,0:T(8,128)(2,1)S(1)} collective-permute-done((bf16[4,4,16,512]{3,2,1,0:T(8,128)(2,1)S(1)}, bf16[4,4,16,512]{3,2,1,0:T(8,128)(2,1)S(1)}, u32[]{:S(2)}, u32[]{:S(2)}) %collective-permute-start.6) | collective-permute-done | bytes 262176 | tf_op jit(solution)/shard_map/ppermute | solution.py:133
  119.4 2.0 collective-permute-done.7
  121.3 0.9 fusion.41
  122.2 4.6 %all-to-all-start.2 = ((bf16[4,4,16,512]{3,2,1,0:T(8,128)(2,1)}), bf16[4,4,16,512]{3,2,1,0:T(8,128)(2,1)S(1)}, u32[]{:S(2)}, u32[]{:S(2)}) async-start(bf16[4,4,16,512]{3,2,1,0:T(8,128)(2,1)} %fusion.41), calls=%async_computation.2 | async-start | bytes 524288 | tf_op jit(solution)/shard_map/all_to_all | solution.py:26
  127.1 0.9 copy-done.8
  128.2 0.9 copy-done.10
  130.3 1.6 pad_maximum_fusion.1
  131.9 15.9 %all-to-all-done.2 = bf16[4,4,16,512]{3,2,1,0:T(8,128)(2,1)S(1)} async-done(((bf16[4,4,16,512]{3,2,1,0:T(8,128)(2,1)}), bf16[4,4,16,512]{3,2,1,0:T(8,128)(2,1)S(1)}, u32[]{:S(2)}, u32[]{:S(2)}) %all-to-all-start.2) | async-done | bytes 262176 | tf_op jit(solution)/shard_map/all_to_all | solution.py:26
  147.9 5.2 %all-to-all-start.4 = ((bf16[16,144,512]{2,1,0:T(8,128)(2,1)}), bf16[16,144,512]{2,1,0:T(8,128)(2,1)}, u32[]{:S(2)}, u32[]{:S(2)}) async-start(bf16[16,144,512]{2,1,0:T(8,128)(2,1)} %pad_maximum_fusion.1), calls=%async_computation.4 | async-start | bytes 4718592 | tf_op jit(solution)/shard_map/all_to_all | solution.py:26
  153.7 34.6 %all-to-all-done.4 = bf16[16,144,512]{2,1,0:T(8,128)(2,1)} async-done(((bf16[16,144,512]{2,1,0:T(8,128)(2,1)}), bf16[16,144,512]{2,1,0:T(8,128)(2,1)}, u32[]{:S(2)}, u32[]{:S(2)}) %all-to-all-start.4) | async-done | bytes 2359328 | tf_op jit(solution)/shard_map/all_to_all | solution.py:26
  188.3 2.0 reduce.1
  190.3 0.8 broadcast_in_dim.36
  191.2 6.3 %all-to-all-start.5 = ((bf16[16,32,512]{2,1,0:T(8,128)(2,1)}), bf16[16,32,512]{2,1,0:T(8,128)(2,1)S(1)}, u32[]{:S(2)}, u32[]{:S(2)}) async-start(bf16[16,32,512]{2,1,0:T(8,128)(2,1)} %broadcast_in_dim.36), calls=%async_computation.5 | async-start | bytes 1048576 | tf_op jit(solution)/shard_map/all_to_all | solution.py:26
  197.5 27.7 %all-to-all-done.5 = bf16[16,32,512]{2,1,0:T(8,128)(2,1)S(1)} async-done(((bf16[16,32,512]{2,1,0:T(8,128)(2,1)}), bf16[16,32,512]{2,1,0:T(8,128)(2,1)S(1)}, u32[]{:S(2)}, u32[]{:S(2)}) %all-to-all-start.5) | async-done | bytes 524320 | tf_op jit(solution)/shard_map/all_to_all | solution.py:26
  225.2 1.4 broadcast_in_dim.35
  226.6 4.5 %all-to-all-start.3 = ((bf16[16,4,16,512]{3,1,2,0:T(4,128)(2,1)}), bf16[16,4,16,512]{3,1,2,0:T(4,128)(2,1)S(1)}, u32[]{:S(2)}, u32[]{:S(2)}) async-start(bf16[16,4,16,512]{3,1,2,0:T(4,128)(2,1)} %broadcast_in_dim.35), calls=%async_computation.3 | async-start | bytes 2097152 | tf_op jit(solution)/shard_map/all_to_all | solution.py:26
  231.1 1.1 convert_reduce_fusion
  232.2 1.9 collective-permute-start.8
  234.2 1.2 collective-permute-done.8
  235.4 9.9 %all-to-all-done.3 = bf16[16,4,16,512]{3,1,2,0:T(4,128)(2,1)S(1)} async-done(((bf16[16,4,16,512]{3,1,2,0:T(4,128)(2,1)}), bf16[16,4,16,512]{3,1,2,0:T(4,128)(2,1)S(1)}, u32[]{:S(2)}, u32[]{:S(2)}) %all-to-all-start.3) | async-done | bytes 1048608 | tf_op jit(solution)/shard_map/all_to_all | solution.py:26
  245.4 0.8 broadcast_in_dim.37
  246.2 4.2 %all-to-all-start.6 = ((bf16[16,32,512]{2,1,0:T(8,128)(2,1)}), bf16[16,32,512]{2,1,0:T(8,128)(2,1)}, u32[]{:S(2)}, u32[]{:S(2)}) async-start(bf16[16,32,512]{2,1,0:T(8,128)(2,1)} %broadcast_in_dim.37), calls=%async_computation.6 | async-start | bytes 1048576 | tf_op jit(solution)/shard_map/all_to_all | solution.py:26
  251.1 1.5 copy.142
  252.6 1.3 reshape.220
  253.9 2.1 convert_bitcast_fusion.1
  256.0 3.9 %copy.149 = bf16[16,128,512]{2,1,0:T(8,128)(2,1)} copy(bf16[16,128,512]{1,2,0:T(8,128)(2,1)} %convert_bitcast_fusion.1) | data formatting | bytes 4194304
  260.6 1.0 slice_reduce_fusion
  262.4 1.7 slice.80
  (100 shorter events, 12.3 us)
Async XLA Ops:
  0.6 2.6 copy-start
  0.6 17.9 %copy-start.15 = (s32[1024]{0:T(1024)S(1)}, s32[1024]{0:T(1024)}, u32[]{:S(2)}) copy-start(s32[1024]{0:T(1024)} %param.16) | copy-start | bytes 12292
  0.7 18.6 %copy-start.16 = (s32[1,32]{1,0:T(1,128)S(1)}, s32[1,32]{1,0:T(1,128)}, u32[]{:S(2)}) copy-start(s32[1,32]{1,0:T(1,128)} %param.19) | copy-start | bytes 388
  0.7 19.6 %copy-start.13 = (s32[1024]{0:T(1024)S(1)}, s32[1024]{0:T(1024)}, u32[]{:S(2)}) copy-start(s32[1024]{0:T(1024)} %param.17) | copy-start | bytes 12292
  0.7 19.7 %copy-start.14 = (s32[1024]{0:T(1024)S(1)}, s32[1024]{0:T(1024)}, u32[]{:S(2)}) copy-start(s32[1024]{0:T(1024)} %param.18) | copy-start | bytes 12292
  0.7 19.9 %copy-start.12 = (bf16[128,512]{1,0:T(8,128)(2,1)S(1)}, bf16[128,512]{1,0:T(8,128)(2,1)}, u32[]{:S(2)}) copy-start(bf16[128,512]{1,0:T(8,128)(2,1)} %param.13) | copy-start | bytes 393220
  4.4 35.1 %all-to-all-start.1 = ((bf16[4,4,16,512]{3,2,1,0:T(8,128)(2,1)}), bf16[4,4,16,512]{3,2,1,0:T(8,128)(2,1)S(1)}, u32[]{:S(2)}, u32[]{:S(2)}) async-start(bf16[4,4,16,512]{3,2,1,0:T(8,128)(2,1)} %broadcast_in_dim.34), calls=%async_computation.1 | async-start | bytes 524288 | tf_op jit(solution)/shard_map/all_to_all | solution.py:26
  39.4 39.2 %all-to-all-start = ((bf16[16,144,512]{2,1,0:T(8,128)(2,1)}), bf16[16,144,512]{2,1,0:T(8,128)(2,1)}, u32[]{:S(2)}, u32[]{:S(2)}) async-start(bf16[16,144,512]{2,1,0:T(8,128)(2,1)} %pad_maximum_fusion), calls=%async_computation | async-start | bytes 4718592 | tf_op jit(solution)/shard_map/all_to_all | solution.py:26
  46.5 13.2 %collective-permute-start.1 = (bf16[4,4,16,512]{3,2,1,0:T(8,128)(2,1)S(1)}, bf16[4,4,16,512]{3,2,1,0:T(8,128)(2,1)S(1)}, u32[]{:S(2)}, u32[]{:S(2)}) collective-permute-start(bf16[4,4,16,512]{3,2,1,0:T(8,128)(2,1)S(1)} %all-to-all-done.1), channel_id=1, source_target_pairs={{0,64},{16,464},{32,96},{48,496},{64,128},{80,16},{96,160},{112,48... | collective-permute-start | bytes 786440 | tf_op jit(solution)/shard_map/ppermute | solution.py:70
  48.5 11.3 %collective-permute-start.2 = (bf16[4,4,16,512]{3,2,1,0:T(8,128)(2,1)S(1)}, bf16[4,4,16,512]{3,2,1,0:T(8,128)(2,1)S(1)}, u32[]{:S(2)}, u32[]{:S(2)}) collective-permute-start(bf16[4,4,16,512]{3,2,1,0:T(8,128)(2,1)S(1)} %all-to-all-done.1), channel_id=1, source_target_pairs={{0,480},{16,496},{32,0},{48,16},{64,32},{80,48},{96,64},{112,80},{... | collective-permute-start | bytes 786440 | tf_op jit(solution)/shard_map/ppermute | solution.py:70
  52.9 10.9 %collective-permute-start = (bf16[4,4,16,512]{3,2,1,0:T(8,128)(2,1)S(1)}, bf16[4,4,16,512]{3,2,1,0:T(8,128)(2,1)S(1)}, u32[]{:S(2)}, u32[]{:S(2)}) collective-permute-start(bf16[4,4,16,512]{3,2,1,0:T(8,128)(2,1)S(1)} %all-to-all-done.1), channel_id=1, source_target_pairs={{0,32},{16,48},{32,64},{48,80},{64,96},{80,112},{96,128},{112,144}... | collective-permute-start | bytes 786440 | tf_op jit(solution)/shard_map/ppermute | solution.py:70
  67.9 4.9 %collective-permute-start.3 = (bf16[4,4,4,16,512]{4,3,2,1,0:T(8,128)(2,1)}, bf16[4,4,4,16,512]{4,3,2,1,0:T(8,128)(2,1)}, u32[]{:S(2)}, u32[]{:S(2)}) collective-permute-start(bf16[4,4,4,16,512]{4,3,2,1,0:T(8,128)(2,1)} %broadcast_select_fusion.1), channel_id=1, source_target_pairs={{0,16},{16,0},{1,17},{17,1},{2,18},{18,2},{3,19},{19,3},{4,20},{20... | collective-permute-start | bytes 3145736 | tf_op jit(solution)/shard_map/ppermute | solution.py:43
  83.4 1.6 copy-start.3
  85.0 1.4 copy-start.11
  86.3 1.0 copy-start.6
  87.3 1.7 copy-start.9
  90.3 1.9 copy-start.1
  93.4 5.0 %collective-permute-start.4 = (bf16[4,4,4,16,512]{4,3,2,1,0:T(8,128)(2,1)}, bf16[4,4,4,16,512]{4,3,2,1,0:T(8,128)(2,1)}, u32[]{:S(2)}, u32[]{:S(2)}) collective-permute-start(bf16[4,4,4,16,512]{4,3,2,1,0:T(8,128)(2,1)} %fusion.33), channel_id=1, source_target_pairs={{0,16},{16,0},{1,17},{17,1},{2,18},{18,2},{3,19},{19,3},{4,20},{20... | collective-permute-start | bytes 3145736 | tf_op jit(solution)/shard_map/ppermute | solution.py:43
  95.3 3.0 %copy-start.2 = (f32[2,1024,512]{2,1,0:T(8,128)S(1)}, f32[2,1024,512]{2,1,0:T(8,128)}, u32[]{:S(2)}) copy-start(f32[2,1024,512]{2,1,0:T(8,128)} %copy-done.1) | copy-start | bytes 12582916
  101.6 9.8 %copy-start.4 = (bf16[4,4,4,2,16,512]{5,4,3,2,1,0:T(8,128)(2,1)S(1)}, bf16[4,4,4,2,16,512]{5,4,3,2,1,0:T(8,128)(2,1)}, u32[]{:S(2)}) copy-start(bf16[4,4,4,2,16,512]{5,4,3,2,1,0:T(8,128)(2,1)} %copy.133) | copy-start | bytes 6291460
  103.2 12.7 %collective-permute-start.5 = (bf16[4,4,16,512]{3,2,1,0:T(8,128)(2,1)S(1)}, bf16[4,4,16,512]{3,2,1,0:T(8,128)(2,1)S(1)}, u32[]{:S(2)}, u32[]{:S(2)}) collective-permute-start(bf16[4,4,16,512]{3,2,1,0:T(8,128)(2,1)S(1)} %get-tuple-element.33), channel_id=1, source_target_pairs={{0,32},{16,48},{32,64},{48,80},{64,96},{80,112},{96,128},{112,144}... | collective-permute-start | bytes 786440 | tf_op jit(solution)/shard_map/ppermute | solution.py:133
  106.1 13.3 %collective-permute-start.6 = (bf16[4,4,16,512]{3,2,1,0:T(8,128)(2,1)S(1)}, bf16[4,4,16,512]{3,2,1,0:T(8,128)(2,1)S(1)}, u32[]{:S(2)}, u32[]{:S(2)}) collective-permute-start(bf16[4,4,16,512]{3,2,1,0:T(8,128)(2,1)S(1)} %get-tuple-element.35), channel_id=1, source_target_pairs={{0,64},{16,464},{32,96},{48,496},{64,128},{80,16},{96,160},{112,48... | collective-permute-start | bytes 786440 | tf_op jit(solution)/shard_map/ppermute | solution.py:133
  108.0 13.3 %collective-permute-start.7 = (bf16[4,4,16,512]{3,2,1,0:T(8,128)(2,1)S(1)}, bf16[4,4,16,512]{3,2,1,0:T(8,128)(2,1)S(1)}, u32[]{:S(2)}, u32[]{:S(2)}) collective-permute-start(bf16[4,4,16,512]{3,2,1,0:T(8,128)(2,1)S(1)} %get-tuple-element.34), channel_id=1, source_target_pairs={{0,480},{16,496},{32,0},{48,16},{64,32},{80,48},{96,64},{112,80},{... | collective-permute-start | bytes 786440 | tf_op jit(solution)/shard_map/ppermute | solution.py:133
  115.2 11.6 %copy-start.7 = (bf16[2,512,512]{2,1,0:T(8,128)(2,1)S(1)}, bf16[2,512,512]{2,1,0:T(8,128)(2,1)}, u32[]{:S(2)}) copy-start(bf16[2,512,512]{2,1,0:T(8,128)(2,1)} %copy-done.6) | copy-start | bytes 3145732
  122.2 25.7 %all-to-all-start.2 = ((bf16[4,4,16,512]{3,2,1,0:T(8,128)(2,1)}), bf16[4,4,16,512]{3,2,1,0:T(8,128)(2,1)S(1)}, u32[]{:S(2)}, u32[]{:S(2)}) async-start(bf16[4,4,16,512]{3,2,1,0:T(8,128)(2,1)} %fusion.41), calls=%async_computation.2 | async-start | bytes 524288 | tf_op jit(solution)/shard_map/all_to_all | solution.py:26
  126.8 1.2 copy-start.8
  128.1 1.0 copy-start.10
  147.9 40.4 %all-to-all-start.4 = ((bf16[16,144,512]{2,1,0:T(8,128)(2,1)}), bf16[16,144,512]{2,1,0:T(8,128)(2,1)}, u32[]{:S(2)}, u32[]{:S(2)}) async-start(bf16[16,144,512]{2,1,0:T(8,128)(2,1)} %pad_maximum_fusion.1), calls=%async_computation.4 | async-start | bytes 4718592 | tf_op jit(solution)/shard_map/all_to_all | solution.py:26
  191.2 34.0 %all-to-all-start.5 = ((bf16[16,32,512]{2,1,0:T(8,128)(2,1)}), bf16[16,32,512]{2,1,0:T(8,128)(2,1)S(1)}, u32[]{:S(2)}, u32[]{:S(2)}) async-start(bf16[16,32,512]{2,1,0:T(8,128)(2,1)} %broadcast_in_dim.36), calls=%async_computation.5 | async-start | bytes 1048576 | tf_op jit(solution)/shard_map/all_to_all | solution.py:26
  225.2 1.4 copy-start.5
  226.6 18.7 %all-to-all-start.3 = ((bf16[16,4,16,512]{3,1,2,0:T(4,128)(2,1)}), bf16[16,4,16,512]{3,1,2,0:T(4,128)(2,1)S(1)}, u32[]{:S(2)}, u32[]{:S(2)}) async-start(bf16[16,4,16,512]{3,1,2,0:T(4,128)(2,1)} %broadcast_in_dim.35), calls=%async_computation.3 | async-start | bytes 2097152 | tf_op jit(solution)/shard_map/all_to_all | solution.py:26
  232.2 3.1 %collective-permute-start.8 = (f32[32,512]{1,0:T(8,128)S(1)}, f32[32,512]{1,0:T(8,128)S(1)}, u32[]{:S(2)}, u32[]{:S(2)}) collective-permute-start(f32[32,512]{1,0:T(8,128)S(1)} %convert_reduce_fusion), channel_id=1, source_target_pairs={{0,16},{16,0},{1,17},{17,1},{2,18},{18,2},{3,19},{19,3},{4,20},{20... | collective-permute-start | bytes 196616 | tf_op jit(solution)/shard_map/ppermute | solution.py:43
  246.2 14.4 %all-to-all-start.6 = ((bf16[16,32,512]{2,1,0:T(8,128)(2,1)}), bf16[16,32,512]{2,1,0:T(8,128)(2,1)}, u32[]{:S(2)}, u32[]{:S(2)}) async-start(bf16[16,32,512]{2,1,0:T(8,128)(2,1)} %broadcast_in_dim.37), calls=%async_computation.6 | async-start | bytes 1048576 | tf_op jit(solution)/shard_map/all_to_all | solution.py:26

commit v2 on v1

--- a/solution.py
+++ b/solution.py
@@ -8,7 +8,7 @@
 REL = ("zh", "zl", "core")
 REP = ("y", "x")
 LINE = ("zh", "zl")
-NEAR = (1, 2, 3)
+STEPS = (0, 1, 2, 3)
 EXTRA = 16
 F32 = jnp.float32
 BF16 = jnp.bfloat16
@@ -30,13 +30,21 @@
     return exchange(jnp.broadcast_to(block[None], (count,) + block.shape), axis)
 
 
-def near_step(near):
+def near_by(step, core):
+    return jnp.where(step == 2, 2 - 4 * core, jnp.where(step == 3, -1, step))
+
+
+def near_move(block, step):
     pairs = []
     for z in range(Z):
         for core in range(CORES):
-            step = {1: 1, 2: 2 if core == 0 else -2, 3: -1}[near]
-            pairs.append((z * CORES + core, (z + step) % Z * CORES + core))
-    return pairs
+            by = (0, 1, 2 - 4 * core, -1)[step]
+            pairs.append((z * CORES + core, (z + by) % Z * CORES + core))
+    return lax.ppermute(block, REL, pairs)
+
+
+def far_move(block, step):
+    return lax.ppermute(block, LINE, [(z, (z + 4 * step) % Z) for z in range(Z)])
 
 
 def swap_core(block):
@@ -54,9 +62,10 @@
     seats = own * cap
     ent_rows = ents.shape[0]
     pool_rows = pool.shape[0]
+    pool_dev = pool_rows // (Z * CORES)
     scale = 1.0 / REPS
     g = lax.axis_index(REP)
-    zl = lax.axis_index("zl")
+    z = lax.axis_index(LINE)
     c = lax.axis_index("core")
 
     rank, slot_of = order_tables(owner_of, per_owner)
@@ -66,13 +75,20 @@
 
     own_rows = lax.dynamic_slice_in_dim(ordered, g * mine, mine, 0)
     part = jnp.einsum("wk,akb->wab", own_rows, core, preferred_element_type=F32).astype(BF16)
-    far = spread(part, "zh", ZH)
-    near = [far] + [lax.ppermute(far, REL, near_step(s)) for s in NEAR]
-    half = jnp.stack(near)
-    half = jnp.take(half, (zl - jnp.arange(ZL)) % ZL, axis=0)
+    far = jnp.stack([part] + [far_move(part, p) for p in STEPS[1:]])
+    half = jnp.stack([far] + [near_move(far, s) for s in STEPS[1:]])
+    half = half.reshape(Z, mine, rows_dev, feats)
     other = swap_core(half)
+    line_z = jnp.arange(Z, dtype=jnp.int32)
+
+    def in_order(blocks, core_of):
+        s = (z - line_z) % 4
+        p = ((z - near_by(s, core_of) - line_z) % Z) // 4
+        return jnp.take(blocks, s * 4 + p, axis=0)
+
+    half, other = in_order(half, c), in_order(other, 1 - c)
     both = jnp.where(c == 0, jnp.stack([half, other]), jnp.stack([other, half]))
-    mats = jnp.transpose(both, (3, 2, 1, 0, 4, 5)).reshape(own, per_owner * feats, feats)
+    mats = jnp.transpose(both, (2, 1, 0, 3, 4)).reshape(own, per_owner * feats, feats)
 
     relhot = rel_ids[None, :] == jnp.arange(rels, dtype=jnp.int32)[:, None]
     rank_slot = jnp.sum(jnp.where(relhot, rank[:, None], 0), axis=0)
@@ -119,20 +135,8 @@
         + jnp.einsum("onp,pf->onf", gneg, pool, preferred_element_type=F32)
     ).astype(BF16)
     dtail = (gpos[..., None] * qfloat).astype(BF16)
-    dpool = jnp.einsum("onp,onf->pf", gneg, query, preferred_element_type=F32).astype(BF16)
+    dpool = jnp.einsum("onp,onf->pf", gneg, query, preferred_element_type=F32)
     dmats = jnp.einsum("oni,onf->oif", heads_wide, dquery, preferred_element_type=F32)
-
-    dm = dmats.reshape(mine, ZH, ZL, CORES, rows_dev, feats)
-    dm = jnp.transpose(dm, (3, 2, 1, 0, 4, 5))
-    kept = lax.dynamic_index_in_dim(dm, c, 0, keepdims=False)
-    given = lax.dynamic_index_in_dim(dm, 1 - c, 0, keepdims=False).astype(BF16)
-    pair = (kept + swap_core(given).astype(F32)).astype(BF16)
-    pair = jnp.take(pair, (zl + jnp.arange(ZL)) % ZL, axis=0)
-    total = pair[0].astype(F32)
-    for s in NEAR:
-        total = total + lax.ppermute(pair[s], REL, near_step(s)).astype(F32)
-    total = exchange(total.astype(BF16), "zh")
-    own_sum = jnp.sum(total.astype(F32), axis=0).astype(BF16)
 
     dwide = jnp.concatenate([m * dquery for m in masks], axis=-1)
     mats4 = mats.reshape(own, per_owner, feats, feats)
@@ -144,30 +148,56 @@
     ).astype(BF16)
     grads = jnp.concatenate([by_source(dhead), by_source(dtail)], axis=1)
     ent_part = jnp.einsum("sen,snf->sef", hot, grads, preferred_element_type=F32).astype(BF16)
-    back = exchange(
-        jnp.concatenate([ent_part, dpool.reshape(REPS, pool_rows // REPS, feats)], axis=1), REP
-    )
-    back = jnp.sum(back.astype(F32), axis=0)
-    ent_grad = back[:ent_rows].astype(BF16)
-    pool_own = back[ent_rows:].astype(BF16)
-
-    all_rows = spread(own_sum, REP, REPS).reshape(rels, rows_dev, feats)
-    core_grad = jnp.einsum(
-        "qk,qab->akb", ordered, all_rows, preferred_element_type=F32
-    ).astype(BF16)
-
-    own_rel = jnp.einsum("wab,akb->wk", own_sum, core, preferred_element_type=F32).astype(BF16)
-    small = jnp.concatenate(
-        [pool_own, jnp.pad(own_rel.reshape(1, feats), ((0, 15), (0, 0)))], axis=0
-    )
-    small = jnp.sum(spread(small, LINE, Z).astype(F32), axis=0)
-    small = (small + swap_core(small)).astype(BF16)
-    small = spread(small, REP, REPS)
-    pool_grad = small[:, : pool_rows // REPS].reshape(pool_rows, feats)
-    rel_ordered = small[:, pool_rows // REPS].reshape(rels, feats_rel)
+
+    dm = dmats.reshape(mine, Z, CORES, rows_dev, feats)
+    dm = jnp.transpose(dm, (2, 1, 0, 3, 4)).reshape(CORES, Z, mine * rows_dev, feats)
+    dp = jnp.swapaxes(dpool.reshape(Z, CORES, pool_dev, feats), 0, 1)
+    dm = jnp.concatenate([dm, dp], axis=2)
+    kept = lax.dynamic_index_in_dim(dm, c, 0, keepdims=False)
+    given = lax.dynamic_index_in_dim(dm, 1 - c, 0, keepdims=False).astype(BF16)
+    pair = (kept + swap_core(given).astype(F32)).astype(BF16)
+    steps = jnp.arange(Z, dtype=jnp.int32) // 4
+    target = (z + near_by(steps, c) + 4 * (jnp.arange(Z, dtype=jnp.int32) % 4)) % Z
+    pair = jnp.take(pair, target, axis=0).reshape(4, 4, mine * rows_dev + pool_dev, feats)
+    pair, ent_part = lax.optimization_barrier((pair, ent_part))
+    back = exchange(ent_part, REP)
+    total = pair[0].astype(F32)
+    for s in STEPS[1:]:
+        total = total + near_move(pair[s], s).astype(F32)
+    total = total.astype(BF16)
+    own_sum = total[0].astype(F32)
+    for p in STEPS[1:]:
+        own_sum = own_sum + far_move(total[p], p).astype(F32)
+    own_sum = own_sum.astype(BF16)
+
+    own_sum, back = lax.optimization_barrier((own_sum, back))
+    ent_grad = jnp.sum(back.astype(F32), axis=0).astype(BF16)
+    all_sums = spread(own_sum, REP, REPS)
+    all_rows = all_sums[:, : mine * rows_dev].reshape(rels, rows_dev, feats)
+    pool_own = jnp.sum(all_sums[:, mine * rows_dev :].astype(F32), axis=0).astype(BF16)
+    rel_own = jnp.einsum("qab,akb->qk", all_rows, core, preferred_element_type=F32).astype(BF16)
+
+    rel_rows = rels * feats_rel // feats
+    pool_z = pool_own[None]
+    for axis in ("zh", "zl"):
+        small = spread(
+            jnp.concatenate([rel_own.reshape(rel_rows, feats), pool_z.reshape(-1, feats)]), axis, 4
+        )
+        rel_own = jnp.sum(small[:, :rel_rows].astype(F32), axis=0).astype(BF16)
+        pool_z = small[:, rel_rows:]
+    small = jnp.concatenate([rel_own, pool_z.reshape(-1, feats)])
+    small_other = swap_core(small)
+    rel_ordered = (small[:rel_rows].astype(F32) + small_other[:rel_rows].astype(F32)).astype(BF16)
+    rel_ordered = rel_ordered.reshape(rels, feats_rel)
+    halves = jnp.stack([small[rel_rows:], small_other[rel_rows:]])
+    halves = jnp.where(c == 0, halves, halves[::-1]).reshape(CORES, ZL, ZH, pool_dev, feats)
+    pool_grad = jnp.transpose(halves, (2, 1, 0, 3, 4)).reshape(pool_rows, feats)
     rel_grad = lax.dot_general(
         order_sel, rel_ordered, (((0,), (0,)), ((), ())), preferred_element_type=F32
     )
+    core_grad = jnp.einsum(
+        "qk,qab->akb", ordered, all_rows, preferred_element_type=F32
+    ).astype(BF16)
     return (core_grad, rel_grad, ent_grad, pool_grad)
 
 

time: 266 us -> 235 us (0.88)
  the two profiles are of different devices: /device:TPU:32 before, /device:TPU:1 now
where the time goes in v2:
time: 235 us; the launch traced here: 233 us
  starting transfers between devices  84.4 us (36%)
  blocking collectives  49.9 us (21%)
  waiting for transfers between devices  28 us (12%)
  local copies, waits for them, and re-layouts  26.9 us (11%)
  other arithmetic  25.7 us (11%)
  matrix products  16.9 us (7%)
    all_to_all x2, blocking collectives, exchange(): return lax.all_to_all(blocks, axis, split_axis=0, concat_axis=0, tiled=True)  49.9 us
    ppermute x6, starting transfers between devices, far_move(): lax.ppermute(block, LINE, [(z, (z + 4 * step) % Z) for z in range(Z)])  40 us
    ppermute x6, waiting for transfers between devices, near_move(): return lax.ppermute(block, REL, pairs)  20.7 us
    all_to_all x3, starting transfers between devices, exchange(): return lax.all_to_all(blocks, axis, split_axis=0, concat_axis=0, tiled=True)  16.8 us
    ppermute x6, starting transfers between devices, near_move(): return lax.ppermute(block, REL, pairs)  16 us
    ppermute x3, starting transfers between devices, swap_core(): return lax.ppermute(block, 'core', [(0, 1), (1, 0)])  11.6 us
    unnamed x31, local copies, waits for them, and re-layouts  10.4 us
    gather x2, local copies, waits for them, and re-layouts, in_order(): return jnp.take(blocks, s * 4 + p, axis=0)  7.19 us
  transfers between devices with their start and end apart: 18, of which 8 were waited for; matrix products, arithmetic and copies ran while one was open for 15% of the time, Pallas kernels for 0%

profile of v2, /device:TPU:1, one launch (start us, length us, event | category | flops | bytes accessed | tf_op | source)
XLA Modules:
  0.0 233.2 jit_solution(7560496075600050132)
XLA Ops:
  0.7 1.0 convert_reduce_fusion
  2.4 0.8 convolution_convert_fusion.2
  3.6 16.3 %collective-permute-start.1 = (bf16[4,16,512]{2,0,1:T(4,128)(2,1)S(1)}, bf16[4,16,512]{2,0,1:T(4,128)(2,1)S(1)}, u32[]{:S(2)}, u32[]{:S(2)}) collective-permute-start(bf16[4,16,512]{2,0,1:T(4,128)(2,1)S(1)} %convolution_convert_fusion.1), channel_id=1, source_target_pairs={{0,256},{32,288},{64,320},{96,352},{128,384},{160,416},{192,448},{... | collective-permute-start | bytes 196616 | tf_op jit(solution)/shard_map/ppermute | solution.py:47
  19.9 1.9 collective-permute-start.2
  21.8 7.3 %collective-permute-start = (bf16[4,16,512]{2,0,1:T(4,128)(2,1)S(1)}, bf16[4,16,512]{2,0,1:T(4,128)(2,1)S(1)}, u32[]{:S(2)}, u32[]{:S(2)}) collective-permute-start(bf16[4,16,512]{2,0,1:T(4,128)(2,1)S(1)} %convolution_convert_fusion.1), channel_id=1, source_target_pairs={{0,128},{32,160},{64,192},{96,224},{128,256},{160,288},{192,320},{... | collective-permute-start | bytes 196616 | tf_op jit(solution)/shard_map/ppermute | solution.py:47
  31.4 1.7 pad_maximum_fusion
  33.0 6.8 %all-to-all-start = ((bf16[16,144,512]{2,1,0:T(8,128)(2,1)}), bf16[16,144,512]{2,1,0:T(8,128)(2,1)}, u32[]{:S(2)}, u32[]{:S(2)}) async-start(bf16[16,144,512]{2,1,0:T(8,128)(2,1)} %pad_maximum_fusion), calls=%async_computation | async-start | bytes 4718592 | tf_op jit(solution)/shard_map/all_to_all | solution.py:26
  40.1 2.6 %collective-permute-start.3 = (bf16[4,4,16,512]{3,1,2,0:T(4,128)(2,1)S(1)}, bf16[4,4,16,512]{3,1,2,0:T(4,128)(2,1)S(1)}, u32[]{:S(2)}, u32[]{:S(2)}) collective-permute-start(bf16[4,4,16,512]{3,1,2,0:T(4,128)(2,1)S(1)} %pad_maximum_fusion.6), channel_id=1, source_target_pairs={{0,32},{16,48},{32,64},{48,80},{64,96},{80,112},{96,128},{112,144}... | collective-permute-start | bytes 786440 | tf_op jit(solution)/shard_map/ppermute | solution.py:43
  42.8 2.2 collective-permute-start.4
  44.9 3.6 %collective-permute-start.5 = (bf16[4,4,16,512]{3,1,2,0:T(4,128)(2,1)S(1)}, bf16[4,4,16,512]{3,1,2,0:T(4,128)(2,1)S(1)}, u32[]{:S(2)}, u32[]{:S(2)}) collective-permute-start(bf16[4,4,16,512]{3,1,2,0:T(4,128)(2,1)S(1)} %pad_maximum_fusion.6), channel_id=1, source_target_pairs={{0,480},{16,496},{32,0},{48,16},{64,32},{80,48},{96,64},{112,80},{... | collective-permute-start | bytes 786440 | tf_op jit(solution)/shard_map/ppermute | solution.py:43
  49.3 4.8 %collective-permute-done.4 = bf16[4,4,16,512]{3,1,2,0:T(4,128)(2,1)S(1)} collective-permute-done((bf16[4,4,16,512]{3,1,2,0:T(4,128)(2,1)S(1)}, bf16[4,4,16,512]{3,1,2,0:T(4,128)(2,1)S(1)}, u32[]{:S(2)}, u32[]{:S(2)}) %collective-permute-start.4) | collective-permute-done | bytes 262176 | tf_op jit(solution)/shard_map/ppermute | solution.py:43
  54.1 5.7 %collective-permute-done.5 = bf16[4,4,16,512]{3,1,2,0:T(4,128)(2,1)S(1)} collective-permute-done((bf16[4,4,16,512]{3,1,2,0:T(4,128)(2,1)S(1)}, bf16[4,4,16,512]{3,1,2,0:T(4,128)(2,1)S(1)}, u32[]{:S(2)}, u32[]{:S(2)}) %collective-permute-start.5) | collective-permute-done | bytes 262176 | tf_op jit(solution)/shard_map/ppermute | solution.py:43
  59.8 1.9 pad_maximum_fusion.5
  61.8 2.3 collective-permute-start.6
  64.2 3.6 %gather_fusion.1 = bf16[16,4,16,512]{3,1,2,0:T(4,128)(2,1)} fusion(bf16[16,4,16,512]{3,1,2,0:T(4,128)(2,1)} %bitcast.16, s32[1024]{0:T(1024)S(1)} %pad_clamp_fusion.2), kind=kCustom, calls=%fused_computation.clone | custom fusion | bytes 2097216 | tf_op jit(solution)/shard_map/jit(_take)/gather | solution.py:87
  67.8 1.8 select_bitcast_fusion.1
  69.6 3.6 %gather_fusion.2 = bf16[16,4,16,512]{3,1,2,0:T(4,128)(2,1)} fusion(bf16[16,4,16,512]{3,1,2,0:T(4,128)(2,1)} %collective-permute-done.6, s32[1024]{0:T(1024)S(1)} %pad_clamp_fusion.1), kind=kCustom, calls=%fused_computation.1.clone | custom fusion | bytes 2097216 | tf_op jit(solution)/shard_map/jit(_take)/gather | solution.py:87
  73.2 1.8 select_bitcast_fusion
  74.9 1.6 fusion.13
  76.5 1.8 copy.85
  78.3 0.9 slice_convert_fusion
  79.9 2.4 %fusion.23 = bf16[16,128,512]{2,1,0:T(8,128)(2,1)S(1)} fusion(bf16[16,144,512]{2,1,0:T(8,128)(2,1)} %all-to-all-done, s32[16,128]{1,0:T(8,128)S(1)} %slice.101), kind=kOutput, calls=%fused_computation.38 | convolution fusion | flops 269746176 | bytes 4202496 | tf_op jit(solution)/shard_map/sen,sef->snf/dot_general | solution.py:109
  83.5 1.2 copy-done.6
  84.7 1.3 fusion.6
  87.4 2.0 broadcast_multiply_fusion.1
  89.5 1.3 fusion.32
  90.8 0.8 copy.90
  91.6 1.4 fusion.34
  93.0 0.9 copy-done.1
  93.9 2.4 %collective-permute-start.7 = (bf16[16,72,512]{2,1,0:T(8,128)(2,1)}, bf16[16,72,512]{2,1,0:T(8,128)(2,1)}, u32[]{:S(2)}, u32[]{:S(2)}) collective-permute-start(bf16[16,72,512]{2,1,0:T(8,128)(2,1)} %fusion.34), channel_id=1, source_target_pairs={{0,16},{16,0},{1,17},{17,1},{2,18},{18,2},{3,19},{19,3},{4,20},{20... | collective-permute-start | bytes 3538952 | tf_op jit(solution)/shard_map/ppermute | solution.py:51
  96.4 1.9 pad_maximum_fusion.2
  98.6 1.3 bitcast_convert_fusion
  100.0 1.1 copy-done.5
  101.5 2.0 fusion.20
  103.6 0.9 copy-done.2
  104.5 2.7 %fusion.5 = bf16[16,72,512]{2,1,0:T(8,128)(2,1)} fusion(s32[]{:T(128)S(6)} %select_n.193, f32[2,16,64,512]{3,2,1,0:T(8,128)S(1)} %bitcast.146, f32[2,16,8,512]{3,2,1,0:T(8,128)S(1)} %bitcast.151, bf16[16,72,512]{2,1,0:T(8,128)(2,1)} %collective-permute-done.7), kind=kLoop, calls=%fused_computation.14 | loop fusion | flops 2359296 | bytes 7077892 | tf_op jit(solution)/shard_map/convert_element_type | solution.py:158
  107.2 2.9 %gather_fusion = bf16[16,72,512]{2,1,0:T(8,128)(2,1)} fusion(bf16[16,72,512]{2,1,0:T(8,128)(2,1)} %fusion.5, s32[1024]{0:T(1024)S(1)} %pad_clamp_fusion), kind=kCustom, calls=%fused_computation.2 | custom fusion | bytes 2359360 | tf_op jit(solution)/shard_map/jit(_take)/gather | solution.py:161
  110.1 1.4 broadcast_select_fusion
  111.5 6.7 %all-to-all-start.1 = ((bf16[16,128,512]{2,1,0:T(8,128)(2,1)}), bf16[16,128,512]{2,1,0:T(8,128)(2,1)}, u32[]{:S(2)}, u32[]{:S(2)}) async-start(bf16[16,128,512]{2,1,0:T(8,128)(2,1)} %fusion.20), calls=%async_computation.1 | async-start | bytes 4194304 | tf_op jit(solution)/shard_map/all_to_all | solution.py:26
  118.3 2.1 collective-permute-start.10
  120.4 3.2 %collective-permute-start.8 = (bf16[4,72,512]{2,1,0:T(8,128)(2,1)S(1)}, bf16[4,72,512]{2,1,0:T(8,128)(2,1)S(1)}, u32[]{:S(2)}, u32[]{:S(2)}) collective-permute-start(bf16[4,72,512]{2,1,0:T(8,128)(2,1)S(1)} %get-tuple-element.35), channel_id=1, source_target_pairs={{0,32},{16,48},{32,64},{48,80},{64,96},{80,112},{96,128},{112,144}... | collective-permute-start | bytes 884744 | tf_op jit(solution)/shard_map/ppermute | solution.py:43
  123.6 2.3 collective-permute-start.9
  125.9 2.5 %collective-permute-done.10 = bf16[4,72,512]{2,1,0:T(8,128)(2,1)S(1)} collective-permute-done((bf16[4,72,512]{2,1,0:T(8,128)(2,1)S(1)}, bf16[4,72,512]{2,1,0:T(8,128)(2,1)S(1)}, u32[]{:S(2)}, u32[]{:S(2)}) %collective-permute-start.10) | collective-permute-done | bytes 294944 | tf_op jit(solution)/shard_map/ppermute | solution.py:43
  128.4 2.7 %collective-permute-done.8 = bf16[4,72,512]{2,1,0:T(8,128)(2,1)S(1)} collective-permute-done((bf16[4,72,512]{2,1,0:T(8,128)(2,1)S(1)}, bf16[4,72,512]{2,1,0:T(8,128)(2,1)S(1)}, u32[]{:S(2)}, u32[]{:S(2)}) %collective-permute-start.8) | collective-permute-done | bytes 294944 | tf_op jit(solution)/shard_map/ppermute | solution.py:43
  131.0 4.5 %collective-permute-done.9 = bf16[4,72,512]{2,1,0:T(8,128)(2,1)S(1)} collective-permute-done((bf16[4,72,512]{2,1,0:T(8,128)(2,1)S(1)}, bf16[4,72,512]{2,1,0:T(8,128)(2,1)S(1)}, u32[]{:S(2)}, u32[]{:S(2)}) %collective-permute-start.9) | collective-permute-done | bytes 294944 | tf_op jit(solution)/shard_map/ppermute | solution.py:43
  135.7 4.7 %collective-permute-start.11 = (bf16[72,512]{1,0:T(8,128)(2,1)S(1)}, bf16[72,512]{1,0:T(8,128)(2,1)S(1)}, u32[]{:S(2)}, u32[]{:S(2)}) collective-permute-start(bf16[72,512]{1,0:T(8,128)(2,1)S(1)} %get-tuple-element.42), channel_id=1, source_target_pairs={{0,128},{32,160},{64,192},{96,224},{128,256},{160,288},{192,320},{... | collective-permute-start | bytes 221192 | tf_op jit(solution)/shard_map/ppermute | solution.py:47
  140.4 4.1 %collective-permute-start.12 = (bf16[72,512]{1,0:T(8,128)(2,1)S(1)}, bf16[72,512]{1,0:T(8,128)(2,1)S(1)}, u32[]{:S(2)}, u32[]{:S(2)}) collective-permute-start(bf16[72,512]{1,0:T(8,128)(2,1)S(1)} %get-tuple-element.44), channel_id=1, source_target_pairs={{0,256},{32,288},{64,320},{96,352},{128,384},{160,416},{192,448},{... | collective-permute-start | bytes 221192 | tf_op jit(solution)/shard_map/ppermute | solution.py:47
  144.5 5.8 %collective-permute-start.13 = (bf16[72,512]{1,0:T(8,128)(2,1)S(1)}, bf16[72,512]{1,0:T(8,128)(2,1)S(1)}, u32[]{:S(2)}, u32[]{:S(2)}) collective-permute-start(bf16[72,512]{1,0:T(8,128)(2,1)S(1)} %get-tuple-element.43), channel_id=1, source_target_pairs={{0,384},{32,416},{64,448},{96,480},{128,0},{160,32},{192,64},{224,... | collective-permute-start | bytes 221192 | tf_op jit(solution)/shard_map/ppermute | solution.py:47
  150.3 4.7 %collective-permute-done.12 = bf16[72,512]{1,0:T(8,128)(2,1)S(1)} collective-permute-done((bf16[72,512]{1,0:T(8,128)(2,1)S(1)}, bf16[72,512]{1,0:T(8,128)(2,1)S(1)}, u32[]{:S(2)}, u32[]{:S(2)}) %collective-permute-start.12) | collective-permute-done | bytes 73760 | tf_op jit(solution)/shard_map/ppermute | solution.py:47
  155.2 19.0 %all_to_all.25 = bf16[16,72,512]{2,1,0:T(8,128)(2,1)S(1)} all-to-all(bf16[16,72,512]{2,1,0:T(8,128)(2,1)S(1)} %broadcast_in_dim.98), channel_id=1, replica_groups=mesh['zh'=4,'zl'=4,'core'=2,'y'=4,'x'=4] {'y','x'}, dimensions={0} | all-to-all | bytes 2359296 | tf_op jit(solution)/shard_map/all_to_all | solution.py:26
  174.2 1.0 copy-done.3
  175.4 1.3 fusion.35
  176.7 0.9 slice_reduce_fusion
  177.7 30.8 %all_to_all.26 = bf16[4,24,512]{2,1,0:T(8,128)(2,1)S(1)} all-to-all(bf16[4,24,512]{2,1,0:T(8,128)(2,1)S(1)} %broadcast_in_dim.99), channel_id=1, replica_groups=mesh['zh'=4,'zl'=4,'core'=2,'y'=4,'x'=4] {'zh'}, dimensions={0} | all-to-all | bytes 196608 | tf_op jit(solution)/shard_map/all_to_all | solution.py:26
  208.5 0.7 broadcast_in_dim.100
  209.2 3.4 %all-to-all-start.4 = ((bf16[4,48,512]{2,1,0:T(8,128)(2,1)}), bf16[4,48,512]{2,1,0:T(8,128)(2,1)S(1)}, u32[]{:S(2)}, u32[]{:S(2)}) async-start(bf16[4,48,512]{2,1,0:T(8,128)(2,1)} %broadcast_in_dim.100), calls=%async_computation.4 | async-start | bytes 393216 | tf_op jit(solution)/shard_map/all_to_all | solution.py:26
  212.6 2.6 %reduce_sum.81 = bf16[128,512]{1,0:T(8,128)(2,1)} reduce(bf16[16,128,512]{2,1,0:T(8,128)(2,1)} %all-to-all-done.1, bf16[]{:T(256)} %constant.159.clone.1), dimensions={0}, to_apply=%region_6.8 | reduce | flops 983040 | bytes 2228226 | tf_op jit(solution)/shard_map/reduce_sum | solution.py:174
  215.2 2.5 %all-to-all-done.4 = bf16[4,48,512]{2,1,0:T(8,128)(2,1)S(1)} async-done(((bf16[4,48,512]{2,1,0:T(8,128)(2,1)}), bf16[4,48,512]{2,1,0:T(8,128)(2,1)S(1)}, u32[]{:S(2)}, u32[]{:S(2)}) %all-to-all-start.4) | async-done | bytes 196640 | tf_op jit(solution)/shard_map/all_to_all | solution.py:26
  217.7 0.7 pad_maximum_fusion.8
  218.4 6.9 %collective-permute-start.14 = (bf16[144,512]{1,0:T(8,128)(2,1)}, bf16[144,512]{1,0:T(8,128)(2,1)S(1)}, u32[]{:S(2)}, u32[]{:S(2)}) collective-permute-start(bf16[144,512]{1,0:T(8,128)(2,1)} %pad_maximum_fusion.8), channel_id=1, source_target_pairs={{0,16},{16,0},{1,17},{17,1},{2,18},{18,2},{3,19},{19,3},{4,20},{20... | collective-permute-start | bytes 442376 | tf_op jit(solution)/shard_map/ppermute | solution.py:51
  225.3 2.3 convert_bitcast_fusion.1
  227.6 3.9 %copy.100 = bf16[16,128,512]{2,1,0:T(8,128)(2,1)} copy(bf16[16,128,512]{1,2,0:T(8,128)(2,1)} %convert_bitcast_fusion.1) | data formatting | bytes 4194304
  231.6 0.7 copy.99
  232.4 0.8 fusion.60
  (108 shorter events, 9.0 us)
Async XLA Ops:
  0.6 2.6 %copy-start = (bf16[16,128,512]{2,1,0:T(8,128)(2,1)S(1)}, bf16[16,128,512]{2,1,0:T(8,128)(2,1)}, u32[]{:S(2)}) copy-start(bf16[16,128,512]{2,1,0:T(8,128)(2,1)} %param.11) | copy-start | bytes 6291460
  0.6 28.4 %copy-start.12 = (s32[1024]{0:T(1024)S(1)}, s32[1024]{0:T(1024)}, u32[]{:S(2)}) copy-start(s32[1024]{0:T(1024)} %param.16) | copy-start | bytes 12292
  0.7 29.1 %copy-start.13 = (s32[1,32]{1,0:T(1,128)S(1)}, s32[1,32]{1,0:T(1,128)}, u32[]{:S(2)}) copy-start(s32[1,32]{1,0:T(1,128)} %param.19) | copy-start | bytes 388
  0.7 30.2 %copy-start.10 = (s32[1024]{0:T(1024)S(1)}, s32[1024]{0:T(1024)}, u32[]{:S(2)}) copy-start(s32[1024]{0:T(1024)} %param.17) | copy-start | bytes 12292
  0.7 30.3 %copy-start.11 = (s32[1024]{0:T(1024)S(1)}, s32[1024]{0:T(1024)}, u32[]{:S(2)}) copy-start(s32[1024]{0:T(1024)} %param.18) | copy-start | bytes 12292
  0.7 30.5 %copy-start.9 = (bf16[128,512]{1,0:T(8,128)(2,1)S(1)}, bf16[128,512]{1,0:T(8,128)(2,1)}, u32[]{:S(2)}) copy-start(bf16[128,512]{1,0:T(8,128)(2,1)} %param.13) | copy-start | bytes 393220
  3.6 36.2 %collective-permute-start.1 = (bf16[4,16,512]{2,0,1:T(4,128)(2,1)S(1)}, bf16[4,16,512]{2,0,1:T(4,128)(2,1)S(1)}, u32[]{:S(2)}, u32[]{:S(2)}) collective-permute-start(bf16[4,16,512]{2,0,1:T(4,128)(2,1)S(1)} %convolution_convert_fusion.1), channel_id=1, source_target_pairs={{0,256},{32,288},{64,320},{96,352},{128,384},{160,416},{192,448},{... | collective-permute-start | bytes 196616 | tf_op jit(solution)/shard_map/ppermute | solution.py:47
  19.9 20.0 %collective-permute-start.2 = (bf16[4,16,512]{2,0,1:T(4,128)(2,1)S(1)}, bf16[4,16,512]{2,0,1:T(4,128)(2,1)S(1)}, u32[]{:S(2)}, u32[]{:S(2)}) collective-permute-start(bf16[4,16,512]{2,0,1:T(4,128)(2,1)S(1)} %convolution_convert_fusion.1), channel_id=1, source_target_pairs={{0,384},{32,416},{64,448},{96,480},{128,0},{160,32},{192,64},{224,... | collective-permute-start | bytes 196616 | tf_op jit(solution)/shard_map/ppermute | solution.py:47
  21.8 18.0 %collective-permute-start = (bf16[4,16,512]{2,0,1:T(4,128)(2,1)S(1)}, bf16[4,16,512]{2,0,1:T(4,128)(2,1)S(1)}, u32[]{:S(2)}, u32[]{:S(2)}) collective-permute-start(bf16[4,16,512]{2,0,1:T(4,128)(2,1)S(1)} %convolution_convert_fusion.1), channel_id=1, source_target_pairs={{0,128},{32,160},{64,192},{96,224},{128,256},{160,288},{192,320},{... | collective-permute-start | bytes 196616 | tf_op jit(solution)/shard_map/ppermute | solution.py:47
  33.0 45.3 %all-to-all-start = ((bf16[16,144,512]{2,1,0:T(8,128)(2,1)}), bf16[16,144,512]{2,1,0:T(8,128)(2,1)}, u32[]{:S(2)}, u32[]{:S(2)}) async-start(bf16[16,144,512]{2,1,0:T(8,128)(2,1)} %pad_maximum_fusion), calls=%async_computation | async-start | bytes 4718592 | tf_op jit(solution)/shard_map/all_to_all | solution.py:26
  40.1 9.2 %collective-permute-start.3 = (bf16[4,4,16,512]{3,1,2,0:T(4,128)(2,1)S(1)}, bf16[4,4,16,512]{3,1,2,0:T(4,128)(2,1)S(1)}, u32[]{:S(2)}, u32[]{:S(2)}) collective-permute-start(bf16[4,4,16,512]{3,1,2,0:T(4,128)(2,1)S(1)} %pad_maximum_fusion.6), channel_id=1, source_target_pairs={{0,32},{16,48},{32,64},{48,80},{64,96},{80,112},{96,128},{112,144}... | collective-permute-start | bytes 786440 | tf_op jit(solution)/shard_map/ppermute | solution.py:43
  42.8 11.4 %collective-permute-start.4 = (bf16[4,4,16,512]{3,1,2,0:T(4,128)(2,1)S(1)}, bf16[4,4,16,512]{3,1,2,0:T(4,128)(2,1)S(1)}, u32[]{:S(2)}, u32[]{:S(2)}) collective-permute-start(bf16[4,4,16,512]{3,1,2,0:T(4,128)(2,1)S(1)} %pad_maximum_fusion.6), channel_id=1, source_target_pairs={{0,64},{16,464},{32,96},{48,496},{64,128},{80,16},{96,160},{112,48... | collective-permute-start | bytes 786440 | tf_op jit(solution)/shard_map/ppermute | solution.py:43
  44.9 14.9 %collective-permute-start.5 = (bf16[4,4,16,512]{3,1,2,0:T(4,128)(2,1)S(1)}, bf16[4,4,16,512]{3,1,2,0:T(4,128)(2,1)S(1)}, u32[]{:S(2)}, u32[]{:S(2)}) collective-permute-start(bf16[4,4,16,512]{3,1,2,0:T(4,128)(2,1)S(1)} %pad_maximum_fusion.6), channel_id=1, source_target_pairs={{0,480},{16,496},{32,0},{48,16},{64,32},{80,48},{96,64},{112,80},{... | collective-permute-start | bytes 786440 | tf_op jit(solution)/shard_map/ppermute | solution.py:43
  61.8 7.8 %collective-permute-start.6 = (bf16[16,4,16,512]{3,1,2,0:T(4,128)(2,1)}, bf16[16,4,16,512]{3,1,2,0:T(4,128)(2,1)}, u32[]{:S(2)}, u32[]{:S(2)}) collective-permute-start(bf16[16,4,16,512]{3,1,2,0:T(4,128)(2,1)} %bitcast.16), channel_id=1, source_target_pairs={{0,16},{16,0},{1,17},{17,1},{2,18},{18,2},{3,19},{19,3},{4,20},{20... | collective-permute-start | bytes 3145736 | tf_op jit(solution)/shard_map/ppermute | solution.py:51
  83.1 1.6 copy-start.6
  84.7 1.4 copy-start.8
  86.0 1.0 copy-start.4
  91.6 2.3 copy-start.1
  93.9 9.6 %collective-permute-start.7 = (bf16[16,72,512]{2,1,0:T(8,128)(2,1)}, bf16[16,72,512]{2,1,0:T(8,128)(2,1)}, u32[]{:S(2)}, u32[]{:S(2)}) collective-permute-start(bf16[16,72,512]{2,1,0:T(8,128)(2,1)} %fusion.34), channel_id=1, source_target_pairs={{0,16},{16,0},{1,17},{17,1},{2,18},{18,2},{3,19},{19,3},{4,20},{20... | collective-permute-start | bytes 3538952 | tf_op jit(solution)/shard_map/ppermute | solution.py:51
  96.4 2.2 copy-start.7
  99.9 1.2 copy-start.5
  101.5 2.9 %copy-start.2 = (f32[4,16,2,16,512]{4,3,0,1,2:T(8,128)S(1)}, f32[4,16,2,16,512]{4,3,0,1,2:T(8,128)}, u32[]{:S(2)}) copy-start(f32[4,16,2,16,512]{4,3,0,1,2:T(8,128)} %copy-done.1) | copy-start | bytes 12582916
  111.5 43.6 %all-to-all-start.1 = ((bf16[16,128,512]{2,1,0:T(8,128)(2,1)}), bf16[16,128,512]{2,1,0:T(8,128)(2,1)}, u32[]{:S(2)}, u32[]{:S(2)}) async-start(bf16[16,128,512]{2,1,0:T(8,128)(2,1)} %fusion.20), calls=%async_computation.1 | async-start | bytes 4194304 | tf_op jit(solution)/shard_map/all_to_all | solution.py:26
  118.3 10.1 %collective-permute-start.10 = (bf16[4,72,512]{2,1,0:T(8,128)(2,1)S(1)}, bf16[4,72,512]{2,1,0:T(8,128)(2,1)S(1)}, u32[]{:S(2)}, u32[]{:S(2)}) collective-permute-start(bf16[4,72,512]{2,1,0:T(8,128)(2,1)S(1)} %get-tuple-element.36), channel_id=1, source_target_pairs={{0,480},{16,496},{32,0},{48,16},{64,32},{80,48},{96,64},{112,80},{... | collective-permute-start | bytes 884744 | tf_op jit(solution)/shard_map/ppermute | solution.py:43
  120.4 10.7 %collective-permute-start.8 = (bf16[4,72,512]{2,1,0:T(8,128)(2,1)S(1)}, bf16[4,72,512]{2,1,0:T(8,128)(2,1)S(1)}, u32[]{:S(2)}, u32[]{:S(2)}) collective-permute-start(bf16[4,72,512]{2,1,0:T(8,128)(2,1)S(1)} %get-tuple-element.35), channel_id=1, source_target_pairs={{0,32},{16,48},{32,64},{48,80},{64,96},{80,112},{96,128},{112,144}... | collective-permute-start | bytes 884744 | tf_op jit(solution)/shard_map/ppermute | solution.py:43
  123.6 11.9 %collective-permute-start.9 = (bf16[4,72,512]{2,1,0:T(8,128)(2,1)S(1)}, bf16[4,72,512]{2,1,0:T(8,128)(2,1)S(1)}, u32[]{:S(2)}, u32[]{:S(2)}) collective-permute-start(bf16[4,72,512]{2,1,0:T(8,128)(2,1)S(1)} %get-tuple-element.37), channel_id=1, source_target_pairs={{0,64},{16,464},{32,96},{48,496},{64,128},{80,16},{96,160},{112,48... | collective-permute-start | bytes 884744 | tf_op jit(solution)/shard_map/ppermute | solution.py:43
  135.7 14.6 %collective-permute-start.11 = (bf16[72,512]{1,0:T(8,128)(2,1)S(1)}, bf16[72,512]{1,0:T(8,128)(2,1)S(1)}, u32[]{:S(2)}, u32[]{:S(2)}) collective-permute-start(bf16[72,512]{1,0:T(8,128)(2,1)S(1)} %get-tuple-element.42), channel_id=1, source_target_pairs={{0,128},{32,160},{64,192},{96,224},{128,256},{160,288},{192,320},{... | collective-permute-start | bytes 221192 | tf_op jit(solution)/shard_map/ppermute | solution.py:47
  140.4 14.6 %collective-permute-start.12 = (bf16[72,512]{1,0:T(8,128)(2,1)S(1)}, bf16[72,512]{1,0:T(8,128)(2,1)S(1)}, u32[]{:S(2)}, u32[]{:S(2)}) collective-permute-start(bf16[72,512]{1,0:T(8,128)(2,1)S(1)} %get-tuple-element.44), channel_id=1, source_target_pairs={{0,256},{32,288},{64,320},{96,352},{128,384},{160,416},{192,448},{... | collective-permute-start | bytes 221192 | tf_op jit(solution)/shard_map/ppermute | solution.py:47
  144.5 10.6 %collective-permute-start.13 = (bf16[72,512]{1,0:T(8,128)(2,1)S(1)}, bf16[72,512]{1,0:T(8,128)(2,1)S(1)}, u32[]{:S(2)}, u32[]{:S(2)}) collective-permute-start(bf16[72,512]{1,0:T(8,128)(2,1)S(1)} %get-tuple-element.43), channel_id=1, source_target_pairs={{0,384},{32,416},{64,448},{96,480},{128,0},{160,32},{192,64},{224,... | collective-permute-start | bytes 221192 | tf_op jit(solution)/shard_map/ppermute | solution.py:47
  174.2 1.0 copy-start.3
  209.2 8.4 %all-to-all-start.4 = ((bf16[4,48,512]{2,1,0:T(8,128)(2,1)}), bf16[4,48,512]{2,1,0:T(8,128)(2,1)S(1)}, u32[]{:S(2)}, u32[]{:S(2)}) async-start(bf16[4,48,512]{2,1,0:T(8,128)(2,1)} %broadcast_in_dim.100), calls=%async_computation.4 | async-start | bytes 393216 | tf_op jit(solution)/shard_map/all_to_all | solution.py:26
  218.4 13.1 %collective-permute-start.14 = (bf16[144,512]{1,0:T(8,128)(2,1)}, bf16[144,512]{1,0:T(8,128)(2,1)S(1)}, u32[]{:S(2)}, u32[]{:S(2)}) collective-permute-start(bf16[144,512]{1,0:T(8,128)(2,1)} %pad_maximum_fusion.8), channel_id=1, source_target_pairs={{0,16},{16,0},{1,17},{17,1},{2,18},{18,2},{3,19},{19,3},{4,20},{20... | collective-permute-start | bytes 442376 | tf_op jit(solution)/shard_map/ppermute | solution.py:51

commit v3 on v2

v3 whole, which is shorter than its diff:
```python
import functools

import jax
import jax.numpy as jnp
from jax import lax
from jax.experimental import pallas as pl
from jax.experimental.pallas import tpu as pltpu
from jax.sharding import Mesh, PartitionSpec as P

ZH, ZL, CORES, REPS = 4, 4, 2, 16
Z = ZH * ZL
REL = ("zh", "zl", "core")
REP = ("y", "x")
LINE = ("zh", "zl")
STEPS = (0, 1, 2, 3)
EXTRA = 16
F32 = jnp.float32
BF16 = jnp.bfloat16


def order_tables(owner_of, per_owner):
    count = owner_of.shape[0]
    index = jnp.arange(count, dtype=jnp.int32)
    same = owner_of[:, None] == owner_of[None, :]
    rank = jnp.sum((same & (index[None, :] < index[:, None])).astype(jnp.int32), axis=1)
    return (rank, owner_of * per_owner + rank)


def exchange(blocks, axis):
    return lax.all_to_all(blocks, axis, split_axis=0, concat_axis=0, tiled=True)


def spread(block, axis, count):
    return exchange(jnp.broadcast_to(block[None], (count,) + block.shape), axis)


def near_by(step, core):
    return jnp.where(step == 2, 2 - 4 * core, jnp.where(step == 3, -1, step))


def near_move(block, step):
    pairs = []
    for z in range(Z):
        for core in range(CORES):
            by = (0, 1, 2 - 4 * core, -1)[step]
            pairs.append((z * CORES + core, (z + by) % Z * CORES + core))
    return lax.ppermute(block, REL, pairs)


def far_move(block, step):
    return lax.ppermute(block, LINE, [(z, (z + 4 * step) % Z) for z in range(Z)])


def swap_core(block):
    return lax.ppermute(block, "core", [(0, 1), (1, 0)])


def dot(a, b, over):
    return lax.dot_general(a, b, (over, ((), ())), preferred_element_type=F32)


NN, NT, TN = ((1,), (0,)), ((1,), (1,)), ((0,), (0,))


def hot_of(line, ent_rows, columns):
    ids = line[:, : -(-columns // 128) * 128].astype(F32)[0:1, :columns]
    entity = lax.broadcasted_iota(jnp.int32, (ent_rows, columns), 0).astype(F32)
    return jnp.where(entity == ids, 1.0, 0.0).astype(BF16)


def gather_kernel(cap, got, heads, tails):
    ent_rows = got.shape[1] - EXTRA
    own = tails.shape[0]
    kinds = heads.shape[0] // own
    columns = (kinds + 1) * own * cap
    for s in range(got.shape[0]):
        hot = hot_of(got[s, ent_rows:, :], ent_rows, columns)
        rows = dot(hot, got[s, :ent_rows, :], TN).astype(BF16)
        for kind in range(kinds + 1):
            for o in range(own):
                at = (kind * own + o) * cap
                block = rows[at : at + cap]
                if kind < kinds:
                    heads[o * kinds + kind, s * cap : (s + 1) * cap, :] = block
                else:
                    tails[o, s * cap : (s + 1) * cap, :] = block


def score_kernel(scale, rows_dev, starts, heads, tails, half, other, pool, mats, dquery, dtail, given, kept, dm, dp):
    own = tails.shape[0]
    kinds = heads.shape[0] // own
    mine = heads.shape[0]
    for i in range(half.shape[0]):
        for which, source in ((0, half), (1, other)):
            at = pl.multiple_of(starts[which, i], rows_dev)
            for w in range(mine):
                mats[w, pl.ds(at, rows_dev), :] = source[i, w * rows_dev : (w + 1) * rows_dev, :]
    negatives = pool[...]
    total = None
    for o in range(own):
        query = dot(heads[o * kinds], mats[o * kinds], NN)
        for w in range(1, kinds):
            query = query + dot(heads[o * kinds + w], mats[o * kinds + w], NN)
        query = query.astype(BF16)
        qfloat = query.astype(F32)
        tail = tails[o].astype(F32)
        gpos = -jax.nn.sigmoid(-jnp.sum(qfloat * tail, axis=1, keepdims=True)) * scale
        gneg = (jax.nn.sigmoid(dot(query, negatives, NT)) * (scale / pool.shape[0])).astype(BF16)
        grad = (gpos * tail + dot(gneg, negatives, NN)).astype(BF16)
        dquery[o] = grad
        dtail[o] = (gpos * qfloat).astype(BF16)
        piece = dot(gneg, query, TN)
        total = piece if total is None else total + piece
        for w in range(kinds):
            dm[o * kinds + w] = dot(heads[o * kinds + w], grad, TN).astype(BF16)
    dp[...] = total
    pool_dev = rows_dev // 2
    for which, target in ((2, kept), (3, given)):
        for s in range(4):
            pieces = []
            for p in range(4):
                at = pl.multiple_of(starts[which, s * 4 + p], rows_dev)
                for w in range(mine):
                    row = (p * mine + w) * rows_dev
                    target[s, row : row + rows_dev, :] = dm[w, pl.ds(at, rows_dev), :]
                at = pl.multiple_of(starts[which, s * 4 + p] // 2, pool_dev)
                pieces.append(dp[pl.ds(at, pool_dev), :])
            target[s, 4 * mine * rows_dev :, :] = jnp.concatenate(pieces, axis=0).astype(BF16)


def scatter_kernel(cap, lines, dquery, dtail, mats, out, dheads):
    own = dquery.shape[0]
    kinds = mats.shape[0] // own
    columns = (kinds + 1) * own * cap
    ent_rows = out.shape[1]
    for o in range(own):
        for w in range(kinds):
            dheads[o * kinds + w] = dot(dquery[o], mats[o * kinds + w], NT).astype(BF16)
    for s in range(out.shape[0]):
        hot = hot_of(lines[s], ent_rows, columns)
        at = slice(s * cap, (s + 1) * cap)
        grads = [dheads[o * kinds + w, at, :] for w in range(kinds) for o in range(own)]
        grads += [dtail[o, at, :] for o in range(own)]
        out[s] = dot(hot, jnp.concatenate(grads, axis=0), NN).astype(BF16)


def call(kernel, outs, flops, in_specs=None, scratch=()):
    vmem = pl.BlockSpec(memory_space=pltpu.VMEM)
    return pl.pallas_call(
        kernel,
        out_shape=tuple(jax.ShapeDtypeStruct(shape, BF16) for shape in outs),
        in_specs=in_specs,
        out_specs=tuple(vmem for _ in outs),
        scratch_shapes=scratch,
        cost_estimate=pl.CostEstimate(flops=flops, bytes_accessed=1 << 23, transcendentals=0),
        compiler_params=pltpu.CompilerParams(vmem_limit_bytes=40 << 20),
    )


def body(core, rel_emb, ents, pool, owner_of, rel_ids, head_ids, tail_ids, fill):
    rels, feats_rel = rel_emb.shape
    rows_dev, _, feats = core.shape
    owners = fill.shape[1]
    cap = rel_ids.shape[0] // owners
    per_owner = rels // owners
    own = owners // REPS
    mine = own * per_owner
    seats = own * cap
    ent_rows = ents.shape[0]
    pool_rows = pool.shape[0]
    pool_dev = pool_rows // (Z * CORES)
    scale = 1.0 / REPS
    g = lax.axis_index(REP)
    z = lax.axis_index(LINE)
    c = lax.axis_index("core")

    rank, slot_of = order_tables(owner_of, per_owner)
    qindex = jnp.arange(rels, dtype=jnp.int32)
    order_sel = (slot_of[None, :] == qindex[:, None]).astype(BF16)
    ordered = jnp.dot(order_sel, rel_emb, preferred_element_type=F32).astype(BF16)

    relhot = rel_ids[None, :] == jnp.arange(rels, dtype=jnp.int32)[:, None]
    rank_slot = jnp.sum(jnp.where(relhot, rank[:, None], 0), axis=0)
    used = (jnp.arange(cap, dtype=jnp.int32)[None, :] < fill[0][:, None]).reshape(-1)
    numbers = [jnp.where(used & (rank_slot == w), head_ids, -1) for w in range(per_owner)]
    numbers.append(jnp.where(used, tail_ids, -1))
    numbers = jnp.concatenate([a.reshape(REPS, seats) for a in numbers], axis=1).astype(BF16)
    numbers = jnp.pad(numbers[:, None, :], ((0, 0), (0, EXTRA - 1), (0, feats - numbers.shape[1])))
    sent = jnp.concatenate(
        [jnp.broadcast_to(ents[None], (REPS, ent_rows, feats)), numbers], axis=1
    )
    own_rows = lax.dynamic_slice_in_dim(ordered, g * mine, mine, 0)
    own_rows, sent = lax.optimization_barrier((own_rows, sent))
    got = exchange(sent, REP)

    part = jnp.einsum("wk,akb->wab", own_rows, core, preferred_element_type=F32).astype(BF16)
    part = part.reshape(mine * rows_dev, feats)
    far = jnp.stack([part] + [far_move(part, p) for p in STEPS[1:]])
    half = jnp.concatenate([far] + [near_move(far, s) for s in STEPS[1:]])
    other = swap_core(half)

    entry = jnp.arange(Z, dtype=jnp.int32)
    starts = []
    for sign in (-1, 1):
        for core_of in (c, 1 - c):
            chip = (z + sign * (near_by(entry // 4, core_of) + 4 * (entry % 4))) % Z
            starts.append((chip * CORES + core_of) * rows_dev)
    starts = jnp.stack(starts)

    vmem = pl.BlockSpec(memory_space=pltpu.VMEM)
    smem = pl.BlockSpec(memory_space=pltpu.SMEM)
    slots = REPS * cap
    block = slots * feats * feats * 2
    heads, tails = call(
        functools.partial(gather_kernel, cap),
        ((mine, slots, feats), (own, slots, feats)),
        REPS * 3 * seats * ent_rows * feats * 2,
        [vmem],
    )(got)
    sum_rows = 4 * (mine * rows_dev + pool_dev)
    mats, dquery, dtail, given, kept = call(
        functools.partial(score_kernel, scale, rows_dev),
        (
            (mine, feats, feats),
            (own, slots, feats),
            (own, slots, feats),
            (4, sum_rows, feats),
            (4, sum_rows, feats),
        ),
        2 * mine * block + 3 * own * block // 2,
        [smem] + [vmem] * 5,
        (pltpu.VMEM((mine, feats, feats), BF16), pltpu.VMEM((pool_rows, feats), F32)),
    )(starts, heads, tails, half, other, pool)

    pair = (kept.astype(F32) + swap_core(given).astype(F32)).astype(BF16)
    pair, dquery = lax.optimization_barrier((pair, dquery))
    (ent_part,) = call(
        functools.partial(scatter_kernel, cap),
        ((REPS, ent_rows, feats),),
        mine * block + REPS * 3 * seats * ent_rows * feats * 2,
        [vmem] * 4,
        (pltpu.VMEM((mine, slots, feats), BF16),),
    )(got[:, ent_rows:], dquery, dtail, mats)
    back = exchange(ent_part, REP)
    total = pair[0].astype(F32)
    for s in STEPS[1:]:
        total = total + near_move(pair[s], s).astype(F32)
    total = total.astype(BF16)
    split = 4 * mine * rows_dev
    blocks = [
        jnp.concatenate(
            [
                total[p * mine * rows_dev : (p + 1) * mine * rows_dev],
                total[split + p * pool_dev : split + (p + 1) * pool_dev],
            ]
        )
        for p in STEPS
    ]
    own_sum = blocks[0].astype(F32)
    for p in STEPS[1:]:
        own_sum = own_sum + far_move(blocks[p], p).astype(F32)
    own_sum = own_sum.astype(BF16)

    own_sum, back = lax.optimization_barrier((own_sum, back))
    ent_grad = jnp.sum(back.astype(F32), axis=0).astype(BF16)
    all_sums = spread(own_sum, REP, REPS)
    all_rows = all_sums[:, : mine * rows_dev].reshape(rels, rows_dev, feats)
    pool_own = jnp.sum(all_sums[:, mine * rows_dev :].astype(F32), axis=0).astype(BF16)
    rel_own = jnp.einsum("qab,akb->qk", all_rows, core, preferred_element_type=F32).astype(BF16)

    rel_rows = rels * feats_rel // feats
    small = spread(jnp.concatenate([rel_own.reshape(rel_rows, feats), pool_own]), LINE, Z)
    rel_own = jnp.sum(small[:, :rel_rows].astype(F32), axis=0).astype(BF16)
    small = jnp.concatenate([rel_own, small[:, rel_rows:].reshape(-1, feats)])
    small_other = swap_core(small)
    rel_ordered = (small[:rel_rows].astype(F32) + small_other[:rel_rows].astype(F32)).astype(BF16)
    rel_ordered = rel_ordered.reshape(rels, feats_rel)
    halves = jnp.stack([small[rel_rows:], small_other[rel_rows:]])
    halves = jnp.where(c == 0, halves, halves[::-1]).reshape(CORES, Z, pool_dev, feats)
    pool_grad = jnp.swapaxes(halves, 0, 1).reshape(pool_rows, feats)
    rel_grad = lax.dot_general(
        order_sel, rel_ordered, (((0,), (0,)), ((), ())), preferred_element_type=F32
    )
    core_grad = jnp.einsum(
        "qk,qab->akb", ordered, all_rows, preferred_element_type=F32
    ).astype(BF16)
    return (core_grad, rel_grad, ent_grad, pool_grad)


def solution(mesh):
    cut = Mesh(mesh.devices.reshape(ZH, ZL, CORES, 4, 4), REL + REP)
    whole = REL + REP
    return jax.shard_map(
        body,
        mesh=cut,
        in_specs=(
            P(REL, None, None),
            P(),
            P(whole, None),
            P(),
            P(),
            P(whole),
            P(whole),
            P(whole),
            P(whole, None),
        ),
        out_specs=(P(REL, None, None), P(), P(whole, None), P()),
        check_vma=False,
    )
```

time: 235 us -> 215 us (0.915)
  waiting for transfers between devices: 28 us -> 55.6 us
  blocking collectives: 49.9 us -> 24 us
  other arithmetic: 25.7 us -> 9.95 us
  local copies, waits for them, and re-layouts: 26.9 us -> 11.9 us
  starting transfers between devices: 84.4 us -> 95.1 us
  matrix products: 16.9 us -> 6.39 us
  Pallas kernels: 0 us -> 9.87 us
    all_to_all x2 -> x1, blocking collectives: 49.9 us -> 24 us  [exchange(): return lax.all_to_all(blocks, axis, split_axis=0, concat_axis=0, tiled=True)]
    all_to_all x3, waiting for transfers between devices: 2.5 us -> 20.3 us  [exchange(): return lax.all_to_all(blocks, axis, split_axis=0, concat_axis=0, tiled=True)]
    dot_general x8 -> x0, matrix products: 11.3 us -> none  [the longest x1 2.35 us: body(): jnp.einsum('sen,sef->snf', hot, table, preferred_element_type=F32)]
    gather x3 -> x0, local copies, waits for them, and re-layouts: 10.1 us -> none  [the longest x2 7.19 us: in_order(): return jnp.take(blocks, s * 4 + p, axis=0)]
    pallas_call x0 -> x3, Pallas kernels: none -> 9.87 us  [the longest x1 5.36 us: body(): call(functools.partial(score_kernel, scale, rows_dev), ((mine, feats, fea...]
    ppermute x6, waiting for transfers between devices: 4.74 us -> 11.8 us  [far_move(): lax.ppermute(block, LINE, [(z, (z + 4 * step) % Z) for z in range(Z)])]
    ppermute x3, starting transfers between devices: 11.6 us -> 18.1 us  [swap_core(): return lax.ppermute(block, 'core', [(0, 1), (1, 0)])]
    convert_element_type x7 -> x1, other arithmetic: 5.66 us -> 0.35 us  [body(): pair = (kept.astype(F32) + swap_core(given).astype(F32)).astype(BF16)]
  transfers between devices with their start and end apart: 18 -> 18, of which waited for: 8 -> 9; matrix products, arithmetic and copies ran while one was open for 15% -> 5% of each run, Pallas kernels for 0% -> 1%
where the time goes in v3:
time: 215 us; the launch traced here: 214 us
  starting transfers between devices  95.1 us (44%)
  waiting for transfers between devices  55.6 us (26%)
  blocking collectives  24 us (11%)
  local copies, waits for them, and re-layouts  11.9 us (6%)
  other arithmetic  9.95 us (5%)
  Pallas kernels  9.87 us (5%)
  matrix products  6.39 us (3%)
    ppermute x6, starting transfers between devices, far_move(): lax.ppermute(block, LINE, [(z, (z + 4 * step) % Z) for z in range(Z)])  38.9 us
    all_to_all x1, blocking collectives, exchange(): return lax.all_to_all(blocks, axis, split_axis=0, concat_axis=0, tiled=True)  24 us
    ppermute x6, waiting for transfers between devices, near_move(): return lax.ppermute(block, REL, pairs)  22 us
    ppermute x6, starting transfers between devices, near_move(): return lax.ppermute(block, REL, pairs)  20.3 us
    all_to_all x3, waiting for transfers between devices, exchange(): return lax.all_to_all(blocks, axis, split_axis=0, concat_axis=0, tiled=True)  20.3 us
    ppermute x3, starting transfers between devices, swap_core(): return lax.ppermute(block, 'core', [(0, 1), (1, 0)])  18.1 us
    all_to_all x3, starting transfers between devices, exchange(): return lax.all_to_all(blocks, axis, split_axis=0, concat_axis=0, tiled=True)  17.7 us
    ppermute x6, waiting for transfers between devices, far_move(): lax.ppermute(block, LINE, [(z, (z + 4 * step) % Z) for z in range(Z)])  11.8 us
  transfers between devices with their start and end apart: 18, of which 9 were waited for; matrix products, arithmetic and copies ran while one was open for 5% of the time, Pallas kernels for 1%

profile of v3, /device:TPU:1, one launch (start us, length us, event | category | flops | bytes accessed | tf_op | source)
XLA Modules:
  0.0 214.0 jit_solution(18070887389806078702)
XLA Ops:
  0.6 0.0 copy-start
  0.7 1.0 convert_reduce_fusion
  1.7 0.7 multiply_add_fusion
  2.3 0.8 select_reduce_fusion
  3.1 0.7 iota_compare_fusion.7
  3.8 0.1 lt.81
  3.9 0.7 select_convert_fusion.2
  4.6 0.1 concatenate.54
  4.7 0.1 concatenate.55
  4.8 0.1 concatenate.56
  4.9 0.8 convolution_convert_fusion.1
  5.7 0.6 copy-done.5
  6.3 0.1 fusion.14
  6.4 1.1 broadcast_in_dim.63
  7.5 1.7 pad_maximum_fusion
  9.2 0.4 convolution_convert_fusion
  9.6 13.3 %collective-permute-start.2 = (bf16[64,512]{1,0:T(8,128)(2,1)S(1)}, bf16[64,512]{1,0:T(8,128)(2,1)S(1)}, u32[]{:S(2)}, u32[]{:S(2)}) collective-permute-start(bf16[64,512]{1,0:T(8,128)(2,1)S(1)} %bitcast.50), channel_id=1, source_target_pairs={{0,384},{32,416},{64,448},{96,480},{128,0},{160,32},{192,64},{224,... | collective-permute-start | bytes 196616 | tf_op jit(solution)/shard_map/ppermute | solution.py:51
  22.9 4.9 %collective-permute-start.1 = (bf16[64,512]{1,0:T(8,128)(2,1)S(1)}, bf16[64,512]{1,0:T(8,128)(2,1)S(1)}, u32[]{:S(2)}, u32[]{:S(2)}) collective-permute-start(bf16[64,512]{1,0:T(8,128)(2,1)S(1)} %bitcast.51), channel_id=1, source_target_pairs={{0,256},{32,288},{64,320},{96,352},{128,384},{160,416},{192,448},{... | collective-permute-start | bytes 196616 | tf_op jit(solution)/shard_map/ppermute | solution.py:51
  27.8 7.3 %collective-permute-start = (bf16[64,512]{1,0:T(8,128)(2,1)S(1)}, bf16[64,512]{1,0:T(8,128)(2,1)S(1)}, u32[]{:S(2)}, u32[]{:S(2)}) collective-permute-start(bf16[64,512]{1,0:T(8,128)(2,1)S(1)} %bitcast.52), channel_id=1, source_target_pairs={{0,128},{32,160},{64,192},{96,224},{128,256},{160,288},{192,320},{... | collective-permute-start | bytes 196616 | tf_op jit(solution)/shard_map/ppermute | solution.py:51
  35.1 6.8 %all-to-all-start = ((bf16[16,144,512]{2,1,0:T(8,128)(2,1)}), bf16[16,144,512]{2,1,0:T(8,128)(2,1)}, u32[]{:S(2)}, u32[]{:S(2)}) async-start(bf16[16,144,512]{2,1,0:T(8,128)(2,1)} %pad_maximum_fusion), calls=%async_computation | async-start | bytes 4718592 | tf_op jit(solution)/shard_map/all_to_all | solution.py:30
  42.0 6.9 %collective-permute-start.5 = (bf16[4,64,512]{2,1,0:T(8,128)(2,1)S(1)}, bf16[4,64,512]{2,1,0:T(8,128)(2,1)S(1)}, u32[]{:S(2)}, u32[]{:S(2)}) collective-permute-start(bf16[4,64,512]{2,1,0:T(8,128)(2,1)S(1)} %pad_maximum_fusion.1), channel_id=1, source_target_pairs={{0,480},{16,496},{32,0},{48,16},{64,32},{80,48},{96,64},{112,80},{... | collective-permute-start | bytes 786440 | tf_op jit(solution)/shard_map/ppermute | solution.py:47
  48.9 1.9 collective-permute-start.4
  50.8 3.1 %collective-permute-start.3 = (bf16[4,64,512]{2,1,0:T(8,128)(2,1)S(1)}, bf16[4,64,512]{2,1,0:T(8,128)(2,1)S(1)}, u32[]{:S(2)}, u32[]{:S(2)}) collective-permute-start(bf16[4,64,512]{2,1,0:T(8,128)(2,1)S(1)} %pad_maximum_fusion.1), channel_id=1, source_target_pairs={{0,32},{16,48},{32,64},{48,80},{64,96},{80,112},{96,128},{112,144}... | collective-permute-start | bytes 786440 | tf_op jit(solution)/shard_map/ppermute | solution.py:47
  54.0 10.0 %collective-permute-done.3 = bf16[4,64,512]{2,1,0:T(8,128)(2,1)S(1)} collective-permute-done((bf16[4,64,512]{2,1,0:T(8,128)(2,1)S(1)}, bf16[4,64,512]{2,1,0:T(8,128)(2,1)S(1)}, u32[]{:S(2)}, u32[]{:S(2)}) %collective-permute-start.3) | collective-permute-done | bytes 262176 | tf_op jit(solution)/shard_map/ppermute | solution.py:47
  64.1 3.4 %collective-permute-start.6 = (bf16[16,64,512]{2,1,0:T(8,128)(2,1)S(1)}, bf16[16,64,512]{2,1,0:T(8,128)(2,1)}, u32[]{:S(2)}, u32[]{:S(2)}) collective-permute-start(bf16[16,64,512]{2,1,0:T(8,128)(2,1)S(1)} %constant_dynamic-update-slice_fusion.half), channel_id=1, source_target_pairs={{0,16},{16,0},{1,17},{17,1},{2,18},{18,2},{3,19},{19,3},{4,20},{20... | collective-permute-start | bytes 3145736 | tf_op jit(solution)/shard_map/ppermute | solution.py:55
  67.6 6.3 %all-to-all-done.got = bf16[16,144,512]{2,1,0:T(8,128)(2,1)} async-done(((bf16[16,144,512]{2,1,0:T(8,128)(2,1)}), bf16[16,144,512]{2,1,0:T(8,128)(2,1)}, u32[]{:S(2)}, u32[]{:S(2)}) %all-to-all-start) | async-done | bytes 2359328 | tf_op jit(solution)/shard_map/all_to_all | solution.py:30
  73.9 2.7 %shard_map.120 = (bf16[4,512,512]{2,1,0:T(8,128)(2,1)S(1)}, bf16[2,512,512]{2,1,0:T(8,128)(2,1)S(1)}) custom-call(bf16[16,144,512]{2,1,0:T(8,128)(2,1)} %all-to-all-done.got), custom_call_target="tpu_custom_call" | custom-call | flops 402653184 | bytes 8388608 | tf_op jit(solution)/shard_map/pallas_call | solution.py:214
  76.6 5.4 %shard_map.121 = (bf16[4,512,512]{2,1,0:T(8,128)(2,1)S(1)}, bf16[2,512,512]{2,1,0:T(8,128)(2,1)S(1)}, bf16[2,512,512]{2,1,0:T(8,128)(2,1)S(1)}, bf16[4,288,512]{2,1,0:T(8,128)(2,1)S(1)}, bf16[4,288,512]{2,1,0:T(8,128)(2,1)S(1)}) custom-call(s32[4,16]{1,0:T(4,128)S(1)} %pad_add_fusion.starts, bf16[4,512,512]{2,1,0:T(8,128)(2,1)S(1)} %get-tuple-element.18.heads, ...), custom_call_target="tpu_custom_call" | custom-call | flops 2952790016 | bytes 8388608 | tf_op jit(solution)/shard_map/pallas_call | solution.py:221
  81.9 5.0 %collective-permute-start.7 = (bf16[4,288,512]{2,1,0:T(8,128)(2,1)S(1)}, bf16[4,288,512]{2,1,0:T(8,128)(2,1)S(1)}, u32[]{:S(2)}, u32[]{:S(2)}) collective-permute-start(bf16[4,288,512]{2,1,0:T(8,128)(2,1)S(1)} %get-tuple-element.22), channel_id=1, source_target_pairs={{0,16},{16,0},{1,17},{17,1},{2,18},{18,2},{3,19},{19,3},{4,20},{20... | collective-permute-start | bytes 3538952 | tf_op jit(solution)/shard_map/ppermute | solution.py:55
  87.0 1.0 slice.84.lines
  87.9 1.5 collective-permute-done.7
  89.4 0.3 add_convert_fusion
  89.8 1.8 shard_map.122
  91.6 1.3 copy-done.1
  92.9 4.4 %all-to-all-start.1 = ((bf16[16,128,512]{2,1,0:T(8,128)(2,1)}), bf16[16,128,512]{2,1,0:T(8,128)(2,1)}, u32[]{:S(2)}, u32[]{:S(2)}) async-start(bf16[16,128,512]{2,1,0:T(8,128)(2,1)} %copy-done.1), calls=%async_computation.1 | async-start | bytes 4194304 | tf_op jit(solution)/shard_map/all_to_all | solution.py:30
  97.4 0.1 slice_bitcast_fusion.2
  97.5 2.7 %collective-permute-start.8 = (bf16[288,512]{1,0:T(8,128)(2,1)S(1)}, bf16[288,512]{1,0:T(8,128)(2,1)S(1)}, u32[]{:S(2)}, u32[]{:S(2)}) collective-permute-start(bf16[288,512]{1,0:T(8,128)(2,1)S(1)} %get-tuple-element.46), channel_id=1, source_target_pairs={{0,32},{16,48},{32,64},{48,80},{64,96},{80,112},{96,128},{112,144}... | collective-permute-start | bytes 884744 | tf_op jit(solution)/shard_map/ppermute | solution.py:47
  100.1 3.8 %collective-permute-start.10 = (bf16[288,512]{1,0:T(8,128)(2,1)S(1)}, bf16[288,512]{1,0:T(8,128)(2,1)S(1)}, u32[]{:S(2)}, u32[]{:S(2)}) collective-permute-start(bf16[288,512]{1,0:T(8,128)(2,1)S(1)} %get-tuple-element.47), channel_id=1, source_target_pairs={{0,480},{16,496},{32,0},{48,16},{64,32},{80,48},{96,64},{112,80},{... | collective-permute-start | bytes 884744 | tf_op jit(solution)/shard_map/ppermute | solution.py:47
  104.0 1.9 collective-permute-start.9
  105.9 3.0 %collective-permute-done.8 = bf16[288,512]{1,0:T(8,128)(2,1)S(1)} collective-permute-done((bf16[288,512]{1,0:T(8,128)(2,1)S(1)}, bf16[288,512]{1,0:T(8,128)(2,1)S(1)}, u32[]{:S(2)}, u32[]{:S(2)}) %collective-permute-start.8) | collective-permute-done | bytes 294944 | tf_op jit(solution)/shard_map/ppermute | solution.py:47
  108.9 1.1 collective-permute-done.10
  110.0 7.9 %collective-permute-done.9 = bf16[288,512]{1,0:T(8,128)(2,1)S(1)} collective-permute-done((bf16[288,512]{1,0:T(8,128)(2,1)S(1)}, bf16[288,512]{1,0:T(8,128)(2,1)S(1)}, u32[]{:S(2)}, u32[]{:S(2)}) %collective-permute-start.9) | collective-permute-done | bytes 294944 | tf_op jit(solution)/shard_map/ppermute | solution.py:47
  117.9 0.2 fusion.5
  118.1 4.0 %collective-permute-start.11 = (bf16[72,512]{1,0:T(8,128)(2,1)S(1)}, bf16[72,512]{1,0:T(8,128)(2,1)S(1)}, u32[]{:S(2)}, u32[]{:S(2)}) collective-permute-start(bf16[72,512]{1,0:T(8,128)(2,1)S(1)} %pad_maximum_fusion.4), channel_id=1, source_target_pairs={{0,128},{32,160},{64,192},{96,224},{128,256},{160,288},{192,320},{... | collective-permute-start | bytes 221192 | tf_op jit(solution)/shard_map/ppermute | solution.py:51
  122.2 5.2 %collective-permute-start.12 = (bf16[72,512]{1,0:T(8,128)(2,1)S(1)}, bf16[72,512]{1,0:T(8,128)(2,1)S(1)}, u32[]{:S(2)}, u32[]{:S(2)}) collective-permute-start(bf16[72,512]{1,0:T(8,128)(2,1)S(1)} %pad_maximum_fusion.5), channel_id=1, source_target_pairs={{0,256},{32,288},{64,320},{96,352},{128,384},{160,416},{192,448},{... | collective-permute-start | bytes 221192 | tf_op jit(solution)/shard_map/ppermute | solution.py:51
  127.3 4.3 %collective-permute-start.13 = (bf16[72,512]{1,0:T(8,128)(2,1)S(1)}, bf16[72,512]{1,0:T(8,128)(2,1)S(1)}, u32[]{:S(2)}, u32[]{:S(2)}) collective-permute-start(bf16[72,512]{1,0:T(8,128)(2,1)S(1)} %pad_maximum_fusion.6), channel_id=1, source_target_pairs={{0,384},{32,416},{64,448},{96,480},{128,0},{160,32},{192,64},{224,... | collective-permute-start | bytes 221192 | tf_op jit(solution)/shard_map/ppermute | solution.py:51
  131.7 4.4 %collective-permute-done.12 = bf16[72,512]{1,0:T(8,128)(2,1)S(1)} collective-permute-done((bf16[72,512]{1,0:T(8,128)(2,1)S(1)}, bf16[72,512]{1,0:T(8,128)(2,1)S(1)}, u32[]{:S(2)}, u32[]{:S(2)}) %collective-permute-start.12) | collective-permute-done | bytes 73760 | tf_op jit(solution)/shard_map/ppermute | solution.py:51
  136.1 7.4 %collective-permute-done.13 = bf16[72,512]{1,0:T(8,128)(2,1)S(1)} collective-permute-done((bf16[72,512]{1,0:T(8,128)(2,1)S(1)}, bf16[72,512]{1,0:T(8,128)(2,1)S(1)}, u32[]{:S(2)}, u32[]{:S(2)}) %collective-permute-start.13) | collective-permute-done | bytes 73760 | tf_op jit(solution)/shard_map/ppermute | solution.py:51
  143.5 0.1 broadcast_in_dim.67
  143.6 24.0 %all_to_all.20 = bf16[16,72,512]{2,1,0:T(8,128)(2,1)S(1)} all-to-all(bf16[16,72,512]{2,1,0:T(8,128)(2,1)S(1)} %broadcast_in_dim.67), channel_id=1, replica_groups=mesh['zh'=4,'zl'=4,'core'=2,'y'=4,'x'=4] {'y','x'}, dimensions={0} | all-to-all | bytes 2359296 | tf_op jit(solution)/shard_map/all_to_all | solution.py:30
  167.7 1.0 copy-done.3
  168.7 0.1 slice.85
  168.8 1.3 fusion
  170.2 0.9 slice_reduce_fusion.1
  171.1 0.8 broadcast_in_dim.68
  171.9 6.5 %all-to-all-start.3 = ((bf16[16,24,512]{2,1,0:T(8,128)(2,1)}), bf16[16,24,512]{2,1,0:T(8,128)(2,1)S(1)}, u32[]{:S(2)}, u32[]{:S(2)}) async-start(bf16[16,24,512]{2,1,0:T(8,128)(2,1)} %broadcast_in_dim.68), calls=%async_computation.3 | async-start | bytes 786432 | tf_op jit(solution)/shard_map/all_to_all | solution.py:30
  178.4 2.6 %reduce_sum.58 = bf16[128,512]{1,0:T(8,128)(2,1)} reduce(bf16[16,128,512]{2,1,0:T(8,128)(2,1)} %all-to-all-done.1, bf16[]{:T(256)} %constant.118.clone.1), dimensions={0}, to_apply=%region_4.5 | reduce | flops 983040 | bytes 2228226 | tf_op jit(solution)/shard_map/reduce_sum | solution.py:265
  181.0 14.0 %all-to-all-done.3 = bf16[16,24,512]{2,1,0:T(8,128)(2,1)S(1)} async-done(((bf16[16,24,512]{2,1,0:T(8,128)(2,1)}), bf16[16,24,512]{2,1,0:T(8,128)(2,1)S(1)}, u32[]{:S(2)}, u32[]{:S(2)}) %all-to-all-start.3) | async-done | bytes 393248 | tf_op jit(solution)/shard_map/all_to_all | solution.py:30
  195.0 0.7 slice_bitcast_fusion.4
  195.7 9.7 %collective-permute-start.14 = (bf16[144,512]{1,0:T(8,128)(2,1)S(1)}, bf16[144,512]{1,0:T(8,128)(2,1)S(1)}, u32[]{:S(2)}, u32[]{:S(2)}) collective-permute-start(bf16[144,512]{1,0:T(8,128)(2,1)S(1)} %pad_maximum_fusion.3), channel_id=1, source_target_pairs={{0,16},{16,0},{1,17},{17,1},{2,18},{18,2},{3,19},{19,3},{4,20},{20... | collective-permute-start | bytes 442376 | tf_op jit(solution)/shard_map/ppermute | solution.py:55
  205.3 3.0 %convert_bitcast_fusion = bf16[16,128,512]{1,2,0:T(8,128)(2,1)} fusion(bf16[64,16,512]{2,1,0:T(8,128)(2,1)S(1)} %bitcast.49, bf16[64,128]{1,0:T(8,128)(2,1)} %copy-done.5), kind=kOutput, calls=%fused_computation.2 | convolution fusion | flops 135266304 | bytes 3162112 | tf_op jit(solution)/shard_map/qk,qab->akb/dot_general | solution.py:284
  208.4 3.9 %copy.41 = bf16[16,128,512]{2,1,0:T(8,128)(2,1)} copy(bf16[16,128,512]{1,2,0:T(8,128)(2,1)} %convert_bitcast_fusion) | data formatting | bytes 4194304
  212.4 0.7 copy.40
  213.2 0.8 fusion.16
  (49 shorter events, 0.6 us)
Async XLA Ops:
  0.6 8.6 %copy-start = (bf16[16,128,512]{2,1,0:T(8,128)(2,1)S(1)}, bf16[16,128,512]{2,1,0:T(8,128)(2,1)}, u32[]{:S(2)}) copy-start(bf16[16,128,512]{2,1,0:T(8,128)(2,1)} %param.9) | copy-start | bytes 6291460
  2.3 6.9 %copy-start.6 = (s32[64]{0:T(128)}, s32[64]{0:T(128)S(1)}, u32[]{:S(2)}) copy-start(s32[64]{0:T(128)S(1)} %multiply_add_fusion) | copy-start | bytes 772
  5.7 0.6 copy-start.5
  9.6 32.3 %collective-permute-start.2 = (bf16[64,512]{1,0:T(8,128)(2,1)S(1)}, bf16[64,512]{1,0:T(8,128)(2,1)S(1)}, u32[]{:S(2)}, u32[]{:S(2)}) collective-permute-start(bf16[64,512]{1,0:T(8,128)(2,1)S(1)} %bitcast.50), channel_id=1, source_target_pairs={{0,384},{32,416},{64,448},{96,480},{128,0},{160,32},{192,64},{224,... | collective-permute-start | bytes 196616 | tf_op jit(solution)/shard_map/ppermute | solution.py:51
  22.9 19.0 %collective-permute-start.1 = (bf16[64,512]{1,0:T(8,128)(2,1)S(1)}, bf16[64,512]{1,0:T(8,128)(2,1)S(1)}, u32[]{:S(2)}, u32[]{:S(2)}) collective-permute-start(bf16[64,512]{1,0:T(8,128)(2,1)S(1)} %bitcast.51), channel_id=1, source_target_pairs={{0,256},{32,288},{64,320},{96,352},{128,384},{160,416},{192,448},{... | collective-permute-start | bytes 196616 | tf_op jit(solution)/shard_map/ppermute | solution.py:51
  27.8 14.1 %collective-permute-start = (bf16[64,512]{1,0:T(8,128)(2,1)S(1)}, bf16[64,512]{1,0:T(8,128)(2,1)S(1)}, u32[]{:S(2)}, u32[]{:S(2)}) collective-permute-start(bf16[64,512]{1,0:T(8,128)(2,1)S(1)} %bitcast.52), channel_id=1, source_target_pairs={{0,128},{32,160},{64,192},{96,224},{128,256},{160,288},{192,320},{... | collective-permute-start | bytes 196616 | tf_op jit(solution)/shard_map/ppermute | solution.py:51
  35.1 38.8 %all-to-all-start = ((bf16[16,144,512]{2,1,0:T(8,128)(2,1)}), bf16[16,144,512]{2,1,0:T(8,128)(2,1)}, u32[]{:S(2)}, u32[]{:S(2)}) async-start(bf16[16,144,512]{2,1,0:T(8,128)(2,1)} %pad_maximum_fusion), calls=%async_computation | async-start | bytes 4718592 | tf_op jit(solution)/shard_map/all_to_all | solution.py:30
  42.0 22.0 %collective-permute-start.5 = (bf16[4,64,512]{2,1,0:T(8,128)(2,1)S(1)}, bf16[4,64,512]{2,1,0:T(8,128)(2,1)S(1)}, u32[]{:S(2)}, u32[]{:S(2)}) collective-permute-start(bf16[4,64,512]{2,1,0:T(8,128)(2,1)S(1)} %pad_maximum_fusion.1), channel_id=1, source_target_pairs={{0,480},{16,496},{32,0},{48,16},{64,32},{80,48},{96,64},{112,80},{... | collective-permute-start | bytes 786440 | tf_op jit(solution)/shard_map/ppermute | solution.py:47
  48.9 15.1 %collective-permute-start.4 = (bf16[4,64,512]{2,1,0:T(8,128)(2,1)S(1)}, bf16[4,64,512]{2,1,0:T(8,128)(2,1)S(1)}, u32[]{:S(2)}, u32[]{:S(2)}) collective-permute-start(bf16[4,64,512]{2,1,0:T(8,128)(2,1)S(1)} %pad_maximum_fusion.1), channel_id=1, source_target_pairs={{0,64},{16,464},{32,96},{48,496},{64,128},{80,16},{96,160},{112,48... | collective-permute-start | bytes 786440 | tf_op jit(solution)/shard_map/ppermute | solution.py:47
  50.8 13.2 %collective-permute-start.3 = (bf16[4,64,512]{2,1,0:T(8,128)(2,1)S(1)}, bf16[4,64,512]{2,1,0:T(8,128)(2,1)S(1)}, u32[]{:S(2)}, u32[]{:S(2)}) collective-permute-start(bf16[4,64,512]{2,1,0:T(8,128)(2,1)S(1)} %pad_maximum_fusion.1), channel_id=1, source_target_pairs={{0,32},{16,48},{32,64},{48,80},{64,96},{80,112},{96,128},{112,144}... | collective-permute-start | bytes 786440 | tf_op jit(solution)/shard_map/ppermute | solution.py:47
  53.9 22.6 %copy-start.2 = (bf16[256,512]{1,0:T(8,128)(2,1)S(1)}, bf16[256,512]{1,0:T(8,128)(2,1)}, u32[]{:S(2)}) copy-start(bf16[256,512]{1,0:T(8,128)(2,1)} %pool.1) | copy-start | bytes 786436
  64.1 12.5 %collective-permute-start.6 = (bf16[16,64,512]{2,1,0:T(8,128)(2,1)S(1)}, bf16[16,64,512]{2,1,0:T(8,128)(2,1)}, u32[]{:S(2)}, u32[]{:S(2)}) collective-permute-start(bf16[16,64,512]{2,1,0:T(8,128)(2,1)S(1)} %constant_dynamic-update-slice_fusion.half), channel_id=1, source_target_pairs={{0,16},{16,0},{1,17},{17,1},{2,18},{18,2},{3,19},{19,3},{4,20},{20... | collective-permute-start | bytes 3145736 | tf_op jit(solution)/shard_map/ppermute | solution.py:55
  81.9 7.5 %collective-permute-start.7 = (bf16[4,288,512]{2,1,0:T(8,128)(2,1)S(1)}, bf16[4,288,512]{2,1,0:T(8,128)(2,1)S(1)}, u32[]{:S(2)}, u32[]{:S(2)}) collective-permute-start(bf16[4,288,512]{2,1,0:T(8,128)(2,1)S(1)} %get-tuple-element.22), channel_id=1, source_target_pairs={{0,16},{16,0},{1,17},{17,1},{2,18},{18,2},{3,19},{19,3},{4,20},{20... | collective-permute-start | bytes 3538952 | tf_op jit(solution)/shard_map/ppermute | solution.py:55
  91.6 1.3 copy-start.1
  92.9 50.6 %all-to-all-start.1 = ((bf16[16,128,512]{2,1,0:T(8,128)(2,1)}), bf16[16,128,512]{2,1,0:T(8,128)(2,1)}, u32[]{:S(2)}, u32[]{:S(2)}) async-start(bf16[16,128,512]{2,1,0:T(8,128)(2,1)} %copy-done.1), calls=%async_computation.1 | async-start | bytes 4194304 | tf_op jit(solution)/shard_map/all_to_all | solution.py:30
  97.5 11.4 %collective-permute-start.8 = (bf16[288,512]{1,0:T(8,128)(2,1)S(1)}, bf16[288,512]{1,0:T(8,128)(2,1)S(1)}, u32[]{:S(2)}, u32[]{:S(2)}) collective-permute-start(bf16[288,512]{1,0:T(8,128)(2,1)S(1)} %get-tuple-element.46), channel_id=1, source_target_pairs={{0,32},{16,48},{32,64},{48,80},{64,96},{80,112},{96,128},{112,144}... | collective-permute-start | bytes 884744 | tf_op jit(solution)/shard_map/ppermute | solution.py:47
  100.1 9.9 %collective-permute-start.10 = (bf16[288,512]{1,0:T(8,128)(2,1)S(1)}, bf16[288,512]{1,0:T(8,128)(2,1)S(1)}, u32[]{:S(2)}, u32[]{:S(2)}) collective-permute-start(bf16[288,512]{1,0:T(8,128)(2,1)S(1)} %get-tuple-element.47), channel_id=1, source_target_pairs={{0,480},{16,496},{32,0},{48,16},{64,32},{80,48},{96,64},{112,80},{... | collective-permute-start | bytes 884744 | tf_op jit(solution)/shard_map/ppermute | solution.py:47
  104.0 14.0 %collective-permute-start.9 = (bf16[288,512]{1,0:T(8,128)(2,1)S(1)}, bf16[288,512]{1,0:T(8,128)(2,1)S(1)}, u32[]{:S(2)}, u32[]{:S(2)}) collective-permute-start(bf16[288,512]{1,0:T(8,128)(2,1)S(1)} %get-tuple-element.48), channel_id=1, source_target_pairs={{0,64},{16,464},{32,96},{48,496},{64,128},{80,16},{96,160},{112,48... | collective-permute-start | bytes 884744 | tf_op jit(solution)/shard_map/ppermute | solution.py:47
  118.1 13.5 %collective-permute-start.11 = (bf16[72,512]{1,0:T(8,128)(2,1)S(1)}, bf16[72,512]{1,0:T(8,128)(2,1)S(1)}, u32[]{:S(2)}, u32[]{:S(2)}) collective-permute-start(bf16[72,512]{1,0:T(8,128)(2,1)S(1)} %pad_maximum_fusion.4), channel_id=1, source_target_pairs={{0,128},{32,160},{64,192},{96,224},{128,256},{160,288},{192,320},{... | collective-permute-start | bytes 221192 | tf_op jit(solution)/shard_map/ppermute | solution.py:51
  122.2 13.9 %collective-permute-start.12 = (bf16[72,512]{1,0:T(8,128)(2,1)S(1)}, bf16[72,512]{1,0:T(8,128)(2,1)S(1)}, u32[]{:S(2)}, u32[]{:S(2)}) collective-permute-start(bf16[72,512]{1,0:T(8,128)(2,1)S(1)} %pad_maximum_fusion.5), channel_id=1, source_target_pairs={{0,256},{32,288},{64,320},{96,352},{128,384},{160,416},{192,448},{... | collective-permute-start | bytes 221192 | tf_op jit(solution)/shard_map/ppermute | solution.py:51
  127.3 16.1 %collective-permute-start.13 = (bf16[72,512]{1,0:T(8,128)(2,1)S(1)}, bf16[72,512]{1,0:T(8,128)(2,1)S(1)}, u32[]{:S(2)}, u32[]{:S(2)}) collective-permute-start(bf16[72,512]{1,0:T(8,128)(2,1)S(1)} %pad_maximum_fusion.6), channel_id=1, source_target_pairs={{0,384},{32,416},{64,448},{96,480},{128,0},{160,32},{192,64},{224,... | collective-permute-start | bytes 221192 | tf_op jit(solution)/shard_map/ppermute | solution.py:51
  167.7 1.0 copy-start.3
  171.9 23.0 %all-to-all-start.3 = ((bf16[16,24,512]{2,1,0:T(8,128)(2,1)}), bf16[16,24,512]{2,1,0:T(8,128)(2,1)S(1)}, u32[]{:S(2)}, u32[]{:S(2)}) async-start(bf16[16,24,512]{2,1,0:T(8,128)(2,1)} %broadcast_in_dim.68), calls=%async_computation.3 | async-start | bytes 786432 | tf_op jit(solution)/shard_map/all_to_all | solution.py:30
  195.7 16.7 %collective-permute-start.14 = (bf16[144,512]{1,0:T(8,128)(2,1)S(1)}, bf16[144,512]{1,0:T(8,128)(2,1)S(1)}, u32[]{:S(2)}, u32[]{:S(2)}) collective-permute-start(bf16[144,512]{1,0:T(8,128)(2,1)S(1)} %pad_maximum_fusion.3), channel_id=1, source_target_pairs={{0,16},{16,0},{1,17},{17,1},{2,18},{18,2},{3,19},{19,3},{4,20},{20... | collective-permute-start | bytes 442376 | tf_op jit(solution)/shard_map/ppermute | solution.py:55
  208.4 4.0 %copy-start.4 = (bf16[1,128,512]{2,1,0:T(8,128)(2,1)S(1)}, bf16[1,128,512]{2,1,0:T(8,128)(2,1)}, u32[]{:S(2)}) copy-start(bf16[1,128,512]{2,1,0:T(8,128)(2,1)} %get-tuple-element.49) | copy-start | bytes 393220
  208.4 4.8 %copy-start.7 = (s32[64]{0:T(128)S(1)}, s32[64]{0:T(128)}, u32[]{:S(2)}) copy-start(s32[64]{0:T(128)} %copy-done.6) | copy-start | bytes 772

commit v4 on v3

--- a/solution.py
+++ b/solution.py
@@ -62,20 +62,37 @@
 NN, NT, TN = ((1,), (0,)), ((1,), (1,)), ((0,), (0,))
 
 
-def hot_of(line, ent_rows, columns):
-    ids = line[:, : -(-columns // 128) * 128].astype(F32)[0:1, :columns]
-    entity = lax.broadcasted_iota(jnp.int32, (ent_rows, columns), 0).astype(F32)
+def hot_of(ids, ent_rows):
+    entity = lax.broadcasted_iota(jnp.int32, (ent_rows, ids.shape[1]), 0).astype(F32)
     return jnp.where(entity == ids, 1.0, 0.0).astype(BF16)
 
 
-def gather_kernel(cap, got, heads, tails):
-    ent_rows = got.shape[1] - EXTRA
+def gather_kernel(cap, names, table, ids, heads, tails):
+    ent_rows = table.shape[1] - EXTRA
     own = tails.shape[0]
     kinds = heads.shape[0] // own
-    columns = (kinds + 1) * own * cap
-    for s in range(got.shape[0]):
-        hot = hot_of(got[s, ent_rows:, :], ent_rows, columns)
-        rows = dot(hot, got[s, :ent_rows, :], TN).astype(BF16)
+    seats = own * cap
+    columns = (kinds + 1) * seats
+    row = lax.broadcasted_iota(jnp.int32, (EXTRA, 4 * seats), 0)
+    lines = []
+    for s in range(table.shape[0]):
+        line = table[s, ent_rows:, :].astype(F32)[:, : 4 * seats]
+        lines.append(jnp.sum(jnp.where(row == names[own * kinds], line, 0.0), axis=0, keepdims=True))
+    lines = jnp.concatenate(lines, axis=0)
+    head, tail, relation, limit = [lines[:, i * seats : (i + 1) * seats] for i in range(4)]
+    seat = lax.broadcasted_iota(jnp.int32, head.shape, 1)
+    live = (seat % cap).astype(F32) < limit
+    found = []
+    for w in range(kinds):
+        name = jnp.full(head.shape, names[w], jnp.int32)
+        for o in range(1, own):
+            name = jnp.where(seat >= o * cap, names[o * kinds + w], name)
+        found.append(jnp.where(live & (relation == name.astype(F32)), head, -1.0))
+    found.append(jnp.where(live, tail, -1.0))
+    ids[...] = jnp.concatenate(found + [jnp.full(head.shape, -1.0, F32)], axis=1)
+    for s in range(table.shape[0]):
+        hot = hot_of(ids[s : s + 1, :columns], ent_rows)
+        rows = dot(hot, table[s, :ent_rows, :], TN).astype(BF16)
         for kind in range(kinds + 1):
             for o in range(own):
                 at = (kind * own + o) * cap
@@ -128,7 +145,7 @@
             target[s, 4 * mine * rows_dev :, :] = jnp.concatenate(pieces, axis=0).astype(BF16)
 
 
-def scatter_kernel(cap, lines, dquery, dtail, mats, out, dheads):
+def scatter_kernel(cap, ids, dquery, dtail, mats, out, dheads):
     own = dquery.shape[0]
     kinds = mats.shape[0] // own
     columns = (kinds + 1) * own * cap
@@ -137,18 +154,34 @@
         for w in range(kinds):
             dheads[o * kinds + w] = dot(dquery[o], mats[o * kinds + w], NT).astype(BF16)
     for s in range(out.shape[0]):
-        hot = hot_of(lines[s], ent_rows, columns)
+        hot = hot_of(ids[s : s + 1, :columns], ent_rows)
         at = slice(s * cap, (s + 1) * cap)
         grads = [dheads[o * kinds + w, at, :] for w in range(kinds) for o in range(own)]
         grads += [dtail[o, at, :] for o in range(own)]
         out[s] = dot(hot, jnp.concatenate(grads, axis=0), NN).astype(BF16)
 
 
-def call(kernel, outs, flops, in_specs=None, scratch=()):
+def core_kernel(rows_dev, ordered, sums, out, wide):
+    rels = ordered.shape[0]
+    each = rels // sums.shape[0] * rows_dev
+    lanes = wide.shape[0]
+    for s in range(sums.shape[0]):
+        rows = sums[s, :each, :].astype(F32)
+        for lane in range(lanes):
+            wide[lane, s * each : (s + 1) * each, :] = rows[:, lane * 128 : (lane + 1) * 128]
+    weights = ordered[...]
+    for a in range(rows_dev):
+        rows = [wide[lane, pl.ds(a, rels, stride=rows_dev), :] for lane in range(lanes)]
+        out[a] = dot(weights, jnp.concatenate(rows, axis=1).astype(BF16), TN).astype(BF16)
+
+
+def call(kernel, outs, flops, in_specs, scratch=(), dtypes=None):
     vmem = pl.BlockSpec(memory_space=pltpu.VMEM)
     return pl.pallas_call(
         kernel,
-        out_shape=tuple(jax.ShapeDtypeStruct(shape, BF16) for shape in outs),
+        out_shape=tuple(
+            jax.ShapeDtypeStruct(shape, dtype) for shape, dtype in zip(outs, dtypes or [BF16] * len(outs))
+        ),
         in_specs=in_specs,
         out_specs=tuple(vmem for _ in outs),
         scratch_shapes=scratch,
@@ -179,25 +212,34 @@
     order_sel = (slot_of[None, :] == qindex[:, None]).astype(BF16)
     ordered = jnp.dot(order_sel, rel_emb, preferred_element_type=F32).astype(BF16)
 
-    relhot = rel_ids[None, :] == jnp.arange(rels, dtype=jnp.int32)[:, None]
-    rank_slot = jnp.sum(jnp.where(relhot, rank[:, None], 0), axis=0)
-    used = (jnp.arange(cap, dtype=jnp.int32)[None, :] < fill[0][:, None]).reshape(-1)
-    numbers = [jnp.where(used & (rank_slot == w), head_ids, -1) for w in range(per_owner)]
-    numbers.append(jnp.where(used, tail_ids, -1))
-    numbers = jnp.concatenate([a.reshape(REPS, seats) for a in numbers], axis=1).astype(BF16)
-    numbers = jnp.pad(numbers[:, None, :], ((0, 0), (0, EXTRA - 1), (0, feats - numbers.shape[1])))
-    sent = jnp.concatenate(
-        [jnp.broadcast_to(ents[None], (REPS, ent_rows, feats)), numbers], axis=1
-    )
+    limits = jnp.broadcast_to(fill[0][:, None], (owners, cap))
+    numbers = [a.reshape(REPS, seats) for a in (head_ids, tail_ids, rel_ids, limits)]
+    numbers = jnp.concatenate(numbers, axis=1).astype(BF16)
+    numbers = jnp.pad(numbers, ((0, EXTRA - REPS), (0, feats - numbers.shape[1])))
+    table = lax.all_gather(jnp.concatenate([ents, numbers]), REP, axis=0, tiled=False)
+
+    vmem = pl.BlockSpec(memory_space=pltpu.VMEM)
+    smem = pl.BlockSpec(memory_space=pltpu.SMEM)
+    slots = REPS * cap
+    block = slots * feats * feats * 2
+
     own_rows = lax.dynamic_slice_in_dim(ordered, g * mine, mine, 0)
-    own_rows, sent = lax.optimization_barrier((own_rows, sent))
-    got = exchange(sent, REP)
-
     part = jnp.einsum("wk,akb->wab", own_rows, core, preferred_element_type=F32).astype(BF16)
     part = part.reshape(mine * rows_dev, feats)
     far = jnp.stack([part] + [far_move(part, p) for p in STEPS[1:]])
     half = jnp.concatenate([far] + [near_move(far, s) for s in STEPS[1:]])
     other = swap_core(half)
+
+    named = slot_of[None, :] == g * mine + jnp.arange(mine, dtype=jnp.int32)[:, None]
+    names = jnp.sum(jnp.where(named, qindex[None, :], 0), axis=1)
+    names = jnp.concatenate([names, g[None]]).astype(jnp.int32)
+    ids, heads, tails = call(
+        functools.partial(gather_kernel, cap),
+        ((REPS, 4 * seats), (mine, slots, feats), (own, slots, feats)),
+        REPS * 3 * seats * ent_rows * feats * 2,
+        [smem, vmem],
+        dtypes=(F32, BF16, BF16),
+    )(names, table)
 
     entry = jnp.arange(Z, dtype=jnp.int32)
     starts = []
@@ -207,17 +249,8 @@
             starts.append((chip * CORES + core_of) * rows_dev)
     starts = jnp.stack(starts)
 
-    vmem = pl.BlockSpec(memory_space=pltpu.VMEM)
-    smem = pl.BlockSpec(memory_space=pltpu.SMEM)
-    slots = REPS * cap
-    block = slots * feats * feats * 2
-    heads, tails = call(
-        functools.partial(gather_kernel, cap),
-        ((mine, slots, feats), (own, slots, feats)),
-        REPS * 3 * seats * ent_rows * feats * 2,
-        [vmem],
-    )(got)
-    sum_rows = 4 * (mine * rows_dev + pool_dev)
+    split = 4 * mine * rows_dev
+    sum_rows = split + 4 * pool_dev
     mats, dquery, dtail, given, kept = call(
         functools.partial(score_kernel, scale, rows_dev),
         (
@@ -232,25 +265,26 @@
         (pltpu.VMEM((mine, feats, feats), BF16), pltpu.VMEM((pool_rows, feats), F32)),
     )(starts, heads, tails, half, other, pool)
 
-    pair = (kept.astype(F32) + swap_core(given).astype(F32)).astype(BF16)
-    pair, dquery = lax.optimization_barrier((pair, dquery))
-    (ent_part,) = call(
+    (sent,) = call(
         functools.partial(scatter_kernel, cap),
         ((REPS, ent_rows, feats),),
         mine * block + REPS * 3 * seats * ent_rows * feats * 2,
         [vmem] * 4,
         (pltpu.VMEM((mine, slots, feats), BF16),),
-    )(got[:, ent_rows:], dquery, dtail, mats)
-    back = exchange(ent_part, REP)
+    )(ids, dquery, dtail, mats)
+
+    given, sent = lax.optimization_barrier((swap_core(given), sent))
+    back = exchange(sent, REP)
+    pair = (kept.astype(F32) + given.astype(F32)).astype(BF16)
     total = pair[0].astype(F32)
     for s in STEPS[1:]:
         total = total + near_move(pair[s], s).astype(F32)
     total = total.astype(BF16)
-    split = 4 * mine * rows_dev
+    each = mine * rows_dev
     blocks = [
         jnp.concatenate(
             [
-                total[p * mine * rows_dev : (p + 1) * mine * rows_dev],
+                total[p * each : (p + 1) * each],
                 total[split + p * pool_dev : split + (p + 1) * pool_dev],
             ]
         )
@@ -259,17 +293,28 @@
     own_sum = blocks[0].astype(F32)
     for p in STEPS[1:]:
         own_sum = own_sum + far_move(blocks[p], p).astype(F32)
-    own_sum = own_sum.astype(BF16)
-
-    own_sum, back = lax.optimization_barrier((own_sum, back))
+    own_sum, back = lax.optimization_barrier((own_sum.astype(BF16), back))
     ent_grad = jnp.sum(back.astype(F32), axis=0).astype(BF16)
-    all_sums = spread(own_sum, REP, REPS)
-    all_rows = all_sums[:, : mine * rows_dev].reshape(rels, rows_dev, feats)
-    pool_own = jnp.sum(all_sums[:, mine * rows_dev :].astype(F32), axis=0).astype(BF16)
-    rel_own = jnp.einsum("qab,akb->qk", all_rows, core, preferred_element_type=F32).astype(BF16)
+
+    sums = spread(own_sum, REP, REPS)
+    rel_own = jnp.einsum(
+        "gwab,akb->gwk",
+        sums[:, :each].reshape(REPS, mine, rows_dev, feats),
+        core,
+        preferred_element_type=F32,
+    ).astype(BF16)
+    pool_own = jnp.sum(sums[:, each:].astype(F32), axis=0).astype(BF16)
 
     rel_rows = rels * feats_rel // feats
     small = spread(jnp.concatenate([rel_own.reshape(rel_rows, feats), pool_own]), LINE, Z)
+    (core_grad,) = call(
+        functools.partial(core_kernel, rows_dev),
+        ((rows_dev, feats_rel, feats),),
+        2 * rows_dev * feats_rel * rels * feats,
+        [vmem] * 2,
+        (pltpu.VMEM((feats // 128, rels * rows_dev, 128), F32),),
+    )(ordered, sums)
+    small, core_grad = lax.optimization_barrier((small, core_grad))
     rel_own = jnp.sum(small[:, :rel_rows].astype(F32), axis=0).astype(BF16)
     small = jnp.concatenate([rel_own, small[:, rel_rows:].reshape(-1, feats)])
     small_other = swap_core(small)
@@ -281,9 +326,6 @@
     rel_grad = lax.dot_general(
         order_sel, rel_ordered, (((0,), (0,)), ((), ())), preferred_element_type=F32
     )
-    core_grad = jnp.einsum(
-        "qk,qab->akb", ordered, all_rows, preferred_element_type=F32
-    ).astype(BF16)
     return (core_grad, rel_grad, ent_grad, pool_grad)
 
 

time: 215 us -> 227 us (1.056)
  between operations: 1.18 us -> 14.5 us
  starting transfers between devices: 95.1 us -> 100 us
  waiting for transfers between devices: 55.6 us -> 52.2 us
  local copies, waits for them, and re-layouts: 11.9 us -> 8.51 us
  matrix products: 6.39 us -> 3.53 us
    ppermute x6, starting transfers between devices: 38.9 us -> 45.4 us  [far_move(): lax.ppermute(block, LINE, [(z, (z + 4 * step) % Z) for z in range(Z)])]
    all_to_all x3 -> x2, waiting for transfers between devices: 20.3 us -> 13.8 us  [exchange(): return lax.all_to_all(blocks, axis, split_axis=0, concat_axis=0, tiled=True)]
    all_gather x0 -> x1, waiting for transfers between devices: none -> 4.47 us  [body(): lax.all_gather(jnp.concatenate([ents, numbers]), REP, axis=0, tiled=False)]
    ppermute x6, starting transfers between devices: 20.3 us -> 24.3 us  [near_move(): return lax.ppermute(block, REL, pairs)]
    all_to_all x3 -> x2, starting transfers between devices: 17.7 us -> 14 us  [exchange(): return lax.all_to_all(blocks, axis, split_axis=0, concat_axis=0, tiled=True)]
    dot_general x2 -> x1, matrix products: 4.36 us -> 1.49 us  [body(): jnp.einsum('gwab,akb->gwk', sums[:, :each].reshape(REPS, mine, rows_dev,...]
    ppermute x6, waiting for transfers between devices: 11.8 us -> 14.2 us  [far_move(): lax.ppermute(block, LINE, [(z, (z + 4 * step) % Z) for z in range(Z)])]
    ppermute x6, waiting for transfers between devices: 22 us -> 19.7 us  [near_move(): return lax.ppermute(block, REL, pairs)]
  transfers between devices with their start and end apart: 18 -> 18, of which waited for: 9 -> 10; matrix products, arithmetic and copies ran while one was open for 5% -> 3% of each run, Pallas kernels for 1% -> 3%
where the time goes in v4:
time: 227 us; the launch traced here: 226 us
  starting transfers between devices  100 us (44%)
  waiting for transfers between devices  52.2 us (23%)
  blocking collectives  22.7 us (10%)
  between operations  14.5 us (6%)
  other arithmetic  12 us (5%)
  Pallas kernels  11.7 us (5%)
  local copies, waits for them, and re-layouts  8.51 us (4%)
  matrix products  3.53 us (2%)
    ppermute x6, starting transfers between devices, far_move(): lax.ppermute(block, LINE, [(z, (z + 4 * step) % Z) for z in range(Z)])  45.4 us
    ppermute x6, starting transfers between devices, near_move(): return lax.ppermute(block, REL, pairs)  24.3 us
    all_to_all x1, blocking collectives, exchange(): return lax.all_to_all(blocks, axis, split_axis=0, concat_axis=0, tiled=True)  22.7 us
    ppermute x6, waiting for transfers between devices, near_move(): return lax.ppermute(block, REL, pairs)  19.7 us
    ppermute x3, starting transfers between devices, swap_core(): return lax.ppermute(block, 'core', [(0, 1), (1, 0)])  16.7 us
    ppermute x6, waiting for transfers between devices, far_move(): lax.ppermute(block, LINE, [(z, (z + 4 * step) % Z) for z in range(Z)])  14.2 us
    all_to_all x2, starting transfers between devices, exchange(): return lax.all_to_all(blocks, axis, split_axis=0, concat_axis=0, tiled=True)  14 us
    all_to_all x2, waiting for transfers between devices, exchange(): return lax.all_to_all(blocks, axis, split_axis=0, concat_axis=0, tiled=True)  13.8 us
  transfers between devices with their start and end apart: 18, of which 10 were waited for; matrix products, arithmetic and copies ran while one was open for 3% of the time, Pallas kernels for 3%

profile of v4, /device:TPU:1, one launch (start us, length us, event | category | flops | bytes accessed | tf_op | source)
XLA Modules:
  0.0 225.5 jit_solution(2316693759950005912)
XLA Ops:
  7.2 0.8 convert_reduce_fusion.1
  8.0 0.7 convert.23
  8.7 0.1 reshape.323
  8.8 0.7 convert.21
  9.5 0.1 reshape.321
  9.6 0.7 convert.22
  10.3 0.1 reshape.322
  10.4 0.1 reshape.331
  10.4 0.1 broadcast_in_dim.65
  10.5 0.1 broadcast_in_dim.66
  10.6 0.1 fusion.24
  10.7 1.6 pad_maximum_fusion.2
  12.3 0.9 convert_reduce_fusion
  13.2 0.7 multiply_add_fusion
  13.9 0.8 convolution_convert_fusion.1.ordered
  14.7 0.4 convolution_convert_fusion
  15.2 13.3 %collective-permute-start.2 = (bf16[64,512]{1,0:T(8,128)(2,1)S(1)}, bf16[64,512]{1,0:T(8,128)(2,1)S(1)}, u32[]{:S(2)}, u32[]{:S(2)}) collective-permute-start(bf16[64,512]{1,0:T(8,128)(2,1)S(1)} %bitcast.64), channel_id=1, source_target_pairs={{0,384},{32,416},{64,448},{96,480},{128,0},{160,32},{192,64},{224,... | collective-permute-start | bytes 196616 | tf_op jit(solution)/shard_map/ppermute | solution.py:51
  28.4 4.9 %collective-permute-start.1 = (bf16[64,512]{1,0:T(8,128)(2,1)S(1)}, bf16[64,512]{1,0:T(8,128)(2,1)S(1)}, u32[]{:S(2)}, u32[]{:S(2)}) collective-permute-start(bf16[64,512]{1,0:T(8,128)(2,1)S(1)} %bitcast.65), channel_id=1, source_target_pairs={{0,256},{32,288},{64,320},{96,352},{128,384},{160,416},{192,448},{... | collective-permute-start | bytes 196616 | tf_op jit(solution)/shard_map/ppermute | solution.py:51
  33.4 7.3 %collective-permute-start = (bf16[64,512]{1,0:T(8,128)(2,1)S(1)}, bf16[64,512]{1,0:T(8,128)(2,1)S(1)}, u32[]{:S(2)}, u32[]{:S(2)}) collective-permute-start(bf16[64,512]{1,0:T(8,128)(2,1)S(1)} %bitcast.66), channel_id=1, source_target_pairs={{0,128},{32,160},{64,192},{96,224},{128,256},{160,288},{192,320},{... | collective-permute-start | bytes 196616 | tf_op jit(solution)/shard_map/ppermute | solution.py:51
  40.7 1.8 collective-permute-done.1
  42.4 4.5 %collective-permute-done = bf16[64,512]{1,0:T(8,128)(2,1)S(1)} collective-permute-done((bf16[64,512]{1,0:T(8,128)(2,1)S(1)}, bf16[64,512]{1,0:T(8,128)(2,1)S(1)}, u32[]{:S(2)}, u32[]{:S(2)}) %collective-permute-start) | collective-permute-done | bytes 65568 | tf_op jit(solution)/shard_map/ppermute | solution.py:51
  47.0 7.4 %collective-permute-start.5 = (bf16[4,64,512]{2,1,0:T(8,128)(2,1)S(1)}, bf16[4,64,512]{2,1,0:T(8,128)(2,1)S(1)}, u32[]{:S(2)}, u32[]{:S(2)}) collective-permute-start(bf16[4,64,512]{2,1,0:T(8,128)(2,1)S(1)} %pad_maximum_fusion), channel_id=1, source_target_pairs={{0,480},{16,496},{32,0},{48,16},{64,32},{80,48},{96,64},{112,80},{... | collective-permute-start | bytes 786440 | tf_op jit(solution)/shard_map/ppermute | solution.py:47
  54.4 1.9 collective-permute-start.4
  56.4 3.1 %collective-permute-start.3 = (bf16[4,64,512]{2,1,0:T(8,128)(2,1)S(1)}, bf16[4,64,512]{2,1,0:T(8,128)(2,1)S(1)}, u32[]{:S(2)}, u32[]{:S(2)}) collective-permute-start(bf16[4,64,512]{2,1,0:T(8,128)(2,1)S(1)} %pad_maximum_fusion), channel_id=1, source_target_pairs={{0,32},{16,48},{32,64},{48,80},{64,96},{80,112},{96,128},{112,144}... | collective-permute-start | bytes 786440 | tf_op jit(solution)/shard_map/ppermute | solution.py:47
  59.5 10.0 %collective-permute-done.3 = bf16[4,64,512]{2,1,0:T(8,128)(2,1)S(1)} collective-permute-done((bf16[4,64,512]{2,1,0:T(8,128)(2,1)S(1)}, bf16[4,64,512]{2,1,0:T(8,128)(2,1)S(1)}, u32[]{:S(2)}, u32[]{:S(2)}) %collective-permute-start.3) | collective-permute-done | bytes 262176 | tf_op jit(solution)/shard_map/ppermute | solution.py:47
  69.6 3.4 %collective-permute-start.6 = (bf16[16,64,512]{2,1,0:T(8,128)(2,1)S(1)}, bf16[16,64,512]{2,1,0:T(8,128)(2,1)}, u32[]{:S(2)}, u32[]{:S(2)}) collective-permute-start(bf16[16,64,512]{2,1,0:T(8,128)(2,1)S(1)} %constant_dynamic-update-slice_fusion.half), channel_id=1, source_target_pairs={{0,16},{16,0},{1,17},{17,1},{2,18},{18,2},{3,19},{19,3},{4,20},{20... | collective-permute-start | bytes 3145736 | tf_op jit(solution)/shard_map/ppermute | solution.py:55
  73.1 0.2 select_reduce_fusion
  73.2 0.1 pad_add_fusion.1.names
  73.4 4.5 %all-gather.3.cloned.1.call-done = bf16[2304,512]{1,0:T(8,128)(2,1)} async-done(((bf16[144,512]{1,0:T(8,128)(2,1)}), bf16[2304,512]{1,0:T(8,128)(2,1)}) %all-gather.3.cloned.1.call-update) | async-done | bytes 2359312 | tf_op jit(solution)/shard_map/all_gather | solution.py:219
  77.9 1.7 copy-done.2
  79.5 1.7 shard_map.120
  81.3 1.2 copy-done.4
  82.5 0.9 copy-done.5
  83.4 5.4 %shard_map.121 = (bf16[4,512,512]{2,1,0:T(8,128)(2,1)S(1)}, bf16[2,512,512]{2,1,0:T(8,128)(2,1)S(1)}, bf16[2,512,512]{2,1,0:T(8,128)(2,1)S(1)}, bf16[4,288,512]{2,1,0:T(8,128)(2,1)S(1)}, bf16[4,288,512]{2,1,0:T(8,128)(2,1)S(1)}) custom-call(s32[4,16]{1,0:T(4,128)S(1)} %pad_add_fusion.starts, bf16[4,512,512]{2,1,0:T(8,128)(2,1)S(1)} %get-tuple-element.18.heads, ...), custom_call_target="tpu_custom_call" | custom-call | flops 2952790016 | bytes 8388608 | tf_op jit(solution)/shard_map/pallas_call | solution.py:254
  88.8 3.6 %collective-permute-start.7 = (bf16[4,288,512]{2,1,0:T(8,128)(2,1)S(1)}, bf16[4,288,512]{2,1,0:T(8,128)(2,1)}, u32[]{:S(2)}, u32[]{:S(2)}) collective-permute-start(bf16[4,288,512]{2,1,0:T(8,128)(2,1)S(1)} %get-tuple-element.21), channel_id=1, source_target_pairs={{0,16},{16,0},{1,17},{17,1},{2,18},{18,2},{3,19},{19,3},{4,20},{20... | collective-permute-start | bytes 3538952 | tf_op jit(solution)/shard_map/ppermute | solution.py:55
  92.4 1.8 shard_map.122
  94.3 1.3 copy-done.1
  95.6 4.6 %all-to-all-start = ((bf16[16,128,512]{2,1,0:T(8,128)(2,1)}), bf16[16,128,512]{2,1,0:T(8,128)(2,1)}, u32[]{:S(2)}, u32[]{:S(2)}) async-start(bf16[16,128,512]{2,1,0:T(8,128)(2,1)} %copy-done.1), calls=%async_computation | async-start | bytes 4194304 | tf_op jit(solution)/shard_map/all_to_all | solution.py:30
  100.2 1.6 add_convert_fusion
  101.8 3.2 %collective-permute-start.8 = (bf16[288,512]{1,0:T(8,128)(2,1)S(1)}, bf16[288,512]{1,0:T(8,128)(2,1)S(1)}, u32[]{:S(2)}, u32[]{:S(2)}) collective-permute-start(bf16[288,512]{1,0:T(8,128)(2,1)S(1)} %get-tuple-element.32), channel_id=1, source_target_pairs={{0,32},{16,48},{32,64},{48,80},{64,96},{80,112},{96,128},{112,144}... | collective-permute-start | bytes 884744 | tf_op jit(solution)/shard_map/ppermute | solution.py:47
  105.0 4.4 %collective-permute-start.10 = (bf16[288,512]{1,0:T(8,128)(2,1)S(1)}, bf16[288,512]{1,0:T(8,128)(2,1)S(1)}, u32[]{:S(2)}, u32[]{:S(2)}) collective-permute-start(bf16[288,512]{1,0:T(8,128)(2,1)S(1)} %get-tuple-element.33), channel_id=1, source_target_pairs={{0,480},{16,496},{32,0},{48,16},{64,32},{80,48},{96,64},{112,80},{... | collective-permute-start | bytes 884744 | tf_op jit(solution)/shard_map/ppermute | solution.py:47
  109.5 4.2 %collective-permute-start.9 = (bf16[288,512]{1,0:T(8,128)(2,1)S(1)}, bf16[288,512]{1,0:T(8,128)(2,1)S(1)}, u32[]{:S(2)}, u32[]{:S(2)}) collective-permute-start(bf16[288,512]{1,0:T(8,128)(2,1)S(1)} %get-tuple-element.34), channel_id=1, source_target_pairs={{0,64},{16,464},{32,96},{48,496},{64,128},{80,16},{96,160},{112,48... | collective-permute-start | bytes 884744 | tf_op jit(solution)/shard_map/ppermute | solution.py:47
  113.7 1.1 collective-permute-done.8
  114.8 1.1 collective-permute-done.10
  115.9 7.4 %collective-permute-done.9 = bf16[288,512]{1,0:T(8,128)(2,1)S(1)} collective-permute-done((bf16[288,512]{1,0:T(8,128)(2,1)S(1)}, bf16[288,512]{1,0:T(8,128)(2,1)S(1)}, u32[]{:S(2)}, u32[]{:S(2)}) %collective-permute-start.9) | collective-permute-done | bytes 294944 | tf_op jit(solution)/shard_map/ppermute | solution.py:47
  123.4 0.2 fusion.14
  123.6 7.4 %collective-permute-start.11 = (bf16[72,512]{1,0:T(8,128)(2,1)S(1)}, bf16[72,512]{1,0:T(8,128)(2,1)S(1)}, u32[]{:S(2)}, u32[]{:S(2)}) collective-permute-start(bf16[72,512]{1,0:T(8,128)(2,1)S(1)} %pad_maximum_fusion.4), channel_id=1, source_target_pairs={{0,128},{32,160},{64,192},{96,224},{128,256},{160,288},{192,320},{... | collective-permute-start | bytes 221192 | tf_op jit(solution)/shard_map/ppermute | solution.py:51
  131.0 6.0 %collective-permute-start.12 = (bf16[72,512]{1,0:T(8,128)(2,1)S(1)}, bf16[72,512]{1,0:T(8,128)(2,1)S(1)}, u32[]{:S(2)}, u32[]{:S(2)}) collective-permute-start(bf16[72,512]{1,0:T(8,128)(2,1)S(1)} %pad_maximum_fusion.5), channel_id=1, source_target_pairs={{0,256},{32,288},{64,320},{96,352},{128,384},{160,416},{192,448},{... | collective-permute-start | bytes 221192 | tf_op jit(solution)/shard_map/ppermute | solution.py:51
  137.0 6.6 %collective-permute-start.13 = (bf16[72,512]{1,0:T(8,128)(2,1)S(1)}, bf16[72,512]{1,0:T(8,128)(2,1)S(1)}, u32[]{:S(2)}, u32[]{:S(2)}) collective-permute-start(bf16[72,512]{1,0:T(8,128)(2,1)S(1)} %pad_maximum_fusion.6), channel_id=1, source_target_pairs={{0,384},{32,416},{64,448},{96,480},{128,0},{160,32},{192,64},{224,... | collective-permute-start | bytes 221192 | tf_op jit(solution)/shard_map/ppermute | solution.py:51
  143.6 2.1 collective-permute-done.12
  145.7 5.7 %collective-permute-done.13 = bf16[72,512]{1,0:T(8,128)(2,1)S(1)} collective-permute-done((bf16[72,512]{1,0:T(8,128)(2,1)S(1)}, bf16[72,512]{1,0:T(8,128)(2,1)S(1)}, u32[]{:S(2)}, u32[]{:S(2)}) %collective-permute-start.13) | collective-permute-done | bytes 73760 | tf_op jit(solution)/shard_map/ppermute | solution.py:51
  151.6 22.7 %all_to_all.15.sums = bf16[16,72,512]{2,1,0:T(8,128)(2,1)S(1)} all-to-all(bf16[16,72,512]{2,1,0:T(8,128)(2,1)S(1)} %broadcast_in_dim.67), channel_id=1, replica_groups=mesh['zh'=4,'zl'=4,'core'=2,'y'=4,'x'=4] {'y','x'}, dimensions={0} | all-to-all | bytes 2359296 | tf_op jit(solution)/shard_map/all_to_all | solution.py:30
  174.3 0.1 slice.84
  174.4 1.5 fusion.8
  176.0 0.8 broadcast_in_dim.68
  176.8 9.4 %all-to-all-start.2 = ((bf16[16,24,512]{2,1,0:T(8,128)(2,1)}), bf16[16,24,512]{2,1,0:T(8,128)(2,1)}, u32[]{:S(2)}, u32[]{:S(2)}) async-start(bf16[16,24,512]{2,1,0:T(8,128)(2,1)} %broadcast_in_dim.68), calls=%async_computation.2 | async-start | bytes 786432 | tf_op jit(solution)/shard_map/all_to_all | solution.py:30
  186.2 2.8 %shard_map.123 = bf16[16,128,512]{2,1,0:T(8,128)(2,1)} custom-call(bf16[64,128]{1,0:T(8,128)(2,1)S(1)} %convolution_convert_fusion.1.ordered, bf16[16,72,512]{2,1,0:T(8,128)(2,1)S(1)} %all_to_all.15.sums), custom_call_target="tpu_custom_call" | custom-call | flops 134217728 | bytes 8388608 | tf_op jit(solution)/shard_map/pallas_call | solution.py:310
  188.9 13.8 %all-to-all-done.2 = bf16[16,24,512]{2,1,0:T(8,128)(2,1)} async-done(((bf16[16,24,512]{2,1,0:T(8,128)(2,1)}), bf16[16,24,512]{2,1,0:T(8,128)(2,1)}, u32[]{:S(2)}, u32[]{:S(2)}) %all-to-all-start.2) | async-done | bytes 393248 | tf_op jit(solution)/shard_map/all_to_all | solution.py:30
  202.8 1.0 slice_reduce_fusion
  203.8 0.9 slice_bitcast_fusion.5
  204.7 9.7 %collective-permute-start.14 = (bf16[144,512]{1,0:T(8,128)(2,1)S(1)}, bf16[144,512]{1,0:T(8,128)(2,1)S(1)}, u32[]{:S(2)}, u32[]{:S(2)}) collective-permute-start(bf16[144,512]{1,0:T(8,128)(2,1)S(1)} %pad_maximum_fusion.3), channel_id=1, source_target_pairs={{0,16},{16,0},{1,17},{17,1},{2,18},{18,2},{3,19},{19,3},{4,20},{20... | collective-permute-start | bytes 442376 | tf_op jit(solution)/shard_map/ppermute | solution.py:55
  214.4 2.6 %reduce_sum.58 = bf16[128,512]{1,0:T(8,128)(2,1)} reduce(bf16[16,128,512]{2,1,0:T(8,128)(2,1)} %all-to-all-done, bf16[]{:T(256)} %constant.115.clone.1), dimensions={0}, to_apply=%region_4.5 | reduce | flops 983040 | bytes 2228226 | tf_op jit(solution)/shard_map/reduce_sum | solution.py:297
  217.1 0.7 copy.29
  217.9 0.8 fusion.20
  (48 shorter events, 0.7 us)
Async XLA Ops:
  7.2 7.6 %copy-start = (bf16[16,128,512]{2,1,0:T(8,128)(2,1)S(1)}, bf16[16,128,512]{2,1,0:T(8,128)(2,1)}, u32[]{:S(2)}) copy-start(bf16[16,128,512]{2,1,0:T(8,128)(2,1)} %param.9) | copy-start | bytes 6291460
  7.2 70.7 %all-gather.3.cloned.1.call-start = ((), (), s32[]{:S(2)}) async-start(), calls=%async_computation.3 | async-start | bytes 2506752 | tf_op jit(solution)/shard_map/all_gather | solution.py:219
  15.2 25.5 %collective-permute-start.2 = (bf16[64,512]{1,0:T(8,128)(2,1)S(1)}, bf16[64,512]{1,0:T(8,128)(2,1)S(1)}, u32[]{:S(2)}, u32[]{:S(2)}) collective-permute-start(bf16[64,512]{1,0:T(8,128)(2,1)S(1)} %bitcast.64), channel_id=1, source_target_pairs={{0,384},{32,416},{64,448},{96,480},{128,0},{160,32},{192,64},{224,... | collective-permute-start | bytes 196616 | tf_op jit(solution)/shard_map/ppermute | solution.py:51
  28.4 14.0 %collective-permute-start.1 = (bf16[64,512]{1,0:T(8,128)(2,1)S(1)}, bf16[64,512]{1,0:T(8,128)(2,1)S(1)}, u32[]{:S(2)}, u32[]{:S(2)}) collective-permute-start(bf16[64,512]{1,0:T(8,128)(2,1)S(1)} %bitcast.65), channel_id=1, source_target_pairs={{0,256},{32,288},{64,320},{96,352},{128,384},{160,416},{192,448},{... | collective-permute-start | bytes 196616 | tf_op jit(solution)/shard_map/ppermute | solution.py:51
  33.4 13.6 %collective-permute-start = (bf16[64,512]{1,0:T(8,128)(2,1)S(1)}, bf16[64,512]{1,0:T(8,128)(2,1)S(1)}, u32[]{:S(2)}, u32[]{:S(2)}) collective-permute-start(bf16[64,512]{1,0:T(8,128)(2,1)S(1)} %bitcast.66), channel_id=1, source_target_pairs={{0,128},{32,160},{64,192},{96,224},{128,256},{160,288},{192,320},{... | collective-permute-start | bytes 196616 | tf_op jit(solution)/shard_map/ppermute | solution.py:51
  47.0 22.6 %collective-permute-start.5 = (bf16[4,64,512]{2,1,0:T(8,128)(2,1)S(1)}, bf16[4,64,512]{2,1,0:T(8,128)(2,1)S(1)}, u32[]{:S(2)}, u32[]{:S(2)}) collective-permute-start(bf16[4,64,512]{2,1,0:T(8,128)(2,1)S(1)} %pad_maximum_fusion), channel_id=1, source_target_pairs={{0,480},{16,496},{32,0},{48,16},{64,32},{80,48},{96,64},{112,80},{... | collective-permute-start | bytes 786440 | tf_op jit(solution)/shard_map/ppermute | solution.py:47
  54.4 15.1 %collective-permute-start.4 = (bf16[4,64,512]{2,1,0:T(8,128)(2,1)S(1)}, bf16[4,64,512]{2,1,0:T(8,128)(2,1)S(1)}, u32[]{:S(2)}, u32[]{:S(2)}) collective-permute-start(bf16[4,64,512]{2,1,0:T(8,128)(2,1)S(1)} %pad_maximum_fusion), channel_id=1, source_target_pairs={{0,64},{16,464},{32,96},{48,496},{64,128},{80,16},{96,160},{112,48... | collective-permute-start | bytes 786440 | tf_op jit(solution)/shard_map/ppermute | solution.py:47
  56.4 13.2 %collective-permute-start.3 = (bf16[4,64,512]{2,1,0:T(8,128)(2,1)S(1)}, bf16[4,64,512]{2,1,0:T(8,128)(2,1)S(1)}, u32[]{:S(2)}, u32[]{:S(2)}) collective-permute-start(bf16[4,64,512]{2,1,0:T(8,128)(2,1)S(1)} %pad_maximum_fusion), channel_id=1, source_target_pairs={{0,32},{16,48},{32,64},{48,80},{64,96},{80,112},{96,128},{112,144}... | collective-permute-start | bytes 786440 | tf_op jit(solution)/shard_map/ppermute | solution.py:47
  69.6 11.6 %copy-start.3 = (bf16[16,64,512]{2,1,0:T(8,128)(2,1)}, bf16[16,64,512]{2,1,0:T(8,128)(2,1)S(1)}, u32[]{:S(2)}) copy-start(bf16[16,64,512]{2,1,0:T(8,128)(2,1)S(1)} %constant_dynamic-update-slice_fusion.half) | copy-start | bytes 3145732
  69.6 11.6 %collective-permute-start.6 = (bf16[16,64,512]{2,1,0:T(8,128)(2,1)S(1)}, bf16[16,64,512]{2,1,0:T(8,128)(2,1)}, u32[]{:S(2)}, u32[]{:S(2)}) collective-permute-start(bf16[16,64,512]{2,1,0:T(8,128)(2,1)S(1)} %constant_dynamic-update-slice_fusion.half), channel_id=1, source_target_pairs={{0,16},{16,0},{1,17},{17,1},{2,18},{18,2},{3,19},{19,3},{4,20},{20... | collective-permute-start | bytes 3145736 | tf_op jit(solution)/shard_map/ppermute | solution.py:55
  77.9 1.7 copy-start.2
  81.3 1.2 copy-start.4
  82.5 0.9 copy-start.5
  88.8 6.8 %collective-permute-start.7 = (bf16[4,288,512]{2,1,0:T(8,128)(2,1)S(1)}, bf16[4,288,512]{2,1,0:T(8,128)(2,1)}, u32[]{:S(2)}, u32[]{:S(2)}) collective-permute-start(bf16[4,288,512]{2,1,0:T(8,128)(2,1)S(1)} %get-tuple-element.21), channel_id=1, source_target_pairs={{0,16},{16,0},{1,17},{17,1},{2,18},{18,2},{3,19},{19,3},{4,20},{20... | collective-permute-start | bytes 3538952 | tf_op jit(solution)/shard_map/ppermute | solution.py:55
  94.3 1.3 copy-start.1
  95.6 55.9 %all-to-all-start = ((bf16[16,128,512]{2,1,0:T(8,128)(2,1)}), bf16[16,128,512]{2,1,0:T(8,128)(2,1)}, u32[]{:S(2)}, u32[]{:S(2)}) async-start(bf16[16,128,512]{2,1,0:T(8,128)(2,1)} %copy-done.1), calls=%async_computation | async-start | bytes 4194304 | tf_op jit(solution)/shard_map/all_to_all | solution.py:30
  101.8 13.0 %collective-permute-start.8 = (bf16[288,512]{1,0:T(8,128)(2,1)S(1)}, bf16[288,512]{1,0:T(8,128)(2,1)S(1)}, u32[]{:S(2)}, u32[]{:S(2)}) collective-permute-start(bf16[288,512]{1,0:T(8,128)(2,1)S(1)} %get-tuple-element.32), channel_id=1, source_target_pairs={{0,32},{16,48},{32,64},{48,80},{64,96},{80,112},{96,128},{112,144}... | collective-permute-start | bytes 884744 | tf_op jit(solution)/shard_map/ppermute | solution.py:47
  105.0 10.9 %collective-permute-start.10 = (bf16[288,512]{1,0:T(8,128)(2,1)S(1)}, bf16[288,512]{1,0:T(8,128)(2,1)S(1)}, u32[]{:S(2)}, u32[]{:S(2)}) collective-permute-start(bf16[288,512]{1,0:T(8,128)(2,1)S(1)} %get-tuple-element.33), channel_id=1, source_target_pairs={{0,480},{16,496},{32,0},{48,16},{64,32},{80,48},{96,64},{112,80},{... | collective-permute-start | bytes 884744 | tf_op jit(solution)/shard_map/ppermute | solution.py:47
  109.5 13.9 %collective-permute-start.9 = (bf16[288,512]{1,0:T(8,128)(2,1)S(1)}, bf16[288,512]{1,0:T(8,128)(2,1)S(1)}, u32[]{:S(2)}, u32[]{:S(2)}) collective-permute-start(bf16[288,512]{1,0:T(8,128)(2,1)S(1)} %get-tuple-element.34), channel_id=1, source_target_pairs={{0,64},{16,464},{32,96},{48,496},{64,128},{80,16},{96,160},{112,48... | collective-permute-start | bytes 884744 | tf_op jit(solution)/shard_map/ppermute | solution.py:47
  123.6 20.0 %collective-permute-start.11 = (bf16[72,512]{1,0:T(8,128)(2,1)S(1)}, bf16[72,512]{1,0:T(8,128)(2,1)S(1)}, u32[]{:S(2)}, u32[]{:S(2)}) collective-permute-start(bf16[72,512]{1,0:T(8,128)(2,1)S(1)} %pad_maximum_fusion.4), channel_id=1, source_target_pairs={{0,128},{32,160},{64,192},{96,224},{128,256},{160,288},{192,320},{... | collective-permute-start | bytes 221192 | tf_op jit(solution)/shard_map/ppermute | solution.py:51
  131.0 14.8 %collective-permute-start.12 = (bf16[72,512]{1,0:T(8,128)(2,1)S(1)}, bf16[72,512]{1,0:T(8,128)(2,1)S(1)}, u32[]{:S(2)}, u32[]{:S(2)}) collective-permute-start(bf16[72,512]{1,0:T(8,128)(2,1)S(1)} %pad_maximum_fusion.5), channel_id=1, source_target_pairs={{0,256},{32,288},{64,320},{96,352},{128,384},{160,416},{192,448},{... | collective-permute-start | bytes 221192 | tf_op jit(solution)/shard_map/ppermute | solution.py:51
  137.0 14.5 %collective-permute-start.13 = (bf16[72,512]{1,0:T(8,128)(2,1)S(1)}, bf16[72,512]{1,0:T(8,128)(2,1)S(1)}, u32[]{:S(2)}, u32[]{:S(2)}) collective-permute-start(bf16[72,512]{1,0:T(8,128)(2,1)S(1)} %pad_maximum_fusion.6), channel_id=1, source_target_pairs={{0,384},{32,416},{64,448},{96,480},{128,0},{160,32},{192,64},{224,... | collective-permute-start | bytes 221192 | tf_op jit(solution)/shard_map/ppermute | solution.py:51
  176.8 26.0 %all-to-all-start.2 = ((bf16[16,24,512]{2,1,0:T(8,128)(2,1)}), bf16[16,24,512]{2,1,0:T(8,128)(2,1)}, u32[]{:S(2)}, u32[]{:S(2)}) async-start(bf16[16,24,512]{2,1,0:T(8,128)(2,1)} %broadcast_in_dim.68), calls=%async_computation.2 | async-start | bytes 786432 | tf_op jit(solution)/shard_map/all_to_all | solution.py:30
  204.7 12.3 %collective-permute-start.14 = (bf16[144,512]{1,0:T(8,128)(2,1)S(1)}, bf16[144,512]{1,0:T(8,128)(2,1)S(1)}, u32[]{:S(2)}, u32[]{:S(2)}) collective-permute-start(bf16[144,512]{1,0:T(8,128)(2,1)S(1)} %pad_maximum_fusion.3), channel_id=1, source_target_pairs={{0,16},{16,0},{1,17},{17,1},{2,18},{18,2},{3,19},{19,3},{4,20},{20... | collective-permute-start | bytes 442376 | tf_op jit(solution)/shard_map/ppermute | solution.py:55
Sparse Core Ops, SparseCore 0:
  12.4 65.3 all-gather.2

commit v5 on v4

--- a/solution.py
+++ b/solution.py
@@ -18,14 +18,6 @@
 BF16 = jnp.bfloat16
 
 
-def order_tables(owner_of, per_owner):
-    count = owner_of.shape[0]
-    index = jnp.arange(count, dtype=jnp.int32)
-    same = owner_of[:, None] == owner_of[None, :]
-    rank = jnp.sum((same & (index[None, :] < index[:, None])).astype(jnp.int32), axis=1)
-    return (rank, owner_of * per_owner + rank)
-
-
 def exchange(blocks, axis):
     return lax.all_to_all(blocks, axis, split_axis=0, concat_axis=0, tiled=True)
 
@@ -62,32 +54,82 @@
 NN, NT, TN = ((1,), (0,)), ((1,), (1,)), ((0,), (0,))
 
 
+def order_kernel(per_owner, mine, where, owners, rel_emb, core, part, ordered, order_sel, slot_of, wide):
+    owner = owners[...].astype(F32)
+    rels = owner.shape[1]
+    rows_dev = core.shape[0]
+    count = rels // per_owner
+    has = jnp.where(lax.broadcasted_iota(jnp.int32, (count, rels), 0).astype(F32) == owner, 1.0, 0.0).astype(BF16)
+    same = dot(has, has, TN)
+    index = lax.broadcasted_iota(jnp.int32, (rels, rels), 0)
+    before = index < lax.broadcasted_iota(jnp.int32, (rels, rels), 1)
+    rank = jnp.sum(jnp.where(before, same, 0.0), axis=0, keepdims=True)
+    slot = owner * per_owner + rank
+    slot_of[...] = slot
+    chosen = jnp.where(index.astype(F32) == slot, 1.0, 0.0).astype(BF16)
+    order_sel[...] = chosen
+    ordered[...] = dot(chosen, rel_emb[...], NN).astype(BF16)
+    first = (where[0] * mine + lax.broadcasted_iota(jnp.int32, (8, rels), 0)).astype(F32)
+    own = dot(jnp.where(first == slot, 1.0, 0.0).astype(BF16), rel_emb[...], NN).astype(BF16)
+    for a in range(rows_dev):
+        rows = dot(own, core[a], NN)
+        for w in range(mine):
+            wide[w * rows_dev + a : w * rows_dev + a + 1, :] = rows[w : w + 1]
+    part[...] = wide[...].astype(BF16)
+
+
+def send_kernel(cap, fill, head_ids, tail_ids, rel_ids, ents, out):
+    ent_rows = ents.shape[0]
+    lane = lax.broadcasted_iota(jnp.int32, (1, 128), 1)
+    limits = []
+    for row in range(8):
+        limit = jnp.full((1, 128), fill[0, row * 128 // cap], jnp.int32)
+        for at in range(cap, 128, cap):
+            limit = jnp.where(lane >= at, fill[0, (row * 128 + at) // cap], limit)
+        limits.append(limit)
+    numbers = [head_ids[...], tail_ids[...], rel_ids[...], jnp.concatenate(limits, axis=0)]
+    numbers = jnp.concatenate([a.astype(F32) for a in numbers], axis=1)
+    numbers = jnp.concatenate([numbers, jnp.zeros_like(numbers)], axis=0).astype(BF16)
+    for s in range(out.shape[0]):
+        out[s, :ent_rows, :] = ents[...]
+        out[s, ent_rows:, :] = numbers
+
+
 def hot_of(ids, ent_rows):
     entity = lax.broadcasted_iota(jnp.int32, (ent_rows, ids.shape[1]), 0).astype(F32)
     return jnp.where(entity == ids, 1.0, 0.0).astype(BF16)
 
 
-def gather_kernel(cap, names, table, ids, heads, tails):
+def gather_kernel(cap, where, slot_of, table, ids, heads, tails):
     ent_rows = table.shape[1] - EXTRA
     own = tails.shape[0]
     kinds = heads.shape[0] // own
     seats = own * cap
     columns = (kinds + 1) * seats
-    row = lax.broadcasted_iota(jnp.int32, (EXTRA, 4 * seats), 0)
+    g = where[0]
+    row = lax.broadcasted_iota(jnp.int32, (EXTRA, 512), 0)
     lines = []
     for s in range(table.shape[0]):
-        line = table[s, ent_rows:, :].astype(F32)[:, : 4 * seats]
-        lines.append(jnp.sum(jnp.where(row == names[own * kinds], line, 0.0), axis=0, keepdims=True))
+        line = table[s, ent_rows:, :].astype(F32)
+        lines.append(jnp.sum(jnp.where(row == g * seats // 128, line, 0.0), axis=0, keepdims=True))
     lines = jnp.concatenate(lines, axis=0)
-    head, tail, relation, limit = [lines[:, i * seats : (i + 1) * seats] for i in range(4)]
+    lines = [lines[:, i * 128 : (i + 1) * 128] for i in range(4)]
+    head, tail, relation, limit = [
+        jnp.where(g * seats % 128 == 0, line[:, :seats], line[:, 128 - seats :]) for line in lines
+    ]
     seat = lax.broadcasted_iota(jnp.int32, head.shape, 1)
     live = (seat % cap).astype(F32) < limit
+    slot = slot_of[...]
+    relations = lax.broadcasted_iota(jnp.int32, slot.shape, 1).astype(F32)
     found = []
     for w in range(kinds):
-        name = jnp.full(head.shape, names[w], jnp.int32)
-        for o in range(1, own):
-            name = jnp.where(seat >= o * cap, names[o * kinds + w], name)
-        found.append(jnp.where(live & (relation == name.astype(F32)), head, -1.0))
+        name = None
+        for o in range(own):
+            mine = (g * own * kinds + o * kinds + w).astype(F32)
+            this = jnp.sum(jnp.where(slot == mine, relations, 0.0), axis=1, keepdims=True)
+            this = jnp.broadcast_to(this, head.shape)
+            name = this if name is None else jnp.where(seat >= o * cap, this, name)
+        found.append(jnp.where(live & (relation == name), head, -1.0))
     found.append(jnp.where(live, tail, -1.0))
     ids[...] = jnp.concatenate(found + [jnp.full(head.shape, -1.0, F32)], axis=1)
     for s in range(table.shape[0]):
@@ -207,39 +249,39 @@
     z = lax.axis_index(LINE)
     c = lax.axis_index("core")
 
-    rank, slot_of = order_tables(owner_of, per_owner)
-    qindex = jnp.arange(rels, dtype=jnp.int32)
-    order_sel = (slot_of[None, :] == qindex[:, None]).astype(BF16)
-    ordered = jnp.dot(order_sel, rel_emb, preferred_element_type=F32).astype(BF16)
-
-    limits = jnp.broadcast_to(fill[0][:, None], (owners, cap))
-    numbers = [a.reshape(REPS, seats) for a in (head_ids, tail_ids, rel_ids, limits)]
-    numbers = jnp.concatenate(numbers, axis=1).astype(BF16)
-    numbers = jnp.pad(numbers, ((0, EXTRA - REPS), (0, feats - numbers.shape[1])))
-    table = lax.all_gather(jnp.concatenate([ents, numbers]), REP, axis=0, tiled=False)
-
     vmem = pl.BlockSpec(memory_space=pltpu.VMEM)
     smem = pl.BlockSpec(memory_space=pltpu.SMEM)
     slots = REPS * cap
     block = slots * feats * feats * 2
-
-    own_rows = lax.dynamic_slice_in_dim(ordered, g * mine, mine, 0)
-    part = jnp.einsum("wk,akb->wab", own_rows, core, preferred_element_type=F32).astype(BF16)
-    part = part.reshape(mine * rows_dev, feats)
+    where = g[None].astype(jnp.int32)
+    part, ordered, order_sel, slot_of = call(
+        functools.partial(order_kernel, per_owner, mine),
+        ((mine * rows_dev, feats), (rels, feats_rel), (rels, rels), (1, rels)),
+        2 * 8 * core.size,
+        [smem] + [vmem] * 3,
+        (pltpu.VMEM((mine * rows_dev, feats), F32),),
+        dtypes=(BF16, BF16, BF16, F32),
+    )(where, owner_of.reshape(1, rels), rel_emb, core)
+
+    (sent,) = call(
+        functools.partial(send_kernel, cap),
+        ((REPS, ent_rows + EXTRA, feats),),
+        1 << 20,
+        [smem] + [vmem] * 4,
+    )(fill, *(a.reshape(-1, 128) for a in (head_ids, tail_ids, rel_ids)), ents)
+    table = exchange(sent, REP)
+
     far = jnp.stack([part] + [far_move(part, p) for p in STEPS[1:]])
     half = jnp.concatenate([far] + [near_move(far, s) for s in STEPS[1:]])
     other = swap_core(half)
 
-    named = slot_of[None, :] == g * mine + jnp.arange(mine, dtype=jnp.int32)[:, None]
-    names = jnp.sum(jnp.where(named, qindex[None, :], 0), axis=1)
-    names = jnp.concatenate([names, g[None]]).astype(jnp.int32)
     ids, heads, tails = call(
         functools.partial(gather_kernel, cap),
         ((REPS, 4 * seats), (mine, slots, feats), (own, slots, feats)),
         REPS * 3 * seats * ent_rows * feats * 2,
-        [smem, vmem],
+        [smem, vmem, vmem],
         dtypes=(F32, BF16, BF16),
-    )(names, table)
+    )(where, slot_of, table)
 
     entry = jnp.arange(Z, dtype=jnp.int32)
     starts = []

time: 227 us -> 202 us (0.89)
  between operations: 14.5 us -> 1.2 us
  other arithmetic: 12 us -> 5.56 us
  starting transfers between devices: 100 us -> 93.7 us
  blocking collectives: 22.7 us -> 25.3 us
    ppermute x6, starting transfers between devices: 45.4 us -> 38.9 us  [far_move(): lax.ppermute(block, LINE, [(z, (z + 4 * step) % Z) for z in range(Z)])]
    ppermute x6, starting transfers between devices: 24.3 us -> 18.3 us  [near_move(): return lax.ppermute(block, REL, pairs)]
    all_to_all x2 -> x3, waiting for transfers between devices: 13.8 us -> 19.5 us  [exchange(): return lax.all_to_all(blocks, axis, split_axis=0, concat_axis=0, tiled=True)]
    all_gather x1 -> x0, waiting for transfers between devices: 4.47 us -> none  [body(): lax.all_gather(jnp.concatenate([ents, numbers]), REP, axis=0, tiled=False)]
    ppermute x6, waiting for transfers between devices: 14.2 us -> 10.3 us  [far_move(): lax.ppermute(block, LINE, [(z, (z + 4 * step) % Z) for z in range(Z)])]
    all_to_all x2 -> x3, starting transfers between devices: 14 us -> 17.8 us  [exchange(): return lax.all_to_all(blocks, axis, split_axis=0, concat_axis=0, tiled=True)]
    another operation x4 -> x0, other arithmetic: 2.88 us -> none
    all_to_all x1, blocking collectives: 22.7 us -> 25.3 us  [exchange(): return lax.all_to_all(blocks, axis, split_axis=0, concat_axis=0, tiled=True)]
  transfers between devices with their start and end apart: 18 -> 18, of which waited for: 10 -> 8; matrix products, arithmetic and copies ran while one was open for 3% -> 4% of each run, Pallas kernels for 3% -> 4%
where the time goes in v5:
time: 202 us; the launch traced here: 201 us
  starting transfers between devices  93.7 us (46%)
  waiting for transfers between devices  50.5 us (25%)
  blocking collectives  25.3 us (13%)
  Pallas kernels  13.9 us (7%)
  local copies, waits for them, and re-layouts  8.83 us (4%)
  other arithmetic  5.56 us (3%)
  matrix products  2.28 us (1%)
    ppermute x6, starting transfers between devices, far_move(): lax.ppermute(block, LINE, [(z, (z + 4 * step) % Z) for z in range(Z)])  38.9 us
    all_to_all x1, blocking collectives, exchange(): return lax.all_to_all(blocks, axis, split_axis=0, concat_axis=0, tiled=True)  25.3 us
    ppermute x6, waiting for transfers between devices, near_move(): return lax.ppermute(block, REL, pairs)  20.7 us
    all_to_all x3, waiting for transfers between devices, exchange(): return lax.all_to_all(blocks, axis, split_axis=0, concat_axis=0, tiled=True)  19.5 us
    ppermute x3, starting transfers between devices, swap_core(): return lax.ppermute(block, 'core', [(0, 1), (1, 0)])  18.6 us
    ppermute x6, starting transfers between devices, near_move(): return lax.ppermute(block, REL, pairs)  18.3 us
    all_to_all x3, starting transfers between devices, exchange(): return lax.all_to_all(blocks, axis, split_axis=0, concat_axis=0, tiled=True)  17.8 us
    ppermute x6, waiting for transfers between devices, far_move(): lax.ppermute(block, LINE, [(z, (z + 4 * step) % Z) for z in range(Z)])  10.3 us
  transfers between devices with their start and end apart: 18, of which 8 were waited for; matrix products, arithmetic and copies ran while one was open for 4% of the time, Pallas kernels for 4%

profile of v5, /device:TPU:1, one launch (start us, length us, event | category | flops | bytes accessed | tf_op | source)
XLA Modules:
  0.0 201.2 jit_solution(10239186307303794670)
XLA Ops:
  0.7 0.0 copy-start.1
  0.7 1.6 copy-done.1
  2.3 0.7 copy-done.4
  3.0 0.7 copy-done.8
  3.7 0.7 shard_map.120
  4.4 13.3 %collective-permute-start.2 = (bf16[64,512]{1,0:T(8,128)(2,1)S(1)}, bf16[64,512]{1,0:T(8,128)(2,1)}, u32[]{:S(2)}, u32[]{:S(2)}) collective-permute-start(bf16[64,512]{1,0:T(8,128)(2,1)S(1)} %get-tuple-element.25), channel_id=1, source_target_pairs={{0,384},{32,416},{64,448},{96,480},{128,0},{160,32},{192,64},{224,... | collective-permute-start | bytes 196616 | tf_op jit(solution)/shard_map/ppermute | solution.py:43
  17.6 4.9 %collective-permute-start.1 = (bf16[64,512]{1,0:T(8,128)(2,1)S(1)}, bf16[64,512]{1,0:T(8,128)(2,1)}, u32[]{:S(2)}, u32[]{:S(2)}) collective-permute-start(bf16[64,512]{1,0:T(8,128)(2,1)S(1)} %get-tuple-element.25), channel_id=1, source_target_pairs={{0,256},{32,288},{64,320},{96,352},{128,384},{160,416},{192,448},{... | collective-permute-start | bytes 196616 | tf_op jit(solution)/shard_map/ppermute | solution.py:43
  22.6 7.3 %collective-permute-start = (bf16[64,512]{1,0:T(8,128)(2,1)S(1)}, bf16[64,512]{1,0:T(8,128)(2,1)}, u32[]{:S(2)}, u32[]{:S(2)}) collective-permute-start(bf16[64,512]{1,0:T(8,128)(2,1)S(1)} %get-tuple-element.25), channel_id=1, source_target_pairs={{0,128},{32,160},{64,192},{96,224},{128,256},{160,288},{192,320},{... | collective-permute-start | bytes 196616 | tf_op jit(solution)/shard_map/ppermute | solution.py:43
  29.9 0.7 shard_map.121
  30.6 1.4 copy-done
  32.0 6.8 %all-to-all-start = ((bf16[16,144,512]{2,1,0:T(8,128)(2,1)}), bf16[16,144,512]{2,1,0:T(8,128)(2,1)S(1)}, u32[]{:S(2)}, u32[]{:S(2)}) async-start(bf16[16,144,512]{2,1,0:T(8,128)(2,1)} %copy-done), calls=%async_computation | async-start | bytes 4718592 | tf_op jit(solution)/shard_map/all_to_all | solution.py:22
  38.8 0.0 collective-permute-done.2
  38.8 0.0 collective-permute-done.1
  38.8 0.0 collective-permute-done
  38.8 0.9 pad_maximum_fusion
  39.8 4.9 %collective-permute-start.5 = (bf16[4,64,512]{2,1,0:T(8,128)(2,1)S(1)}, bf16[4,64,512]{2,1,0:T(8,128)(2,1)S(1)}, u32[]{:S(2)}, u32[]{:S(2)}) collective-permute-start(bf16[4,64,512]{2,1,0:T(8,128)(2,1)S(1)} %pad_maximum_fusion), channel_id=1, source_target_pairs={{0,480},{16,496},{32,0},{48,16},{64,32},{80,48},{96,64},{112,80},{... | collective-permute-start | bytes 786440 | tf_op jit(solution)/shard_map/ppermute | solution.py:39
  44.6 1.9 collective-permute-start.4
  46.6 3.1 %collective-permute-start.3 = (bf16[4,64,512]{2,1,0:T(8,128)(2,1)S(1)}, bf16[4,64,512]{2,1,0:T(8,128)(2,1)S(1)}, u32[]{:S(2)}, u32[]{:S(2)}) collective-permute-start(bf16[4,64,512]{2,1,0:T(8,128)(2,1)S(1)} %pad_maximum_fusion), channel_id=1, source_target_pairs={{0,32},{16,48},{32,64},{48,80},{64,96},{80,112},{96,128},{112,144}... | collective-permute-start | bytes 786440 | tf_op jit(solution)/shard_map/ppermute | solution.py:39
  49.7 0.8 constant_dynamic-update-slice_fusion.5
  50.5 0.8 constant_dynamic-update-slice_fusion.4
  51.4 0.8 constant_dynamic-update-slice_fusion.3
  52.2 8.6 %collective-permute-done.3 = bf16[4,64,512]{2,1,0:T(8,128)(2,1)S(1)} collective-permute-done((bf16[4,64,512]{2,1,0:T(8,128)(2,1)S(1)}, bf16[4,64,512]{2,1,0:T(8,128)(2,1)S(1)}, u32[]{:S(2)}, u32[]{:S(2)}) %collective-permute-start.3) | collective-permute-done | bytes 262176 | tf_op jit(solution)/shard_map/ppermute | solution.py:39
  60.9 0.0 collective-permute-done.4
  60.9 0.0 collective-permute-done.5
  60.9 3.9 %collective-permute-start.6 = (bf16[16,64,512]{2,1,0:T(8,128)(2,1)S(1)}, bf16[16,64,512]{2,1,0:T(8,128)(2,1)}, u32[]{:S(2)}, u32[]{:S(2)}) collective-permute-start(bf16[16,64,512]{2,1,0:T(8,128)(2,1)S(1)} %constant_dynamic-update-slice_fusion.half), channel_id=1, source_target_pairs={{0,16},{16,0},{1,17},{17,1},{2,18},{18,2},{3,19},{19,3},{4,20},{20... | collective-permute-start | bytes 3145736 | tf_op jit(solution)/shard_map/ppermute | solution.py:47
  64.9 5.7 %all-to-all-done.table = bf16[16,144,512]{2,1,0:T(8,128)(2,1)S(1)} async-done(((bf16[16,144,512]{2,1,0:T(8,128)(2,1)}), bf16[16,144,512]{2,1,0:T(8,128)(2,1)S(1)}, u32[]{:S(2)}, u32[]{:S(2)}) %all-to-all-start) | async-done | bytes 2359328 | tf_op jit(solution)/shard_map/all_to_all | solution.py:22
  70.7 1.2 shard_map.122
  71.9 0.0 collective-permute-done.6.other
  71.9 5.4 %shard_map.123 = (bf16[4,512,512]{2,1,0:T(8,128)(2,1)S(1)}, bf16[2,512,512]{2,1,0:T(8,128)(2,1)S(1)}, bf16[2,512,512]{2,1,0:T(8,128)(2,1)S(1)}, bf16[4,288,512]{2,1,0:T(8,128)(2,1)S(1)}, bf16[4,288,512]{2,1,0:T(8,128)(2,1)S(1)}) custom-call(s32[4,16]{1,0:T(4,128)S(1)} %pad_add_fusion.starts, bf16[4,512,512]{2,1,0:T(8,128)(2,1)S(1)} %get-tuple-element.23.heads, ...), custom_call_target="tpu_custom_call" | custom-call | flops 2952790016 | bytes 8388608 | tf_op jit(solution)/shard_map/pallas_call | solution.py:296
  77.3 5.0 %collective-permute-start.7 = (bf16[4,288,512]{2,1,0:T(8,128)(2,1)S(1)}, bf16[4,288,512]{2,1,0:T(8,128)(2,1)}, u32[]{:S(2)}, u32[]{:S(2)}) collective-permute-start(bf16[4,288,512]{2,1,0:T(8,128)(2,1)S(1)} %get-tuple-element.27), channel_id=1, source_target_pairs={{0,16},{16,0},{1,17},{17,1},{2,18},{18,2},{3,19},{19,3},{4,20},{20... | collective-permute-start | bytes 3538952 | tf_op jit(solution)/shard_map/ppermute | solution.py:47
  82.3 3.2 %shard_map.124 = bf16[16,128,512]{2,1,0:T(8,128)(2,1)} custom-call(f32[16,256]{1,0:T(8,128)S(1)} %get-tuple-element.28.ids, bf16[2,512,512]{2,1,0:T(8,128)(2,1)S(1)} %get-tuple-element.29.dquery, bf16[2,512,512]{2,1,0:T(8,128)(2,1)S(1)} %get-tuple-element.30.dtail, bf16[4,512,512]{2,1,0:T(8,128)(2,1)S(1)} %get-tuple-element.31.mats), custom_call_target="tpu_custom_call" | custom-call | flops 1476395008 | bytes 8388608 | tf_op jit(solution)/shard_map/pallas_call | solution.py:310
  85.5 0.0 collective-permute-done.7
  85.5 4.4 %all-to-all-start.1 = ((bf16[16,128,512]{2,1,0:T(8,128)(2,1)}), bf16[16,128,512]{2,1,0:T(8,128)(2,1)}, u32[]{:S(2)}, u32[]{:S(2)}) async-start(bf16[16,128,512]{2,1,0:T(8,128)(2,1)} %shard_map.124), calls=%async_computation.1 | async-start | bytes 4194304 | tf_op jit(solution)/shard_map/all_to_all | solution.py:22
  89.9 1.6 add_convert_fusion
  91.5 0.1 slice_bitcast_fusion.2
  91.6 2.6 %collective-permute-start.8 = (bf16[288,512]{1,0:T(8,128)(2,1)S(1)}, bf16[288,512]{1,0:T(8,128)(2,1)S(1)}, u32[]{:S(2)}, u32[]{:S(2)}) collective-permute-start(bf16[288,512]{1,0:T(8,128)(2,1)S(1)} %get-tuple-element.40), channel_id=1, source_target_pairs={{0,32},{16,48},{32,64},{48,80},{64,96},{80,112},{96,128},{112,144}... | collective-permute-start | bytes 884744 | tf_op jit(solution)/shard_map/ppermute | solution.py:39
  94.2 3.8 %collective-permute-start.10 = (bf16[288,512]{1,0:T(8,128)(2,1)S(1)}, bf16[288,512]{1,0:T(8,128)(2,1)S(1)}, u32[]{:S(2)}, u32[]{:S(2)}) collective-permute-start(bf16[288,512]{1,0:T(8,128)(2,1)S(1)} %get-tuple-element.41), channel_id=1, source_target_pairs={{0,480},{16,496},{32,0},{48,16},{64,32},{80,48},{96,64},{112,80},{... | collective-permute-start | bytes 884744 | tf_op jit(solution)/shard_map/ppermute | solution.py:39
  98.1 1.9 collective-permute-start.9
  100.0 3.3 %collective-permute-done.8 = bf16[288,512]{1,0:T(8,128)(2,1)S(1)} collective-permute-done((bf16[288,512]{1,0:T(8,128)(2,1)S(1)}, bf16[288,512]{1,0:T(8,128)(2,1)S(1)}, u32[]{:S(2)}, u32[]{:S(2)}) %collective-permute-start.8) | collective-permute-done | bytes 294944 | tf_op jit(solution)/shard_map/ppermute | solution.py:39
  103.3 1.2 collective-permute-done.10
  104.6 7.5 %collective-permute-done.9 = bf16[288,512]{1,0:T(8,128)(2,1)S(1)} collective-permute-done((bf16[288,512]{1,0:T(8,128)(2,1)S(1)}, bf16[288,512]{1,0:T(8,128)(2,1)S(1)}, u32[]{:S(2)}, u32[]{:S(2)}) %collective-permute-start.9) | collective-permute-done | bytes 294944 | tf_op jit(solution)/shard_map/ppermute | solution.py:39
  112.0 0.2 fusion.14
  112.3 4.0 %collective-permute-start.11 = (bf16[72,512]{1,0:T(8,128)(2,1)S(1)}, bf16[72,512]{1,0:T(8,128)(2,1)S(1)}, u32[]{:S(2)}, u32[]{:S(2)}) collective-permute-start(bf16[72,512]{1,0:T(8,128)(2,1)S(1)} %pad_maximum_fusion.3), channel_id=1, source_target_pairs={{0,128},{32,160},{64,192},{96,224},{128,256},{160,288},{192,320},{... | collective-permute-start | bytes 221192 | tf_op jit(solution)/shard_map/ppermute | solution.py:43
  116.3 5.4 %collective-permute-start.12 = (bf16[72,512]{1,0:T(8,128)(2,1)S(1)}, bf16[72,512]{1,0:T(8,128)(2,1)S(1)}, u32[]{:S(2)}, u32[]{:S(2)}) collective-permute-start(bf16[72,512]{1,0:T(8,128)(2,1)S(1)} %pad_maximum_fusion.4), channel_id=1, source_target_pairs={{0,256},{32,288},{64,320},{96,352},{128,384},{160,416},{192,448},{... | collective-permute-start | bytes 221192 | tf_op jit(solution)/shard_map/ppermute | solution.py:43
  121.7 4.1 %collective-permute-start.13 = (bf16[72,512]{1,0:T(8,128)(2,1)S(1)}, bf16[72,512]{1,0:T(8,128)(2,1)S(1)}, u32[]{:S(2)}, u32[]{:S(2)}) collective-permute-start(bf16[72,512]{1,0:T(8,128)(2,1)S(1)} %pad_maximum_fusion.5), channel_id=1, source_target_pairs={{0,384},{32,416},{64,448},{96,480},{128,0},{160,32},{192,64},{224,... | collective-permute-start | bytes 221192 | tf_op jit(solution)/shard_map/ppermute | solution.py:43
  125.8 0.0 collective-permute-done.11
  125.8 4.7 %collective-permute-done.12 = bf16[72,512]{1,0:T(8,128)(2,1)S(1)} collective-permute-done((bf16[72,512]{1,0:T(8,128)(2,1)S(1)}, bf16[72,512]{1,0:T(8,128)(2,1)S(1)}, u32[]{:S(2)}, u32[]{:S(2)}) %collective-permute-start.12) | collective-permute-done | bytes 73760 | tf_op jit(solution)/shard_map/ppermute | solution.py:43
  130.5 5.6 %collective-permute-done.13 = bf16[72,512]{1,0:T(8,128)(2,1)S(1)} collective-permute-done((bf16[72,512]{1,0:T(8,128)(2,1)S(1)}, bf16[72,512]{1,0:T(8,128)(2,1)S(1)}, u32[]{:S(2)}, u32[]{:S(2)}) %collective-permute-start.13) | collective-permute-done | bytes 73760 | tf_op jit(solution)/shard_map/ppermute | solution.py:43
  136.1 0.1 add_convert_fusion.1
  136.2 0.0 all-to-all-done.1
  136.2 0.1 broadcast_in_dim.32
  136.3 0.0 copy-start.2
  136.3 25.3 %all_to_all.20.sums = bf16[16,72,512]{2,1,0:T(8,128)(2,1)S(1)} all-to-all(bf16[16,72,512]{2,1,0:T(8,128)(2,1)S(1)} %broadcast_in_dim.32), channel_id=1, replica_groups=mesh['zh'=4,'zl'=4,'core'=2,'y'=4,'x'=4] {'y','x'}, dimensions={0} | all-to-all | bytes 2359296 | tf_op jit(solution)/shard_map/all_to_all | solution.py:22
  161.6 0.1 slice.84
  161.7 1.5 fusion.8
  163.3 0.8 broadcast_in_dim.33
  164.0 6.6 %all-to-all-start.3 = ((bf16[16,24,512]{2,1,0:T(8,128)(2,1)}), bf16[16,24,512]{2,1,0:T(8,128)(2,1)S(1)}, u32[]{:S(2)}, u32[]{:S(2)}) async-start(bf16[16,24,512]{2,1,0:T(8,128)(2,1)} %broadcast_in_dim.33), calls=%async_computation.3 | async-start | bytes 786432 | tf_op jit(solution)/shard_map/all_to_all | solution.py:22
  170.7 2.8 %shard_map.125 = bf16[16,128,512]{2,1,0:T(8,128)(2,1)} custom-call(bf16[64,128]{1,0:T(8,128)(2,1)S(1)} %get-tuple-element.35.ordered, bf16[16,72,512]{2,1,0:T(8,128)(2,1)S(1)} %all_to_all.20.sums), custom_call_target="tpu_custom_call" | custom-call | flops 134217728 | bytes 8388608 | tf_op jit(solution)/shard_map/pallas_call | solution.py:352
  173.5 13.8 %all-to-all-done.3 = bf16[16,24,512]{2,1,0:T(8,128)(2,1)S(1)} async-done(((bf16[16,24,512]{2,1,0:T(8,128)(2,1)}), bf16[16,24,512]{2,1,0:T(8,128)(2,1)S(1)}, u32[]{:S(2)}, u32[]{:S(2)}) %all-to-all-start.3) | async-done | bytes 393248 | tf_op jit(solution)/shard_map/all_to_all | solution.py:22
  187.3 9.7 %collective-permute-start.14 = (bf16[144,512]{1,0:T(8,128)(2,1)S(1)}, bf16[144,512]{1,0:T(8,128)(2,1)S(1)}, u32[]{:S(2)}, u32[]{:S(2)}) collective-permute-start(bf16[144,512]{1,0:T(8,128)(2,1)S(1)} %pad_maximum_fusion.2), channel_id=1, source_target_pairs={{0,16},{16,0},{1,17},{17,1},{2,18},{18,2},{3,19},{19,3},{4,20},{20... | collective-permute-start | bytes 442376 | tf_op jit(solution)/shard_map/ppermute | solution.py:47
  197.0 2.6 %reduce_sum.38 = bf16[128,512]{1,0:T(8,128)(2,1)} reduce(bf16[16,128,512]{2,1,0:T(8,128)(2,1)} %all-to-all-done.1, bf16[]{:T(256)} %constant.112.clone.1), dimensions={0}, to_apply=%region_2.3 | reduce | flops 983040 | bytes 2228226 | tf_op jit(solution)/shard_map/reduce_sum | solution.py:339
  199.6 0.0 collective-permute-done.14
  199.7 0.7 copy.18
  200.5 0.8 fusion.37
  (39 shorter events, 0.4 us)
Async XLA Ops:
  0.6 29.2 %copy-start.9 = (s32[1,32]{1,0:T(1,128)S(1)}, s32[1,32]{1,0:T(1,128)}, u32[]{:S(2)}) copy-start(s32[1,32]{1,0:T(1,128)} %fill.1) | copy-start | bytes 388
  0.6 29.2 %copy-start.6 = (s32[1024]{0:T(1024)S(1)}, s32[1024]{0:T(1024)}, u32[]{:S(2)}) copy-start(s32[1024]{0:T(1024)} %param.16) | copy-start | bytes 12292
  0.7 29.2 %copy-start.5 = (s32[1024]{0:T(1024)S(1)}, s32[1024]{0:T(1024)}, u32[]{:S(2)}) copy-start(s32[1024]{0:T(1024)} %param.15) | copy-start | bytes 12292
  0.7 29.2 %copy-start.7 = (s32[1024]{0:T(1024)S(1)}, s32[1024]{0:T(1024)}, u32[]{:S(2)}) copy-start(s32[1024]{0:T(1024)} %param.14) | copy-start | bytes 12292
  0.7 1.6 copy-start.1
  2.3 0.7 copy-start.4
  3.0 0.7 copy-start.8
  3.7 26.2 %copy-start.3 = (bf16[128,512]{1,0:T(8,128)(2,1)S(1)}, bf16[128,512]{1,0:T(8,128)(2,1)}, u32[]{:S(2)}) copy-start(bf16[128,512]{1,0:T(8,128)(2,1)} %ents.1) | copy-start | bytes 393220
  4.4 34.4 %collective-permute-start.2 = (bf16[64,512]{1,0:T(8,128)(2,1)S(1)}, bf16[64,512]{1,0:T(8,128)(2,1)}, u32[]{:S(2)}, u32[]{:S(2)}) collective-permute-start(bf16[64,512]{1,0:T(8,128)(2,1)S(1)} %get-tuple-element.25), channel_id=1, source_target_pairs={{0,384},{32,416},{64,448},{96,480},{128,0},{160,32},{192,64},{224,... | collective-permute-start | bytes 196616 | tf_op jit(solution)/shard_map/ppermute | solution.py:43
  17.6 21.2 %collective-permute-start.1 = (bf16[64,512]{1,0:T(8,128)(2,1)S(1)}, bf16[64,512]{1,0:T(8,128)(2,1)}, u32[]{:S(2)}, u32[]{:S(2)}) collective-permute-start(bf16[64,512]{1,0:T(8,128)(2,1)S(1)} %get-tuple-element.25), channel_id=1, source_target_pairs={{0,256},{32,288},{64,320},{96,352},{128,384},{160,416},{192,448},{... | collective-permute-start | bytes 196616 | tf_op jit(solution)/shard_map/ppermute | solution.py:43
  22.6 16.2 %collective-permute-start = (bf16[64,512]{1,0:T(8,128)(2,1)S(1)}, bf16[64,512]{1,0:T(8,128)(2,1)}, u32[]{:S(2)}, u32[]{:S(2)}) collective-permute-start(bf16[64,512]{1,0:T(8,128)(2,1)S(1)} %get-tuple-element.25), channel_id=1, source_target_pairs={{0,128},{32,160},{64,192},{96,224},{128,256},{160,288},{192,320},{... | collective-permute-start | bytes 196616 | tf_op jit(solution)/shard_map/ppermute | solution.py:43
  30.6 1.4 copy-start
  32.0 38.6 %all-to-all-start = ((bf16[16,144,512]{2,1,0:T(8,128)(2,1)}), bf16[16,144,512]{2,1,0:T(8,128)(2,1)S(1)}, u32[]{:S(2)}, u32[]{:S(2)}) async-start(bf16[16,144,512]{2,1,0:T(8,128)(2,1)} %copy-done), calls=%async_computation | async-start | bytes 4718592 | tf_op jit(solution)/shard_map/all_to_all | solution.py:22
  39.8 21.1 %collective-permute-start.5 = (bf16[4,64,512]{2,1,0:T(8,128)(2,1)S(1)}, bf16[4,64,512]{2,1,0:T(8,128)(2,1)S(1)}, u32[]{:S(2)}, u32[]{:S(2)}) collective-permute-start(bf16[4,64,512]{2,1,0:T(8,128)(2,1)S(1)} %pad_maximum_fusion), channel_id=1, source_target_pairs={{0,480},{16,496},{32,0},{48,16},{64,32},{80,48},{96,64},{112,80},{... | collective-permute-start | bytes 786440 | tf_op jit(solution)/shard_map/ppermute | solution.py:39
  44.6 16.2 %collective-permute-start.4 = (bf16[4,64,512]{2,1,0:T(8,128)(2,1)S(1)}, bf16[4,64,512]{2,1,0:T(8,128)(2,1)S(1)}, u32[]{:S(2)}, u32[]{:S(2)}) collective-permute-start(bf16[4,64,512]{2,1,0:T(8,128)(2,1)S(1)} %pad_maximum_fusion), channel_id=1, source_target_pairs={{0,64},{16,464},{32,96},{48,496},{64,128},{80,16},{96,160},{112,48... | collective-permute-start | bytes 786440 | tf_op jit(solution)/shard_map/ppermute | solution.py:39
  46.6 14.3 %collective-permute-start.3 = (bf16[4,64,512]{2,1,0:T(8,128)(2,1)S(1)}, bf16[4,64,512]{2,1,0:T(8,128)(2,1)S(1)}, u32[]{:S(2)}, u32[]{:S(2)}) collective-permute-start(bf16[4,64,512]{2,1,0:T(8,128)(2,1)S(1)} %pad_maximum_fusion), channel_id=1, source_target_pairs={{0,32},{16,48},{32,64},{48,80},{64,96},{80,112},{96,128},{112,144}... | collective-permute-start | bytes 786440 | tf_op jit(solution)/shard_map/ppermute | solution.py:39
  60.9 10.9 %collective-permute-start.6 = (bf16[16,64,512]{2,1,0:T(8,128)(2,1)S(1)}, bf16[16,64,512]{2,1,0:T(8,128)(2,1)}, u32[]{:S(2)}, u32[]{:S(2)}) collective-permute-start(bf16[16,64,512]{2,1,0:T(8,128)(2,1)S(1)} %constant_dynamic-update-slice_fusion.half), channel_id=1, source_target_pairs={{0,16},{16,0},{1,17},{17,1},{2,18},{18,2},{3,19},{19,3},{4,20},{20... | collective-permute-start | bytes 3145736 | tf_op jit(solution)/shard_map/ppermute | solution.py:47
  70.6 1.2 copy-start.10
  77.3 8.2 %collective-permute-start.7 = (bf16[4,288,512]{2,1,0:T(8,128)(2,1)S(1)}, bf16[4,288,512]{2,1,0:T(8,128)(2,1)}, u32[]{:S(2)}, u32[]{:S(2)}) collective-permute-start(bf16[4,288,512]{2,1,0:T(8,128)(2,1)S(1)} %get-tuple-element.27), channel_id=1, source_target_pairs={{0,16},{16,0},{1,17},{17,1},{2,18},{18,2},{3,19},{19,3},{4,20},{20... | collective-permute-start | bytes 3538952 | tf_op jit(solution)/shard_map/ppermute | solution.py:47
  85.5 50.7 %all-to-all-start.1 = ((bf16[16,128,512]{2,1,0:T(8,128)(2,1)}), bf16[16,128,512]{2,1,0:T(8,128)(2,1)}, u32[]{:S(2)}, u32[]{:S(2)}) async-start(bf16[16,128,512]{2,1,0:T(8,128)(2,1)} %shard_map.124), calls=%async_computation.1 | async-start | bytes 4194304 | tf_op jit(solution)/shard_map/all_to_all | solution.py:22
  91.6 11.7 %collective-permute-start.8 = (bf16[288,512]{1,0:T(8,128)(2,1)S(1)}, bf16[288,512]{1,0:T(8,128)(2,1)S(1)}, u32[]{:S(2)}, u32[]{:S(2)}) collective-permute-start(bf16[288,512]{1,0:T(8,128)(2,1)S(1)} %get-tuple-element.40), channel_id=1, source_target_pairs={{0,32},{16,48},{32,64},{48,80},{64,96},{80,112},{96,128},{112,144}... | collective-permute-start | bytes 884744 | tf_op jit(solution)/shard_map/ppermute | solution.py:39
  94.2 10.3 %collective-permute-start.10 = (bf16[288,512]{1,0:T(8,128)(2,1)S(1)}, bf16[288,512]{1,0:T(8,128)(2,1)S(1)}, u32[]{:S(2)}, u32[]{:S(2)}) collective-permute-start(bf16[288,512]{1,0:T(8,128)(2,1)S(1)} %get-tuple-element.41), channel_id=1, source_target_pairs={{0,480},{16,496},{32,0},{48,16},{64,32},{80,48},{96,64},{112,80},{... | collective-permute-start | bytes 884744 | tf_op jit(solution)/shard_map/ppermute | solution.py:39
  98.1 14.0 %collective-permute-start.9 = (bf16[288,512]{1,0:T(8,128)(2,1)S(1)}, bf16[288,512]{1,0:T(8,128)(2,1)S(1)}, u32[]{:S(2)}, u32[]{:S(2)}) collective-permute-start(bf16[288,512]{1,0:T(8,128)(2,1)S(1)} %get-tuple-element.42), channel_id=1, source_target_pairs={{0,64},{16,464},{32,96},{48,496},{64,128},{80,16},{96,160},{112,48... | collective-permute-start | bytes 884744 | tf_op jit(solution)/shard_map/ppermute | solution.py:39
  112.3 13.5 %collective-permute-start.11 = (bf16[72,512]{1,0:T(8,128)(2,1)S(1)}, bf16[72,512]{1,0:T(8,128)(2,1)S(1)}, u32[]{:S(2)}, u32[]{:S(2)}) collective-permute-start(bf16[72,512]{1,0:T(8,128)(2,1)S(1)} %pad_maximum_fusion.3), channel_id=1, source_target_pairs={{0,128},{32,160},{64,192},{96,224},{128,256},{160,288},{192,320},{... | collective-permute-start | bytes 221192 | tf_op jit(solution)/shard_map/ppermute | solution.py:43
  116.3 14.2 %collective-permute-start.12 = (bf16[72,512]{1,0:T(8,128)(2,1)S(1)}, bf16[72,512]{1,0:T(8,128)(2,1)S(1)}, u32[]{:S(2)}, u32[]{:S(2)}) collective-permute-start(bf16[72,512]{1,0:T(8,128)(2,1)S(1)} %pad_maximum_fusion.4), channel_id=1, source_target_pairs={{0,256},{32,288},{64,320},{96,352},{128,384},{160,416},{192,448},{... | collective-permute-start | bytes 221192 | tf_op jit(solution)/shard_map/ppermute | solution.py:43
  121.7 14.4 %collective-permute-start.13 = (bf16[72,512]{1,0:T(8,128)(2,1)S(1)}, bf16[72,512]{1,0:T(8,128)(2,1)S(1)}, u32[]{:S(2)}, u32[]{:S(2)}) collective-permute-start(bf16[72,512]{1,0:T(8,128)(2,1)S(1)} %pad_maximum_fusion.5), channel_id=1, source_target_pairs={{0,384},{32,416},{64,448},{96,480},{128,0},{160,32},{192,64},{224,... | collective-permute-start | bytes 221192 | tf_op jit(solution)/shard_map/ppermute | solution.py:43
  136.3 25.4 %copy-start.2 = (bf16[16,128,512]{2,1,0:T(8,128)(2,1)S(1)}, bf16[16,128,512]{2,1,0:T(8,128)(2,1)}, u32[]{:S(2)}) copy-start(bf16[16,128,512]{2,1,0:T(8,128)(2,1)} %core.1) | copy-start | bytes 6291460
  164.0 23.2 %all-to-all-start.3 = ((bf16[16,24,512]{2,1,0:T(8,128)(2,1)}), bf16[16,24,512]{2,1,0:T(8,128)(2,1)S(1)}, u32[]{:S(2)}, u32[]{:S(2)}) async-start(bf16[16,24,512]{2,1,0:T(8,128)(2,1)} %broadcast_in_dim.33), calls=%async_computation.3 | async-start | bytes 786432 | tf_op jit(solution)/shard_map/all_to_all | solution.py:22
  187.3 12.3 %collective-permute-start.14 = (bf16[144,512]{1,0:T(8,128)(2,1)S(1)}, bf16[144,512]{1,0:T(8,128)(2,1)S(1)}, u32[]{:S(2)}, u32[]{:S(2)}) collective-permute-start(bf16[144,512]{1,0:T(8,128)(2,1)S(1)} %pad_maximum_fusion.2), channel_id=1, source_target_pairs={{0,16},{16,0},{1,17},{17,1},{2,18},{18,2},{3,19},{19,3},{4,20},{20... | collective-permute-start | bytes 442376 | tf_op jit(solution)/shard_map/ppermute | solution.py:47

commit v6 on v5

--- a/solution.py
+++ b/solution.py
@@ -54,28 +54,40 @@
 NN, NT, TN = ((1,), (0,)), ((1,), (1,)), ((0,), (0,))
 
 
-def order_kernel(per_owner, mine, where, owners, rel_emb, core, part, ordered, order_sel, slot_of, wide):
-    owner = owners[...].astype(F32)
-    rels = owner.shape[1]
-    rows_dev = core.shape[0]
-    count = rels // per_owner
-    has = jnp.where(lax.broadcasted_iota(jnp.int32, (count, rels), 0).astype(F32) == owner, 1.0, 0.0).astype(BF16)
-    same = dot(has, has, TN)
-    index = lax.broadcasted_iota(jnp.int32, (rels, rels), 0)
-    before = index < lax.broadcasted_iota(jnp.int32, (rels, rels), 1)
-    rank = jnp.sum(jnp.where(before, same, 0.0), axis=0, keepdims=True)
-    slot = owner * per_owner + rank
-    slot_of[...] = slot
-    chosen = jnp.where(index.astype(F32) == slot, 1.0, 0.0).astype(BF16)
-    order_sel[...] = chosen
-    ordered[...] = dot(chosen, rel_emb[...], NN).astype(BF16)
-    first = (where[0] * mine + lax.broadcasted_iota(jnp.int32, (8, rels), 0)).astype(F32)
-    own = dot(jnp.where(first == slot, 1.0, 0.0).astype(BF16), rel_emb[...], NN).astype(BF16)
-    for a in range(rows_dev):
-        rows = dot(own, core[a], NN)
+def order_kernel(per_owner, mine, where, owners, rel_emb, core, part, ordered, order_sel, slot_of, own, wide):
+    step = pl.program_id(0)
+    rels = owners.shape[1]
+    block = core.shape[0]
+    rows_dev = wide.shape[0] // mine
+
+    @pl.when(step == 0)
+    def _():
+        owner = owners[...].astype(F32)
+        count = rels // per_owner
+        has = lax.broadcasted_iota(jnp.int32, (count, rels), 0).astype(F32) == owner
+        has = jnp.where(has, 1.0, 0.0).astype(BF16)
+        same = dot(has, has, TN)
+        index = lax.broadcasted_iota(jnp.int32, (rels, rels), 0)
+        before = index < lax.broadcasted_iota(jnp.int32, (rels, rels), 1)
+        rank = jnp.sum(jnp.where(before, same, 0.0), axis=0, keepdims=True)
+        slot = owner * per_owner + rank
+        slot_of[...] = slot
+        chosen = jnp.where(index.astype(F32) == slot, 1.0, 0.0).astype(BF16)
+        quarter = lax.broadcasted_iota(jnp.int32, (rels // 4, rels), 0)
+        for i in range(4):
+            order_sel[i] = jnp.where((quarter * 4 + i).astype(F32) == slot, 1.0, 0.0).astype(BF16)
+        ordered[...] = dot(chosen, rel_emb[...], NN).astype(BF16)
+        first = (where[0] * mine + lax.broadcasted_iota(jnp.int32, own.shape[:1] + (rels,), 0)).astype(F32)
+        own[...] = dot(jnp.where(first == slot, 1.0, 0.0).astype(BF16), rel_emb[...], NN).astype(BF16)
+
+    for a in range(block):
+        rows = dot(own[...], core[a], NN)
         for w in range(mine):
-            wide[w * rows_dev + a : w * rows_dev + a + 1, :] = rows[w : w + 1]
-    part[...] = wide[...].astype(BF16)
+            wide[pl.ds(w * rows_dev + step * block + a, 1), :] = rows[w : w + 1]
+
+    @pl.when(step == pl.num_programs(0) - 1)
+    def _():
+        part[...] = wide[...].astype(BF16)
 
 
 def send_kernel(cap, fill, head_ids, tail_ids, rel_ids, ents, out):
@@ -217,6 +229,27 @@
         out[a] = dot(weights, jnp.concatenate(rows, axis=1).astype(BF16), TN).astype(BF16)
 
 
+def last_kernel(where, own, other, order_sel, rel_grad, pool_grad):
+    rel_rows = order_sel.shape[1]
+    pool_dev = own.shape[1] - rel_rows
+    first = where[1] == 0
+    total = None
+    for s in range(own.shape[0]):
+        mine, theirs = own[s].astype(F32), other[s].astype(F32)
+        both = mine[:rel_rows] + theirs[:rel_rows]
+        total = both if total is None else total + both
+        mine, theirs = mine[rel_rows:], theirs[rel_rows:]
+        rows = [jnp.where(first, mine, theirs), jnp.where(first, theirs, mine)]
+        at = 2 * pool_dev * s
+        pool_grad[at : at + 2 * pool_dev, :] = jnp.concatenate(rows, axis=0).astype(BF16)
+    total = total.astype(BF16)
+    grad = None
+    for i in range(4):
+        piece = dot(order_sel[i], total[:, i * 128 : (i + 1) * 128], TN)
+        grad = piece if grad is None else grad + piece
+    rel_grad[...] = grad
+
+
 def call(kernel, outs, flops, in_specs, scratch=(), dtypes=None):
     vmem = pl.BlockSpec(memory_space=pltpu.VMEM)
     return pl.pallas_call(
@@ -253,14 +286,25 @@
     smem = pl.BlockSpec(memory_space=pltpu.SMEM)
     slots = REPS * cap
     block = slots * feats * feats * 2
-    where = g[None].astype(jnp.int32)
-    part, ordered, order_sel, slot_of = call(
+    where = jnp.stack([g, c]).astype(jnp.int32)
+    shapes = ((mine * rows_dev, feats), (rels, feats_rel), (4, rels // 4, rels), (1, rels))
+    steps = 1
+    part, ordered, order_sel, slot_of = pl.pallas_call(
         functools.partial(order_kernel, per_owner, mine),
-        ((mine * rows_dev, feats), (rels, feats_rel), (rels, rels), (1, rels)),
-        2 * 8 * core.size,
-        [smem] + [vmem] * 3,
-        (pltpu.VMEM((mine * rows_dev, feats), F32),),
-        dtypes=(BF16, BF16, BF16, F32),
+        grid=(steps,),
+        out_shape=tuple(
+            jax.ShapeDtypeStruct(shape, dtype) for shape, dtype in zip(shapes, (BF16, BF16, BF16, F32))
+        ),
+        in_specs=[
+            smem,
+            pl.BlockSpec((1, rels), lambda i: (0, 0)),
+            pl.BlockSpec((rels, feats_rel), lambda i: (0, 0)),
+            pl.BlockSpec((rows_dev // steps, feats_rel, feats), lambda i: (i, 0, 0)),
+        ],
+        out_specs=tuple(pl.BlockSpec(shape, lambda i, n=len(shape): (0,) * n) for shape in shapes),
+        scratch_shapes=(pltpu.VMEM((16, feats_rel), BF16), pltpu.VMEM((mine * rows_dev, feats), F32)),
+        cost_estimate=pl.CostEstimate(flops=16 * 2 * core.size, bytes_accessed=1 << 21, transcendentals=0),
+        compiler_params=pltpu.CompilerParams(vmem_limit_bytes=60 << 20),
     )(where, owner_of.reshape(1, rels), rel_emb, core)
 
     (sent,) = call(
@@ -356,18 +400,14 @@
         [vmem] * 2,
         (pltpu.VMEM((feats // 128, rels * rows_dev, 128), F32),),
     )(ordered, sums)
-    small, core_grad = lax.optimization_barrier((small, core_grad))
-    rel_own = jnp.sum(small[:, :rel_rows].astype(F32), axis=0).astype(BF16)
-    small = jnp.concatenate([rel_own, small[:, rel_rows:].reshape(-1, feats)])
-    small_other = swap_core(small)
-    rel_ordered = (small[:rel_rows].astype(F32) + small_other[:rel_rows].astype(F32)).astype(BF16)
-    rel_ordered = rel_ordered.reshape(rels, feats_rel)
-    halves = jnp.stack([small[rel_rows:], small_other[rel_rows:]])
-    halves = jnp.where(c == 0, halves, halves[::-1]).reshape(CORES, Z, pool_dev, feats)
-    pool_grad = jnp.swapaxes(halves, 0, 1).reshape(pool_rows, feats)
-    rel_grad = lax.dot_general(
-        order_sel, rel_ordered, (((0,), (0,)), ((), ())), preferred_element_type=F32
-    )
+    small, core_grad, ent_grad = lax.optimization_barrier((small, core_grad, ent_grad))
+    rel_grad, pool_grad = call(
+        last_kernel,
+        ((rels, feats_rel), (pool_rows, feats)),
+        1 << 20,
+        [smem] + [vmem] * 3,
+        dtypes=(F32, BF16),
+    )(where, small, swap_core(small), order_sel)
     return (core_grad, rel_grad, ent_grad, pool_grad)
 
 

time: 202 us -> 200 us (0.990)
  local copies, waits for them, and re-layouts: 8.83 us -> 4.27 us
  Pallas kernels: 13.9 us -> 18.2 us
    unnamed x28 -> x30, local copies, waits for them, and re-layouts: 6.99 us -> 3.2 us
    pallas_call x1 -> x2, Pallas kernels: 0.68 us -> 4.34 us  [the longest x1 2.97 us: body(): pl.pallas_call(functools.partial(order_kernel, per_owner, mine), grid=(st...]
    all_to_all x3, waiting for transfers between devices: 19.5 us -> 16.1 us  [exchange(): return lax.all_to_all(blocks, axis, split_axis=0, concat_axis=0, tiled=True)]
  transfers between devices with their start and end apart: 18 -> 18, of which waited for: 8 -> 9; matrix products, arithmetic and copies ran while one was open for 4% -> 3% of each run, Pallas kernels for 4% -> 4%
where the time goes in v6:
time: 200 us; the launch traced here: 199 us
  starting transfers between devices  93.7 us (47%)
  waiting for transfers between devices  49.9 us (25%)
  blocking collectives  25.4 us (13%)
  Pallas kernels  18.2 us (9%)
  other arithmetic  4.8 us (2%)
  local copies, waits for them, and re-layouts  4.27 us (2%)
    ppermute x6, starting transfers between devices, far_move(): lax.ppermute(block, LINE, [(z, (z + 4 * step) % Z) for z in range(Z)])  38.9 us
    all_to_all x1, blocking collectives, exchange(): return lax.all_to_all(blocks, axis, split_axis=0, concat_axis=0, tiled=True)  25.4 us
    ppermute x6, waiting for transfers between devices, near_move(): return lax.ppermute(block, REL, pairs)  22.2 us
    ppermute x3, starting transfers between devices, swap_core(): return lax.ppermute(block, 'core', [(0, 1), (1, 0)])  19.3 us
    all_to_all x3, starting transfers between devices, exchange(): return lax.all_to_all(blocks, axis, split_axis=0, concat_axis=0, tiled=True)  17.8 us
    ppermute x6, starting transfers between devices, near_move(): return lax.ppermute(block, REL, pairs)  17.7 us
    all_to_all x3, waiting for transfers between devices, exchange(): return lax.all_to_all(blocks, axis, split_axis=0, concat_axis=0, tiled=True)  16.1 us
    ppermute x6, waiting for transfers between devices, far_move(): lax.ppermute(block, LINE, [(z, (z + 4 * step) % Z) for z in range(Z)])  10.3 us
  transfers between devices with their start and end apart: 18, of which 9 were waited for; matrix products, arithmetic and copies ran while one was open for 3% of the time, Pallas kernels for 4%

profile of v6, /device:TPU:1, one launch (start us, length us, event | category | flops | bytes accessed | tf_op | source)
XLA Modules:
  0.0 198.8 jit_solution(11823331642446400485)
XLA Ops:
  0.7 0.6 pad_add_fusion.1.where
  1.3 3.0 %shard_map.120 = (bf16[64,512]{1,0:T(8,128)(2,1)}, bf16[64,128]{1,0:T(8,128)(2,1)}, bf16[4,16,64]{2,1,0:T(8,128)(2,1)}, f32[1,64]{1,0:T(1,128)}) custom-call(s32[2]{0:T(128)} %pad_add_fusion.1.where, s32[1,64]{1,0:T(1,128)} %bitcast.55, bf16[64,128]{1,0:T(8,128)(2,1)} %rel_emb.1, bf16[16,128,512]{2,1,0:T(8,128)(2,1)} %core.1), custom_call_target="tpu_custom_call" | custom-call | flops 33554432 | bytes 2097152 | tf_op jit(solution)/shard_map/pallas_call | solution.py:292
  4.3 13.3 %collective-permute-start.2 = (bf16[64,512]{1,0:T(8,128)(2,1)}, bf16[64,512]{1,0:T(8,128)(2,1)S(1)}, u32[]{:S(2)}, u32[]{:S(2)}) collective-permute-start(bf16[64,512]{1,0:T(8,128)(2,1)} %get-tuple-element.28), channel_id=1, source_target_pairs={{0,384},{32,416},{64,448},{96,480},{128,0},{160,32},{192,64},{224,... | collective-permute-start | bytes 196616 | tf_op jit(solution)/shard_map/ppermute | solution.py:43
  17.6 4.9 %collective-permute-start.1 = (bf16[64,512]{1,0:T(8,128)(2,1)}, bf16[64,512]{1,0:T(8,128)(2,1)S(1)}, u32[]{:S(2)}, u32[]{:S(2)}) collective-permute-start(bf16[64,512]{1,0:T(8,128)(2,1)} %get-tuple-element.28), channel_id=1, source_target_pairs={{0,256},{32,288},{64,320},{96,352},{128,384},{160,416},{192,448},{... | collective-permute-start | bytes 196616 | tf_op jit(solution)/shard_map/ppermute | solution.py:43
  22.5 7.3 %collective-permute-start = (bf16[64,512]{1,0:T(8,128)(2,1)}, bf16[64,512]{1,0:T(8,128)(2,1)}, u32[]{:S(2)}, u32[]{:S(2)}) collective-permute-start(bf16[64,512]{1,0:T(8,128)(2,1)} %get-tuple-element.28), channel_id=1, source_target_pairs={{0,128},{32,160},{64,192},{96,224},{128,256},{160,288},{192,320},{... | collective-permute-start | bytes 196616 | tf_op jit(solution)/shard_map/ppermute | solution.py:43
  29.8 0.0 copy-done.8
  29.8 0.0 copy-done.6
  29.8 0.0 copy-done.5
  29.8 0.0 copy-done.7
  29.8 0.0 copy-done.1
  29.8 0.7 shard_map.121
  30.5 1.4 copy-done
  31.9 6.8 %all-to-all-start = ((bf16[16,144,512]{2,1,0:T(8,128)(2,1)}), bf16[16,144,512]{2,1,0:T(8,128)(2,1)S(1)}, u32[]{:S(2)}, u32[]{:S(2)}) async-start(bf16[16,144,512]{2,1,0:T(8,128)(2,1)} %copy-done), calls=%async_computation | async-start | bytes 4718592 | tf_op jit(solution)/shard_map/all_to_all | solution.py:22
  38.7 0.8 constant_dynamic-update-slice_fusion.6
  39.6 0.0 collective-permute-done.2
  39.6 0.0 collective-permute-done.1
  39.6 0.0 collective-permute-done
  39.6 0.9 pad_maximum_fusion
  40.5 4.2 %collective-permute-start.5 = (bf16[4,64,512]{2,1,0:T(8,128)(2,1)S(1)}, bf16[4,64,512]{2,1,0:T(8,128)(2,1)S(1)}, u32[]{:S(2)}, u32[]{:S(2)}) collective-permute-start(bf16[4,64,512]{2,1,0:T(8,128)(2,1)S(1)} %pad_maximum_fusion), channel_id=1, source_target_pairs={{0,480},{16,496},{32,0},{48,16},{64,32},{80,48},{96,64},{112,80},{... | collective-permute-start | bytes 786440 | tf_op jit(solution)/shard_map/ppermute | solution.py:39
  44.8 1.9 collective-permute-start.4
  46.7 3.1 %collective-permute-start.3 = (bf16[4,64,512]{2,1,0:T(8,128)(2,1)S(1)}, bf16[4,64,512]{2,1,0:T(8,128)(2,1)S(1)}, u32[]{:S(2)}, u32[]{:S(2)}) collective-permute-start(bf16[4,64,512]{2,1,0:T(8,128)(2,1)S(1)} %pad_maximum_fusion), channel_id=1, source_target_pairs={{0,32},{16,48},{32,64},{48,80},{64,96},{80,112},{96,128},{112,144}... | collective-permute-start | bytes 786440 | tf_op jit(solution)/shard_map/ppermute | solution.py:39
  49.8 0.8 constant_dynamic-update-slice_fusion.5
  50.7 10.2 %collective-permute-done.3 = bf16[4,64,512]{2,1,0:T(8,128)(2,1)S(1)} collective-permute-done((bf16[4,64,512]{2,1,0:T(8,128)(2,1)S(1)}, bf16[4,64,512]{2,1,0:T(8,128)(2,1)S(1)}, u32[]{:S(2)}, u32[]{:S(2)}) %collective-permute-start.3) | collective-permute-done | bytes 262176 | tf_op jit(solution)/shard_map/ppermute | solution.py:39
  60.9 0.0 collective-permute-done.4
  60.9 0.0 collective-permute-done.5
  61.0 4.6 %collective-permute-start.6 = (bf16[16,64,512]{2,1,0:T(8,128)(2,1)S(1)}, bf16[16,64,512]{2,1,0:T(8,128)(2,1)}, u32[]{:S(2)}, u32[]{:S(2)}) collective-permute-start(bf16[16,64,512]{2,1,0:T(8,128)(2,1)S(1)} %constant_dynamic-update-slice_fusion.half), channel_id=1, source_target_pairs={{0,16},{16,0},{1,17},{17,1},{2,18},{18,2},{3,19},{19,3},{4,20},{20... | collective-permute-start | bytes 3145736 | tf_op jit(solution)/shard_map/ppermute | solution.py:47
  65.7 4.9 %all-to-all-done.table = bf16[16,144,512]{2,1,0:T(8,128)(2,1)S(1)} async-done(((bf16[16,144,512]{2,1,0:T(8,128)(2,1)}), bf16[16,144,512]{2,1,0:T(8,128)(2,1)S(1)}, u32[]{:S(2)}, u32[]{:S(2)}) %all-to-all-start) | async-done | bytes 2359328 | tf_op jit(solution)/shard_map/all_to_all | solution.py:22
  70.6 1.8 shard_map.122
  72.4 0.0 collective-permute-done.6.other
  72.4 5.5 %shard_map.123 = (bf16[4,512,512]{2,1,0:T(8,128)(2,1)S(1)}, bf16[2,512,512]{2,1,0:T(8,128)(2,1)S(1)}, bf16[2,512,512]{2,1,0:T(8,128)(2,1)S(1)}, bf16[4,288,512]{2,1,0:T(8,128)(2,1)S(1)}, bf16[4,288,512]{2,1,0:T(8,128)(2,1)S(1)}) custom-call(s32[4,16]{1,0:T(4,128)S(1)} %pad_add_fusion.starts, bf16[4,512,512]{2,1,0:T(8,128)(2,1)S(1)} %get-tuple-element.26.heads, ...), custom_call_target="tpu_custom_call" | custom-call | flops 2952790016 | bytes 8388608 | tf_op jit(solution)/shard_map/pallas_call | solution.py:340
  77.9 5.0 %collective-permute-start.7 = (bf16[4,288,512]{2,1,0:T(8,128)(2,1)S(1)}, bf16[4,288,512]{2,1,0:T(8,128)(2,1)S(1)}, u32[]{:S(2)}, u32[]{:S(2)}) collective-permute-start(bf16[4,288,512]{2,1,0:T(8,128)(2,1)S(1)} %get-tuple-element.30), channel_id=1, source_target_pairs={{0,16},{16,0},{1,17},{17,1},{2,18},{18,2},{3,19},{19,3},{4,20},{20... | collective-permute-start | bytes 3538952 | tf_op jit(solution)/shard_map/ppermute | solution.py:47
  82.9 3.2 %shard_map.124 = bf16[16,128,512]{2,1,0:T(8,128)(2,1)} custom-call(f32[16,256]{1,0:T(8,128)S(1)} %get-tuple-element.31.ids, bf16[2,512,512]{2,1,0:T(8,128)(2,1)S(1)} %get-tuple-element.32.dquery, bf16[2,512,512]{2,1,0:T(8,128)(2,1)S(1)} %get-tuple-element.33.dtail, bf16[4,512,512]{2,1,0:T(8,128)(2,1)S(1)} %get-tuple-element.34.mats), custom_call_target="tpu_custom_call" | custom-call | flops 1476395008 | bytes 8388608 | tf_op jit(solution)/shard_map/pallas_call | solution.py:354
  86.1 0.0 collective-permute-done.7
  86.1 4.4 %all-to-all-start.1 = ((bf16[16,128,512]{2,1,0:T(8,128)(2,1)}), bf16[16,128,512]{2,1,0:T(8,128)(2,1)}, u32[]{:S(2)}, u32[]{:S(2)}) async-start(bf16[16,128,512]{2,1,0:T(8,128)(2,1)} %shard_map.124), calls=%async_computation.1 | async-start | bytes 4194304 | tf_op jit(solution)/shard_map/all_to_all | solution.py:22
  90.5 0.4 add_convert_fusion
  90.9 0.1 slice_bitcast_fusion.2
  91.0 2.7 %collective-permute-start.8 = (bf16[288,512]{1,0:T(8,128)(2,1)S(1)}, bf16[288,512]{1,0:T(8,128)(2,1)S(1)}, u32[]{:S(2)}, u32[]{:S(2)}) collective-permute-start(bf16[288,512]{1,0:T(8,128)(2,1)S(1)} %get-tuple-element.46), channel_id=1, source_target_pairs={{0,32},{16,48},{32,64},{48,80},{64,96},{80,112},{96,128},{112,144}... | collective-permute-start | bytes 884744 | tf_op jit(solution)/shard_map/ppermute | solution.py:39
  93.6 3.8 %collective-permute-start.10 = (bf16[288,512]{1,0:T(8,128)(2,1)S(1)}, bf16[288,512]{1,0:T(8,128)(2,1)S(1)}, u32[]{:S(2)}, u32[]{:S(2)}) collective-permute-start(bf16[288,512]{1,0:T(8,128)(2,1)S(1)} %get-tuple-element.47), channel_id=1, source_target_pairs={{0,480},{16,496},{32,0},{48,16},{64,32},{80,48},{96,64},{112,80},{... | collective-permute-start | bytes 884744 | tf_op jit(solution)/shard_map/ppermute | solution.py:39
  97.5 1.9 collective-permute-start.9
  99.4 3.4 %collective-permute-done.8 = bf16[288,512]{1,0:T(8,128)(2,1)S(1)} collective-permute-done((bf16[288,512]{1,0:T(8,128)(2,1)S(1)}, bf16[288,512]{1,0:T(8,128)(2,1)S(1)}, u32[]{:S(2)}, u32[]{:S(2)}) %collective-permute-start.8) | collective-permute-done | bytes 294944 | tf_op jit(solution)/shard_map/ppermute | solution.py:39
  102.8 1.1 collective-permute-done.10
  103.9 7.5 %collective-permute-done.9 = bf16[288,512]{1,0:T(8,128)(2,1)S(1)} collective-permute-done((bf16[288,512]{1,0:T(8,128)(2,1)S(1)}, bf16[288,512]{1,0:T(8,128)(2,1)S(1)}, u32[]{:S(2)}, u32[]{:S(2)}) %collective-permute-start.9) | collective-permute-done | bytes 294944 | tf_op jit(solution)/shard_map/ppermute | solution.py:39
  111.4 0.2 fusion.14
  111.6 4.0 %collective-permute-start.11 = (bf16[72,512]{1,0:T(8,128)(2,1)S(1)}, bf16[72,512]{1,0:T(8,128)(2,1)S(1)}, u32[]{:S(2)}, u32[]{:S(2)}) collective-permute-start(bf16[72,512]{1,0:T(8,128)(2,1)S(1)} %pad_maximum_fusion.1), channel_id=1, source_target_pairs={{0,128},{32,160},{64,192},{96,224},{128,256},{160,288},{192,320},{... | collective-permute-start | bytes 221192 | tf_op jit(solution)/shard_map/ppermute | solution.py:43
  115.7 5.4 %collective-permute-start.12 = (bf16[72,512]{1,0:T(8,128)(2,1)S(1)}, bf16[72,512]{1,0:T(8,128)(2,1)S(1)}, u32[]{:S(2)}, u32[]{:S(2)}) collective-permute-start(bf16[72,512]{1,0:T(8,128)(2,1)S(1)} %pad_maximum_fusion.2), channel_id=1, source_target_pairs={{0,256},{32,288},{64,320},{96,352},{128,384},{160,416},{192,448},{... | collective-permute-start | bytes 221192 | tf_op jit(solution)/shard_map/ppermute | solution.py:43
  121.1 4.1 %collective-permute-start.13 = (bf16[72,512]{1,0:T(8,128)(2,1)S(1)}, bf16[72,512]{1,0:T(8,128)(2,1)S(1)}, u32[]{:S(2)}, u32[]{:S(2)}) collective-permute-start(bf16[72,512]{1,0:T(8,128)(2,1)S(1)} %pad_maximum_fusion.3), channel_id=1, source_target_pairs={{0,384},{32,416},{64,448},{96,480},{128,0},{160,32},{192,64},{224,... | collective-permute-start | bytes 221192 | tf_op jit(solution)/shard_map/ppermute | solution.py:43
  125.1 0.0 collective-permute-done.11
  125.2 4.7 %collective-permute-done.12 = bf16[72,512]{1,0:T(8,128)(2,1)S(1)} collective-permute-done((bf16[72,512]{1,0:T(8,128)(2,1)S(1)}, bf16[72,512]{1,0:T(8,128)(2,1)S(1)}, u32[]{:S(2)}, u32[]{:S(2)}) %collective-permute-start.12) | collective-permute-done | bytes 73760 | tf_op jit(solution)/shard_map/ppermute | solution.py:43
  129.8 5.7 %collective-permute-done.13 = bf16[72,512]{1,0:T(8,128)(2,1)S(1)} collective-permute-done((bf16[72,512]{1,0:T(8,128)(2,1)S(1)}, bf16[72,512]{1,0:T(8,128)(2,1)S(1)}, u32[]{:S(2)}, u32[]{:S(2)}) %collective-permute-start.13) | collective-permute-done | bytes 73760 | tf_op jit(solution)/shard_map/ppermute | solution.py:43
  135.5 0.0 all-to-all-done.1
  135.5 0.1 broadcast_in_dim.28
  135.6 0.0 copy-start.11
  135.6 25.4 %all_to_all.20.sums = bf16[16,72,512]{2,1,0:T(8,128)(2,1)S(1)} all-to-all(bf16[16,72,512]{2,1,0:T(8,128)(2,1)S(1)} %broadcast_in_dim.28), channel_id=1, replica_groups=mesh['zh'=4,'zl'=4,'core'=2,'y'=4,'x'=4] {'y','x'}, dimensions={0} | all-to-all | bytes 2359296 | tf_op jit(solution)/shard_map/all_to_all | solution.py:22
  161.0 0.1 slice.68
  161.1 1.3 fusion.8
  162.4 0.0 copy-start.2
  162.5 0.8 broadcast_in_dim.29
  163.3 6.6 %all-to-all-start.3 = ((bf16[16,24,512]{2,1,0:T(8,128)(2,1)}), bf16[16,24,512]{2,1,0:T(8,128)(2,1)S(1)}, u32[]{:S(2)}, u32[]{:S(2)}) async-start(bf16[16,24,512]{2,1,0:T(8,128)(2,1)} %broadcast_in_dim.29), calls=%async_computation.3 | async-start | bytes 786432 | tf_op jit(solution)/shard_map/all_to_all | solution.py:22
  169.9 2.6 %reduce_sum.25 = bf16[128,512]{1,0:T(8,128)(2,1)} reduce(bf16[16,128,512]{2,1,0:T(8,128)(2,1)} %all-to-all-done.1, bf16[]{:T(256)} %constant.110.clone.1), dimensions={0}, to_apply=%region_1.2 | reduce | flops 983040 | bytes 2228226 | tf_op jit(solution)/shard_map/reduce_sum | solution.py:383
  172.5 2.8 %shard_map.125 = bf16[16,128,512]{2,1,0:T(8,128)(2,1)} custom-call(bf16[64,128]{1,0:T(8,128)(2,1)S(1)} %copy-done.2, bf16[16,72,512]{2,1,0:T(8,128)(2,1)S(1)} %all_to_all.20.sums), custom_call_target="tpu_custom_call" | custom-call | flops 134217728 | bytes 8388608 | tf_op jit(solution)/shard_map/pallas_call | solution.py:396
  175.3 11.2 %all-to-all-done.3.own = bf16[16,24,512]{2,1,0:T(8,128)(2,1)S(1)} async-done(((bf16[16,24,512]{2,1,0:T(8,128)(2,1)}), bf16[16,24,512]{2,1,0:T(8,128)(2,1)S(1)}, u32[]{:S(2)}, u32[]{:S(2)}) %all-to-all-start.3) | async-done | bytes 393248 | tf_op jit(solution)/shard_map/all_to_all | solution.py:22
  186.5 9.7 %collective-permute-start.14 = (bf16[16,24,512]{2,1,0:T(8,128)(2,1)S(1)}, bf16[16,24,512]{2,1,0:T(8,128)(2,1)S(1)}, u32[]{:S(2)}, u32[]{:S(2)}) collective-permute-start(bf16[16,24,512]{2,1,0:T(8,128)(2,1)S(1)} %all-to-all-done.3.own), channel_id=1, source_target_pairs={{0,16},{16,0},{1,17},{17,1},{2,18},{18,2},{3,19},{19,3},{4,20},{20... | collective-permute-start | bytes 1179656 | tf_op jit(solution)/shard_map/ppermute | solution.py:47
  196.1 1.3 collective-permute-done.14.other
  197.5 1.4 shard_map.126
  (33 shorter events, 0.3 us)
Async XLA Ops:
  0.6 29.1 %copy-start.8 = (s32[1,32]{1,0:T(1,128)S(1)}, s32[1,32]{1,0:T(1,128)}, u32[]{:S(2)}) copy-start(s32[1,32]{1,0:T(1,128)} %fill.1) | copy-start | bytes 388
  0.6 29.1 %copy-start.6 = (s32[1024]{0:T(1024)S(1)}, s32[1024]{0:T(1024)}, u32[]{:S(2)}) copy-start(s32[1024]{0:T(1024)} %param.16) | copy-start | bytes 12292
  0.7 29.1 %copy-start.5 = (s32[1024]{0:T(1024)S(1)}, s32[1024]{0:T(1024)}, u32[]{:S(2)}) copy-start(s32[1024]{0:T(1024)} %param.15) | copy-start | bytes 12292
  0.7 29.1 %copy-start.7 = (s32[1024]{0:T(1024)S(1)}, s32[1024]{0:T(1024)}, u32[]{:S(2)}) copy-start(s32[1024]{0:T(1024)} %param.14) | copy-start | bytes 12292
  0.7 29.1 %copy-start.1 = (bf16[128,512]{1,0:T(8,128)(2,1)S(1)}, bf16[128,512]{1,0:T(8,128)(2,1)}, u32[]{:S(2)}) copy-start(bf16[128,512]{1,0:T(8,128)(2,1)} %ents.1) | copy-start | bytes 393220
  4.3 35.3 %collective-permute-start.2 = (bf16[64,512]{1,0:T(8,128)(2,1)}, bf16[64,512]{1,0:T(8,128)(2,1)S(1)}, u32[]{:S(2)}, u32[]{:S(2)}) collective-permute-start(bf16[64,512]{1,0:T(8,128)(2,1)} %get-tuple-element.28), channel_id=1, source_target_pairs={{0,384},{32,416},{64,448},{96,480},{128,0},{160,32},{192,64},{224,... | collective-permute-start | bytes 196616 | tf_op jit(solution)/shard_map/ppermute | solution.py:43
  17.6 22.0 %collective-permute-start.1 = (bf16[64,512]{1,0:T(8,128)(2,1)}, bf16[64,512]{1,0:T(8,128)(2,1)S(1)}, u32[]{:S(2)}, u32[]{:S(2)}) collective-permute-start(bf16[64,512]{1,0:T(8,128)(2,1)} %get-tuple-element.28), channel_id=1, source_target_pairs={{0,256},{32,288},{64,320},{96,352},{128,384},{160,416},{192,448},{... | collective-permute-start | bytes 196616 | tf_op jit(solution)/shard_map/ppermute | solution.py:43
  22.5 17.1 %collective-permute-start = (bf16[64,512]{1,0:T(8,128)(2,1)}, bf16[64,512]{1,0:T(8,128)(2,1)}, u32[]{:S(2)}, u32[]{:S(2)}) collective-permute-start(bf16[64,512]{1,0:T(8,128)(2,1)} %get-tuple-element.28), channel_id=1, source_target_pairs={{0,128},{32,160},{64,192},{96,224},{128,256},{160,288},{192,320},{... | collective-permute-start | bytes 196616 | tf_op jit(solution)/shard_map/ppermute | solution.py:43
  30.5 1.4 copy-start
  31.9 38.6 %all-to-all-start = ((bf16[16,144,512]{2,1,0:T(8,128)(2,1)}), bf16[16,144,512]{2,1,0:T(8,128)(2,1)S(1)}, u32[]{:S(2)}, u32[]{:S(2)}) async-start(bf16[16,144,512]{2,1,0:T(8,128)(2,1)} %copy-done), calls=%async_computation | async-start | bytes 4718592 | tf_op jit(solution)/shard_map/all_to_all | solution.py:22
  38.7 31.9 %copy-start.4 = (s32[2]{0:T(128)S(1)}, s32[2]{0:T(128)}, u32[]{:S(2)}) copy-start(s32[2]{0:T(128)} %pad_add_fusion.1.where) | copy-start | bytes 28
  38.7 31.9 %copy-start.9 = (f32[1,64]{1,0:T(1,128)S(1)}, f32[1,64]{1,0:T(1,128)}, u32[]{:S(2)}) copy-start(f32[1,64]{1,0:T(1,128)} %get-tuple-element.25.slot_of) | copy-start | bytes 772
  40.5 20.4 %collective-permute-start.5 = (bf16[4,64,512]{2,1,0:T(8,128)(2,1)S(1)}, bf16[4,64,512]{2,1,0:T(8,128)(2,1)S(1)}, u32[]{:S(2)}, u32[]{:S(2)}) collective-permute-start(bf16[4,64,512]{2,1,0:T(8,128)(2,1)S(1)} %pad_maximum_fusion), channel_id=1, source_target_pairs={{0,480},{16,496},{32,0},{48,16},{64,32},{80,48},{96,64},{112,80},{... | collective-permute-start | bytes 786440 | tf_op jit(solution)/shard_map/ppermute | solution.py:39
  44.8 16.1 %collective-permute-start.4 = (bf16[4,64,512]{2,1,0:T(8,128)(2,1)S(1)}, bf16[4,64,512]{2,1,0:T(8,128)(2,1)S(1)}, u32[]{:S(2)}, u32[]{:S(2)}) collective-permute-start(bf16[4,64,512]{2,1,0:T(8,128)(2,1)S(1)} %pad_maximum_fusion), channel_id=1, source_target_pairs={{0,64},{16,464},{32,96},{48,496},{64,128},{80,16},{96,160},{112,48... | collective-permute-start | bytes 786440 | tf_op jit(solution)/shard_map/ppermute | solution.py:39
  46.7 14.2 %collective-permute-start.3 = (bf16[4,64,512]{2,1,0:T(8,128)(2,1)S(1)}, bf16[4,64,512]{2,1,0:T(8,128)(2,1)S(1)}, u32[]{:S(2)}, u32[]{:S(2)}) collective-permute-start(bf16[4,64,512]{2,1,0:T(8,128)(2,1)S(1)} %pad_maximum_fusion), channel_id=1, source_target_pairs={{0,32},{16,48},{32,64},{48,80},{64,96},{80,112},{96,128},{112,144}... | collective-permute-start | bytes 786440 | tf_op jit(solution)/shard_map/ppermute | solution.py:39
  61.0 11.4 %collective-permute-start.6 = (bf16[16,64,512]{2,1,0:T(8,128)(2,1)S(1)}, bf16[16,64,512]{2,1,0:T(8,128)(2,1)}, u32[]{:S(2)}, u32[]{:S(2)}) collective-permute-start(bf16[16,64,512]{2,1,0:T(8,128)(2,1)S(1)} %constant_dynamic-update-slice_fusion.half), channel_id=1, source_target_pairs={{0,16},{16,0},{1,17},{17,1},{2,18},{18,2},{3,19},{19,3},{4,20},{20... | collective-permute-start | bytes 3145736 | tf_op jit(solution)/shard_map/ppermute | solution.py:47
  70.6 1.8 copy-start.10
  77.9 8.2 %collective-permute-start.7 = (bf16[4,288,512]{2,1,0:T(8,128)(2,1)S(1)}, bf16[4,288,512]{2,1,0:T(8,128)(2,1)S(1)}, u32[]{:S(2)}, u32[]{:S(2)}) collective-permute-start(bf16[4,288,512]{2,1,0:T(8,128)(2,1)S(1)} %get-tuple-element.30), channel_id=1, source_target_pairs={{0,16},{16,0},{1,17},{17,1},{2,18},{18,2},{3,19},{19,3},{4,20},{20... | collective-permute-start | bytes 3538952 | tf_op jit(solution)/shard_map/ppermute | solution.py:47
  86.1 49.4 %all-to-all-start.1 = ((bf16[16,128,512]{2,1,0:T(8,128)(2,1)}), bf16[16,128,512]{2,1,0:T(8,128)(2,1)}, u32[]{:S(2)}, u32[]{:S(2)}) async-start(bf16[16,128,512]{2,1,0:T(8,128)(2,1)} %shard_map.124), calls=%async_computation.1 | async-start | bytes 4194304 | tf_op jit(solution)/shard_map/all_to_all | solution.py:22
  91.0 11.8 %collective-permute-start.8 = (bf16[288,512]{1,0:T(8,128)(2,1)S(1)}, bf16[288,512]{1,0:T(8,128)(2,1)S(1)}, u32[]{:S(2)}, u32[]{:S(2)}) collective-permute-start(bf16[288,512]{1,0:T(8,128)(2,1)S(1)} %get-tuple-element.46), channel_id=1, source_target_pairs={{0,32},{16,48},{32,64},{48,80},{64,96},{80,112},{96,128},{112,144}... | collective-permute-start | bytes 884744 | tf_op jit(solution)/shard_map/ppermute | solution.py:39
  93.6 10.3 %collective-permute-start.10 = (bf16[288,512]{1,0:T(8,128)(2,1)S(1)}, bf16[288,512]{1,0:T(8,128)(2,1)S(1)}, u32[]{:S(2)}, u32[]{:S(2)}) collective-permute-start(bf16[288,512]{1,0:T(8,128)(2,1)S(1)} %get-tuple-element.47), channel_id=1, source_target_pairs={{0,480},{16,496},{32,0},{48,16},{64,32},{80,48},{96,64},{112,80},{... | collective-permute-start | bytes 884744 | tf_op jit(solution)/shard_map/ppermute | solution.py:39
  97.5 13.9 %collective-permute-start.9 = (bf16[288,512]{1,0:T(8,128)(2,1)S(1)}, bf16[288,512]{1,0:T(8,128)(2,1)S(1)}, u32[]{:S(2)}, u32[]{:S(2)}) collective-permute-start(bf16[288,512]{1,0:T(8,128)(2,1)S(1)} %get-tuple-element.48), channel_id=1, source_target_pairs={{0,64},{16,464},{32,96},{48,496},{64,128},{80,16},{96,160},{112,48... | collective-permute-start | bytes 884744 | tf_op jit(solution)/shard_map/ppermute | solution.py:39
  111.6 13.5 %collective-permute-start.11 = (bf16[72,512]{1,0:T(8,128)(2,1)S(1)}, bf16[72,512]{1,0:T(8,128)(2,1)S(1)}, u32[]{:S(2)}, u32[]{:S(2)}) collective-permute-start(bf16[72,512]{1,0:T(8,128)(2,1)S(1)} %pad_maximum_fusion.1), channel_id=1, source_target_pairs={{0,128},{32,160},{64,192},{96,224},{128,256},{160,288},{192,320},{... | collective-permute-start | bytes 221192 | tf_op jit(solution)/shard_map/ppermute | solution.py:43
  115.7 14.2 %collective-permute-start.12 = (bf16[72,512]{1,0:T(8,128)(2,1)S(1)}, bf16[72,512]{1,0:T(8,128)(2,1)S(1)}, u32[]{:S(2)}, u32[]{:S(2)}) collective-permute-start(bf16[72,512]{1,0:T(8,128)(2,1)S(1)} %pad_maximum_fusion.2), channel_id=1, source_target_pairs={{0,256},{32,288},{64,320},{96,352},{128,384},{160,416},{192,448},{... | collective-permute-start | bytes 221192 | tf_op jit(solution)/shard_map/ppermute | solution.py:43
  121.1 14.4 %collective-permute-start.13 = (bf16[72,512]{1,0:T(8,128)(2,1)S(1)}, bf16[72,512]{1,0:T(8,128)(2,1)S(1)}, u32[]{:S(2)}, u32[]{:S(2)}) collective-permute-start(bf16[72,512]{1,0:T(8,128)(2,1)S(1)} %pad_maximum_fusion.3), channel_id=1, source_target_pairs={{0,384},{32,416},{64,448},{96,480},{128,0},{160,32},{192,64},{224,... | collective-permute-start | bytes 221192 | tf_op jit(solution)/shard_map/ppermute | solution.py:43
  135.6 25.5 %copy-start.11 = (bf16[16,128,512]{2,1,0:T(8,128)(2,1)S(1)}, bf16[16,128,512]{2,1,0:T(8,128)(2,1)}, u32[]{:S(2)}) copy-start(bf16[16,128,512]{2,1,0:T(8,128)(2,1)} %core.1) | copy-start | bytes 6291460
  162.4 10.1 %copy-start.2 = (bf16[64,128]{1,0:T(8,128)(2,1)S(1)}, bf16[64,128]{1,0:T(8,128)(2,1)}, u32[]{:S(2)}) copy-start(bf16[64,128]{1,0:T(8,128)(2,1)} %get-tuple-element.38.ordered) | copy-start | bytes 49156
  163.3 23.2 %all-to-all-start.3 = ((bf16[16,24,512]{2,1,0:T(8,128)(2,1)}), bf16[16,24,512]{2,1,0:T(8,128)(2,1)S(1)}, u32[]{:S(2)}, u32[]{:S(2)}) async-start(bf16[16,24,512]{2,1,0:T(8,128)(2,1)} %broadcast_in_dim.29), calls=%async_computation.3 | async-start | bytes 786432 | tf_op jit(solution)/shard_map/all_to_all | solution.py:22
  172.5 25.0 %copy-start.3 = (bf16[4,16,64]{2,1,0:T(8,128)(2,1)S(1)}, bf16[4,16,64]{2,1,0:T(8,128)(2,1)}, u32[]{:S(2)}) copy-start(bf16[4,16,64]{2,1,0:T(8,128)(2,1)} %get-tuple-element.42.order_sel) | copy-start | bytes 24580
  186.5 11.0 %collective-permute-start.14 = (bf16[16,24,512]{2,1,0:T(8,128)(2,1)S(1)}, bf16[16,24,512]{2,1,0:T(8,128)(2,1)S(1)}, u32[]{:S(2)}, u32[]{:S(2)}) collective-permute-start(bf16[16,24,512]{2,1,0:T(8,128)(2,1)S(1)} %all-to-all-done.3.own), channel_id=1, source_target_pairs={{0,16},{16,0},{1,17},{17,1},{2,18},{18,2},{3,19},{19,3},{4,20},{20... | collective-permute-start | bytes 1179656 | tf_op jit(solution)/shard_map/ppermute | solution.py:47

commit v7 on v6

--- a/solution.py
+++ b/solution.py
@@ -54,7 +54,7 @@
 NN, NT, TN = ((1,), (0,)), ((1,), (1,)), ((0,), (0,))
 
 
-def order_kernel(per_owner, mine, where, owners, rel_emb, core, part, ordered, order_sel, slot_of, own, wide):
+def order_kernel(per_owner, mine, owners, rel_emb, core, part, ordered, order_sel, slot_of, own, wide):
     step = pl.program_id(0)
     rels = owners.shape[1]
     block = core.shape[0]
@@ -77,7 +77,7 @@
         for i in range(4):
             order_sel[i] = jnp.where((quarter * 4 + i).astype(F32) == slot, 1.0, 0.0).astype(BF16)
         ordered[...] = dot(chosen, rel_emb[...], NN).astype(BF16)
-        first = (where[0] * mine + lax.broadcasted_iota(jnp.int32, own.shape[:1] + (rels,), 0)).astype(F32)
+        first = (lax.axis_index(REP) * mine + lax.broadcasted_iota(jnp.int32, own.shape[:1] + (rels,), 0)).astype(F32)
         own[...] = dot(jnp.where(first == slot, 1.0, 0.0).astype(BF16), rel_emb[...], NN).astype(BF16)
 
     for a in range(block):
@@ -296,7 +296,6 @@
             jax.ShapeDtypeStruct(shape, dtype) for shape, dtype in zip(shapes, (BF16, BF16, BF16, F32))
         ),
         in_specs=[
-            smem,
             pl.BlockSpec((1, rels), lambda i: (0, 0)),
             pl.BlockSpec((rels, feats_rel), lambda i: (0, 0)),
             pl.BlockSpec((rows_dev // steps, feats_rel, feats), lambda i: (i, 0, 0)),
@@ -305,7 +304,7 @@
         scratch_shapes=(pltpu.VMEM((16, feats_rel), BF16), pltpu.VMEM((mine * rows_dev, feats), F32)),
         cost_estimate=pl.CostEstimate(flops=16 * 2 * core.size, bytes_accessed=1 << 21, transcendentals=0),
         compiler_params=pltpu.CompilerParams(vmem_limit_bytes=60 << 20),
-    )(where, owner_of.reshape(1, rels), rel_emb, core)
+    )(owner_of.reshape(1, rels), rel_emb, core)
 
     (sent,) = call(
         functools.partial(send_kernel, cap),

time: 200 us -> 199 us (level)
  no operation moved by 1% of the time
where the time goes in v7:
time: 199 us; the launch traced here: 198 us
  starting transfers between devices  93.7 us (47%)
  waiting for transfers between devices  49.9 us (25%)
  blocking collectives  25.3 us (13%)
  Pallas kernels  18.3 us (9%)
  local copies, waits for them, and re-layouts  4.27 us (2%)
  other arithmetic  4.23 us (2%)
    ppermute x6, starting transfers between devices, far_move(): lax.ppermute(block, LINE, [(z, (z + 4 * step) % Z) for z in range(Z)])  38.9 us
    all_to_all x1, blocking collectives, exchange(): return lax.all_to_all(blocks, axis, split_axis=0, concat_axis=0, tiled=True)  25.3 us
    ppermute x6, waiting for transfers between devices, near_move(): return lax.ppermute(block, REL, pairs)  22.2 us
    ppermute x3, starting transfers between devices, swap_core(): return lax.ppermute(block, 'core', [(0, 1), (1, 0)])  19.3 us
    all_to_all x3, starting transfers between devices, exchange(): return lax.all_to_all(blocks, axis, split_axis=0, concat_axis=0, tiled=True)  17.8 us
    ppermute x6, starting transfers between devices, near_move(): return lax.ppermute(block, REL, pairs)  17.7 us
    all_to_all x3, waiting for transfers between devices, exchange(): return lax.all_to_all(blocks, axis, split_axis=0, concat_axis=0, tiled=True)  16 us
    ppermute x6, waiting for transfers between devices, far_move(): lax.ppermute(block, LINE, [(z, (z + 4 * step) % Z) for z in range(Z)])  10.3 us
  transfers between devices with their start and end apart: 18, of which 9 were waited for; matrix products, arithmetic and copies ran while one was open for 3% of the time, Pallas kernels for 4%

profile of v7, /device:TPU:1, one launch (start us, length us, event | category | flops | bytes accessed | tf_op | source)
XLA Modules:
  0.0 198.2 jit_solution(5588046610268403189)
XLA Ops:
  0.6 0.0 copy-start.7
  0.6 0.0 copy-start.5
  0.7 0.0 copy-start.4
  0.7 3.0 %shard_map.120 = (bf16[64,512]{1,0:T(8,128)(2,1)}, bf16[64,128]{1,0:T(8,128)(2,1)}, bf16[4,16,64]{2,1,0:T(8,128)(2,1)}, f32[1,64]{1,0:T(1,128)}) custom-call(s32[1,64]{1,0:T(1,128)} %bitcast.55, bf16[64,128]{1,0:T(8,128)(2,1)} %rel_emb.1, bf16[16,128,512]{2,1,0:T(8,128)(2,1)} %core.1), custom_call_target="tpu_custom_call" | custom-call | flops 33554432 | bytes 2097152 | tf_op jit(solution)/shard_map/pallas_call | solution.py:292
  3.7 13.3 %collective-permute-start.2 = (bf16[64,512]{1,0:T(8,128)(2,1)}, bf16[64,512]{1,0:T(8,128)(2,1)S(1)}, u32[]{:S(2)}, u32[]{:S(2)}) collective-permute-start(bf16[64,512]{1,0:T(8,128)(2,1)} %get-tuple-element.28), channel_id=1, source_target_pairs={{0,384},{32,416},{64,448},{96,480},{128,0},{160,32},{192,64},{224,... | collective-permute-start | bytes 196616 | tf_op jit(solution)/shard_map/ppermute | solution.py:43
  17.0 4.9 %collective-permute-start.1 = (bf16[64,512]{1,0:T(8,128)(2,1)}, bf16[64,512]{1,0:T(8,128)(2,1)S(1)}, u32[]{:S(2)}, u32[]{:S(2)}) collective-permute-start(bf16[64,512]{1,0:T(8,128)(2,1)} %get-tuple-element.28), channel_id=1, source_target_pairs={{0,256},{32,288},{64,320},{96,352},{128,384},{160,416},{192,448},{... | collective-permute-start | bytes 196616 | tf_op jit(solution)/shard_map/ppermute | solution.py:43
  21.9 7.3 %collective-permute-start = (bf16[64,512]{1,0:T(8,128)(2,1)}, bf16[64,512]{1,0:T(8,128)(2,1)}, u32[]{:S(2)}, u32[]{:S(2)}) collective-permute-start(bf16[64,512]{1,0:T(8,128)(2,1)} %get-tuple-element.28), channel_id=1, source_target_pairs={{0,128},{32,160},{64,192},{96,224},{128,256},{160,288},{192,320},{... | collective-permute-start | bytes 196616 | tf_op jit(solution)/shard_map/ppermute | solution.py:43
  29.2 0.7 shard_map.121
  29.9 1.4 copy-done
  31.3 6.8 %all-to-all-start = ((bf16[16,144,512]{2,1,0:T(8,128)(2,1)}), bf16[16,144,512]{2,1,0:T(8,128)(2,1)S(1)}, u32[]{:S(2)}, u32[]{:S(2)}) async-start(bf16[16,144,512]{2,1,0:T(8,128)(2,1)} %copy-done), calls=%async_computation | async-start | bytes 4718592 | tf_op jit(solution)/shard_map/all_to_all | solution.py:22
  38.1 0.0 copy-start.8
  38.1 0.9 constant_dynamic-update-slice_fusion.6
  39.0 0.0 collective-permute-done.2
  39.0 0.0 collective-permute-done.1
  39.0 0.0 collective-permute-done
  39.0 0.9 pad_maximum_fusion
  39.9 4.2 %collective-permute-start.5 = (bf16[4,64,512]{2,1,0:T(8,128)(2,1)S(1)}, bf16[4,64,512]{2,1,0:T(8,128)(2,1)S(1)}, u32[]{:S(2)}, u32[]{:S(2)}) collective-permute-start(bf16[4,64,512]{2,1,0:T(8,128)(2,1)S(1)} %pad_maximum_fusion), channel_id=1, source_target_pairs={{0,480},{16,496},{32,0},{48,16},{64,32},{80,48},{96,64},{112,80},{... | collective-permute-start | bytes 786440 | tf_op jit(solution)/shard_map/ppermute | solution.py:39
  44.1 1.9 collective-permute-start.4
  46.1 3.1 %collective-permute-start.3 = (bf16[4,64,512]{2,1,0:T(8,128)(2,1)S(1)}, bf16[4,64,512]{2,1,0:T(8,128)(2,1)S(1)}, u32[]{:S(2)}, u32[]{:S(2)}) collective-permute-start(bf16[4,64,512]{2,1,0:T(8,128)(2,1)S(1)} %pad_maximum_fusion), channel_id=1, source_target_pairs={{0,32},{16,48},{32,64},{48,80},{64,96},{80,112},{96,128},{112,144}... | collective-permute-start | bytes 786440 | tf_op jit(solution)/shard_map/ppermute | solution.py:39
  49.2 0.8 constant_dynamic-update-slice_fusion.5
  50.0 10.2 %collective-permute-done.3 = bf16[4,64,512]{2,1,0:T(8,128)(2,1)S(1)} collective-permute-done((bf16[4,64,512]{2,1,0:T(8,128)(2,1)S(1)}, bf16[4,64,512]{2,1,0:T(8,128)(2,1)S(1)}, u32[]{:S(2)}, u32[]{:S(2)}) %collective-permute-start.3) | collective-permute-done | bytes 262176 | tf_op jit(solution)/shard_map/ppermute | solution.py:39
  60.3 0.0 collective-permute-done.4
  60.3 0.0 collective-permute-done.5
  60.3 4.6 %collective-permute-start.6 = (bf16[16,64,512]{2,1,0:T(8,128)(2,1)S(1)}, bf16[16,64,512]{2,1,0:T(8,128)(2,1)}, u32[]{:S(2)}, u32[]{:S(2)}) collective-permute-start(bf16[16,64,512]{2,1,0:T(8,128)(2,1)S(1)} %constant_dynamic-update-slice_fusion.half), channel_id=1, source_target_pairs={{0,16},{16,0},{1,17},{17,1},{2,18},{18,2},{3,19},{19,3},{4,20},{20... | collective-permute-start | bytes 3145736 | tf_op jit(solution)/shard_map/ppermute | solution.py:47
  65.0 0.1 pad_add_fusion.1.where
  65.1 4.8 %all-to-all-done.table = bf16[16,144,512]{2,1,0:T(8,128)(2,1)S(1)} async-done(((bf16[16,144,512]{2,1,0:T(8,128)(2,1)}), bf16[16,144,512]{2,1,0:T(8,128)(2,1)S(1)}, u32[]{:S(2)}, u32[]{:S(2)}) %all-to-all-start) | async-done | bytes 2359328 | tf_op jit(solution)/shard_map/all_to_all | solution.py:22
  70.0 1.8 shard_map.122
  71.7 0.0 collective-permute-done.6.other
  71.8 0.0 copy-done.9
  71.8 5.5 %shard_map.123 = (bf16[4,512,512]{2,1,0:T(8,128)(2,1)S(1)}, bf16[2,512,512]{2,1,0:T(8,128)(2,1)S(1)}, bf16[2,512,512]{2,1,0:T(8,128)(2,1)S(1)}, bf16[4,288,512]{2,1,0:T(8,128)(2,1)S(1)}, bf16[4,288,512]{2,1,0:T(8,128)(2,1)S(1)}) custom-call(s32[4,16]{1,0:T(4,128)S(1)} %pad_add_fusion.starts, bf16[4,512,512]{2,1,0:T(8,128)(2,1)S(1)} %get-tuple-element.26.heads, ...), custom_call_target="tpu_custom_call" | custom-call | flops 2952790016 | bytes 8388608 | tf_op jit(solution)/shard_map/pallas_call | solution.py:339
  77.2 5.0 %collective-permute-start.7 = (bf16[4,288,512]{2,1,0:T(8,128)(2,1)S(1)}, bf16[4,288,512]{2,1,0:T(8,128)(2,1)S(1)}, u32[]{:S(2)}, u32[]{:S(2)}) collective-permute-start(bf16[4,288,512]{2,1,0:T(8,128)(2,1)S(1)} %get-tuple-element.30), channel_id=1, source_target_pairs={{0,16},{16,0},{1,17},{17,1},{2,18},{18,2},{3,19},{19,3},{4,20},{20... | collective-permute-start | bytes 3538952 | tf_op jit(solution)/shard_map/ppermute | solution.py:47
  82.3 3.2 %shard_map.124 = bf16[16,128,512]{2,1,0:T(8,128)(2,1)} custom-call(f32[16,256]{1,0:T(8,128)S(1)} %get-tuple-element.31.ids, bf16[2,512,512]{2,1,0:T(8,128)(2,1)S(1)} %get-tuple-element.32.dquery, bf16[2,512,512]{2,1,0:T(8,128)(2,1)S(1)} %get-tuple-element.33.dtail, bf16[4,512,512]{2,1,0:T(8,128)(2,1)S(1)} %get-tuple-element.34.mats), custom_call_target="tpu_custom_call" | custom-call | flops 1476395008 | bytes 8388608 | tf_op jit(solution)/shard_map/pallas_call | solution.py:353
  85.5 0.0 collective-permute-done.7
  85.5 4.4 %all-to-all-start.1 = ((bf16[16,128,512]{2,1,0:T(8,128)(2,1)}), bf16[16,128,512]{2,1,0:T(8,128)(2,1)}, u32[]{:S(2)}, u32[]{:S(2)}) async-start(bf16[16,128,512]{2,1,0:T(8,128)(2,1)} %shard_map.124), calls=%async_computation.1 | async-start | bytes 4194304 | tf_op jit(solution)/shard_map/all_to_all | solution.py:22
  89.9 0.4 add_convert_fusion
  90.3 0.1 slice_bitcast_fusion.2
  90.3 2.6 %collective-permute-start.8 = (bf16[288,512]{1,0:T(8,128)(2,1)S(1)}, bf16[288,512]{1,0:T(8,128)(2,1)S(1)}, u32[]{:S(2)}, u32[]{:S(2)}) collective-permute-start(bf16[288,512]{1,0:T(8,128)(2,1)S(1)} %get-tuple-element.46), channel_id=1, source_target_pairs={{0,32},{16,48},{32,64},{48,80},{64,96},{80,112},{96,128},{112,144}... | collective-permute-start | bytes 884744 | tf_op jit(solution)/shard_map/ppermute | solution.py:39
  93.0 3.9 %collective-permute-start.10 = (bf16[288,512]{1,0:T(8,128)(2,1)S(1)}, bf16[288,512]{1,0:T(8,128)(2,1)S(1)}, u32[]{:S(2)}, u32[]{:S(2)}) collective-permute-start(bf16[288,512]{1,0:T(8,128)(2,1)S(1)} %get-tuple-element.47), channel_id=1, source_target_pairs={{0,480},{16,496},{32,0},{48,16},{64,32},{80,48},{96,64},{112,80},{... | collective-permute-start | bytes 884744 | tf_op jit(solution)/shard_map/ppermute | solution.py:39
  96.9 1.9 collective-permute-start.9
  98.8 3.4 %collective-permute-done.8 = bf16[288,512]{1,0:T(8,128)(2,1)S(1)} collective-permute-done((bf16[288,512]{1,0:T(8,128)(2,1)S(1)}, bf16[288,512]{1,0:T(8,128)(2,1)S(1)}, u32[]{:S(2)}, u32[]{:S(2)}) %collective-permute-start.8) | collective-permute-done | bytes 294944 | tf_op jit(solution)/shard_map/ppermute | solution.py:39
  102.2 1.1 collective-permute-done.10
  103.3 7.5 %collective-permute-done.9 = bf16[288,512]{1,0:T(8,128)(2,1)S(1)} collective-permute-done((bf16[288,512]{1,0:T(8,128)(2,1)S(1)}, bf16[288,512]{1,0:T(8,128)(2,1)S(1)}, u32[]{:S(2)}, u32[]{:S(2)}) %collective-permute-start.9) | collective-permute-done | bytes 294944 | tf_op jit(solution)/shard_map/ppermute | solution.py:39
  110.8 0.2 fusion.14
  111.0 4.0 %collective-permute-start.11 = (bf16[72,512]{1,0:T(8,128)(2,1)S(1)}, bf16[72,512]{1,0:T(8,128)(2,1)S(1)}, u32[]{:S(2)}, u32[]{:S(2)}) collective-permute-start(bf16[72,512]{1,0:T(8,128)(2,1)S(1)} %pad_maximum_fusion.1), channel_id=1, source_target_pairs={{0,128},{32,160},{64,192},{96,224},{128,256},{160,288},{192,320},{... | collective-permute-start | bytes 221192 | tf_op jit(solution)/shard_map/ppermute | solution.py:43
  115.0 5.4 %collective-permute-start.12 = (bf16[72,512]{1,0:T(8,128)(2,1)S(1)}, bf16[72,512]{1,0:T(8,128)(2,1)S(1)}, u32[]{:S(2)}, u32[]{:S(2)}) collective-permute-start(bf16[72,512]{1,0:T(8,128)(2,1)S(1)} %pad_maximum_fusion.2), channel_id=1, source_target_pairs={{0,256},{32,288},{64,320},{96,352},{128,384},{160,416},{192,448},{... | collective-permute-start | bytes 221192 | tf_op jit(solution)/shard_map/ppermute | solution.py:43
  120.5 4.1 %collective-permute-start.13 = (bf16[72,512]{1,0:T(8,128)(2,1)S(1)}, bf16[72,512]{1,0:T(8,128)(2,1)S(1)}, u32[]{:S(2)}, u32[]{:S(2)}) collective-permute-start(bf16[72,512]{1,0:T(8,128)(2,1)S(1)} %pad_maximum_fusion.3), channel_id=1, source_target_pairs={{0,384},{32,416},{64,448},{96,480},{128,0},{160,32},{192,64},{224,... | collective-permute-start | bytes 221192 | tf_op jit(solution)/shard_map/ppermute | solution.py:43
  124.5 0.0 collective-permute-done.11
  124.5 4.7 %collective-permute-done.12 = bf16[72,512]{1,0:T(8,128)(2,1)S(1)} collective-permute-done((bf16[72,512]{1,0:T(8,128)(2,1)S(1)}, bf16[72,512]{1,0:T(8,128)(2,1)S(1)}, u32[]{:S(2)}, u32[]{:S(2)}) %collective-permute-start.12) | collective-permute-done | bytes 73760 | tf_op jit(solution)/shard_map/ppermute | solution.py:43
  129.2 5.6 %collective-permute-done.13 = bf16[72,512]{1,0:T(8,128)(2,1)S(1)} collective-permute-done((bf16[72,512]{1,0:T(8,128)(2,1)S(1)}, bf16[72,512]{1,0:T(8,128)(2,1)S(1)}, u32[]{:S(2)}, u32[]{:S(2)}) %collective-permute-start.13) | collective-permute-done | bytes 73760 | tf_op jit(solution)/shard_map/ppermute | solution.py:43
  134.9 0.0 all-to-all-done.1
  134.9 0.1 broadcast_in_dim.28
  135.0 0.0 copy-start.10
  135.0 25.3 %all_to_all.20.sums = bf16[16,72,512]{2,1,0:T(8,128)(2,1)S(1)} all-to-all(bf16[16,72,512]{2,1,0:T(8,128)(2,1)S(1)} %broadcast_in_dim.28), channel_id=1, replica_groups=mesh['zh'=4,'zl'=4,'core'=2,'y'=4,'x'=4] {'y','x'}, dimensions={0} | all-to-all | bytes 2359296 | tf_op jit(solution)/shard_map/all_to_all | solution.py:22
  160.4 0.1 slice.68
  160.5 1.3 fusion.8
  161.8 0.0 copy-start.2
  161.9 0.8 broadcast_in_dim.29
  162.6 6.6 %all-to-all-start.3 = ((bf16[16,24,512]{2,1,0:T(8,128)(2,1)}), bf16[16,24,512]{2,1,0:T(8,128)(2,1)S(1)}, u32[]{:S(2)}, u32[]{:S(2)}) async-start(bf16[16,24,512]{2,1,0:T(8,128)(2,1)} %broadcast_in_dim.29), calls=%async_computation.3 | async-start | bytes 786432 | tf_op jit(solution)/shard_map/all_to_all | solution.py:22
  169.3 2.6 %reduce_sum.25 = bf16[128,512]{1,0:T(8,128)(2,1)} reduce(bf16[16,128,512]{2,1,0:T(8,128)(2,1)} %all-to-all-done.1, bf16[]{:T(256)} %constant.110.clone.1), dimensions={0}, to_apply=%region_1.2 | reduce | flops 983040 | bytes 2228226 | tf_op jit(solution)/shard_map/reduce_sum | solution.py:382
  171.9 2.8 %shard_map.125 = bf16[16,128,512]{2,1,0:T(8,128)(2,1)} custom-call(bf16[64,128]{1,0:T(8,128)(2,1)S(1)} %copy-done.2, bf16[16,72,512]{2,1,0:T(8,128)(2,1)S(1)} %all_to_all.20.sums), custom_call_target="tpu_custom_call" | custom-call | flops 134217728 | bytes 8388608 | tf_op jit(solution)/shard_map/pallas_call | solution.py:395
  174.7 11.2 %all-to-all-done.3.own = bf16[16,24,512]{2,1,0:T(8,128)(2,1)S(1)} async-done(((bf16[16,24,512]{2,1,0:T(8,128)(2,1)}), bf16[16,24,512]{2,1,0:T(8,128)(2,1)S(1)}, u32[]{:S(2)}, u32[]{:S(2)}) %all-to-all-start.3) | async-done | bytes 393248 | tf_op jit(solution)/shard_map/all_to_all | solution.py:22
  185.8 9.7 %collective-permute-start.14 = (bf16[16,24,512]{2,1,0:T(8,128)(2,1)S(1)}, bf16[16,24,512]{2,1,0:T(8,128)(2,1)S(1)}, u32[]{:S(2)}, u32[]{:S(2)}) collective-permute-start(bf16[16,24,512]{2,1,0:T(8,128)(2,1)S(1)} %all-to-all-done.3.own), channel_id=1, source_target_pairs={{0,16},{16,0},{1,17},{17,1},{2,18},{18,2},{3,19},{19,3},{4,20},{20... | collective-permute-start | bytes 1179656 | tf_op jit(solution)/shard_map/ppermute | solution.py:47
  195.5 1.3 collective-permute-done.14.other
  196.8 1.4 shard_map.126
  (31 shorter events, 0.3 us)
Async XLA Ops:
  0.6 28.5 %copy-start.7 = (s32[1,32]{1,0:T(1,128)S(1)}, s32[1,32]{1,0:T(1,128)}, u32[]{:S(2)}) copy-start(s32[1,32]{1,0:T(1,128)} %fill.1) | copy-start | bytes 388
  0.6 28.5 %copy-start.5 = (s32[1024]{0:T(1024)S(1)}, s32[1024]{0:T(1024)}, u32[]{:S(2)}) copy-start(s32[1024]{0:T(1024)} %param.16) | copy-start | bytes 12292
  0.7 28.5 %copy-start.4 = (s32[1024]{0:T(1024)S(1)}, s32[1024]{0:T(1024)}, u32[]{:S(2)}) copy-start(s32[1024]{0:T(1024)} %param.15) | copy-start | bytes 12292
  0.7 28.5 %copy-start.6 = (s32[1024]{0:T(1024)S(1)}, s32[1024]{0:T(1024)}, u32[]{:S(2)}) copy-start(s32[1024]{0:T(1024)} %param.14) | copy-start | bytes 12292
  0.7 28.5 %copy-start.1 = (bf16[128,512]{1,0:T(8,128)(2,1)S(1)}, bf16[128,512]{1,0:T(8,128)(2,1)}, u32[]{:S(2)}) copy-start(bf16[128,512]{1,0:T(8,128)(2,1)} %ents.1) | copy-start | bytes 393220
  3.7 35.3 %collective-permute-start.2 = (bf16[64,512]{1,0:T(8,128)(2,1)}, bf16[64,512]{1,0:T(8,128)(2,1)S(1)}, u32[]{:S(2)}, u32[]{:S(2)}) collective-permute-start(bf16[64,512]{1,0:T(8,128)(2,1)} %get-tuple-element.28), channel_id=1, source_target_pairs={{0,384},{32,416},{64,448},{96,480},{128,0},{160,32},{192,64},{224,... | collective-permute-start | bytes 196616 | tf_op jit(solution)/shard_map/ppermute | solution.py:43
  17.0 22.0 %collective-permute-start.1 = (bf16[64,512]{1,0:T(8,128)(2,1)}, bf16[64,512]{1,0:T(8,128)(2,1)S(1)}, u32[]{:S(2)}, u32[]{:S(2)}) collective-permute-start(bf16[64,512]{1,0:T(8,128)(2,1)} %get-tuple-element.28), channel_id=1, source_target_pairs={{0,256},{32,288},{64,320},{96,352},{128,384},{160,416},{192,448},{... | collective-permute-start | bytes 196616 | tf_op jit(solution)/shard_map/ppermute | solution.py:43
  21.9 17.1 %collective-permute-start = (bf16[64,512]{1,0:T(8,128)(2,1)}, bf16[64,512]{1,0:T(8,128)(2,1)}, u32[]{:S(2)}, u32[]{:S(2)}) collective-permute-start(bf16[64,512]{1,0:T(8,128)(2,1)} %get-tuple-element.28), channel_id=1, source_target_pairs={{0,128},{32,160},{64,192},{96,224},{128,256},{160,288},{192,320},{... | collective-permute-start | bytes 196616 | tf_op jit(solution)/shard_map/ppermute | solution.py:43
  29.9 1.4 copy-start
  31.3 38.6 %all-to-all-start = ((bf16[16,144,512]{2,1,0:T(8,128)(2,1)}), bf16[16,144,512]{2,1,0:T(8,128)(2,1)S(1)}, u32[]{:S(2)}, u32[]{:S(2)}) async-start(bf16[16,144,512]{2,1,0:T(8,128)(2,1)} %copy-done), calls=%async_computation | async-start | bytes 4718592 | tf_op jit(solution)/shard_map/all_to_all | solution.py:22
  38.1 31.9 %copy-start.8 = (f32[1,64]{1,0:T(1,128)S(1)}, f32[1,64]{1,0:T(1,128)}, u32[]{:S(2)}) copy-start(f32[1,64]{1,0:T(1,128)} %get-tuple-element.25.slot_of) | copy-start | bytes 772
  39.9 20.4 %collective-permute-start.5 = (bf16[4,64,512]{2,1,0:T(8,128)(2,1)S(1)}, bf16[4,64,512]{2,1,0:T(8,128)(2,1)S(1)}, u32[]{:S(2)}, u32[]{:S(2)}) collective-permute-start(bf16[4,64,512]{2,1,0:T(8,128)(2,1)S(1)} %pad_maximum_fusion), channel_id=1, source_target_pairs={{0,480},{16,496},{32,0},{48,16},{64,32},{80,48},{96,64},{112,80},{... | collective-permute-start | bytes 786440 | tf_op jit(solution)/shard_map/ppermute | solution.py:39
  44.1 16.1 %collective-permute-start.4 = (bf16[4,64,512]{2,1,0:T(8,128)(2,1)S(1)}, bf16[4,64,512]{2,1,0:T(8,128)(2,1)S(1)}, u32[]{:S(2)}, u32[]{:S(2)}) collective-permute-start(bf16[4,64,512]{2,1,0:T(8,128)(2,1)S(1)} %pad_maximum_fusion), channel_id=1, source_target_pairs={{0,64},{16,464},{32,96},{48,496},{64,128},{80,16},{96,160},{112,48... | collective-permute-start | bytes 786440 | tf_op jit(solution)/shard_map/ppermute | solution.py:39
  46.1 14.2 %collective-permute-start.3 = (bf16[4,64,512]{2,1,0:T(8,128)(2,1)S(1)}, bf16[4,64,512]{2,1,0:T(8,128)(2,1)S(1)}, u32[]{:S(2)}, u32[]{:S(2)}) collective-permute-start(bf16[4,64,512]{2,1,0:T(8,128)(2,1)S(1)} %pad_maximum_fusion), channel_id=1, source_target_pairs={{0,32},{16,48},{32,64},{48,80},{64,96},{80,112},{96,128},{112,144}... | collective-permute-start | bytes 786440 | tf_op jit(solution)/shard_map/ppermute | solution.py:39
  60.3 11.4 %collective-permute-start.6 = (bf16[16,64,512]{2,1,0:T(8,128)(2,1)S(1)}, bf16[16,64,512]{2,1,0:T(8,128)(2,1)}, u32[]{:S(2)}, u32[]{:S(2)}) collective-permute-start(bf16[16,64,512]{2,1,0:T(8,128)(2,1)S(1)} %constant_dynamic-update-slice_fusion.half), channel_id=1, source_target_pairs={{0,16},{16,0},{1,17},{17,1},{2,18},{18,2},{3,19},{19,3},{4,20},{20... | collective-permute-start | bytes 3145736 | tf_op jit(solution)/shard_map/ppermute | solution.py:47
  70.0 1.8 copy-start.9
  77.2 8.2 %collective-permute-start.7 = (bf16[4,288,512]{2,1,0:T(8,128)(2,1)S(1)}, bf16[4,288,512]{2,1,0:T(8,128)(2,1)S(1)}, u32[]{:S(2)}, u32[]{:S(2)}) collective-permute-start(bf16[4,288,512]{2,1,0:T(8,128)(2,1)S(1)} %get-tuple-element.30), channel_id=1, source_target_pairs={{0,16},{16,0},{1,17},{17,1},{2,18},{18,2},{3,19},{19,3},{4,20},{20... | collective-permute-start | bytes 3538952 | tf_op jit(solution)/shard_map/ppermute | solution.py:47
  85.5 49.4 %all-to-all-start.1 = ((bf16[16,128,512]{2,1,0:T(8,128)(2,1)}), bf16[16,128,512]{2,1,0:T(8,128)(2,1)}, u32[]{:S(2)}, u32[]{:S(2)}) async-start(bf16[16,128,512]{2,1,0:T(8,128)(2,1)} %shard_map.124), calls=%async_computation.1 | async-start | bytes 4194304 | tf_op jit(solution)/shard_map/all_to_all | solution.py:22
  90.3 11.8 %collective-permute-start.8 = (bf16[288,512]{1,0:T(8,128)(2,1)S(1)}, bf16[288,512]{1,0:T(8,128)(2,1)S(1)}, u32[]{:S(2)}, u32[]{:S(2)}) collective-permute-start(bf16[288,512]{1,0:T(8,128)(2,1)S(1)} %get-tuple-element.46), channel_id=1, source_target_pairs={{0,32},{16,48},{32,64},{48,80},{64,96},{80,112},{96,128},{112,144}... | collective-permute-start | bytes 884744 | tf_op jit(solution)/shard_map/ppermute | solution.py:39
  93.0 10.3 %collective-permute-start.10 = (bf16[288,512]{1,0:T(8,128)(2,1)S(1)}, bf16[288,512]{1,0:T(8,128)(2,1)S(1)}, u32[]{:S(2)}, u32[]{:S(2)}) collective-permute-start(bf16[288,512]{1,0:T(8,128)(2,1)S(1)} %get-tuple-element.47), channel_id=1, source_target_pairs={{0,480},{16,496},{32,0},{48,16},{64,32},{80,48},{96,64},{112,80},{... | collective-permute-start | bytes 884744 | tf_op jit(solution)/shard_map/ppermute | solution.py:39
  96.9 13.9 %collective-permute-start.9 = (bf16[288,512]{1,0:T(8,128)(2,1)S(1)}, bf16[288,512]{1,0:T(8,128)(2,1)S(1)}, u32[]{:S(2)}, u32[]{:S(2)}) collective-permute-start(bf16[288,512]{1,0:T(8,128)(2,1)S(1)} %get-tuple-element.48), channel_id=1, source_target_pairs={{0,64},{16,464},{32,96},{48,496},{64,128},{80,16},{96,160},{112,48... | collective-permute-start | bytes 884744 | tf_op jit(solution)/shard_map/ppermute | solution.py:39
  111.0 13.5 %collective-permute-start.11 = (bf16[72,512]{1,0:T(8,128)(2,1)S(1)}, bf16[72,512]{1,0:T(8,128)(2,1)S(1)}, u32[]{:S(2)}, u32[]{:S(2)}) collective-permute-start(bf16[72,512]{1,0:T(8,128)(2,1)S(1)} %pad_maximum_fusion.1), channel_id=1, source_target_pairs={{0,128},{32,160},{64,192},{96,224},{128,256},{160,288},{192,320},{... | collective-permute-start | bytes 221192 | tf_op jit(solution)/shard_map/ppermute | solution.py:43
  115.0 14.2 %collective-permute-start.12 = (bf16[72,512]{1,0:T(8,128)(2,1)S(1)}, bf16[72,512]{1,0:T(8,128)(2,1)S(1)}, u32[]{:S(2)}, u32[]{:S(2)}) collective-permute-start(bf16[72,512]{1,0:T(8,128)(2,1)S(1)} %pad_maximum_fusion.2), channel_id=1, source_target_pairs={{0,256},{32,288},{64,320},{96,352},{128,384},{160,416},{192,448},{... | collective-permute-start | bytes 221192 | tf_op jit(solution)/shard_map/ppermute | solution.py:43
  120.5 14.4 %collective-permute-start.13 = (bf16[72,512]{1,0:T(8,128)(2,1)S(1)}, bf16[72,512]{1,0:T(8,128)(2,1)S(1)}, u32[]{:S(2)}, u32[]{:S(2)}) collective-permute-start(bf16[72,512]{1,0:T(8,128)(2,1)S(1)} %pad_maximum_fusion.3), channel_id=1, source_target_pairs={{0,384},{32,416},{64,448},{96,480},{128,0},{160,32},{192,64},{224,... | collective-permute-start | bytes 221192 | tf_op jit(solution)/shard_map/ppermute | solution.py:43
  135.0 25.5 %copy-start.10 = (bf16[16,128,512]{2,1,0:T(8,128)(2,1)S(1)}, bf16[16,128,512]{2,1,0:T(8,128)(2,1)}, u32[]{:S(2)}) copy-start(bf16[16,128,512]{2,1,0:T(8,128)(2,1)} %core.1) | copy-start | bytes 6291460
  161.8 10.1 %copy-start.2 = (bf16[64,128]{1,0:T(8,128)(2,1)S(1)}, bf16[64,128]{1,0:T(8,128)(2,1)}, u32[]{:S(2)}) copy-start(bf16[64,128]{1,0:T(8,128)(2,1)} %get-tuple-element.38.ordered) | copy-start | bytes 49156
  162.6 23.2 %all-to-all-start.3 = ((bf16[16,24,512]{2,1,0:T(8,128)(2,1)}), bf16[16,24,512]{2,1,0:T(8,128)(2,1)S(1)}, u32[]{:S(2)}, u32[]{:S(2)}) async-start(bf16[16,24,512]{2,1,0:T(8,128)(2,1)} %broadcast_in_dim.29), calls=%async_computation.3 | async-start | bytes 786432 | tf_op jit(solution)/shard_map/all_to_all | solution.py:22
  171.9 25.0 %copy-start.3 = (bf16[4,16,64]{2,1,0:T(8,128)(2,1)S(1)}, bf16[4,16,64]{2,1,0:T(8,128)(2,1)}, u32[]{:S(2)}) copy-start(bf16[4,16,64]{2,1,0:T(8,128)(2,1)} %get-tuple-element.42.order_sel) | copy-start | bytes 24580
  185.8 11.0 %collective-permute-start.14 = (bf16[16,24,512]{2,1,0:T(8,128)(2,1)S(1)}, bf16[16,24,512]{2,1,0:T(8,128)(2,1)S(1)}, u32[]{:S(2)}, u32[]{:S(2)}) collective-permute-start(bf16[16,24,512]{2,1,0:T(8,128)(2,1)S(1)} %all-to-all-done.3.own), channel_id=1, source_target_pairs={{0,16},{16,0},{1,17},{17,1},{2,18},{18,2},{3,19},{19,3},{4,20},{20... | collective-permute-start | bytes 1179656 | tf_op jit(solution)/shard_map/ppermute | solution.py:47

commit v8 on v7

--- a/solution.py
+++ b/solution.py
@@ -54,7 +54,10 @@
 NN, NT, TN = ((1,), (0,)), ((1,), (1,)), ((0,), (0,))
 
 
-def order_kernel(per_owner, mine, owners, rel_emb, core, part, ordered, order_sel, slot_of, own, wide):
+def order_kernel(
+    per_owner, mine, cap, fill, owners, rel_emb, core, head_ids, tail_ids, rel_ids, ents,
+    part, ordered, order_sel, slot_of, sent, own, wide
+):
     step = pl.program_id(0)
     rels = owners.shape[1]
     block = core.shape[0]
@@ -62,6 +65,7 @@
 
     @pl.when(step == 0)
     def _():
+        fill_send(cap, fill, head_ids, tail_ids, rel_ids, ents, sent)
         owner = owners[...].astype(F32)
         count = rels // per_owner
         has = lax.broadcasted_iota(jnp.int32, (count, rels), 0).astype(F32) == owner
@@ -90,7 +94,7 @@
         part[...] = wide[...].astype(BF16)
 
 
-def send_kernel(cap, fill, head_ids, tail_ids, rel_ids, ents, out):
+def fill_send(cap, fill, head_ids, tail_ids, rel_ids, ents, out):
     ent_rows = ents.shape[0]
     lane = lax.broadcasted_iota(jnp.int32, (1, 128), 1)
     limits = []
@@ -287,31 +291,44 @@
     slots = REPS * cap
     block = slots * feats * feats * 2
     where = jnp.stack([g, c]).astype(jnp.int32)
-    shapes = ((mine * rows_dev, feats), (rels, feats_rel), (4, rels // 4, rels), (1, rels))
+    shapes = (
+        (mine * rows_dev, feats),
+        (rels, feats_rel),
+        (4, rels // 4, rels),
+        (1, rels),
+        (REPS, ent_rows + EXTRA, feats),
+    )
+    lines = (slots * own // 128, 128)
     steps = 1
-    part, ordered, order_sel, slot_of = pl.pallas_call(
-        functools.partial(order_kernel, per_owner, mine),
+    part, ordered, order_sel, slot_of, sent = pl.pallas_call(
+        functools.partial(order_kernel, per_owner, mine, cap),
         grid=(steps,),
         out_shape=tuple(
-            jax.ShapeDtypeStruct(shape, dtype) for shape, dtype in zip(shapes, (BF16, BF16, BF16, F32))
+            jax.ShapeDtypeStruct(shape, dtype) for shape, dtype in zip(shapes, (BF16, BF16, BF16, F32, BF16))
         ),
         in_specs=[
+            smem,
             pl.BlockSpec((1, rels), lambda i: (0, 0)),
             pl.BlockSpec((rels, feats_rel), lambda i: (0, 0)),
             pl.BlockSpec((rows_dev // steps, feats_rel, feats), lambda i: (i, 0, 0)),
+            pl.BlockSpec(lines, lambda i: (0, 0)),
+            pl.BlockSpec(lines, lambda i: (0, 0)),
+            pl.BlockSpec(lines, lambda i: (0, 0)),
+            pl.BlockSpec((ent_rows, feats), lambda i: (0, 0)),
         ],
         out_specs=tuple(pl.BlockSpec(shape, lambda i, n=len(shape): (0,) * n) for shape in shapes),
         scratch_shapes=(pltpu.VMEM((16, feats_rel), BF16), pltpu.VMEM((mine * rows_dev, feats), F32)),
         cost_estimate=pl.CostEstimate(flops=16 * 2 * core.size, bytes_accessed=1 << 21, transcendentals=0),
         compiler_params=pltpu.CompilerParams(vmem_limit_bytes=60 << 20),
-    )(owner_of.reshape(1, rels), rel_emb, core)
-
-    (sent,) = call(
-        functools.partial(send_kernel, cap),
-        ((REPS, ent_rows + EXTRA, feats),),
-        1 << 20,
-        [smem] + [vmem] * 4,
-    )(fill, *(a.reshape(-1, 128) for a in (head_ids, tail_ids, rel_ids)), ents)
+    )(
+        fill,
+        owner_of.reshape(1, rels),
+        rel_emb,
+        core,
+        *(a.reshape(lines) for a in (head_ids, tail_ids, rel_ids)),
+        ents,
+    )
+
     table = exchange(sent, REP)
 
     far = jnp.stack([part] + [far_move(part, p) for p in STEPS[1:]])

time: 199 us -> 198 us (level)
    ppermute x6, starting transfers between devices: 17.7 us -> 19.8 us  [near_move(): return lax.ppermute(block, REL, pairs)]
where the time goes in v8:
time: 198 us; the launch traced here: 197 us
  starting transfers between devices  94.6 us (48%)
  waiting for transfers between devices  49 us (25%)
  blocking collectives  25.3 us (13%)
  Pallas kernels  18.4 us (9%)
  other arithmetic  4.23 us (2%)
  local copies, waits for them, and re-layouts  2.83 us (1%)
    ppermute x6, starting transfers between devices, far_move(): lax.ppermute(block, LINE, [(z, (z + 4 * step) % Z) for z in range(Z)])  38.9 us
    all_to_all x1, blocking collectives, exchange(): return lax.all_to_all(blocks, axis, split_axis=0, concat_axis=0, tiled=True)  25.3 us
    ppermute x6, waiting for transfers between devices, near_move(): return lax.ppermute(block, REL, pairs)  21.4 us
    ppermute x6, starting transfers between devices, near_move(): return lax.ppermute(block, REL, pairs)  19.8 us
    ppermute x3, starting transfers between devices, swap_core(): return lax.ppermute(block, 'core', [(0, 1), (1, 0)])  18 us
    all_to_all x3, starting transfers between devices, exchange(): return lax.all_to_all(blocks, axis, split_axis=0, concat_axis=0, tiled=True)  17.8 us
    all_to_all x3, waiting for transfers between devices, exchange(): return lax.all_to_all(blocks, axis, split_axis=0, concat_axis=0, tiled=True)  16 us
    ppermute x6, waiting for transfers between devices, far_move(): lax.ppermute(block, LINE, [(z, (z + 4 * step) % Z) for z in range(Z)])  10.3 us
  transfers between devices with their start and end apart: 18, of which 9 were waited for; matrix products, arithmetic and copies ran while one was open for 3% of the time, Pallas kernels for 4%

profile of v8, /device:TPU:1, one launch (start us, length us, event | category | flops | bytes accessed | tf_op | source)
XLA Modules:
  0.0 196.8 jit_solution(18071856298514851518)
XLA Ops:
  0.6 3.8 %shard_map.120 = (bf16[64,512]{1,0:T(8,128)(2,1)}, bf16[64,128]{1,0:T(8,128)(2,1)}, bf16[4,16,64]{2,1,0:T(8,128)(2,1)}, f32[1,64]{1,0:T(1,128)}, bf16[16,144,512]{2,1,0:T(8,128)(2,1)}) custom-call(s32[1,32]{1,0:T(1,128)} %fill.1, s32[1,64]{1,0:T(1,128)} %bitcast.55, bf16[64,128]{1,0:T(8,128)(2,1)} %rel_emb.1, bf16[16,128,512]{2,1,0:T(8,128)(2,1)} %core.1, ...), custom_call_target="tpu_custom_call" | custom-call | flops 33554432 | bytes 2097152 | tf_op jit(solution)/shard_map/pallas_call | solution.py:303
  4.5 13.3 %collective-permute-start.2 = (bf16[64,512]{1,0:T(8,128)(2,1)}, bf16[64,512]{1,0:T(8,128)(2,1)S(1)}, u32[]{:S(2)}, u32[]{:S(2)}) collective-permute-start(bf16[64,512]{1,0:T(8,128)(2,1)} %get-tuple-element.30), channel_id=1, source_target_pairs={{0,384},{32,416},{64,448},{96,480},{128,0},{160,32},{192,64},{224,... | collective-permute-start | bytes 196616 | tf_op jit(solution)/shard_map/ppermute | solution.py:43
  17.8 4.9 %collective-permute-start.1 = (bf16[64,512]{1,0:T(8,128)(2,1)}, bf16[64,512]{1,0:T(8,128)(2,1)S(1)}, u32[]{:S(2)}, u32[]{:S(2)}) collective-permute-start(bf16[64,512]{1,0:T(8,128)(2,1)} %get-tuple-element.30), channel_id=1, source_target_pairs={{0,256},{32,288},{64,320},{96,352},{128,384},{160,416},{192,448},{... | collective-permute-start | bytes 196616 | tf_op jit(solution)/shard_map/ppermute | solution.py:43
  22.7 7.3 %collective-permute-start = (bf16[64,512]{1,0:T(8,128)(2,1)}, bf16[64,512]{1,0:T(8,128)(2,1)}, u32[]{:S(2)}, u32[]{:S(2)}) collective-permute-start(bf16[64,512]{1,0:T(8,128)(2,1)} %get-tuple-element.30), channel_id=1, source_target_pairs={{0,128},{32,160},{64,192},{96,224},{128,256},{160,288},{192,320},{... | collective-permute-start | bytes 196616 | tf_op jit(solution)/shard_map/ppermute | solution.py:43
  29.9 6.8 %all-to-all-start = ((bf16[16,144,512]{2,1,0:T(8,128)(2,1)}), bf16[16,144,512]{2,1,0:T(8,128)(2,1)S(1)}, u32[]{:S(2)}, u32[]{:S(2)}) async-start(bf16[16,144,512]{2,1,0:T(8,128)(2,1)} %get-tuple-element.27), calls=%async_computation | async-start | bytes 4718592 | tf_op jit(solution)/shard_map/all_to_all | solution.py:22
  36.7 0.0 copy-start.2
  36.7 0.9 constant_dynamic-update-slice_fusion.6
  37.6 0.0 collective-permute-done.2
  37.6 0.0 collective-permute-done.1
  37.6 0.0 collective-permute-done
  37.6 0.9 pad_maximum_fusion
  38.5 6.4 %collective-permute-start.5 = (bf16[4,64,512]{2,1,0:T(8,128)(2,1)S(1)}, bf16[4,64,512]{2,1,0:T(8,128)(2,1)S(1)}, u32[]{:S(2)}, u32[]{:S(2)}) collective-permute-start(bf16[4,64,512]{2,1,0:T(8,128)(2,1)S(1)} %pad_maximum_fusion), channel_id=1, source_target_pairs={{0,480},{16,496},{32,0},{48,16},{64,32},{80,48},{96,64},{112,80},{... | collective-permute-start | bytes 786440 | tf_op jit(solution)/shard_map/ppermute | solution.py:39
  44.9 1.9 collective-permute-start.4
  46.9 3.1 %collective-permute-start.3 = (bf16[4,64,512]{2,1,0:T(8,128)(2,1)S(1)}, bf16[4,64,512]{2,1,0:T(8,128)(2,1)S(1)}, u32[]{:S(2)}, u32[]{:S(2)}) collective-permute-start(bf16[4,64,512]{2,1,0:T(8,128)(2,1)S(1)} %pad_maximum_fusion), channel_id=1, source_target_pairs={{0,32},{16,48},{32,64},{48,80},{64,96},{80,112},{96,128},{112,144}... | collective-permute-start | bytes 786440 | tf_op jit(solution)/shard_map/ppermute | solution.py:39
  50.0 0.8 constant_dynamic-update-slice_fusion.5
  50.8 9.4 %collective-permute-done.3 = bf16[4,64,512]{2,1,0:T(8,128)(2,1)S(1)} collective-permute-done((bf16[4,64,512]{2,1,0:T(8,128)(2,1)S(1)}, bf16[4,64,512]{2,1,0:T(8,128)(2,1)S(1)}, u32[]{:S(2)}, u32[]{:S(2)}) %collective-permute-start.3) | collective-permute-done | bytes 262176 | tf_op jit(solution)/shard_map/ppermute | solution.py:39
  60.2 0.0 collective-permute-done.4
  60.3 0.0 collective-permute-done.5
  60.3 3.3 %collective-permute-start.6 = (bf16[16,64,512]{2,1,0:T(8,128)(2,1)S(1)}, bf16[16,64,512]{2,1,0:T(8,128)(2,1)}, u32[]{:S(2)}, u32[]{:S(2)}) collective-permute-start(bf16[16,64,512]{2,1,0:T(8,128)(2,1)S(1)} %constant_dynamic-update-slice_fusion.half), channel_id=1, source_target_pairs={{0,16},{16,0},{1,17},{17,1},{2,18},{18,2},{3,19},{19,3},{4,20},{20... | collective-permute-start | bytes 3145736 | tf_op jit(solution)/shard_map/ppermute | solution.py:47
  63.7 0.1 pad_add_fusion.1.where
  63.8 4.8 %all-to-all-done.table = bf16[16,144,512]{2,1,0:T(8,128)(2,1)S(1)} async-done(((bf16[16,144,512]{2,1,0:T(8,128)(2,1)}), bf16[16,144,512]{2,1,0:T(8,128)(2,1)S(1)}, u32[]{:S(2)}, u32[]{:S(2)}) %all-to-all-start) | async-done | bytes 2359328 | tf_op jit(solution)/shard_map/all_to_all | solution.py:22
  68.6 0.0 copy-start.3
  68.6 0.0 copy-done.2
  68.6 1.8 shard_map.121
  70.4 0.0 collective-permute-done.6.other
  70.4 0.0 copy-done.3
  70.4 5.5 %shard_map.122 = (bf16[4,512,512]{2,1,0:T(8,128)(2,1)S(1)}, bf16[2,512,512]{2,1,0:T(8,128)(2,1)S(1)}, bf16[2,512,512]{2,1,0:T(8,128)(2,1)S(1)}, bf16[4,288,512]{2,1,0:T(8,128)(2,1)S(1)}, bf16[4,288,512]{2,1,0:T(8,128)(2,1)S(1)}) custom-call(s32[4,16]{1,0:T(4,128)S(1)} %pad_add_fusion.starts, bf16[4,512,512]{2,1,0:T(8,128)(2,1)S(1)} %get-tuple-element.28.heads, ...), custom_call_target="tpu_custom_call" | custom-call | flops 2952790016 | bytes 8388608 | tf_op jit(solution)/shard_map/pallas_call | solution.py:356
  75.9 5.0 %collective-permute-start.7 = (bf16[4,288,512]{2,1,0:T(8,128)(2,1)S(1)}, bf16[4,288,512]{2,1,0:T(8,128)(2,1)S(1)}, u32[]{:S(2)}, u32[]{:S(2)}) collective-permute-start(bf16[4,288,512]{2,1,0:T(8,128)(2,1)S(1)} %get-tuple-element.32), channel_id=1, source_target_pairs={{0,16},{16,0},{1,17},{17,1},{2,18},{18,2},{3,19},{19,3},{4,20},{20... | collective-permute-start | bytes 3538952 | tf_op jit(solution)/shard_map/ppermute | solution.py:47
  80.9 3.2 %shard_map.123 = bf16[16,128,512]{2,1,0:T(8,128)(2,1)} custom-call(f32[16,256]{1,0:T(8,128)S(1)} %get-tuple-element.33.ids, bf16[2,512,512]{2,1,0:T(8,128)(2,1)S(1)} %get-tuple-element.34.dquery, bf16[2,512,512]{2,1,0:T(8,128)(2,1)S(1)} %get-tuple-element.35.dtail, bf16[4,512,512]{2,1,0:T(8,128)(2,1)S(1)} %get-tuple-element.36.mats), custom_call_target="tpu_custom_call" | custom-call | flops 1476395008 | bytes 8388608 | tf_op jit(solution)/shard_map/pallas_call | solution.py:370
  84.1 0.0 collective-permute-done.7
  84.1 4.4 %all-to-all-start.1 = ((bf16[16,128,512]{2,1,0:T(8,128)(2,1)}), bf16[16,128,512]{2,1,0:T(8,128)(2,1)}, u32[]{:S(2)}, u32[]{:S(2)}) async-start(bf16[16,128,512]{2,1,0:T(8,128)(2,1)} %shard_map.123), calls=%async_computation.1 | async-start | bytes 4194304 | tf_op jit(solution)/shard_map/all_to_all | solution.py:22
  88.5 0.4 add_convert_fusion
  88.9 0.1 slice_bitcast_fusion.2
  89.0 2.6 %collective-permute-start.8 = (bf16[288,512]{1,0:T(8,128)(2,1)S(1)}, bf16[288,512]{1,0:T(8,128)(2,1)S(1)}, u32[]{:S(2)}, u32[]{:S(2)}) collective-permute-start(bf16[288,512]{1,0:T(8,128)(2,1)S(1)} %get-tuple-element.48), channel_id=1, source_target_pairs={{0,32},{16,48},{32,64},{48,80},{64,96},{80,112},{96,128},{112,144}... | collective-permute-start | bytes 884744 | tf_op jit(solution)/shard_map/ppermute | solution.py:39
  91.6 3.8 %collective-permute-start.10 = (bf16[288,512]{1,0:T(8,128)(2,1)S(1)}, bf16[288,512]{1,0:T(8,128)(2,1)S(1)}, u32[]{:S(2)}, u32[]{:S(2)}) collective-permute-start(bf16[288,512]{1,0:T(8,128)(2,1)S(1)} %get-tuple-element.49), channel_id=1, source_target_pairs={{0,480},{16,496},{32,0},{48,16},{64,32},{80,48},{96,64},{112,80},{... | collective-permute-start | bytes 884744 | tf_op jit(solution)/shard_map/ppermute | solution.py:39
  95.5 1.9 collective-permute-start.9
  97.4 3.4 %collective-permute-done.8 = bf16[288,512]{1,0:T(8,128)(2,1)S(1)} collective-permute-done((bf16[288,512]{1,0:T(8,128)(2,1)S(1)}, bf16[288,512]{1,0:T(8,128)(2,1)S(1)}, u32[]{:S(2)}, u32[]{:S(2)}) %collective-permute-start.8) | collective-permute-done | bytes 294944 | tf_op jit(solution)/shard_map/ppermute | solution.py:39
  100.8 1.1 collective-permute-done.10
  101.9 7.5 %collective-permute-done.9 = bf16[288,512]{1,0:T(8,128)(2,1)S(1)} collective-permute-done((bf16[288,512]{1,0:T(8,128)(2,1)S(1)}, bf16[288,512]{1,0:T(8,128)(2,1)S(1)}, u32[]{:S(2)}, u32[]{:S(2)}) %collective-permute-start.9) | collective-permute-done | bytes 294944 | tf_op jit(solution)/shard_map/ppermute | solution.py:39
  109.4 0.2 fusion.14
  109.6 4.0 %collective-permute-start.11 = (bf16[72,512]{1,0:T(8,128)(2,1)S(1)}, bf16[72,512]{1,0:T(8,128)(2,1)S(1)}, u32[]{:S(2)}, u32[]{:S(2)}) collective-permute-start(bf16[72,512]{1,0:T(8,128)(2,1)S(1)} %pad_maximum_fusion.1), channel_id=1, source_target_pairs={{0,128},{32,160},{64,192},{96,224},{128,256},{160,288},{192,320},{... | collective-permute-start | bytes 221192 | tf_op jit(solution)/shard_map/ppermute | solution.py:43
  113.7 5.4 %collective-permute-start.12 = (bf16[72,512]{1,0:T(8,128)(2,1)S(1)}, bf16[72,512]{1,0:T(8,128)(2,1)S(1)}, u32[]{:S(2)}, u32[]{:S(2)}) collective-permute-start(bf16[72,512]{1,0:T(8,128)(2,1)S(1)} %pad_maximum_fusion.2), channel_id=1, source_target_pairs={{0,256},{32,288},{64,320},{96,352},{128,384},{160,416},{192,448},{... | collective-permute-start | bytes 221192 | tf_op jit(solution)/shard_map/ppermute | solution.py:43
  119.1 4.1 %collective-permute-start.13 = (bf16[72,512]{1,0:T(8,128)(2,1)S(1)}, bf16[72,512]{1,0:T(8,128)(2,1)S(1)}, u32[]{:S(2)}, u32[]{:S(2)}) collective-permute-start(bf16[72,512]{1,0:T(8,128)(2,1)S(1)} %pad_maximum_fusion.3), channel_id=1, source_target_pairs={{0,384},{32,416},{64,448},{96,480},{128,0},{160,32},{192,64},{224,... | collective-permute-start | bytes 221192 | tf_op jit(solution)/shard_map/ppermute | solution.py:43
  123.2 0.0 collective-permute-done.11
  123.2 4.7 %collective-permute-done.12 = bf16[72,512]{1,0:T(8,128)(2,1)S(1)} collective-permute-done((bf16[72,512]{1,0:T(8,128)(2,1)S(1)}, bf16[72,512]{1,0:T(8,128)(2,1)S(1)}, u32[]{:S(2)}, u32[]{:S(2)}) %collective-permute-start.12) | collective-permute-done | bytes 73760 | tf_op jit(solution)/shard_map/ppermute | solution.py:43
  127.8 5.6 %collective-permute-done.13 = bf16[72,512]{1,0:T(8,128)(2,1)S(1)} collective-permute-done((bf16[72,512]{1,0:T(8,128)(2,1)S(1)}, bf16[72,512]{1,0:T(8,128)(2,1)S(1)}, u32[]{:S(2)}, u32[]{:S(2)}) %collective-permute-start.13) | collective-permute-done | bytes 73760 | tf_op jit(solution)/shard_map/ppermute | solution.py:43
  133.5 0.0 all-to-all-done.1
  133.5 0.1 broadcast_in_dim.28
  133.6 0.0 copy-start.4
  133.6 25.3 %all_to_all.20.sums = bf16[16,72,512]{2,1,0:T(8,128)(2,1)S(1)} all-to-all(bf16[16,72,512]{2,1,0:T(8,128)(2,1)S(1)} %broadcast_in_dim.28), channel_id=1, replica_groups=mesh['zh'=4,'zl'=4,'core'=2,'y'=4,'x'=4] {'y','x'}, dimensions={0} | all-to-all | bytes 2359296 | tf_op jit(solution)/shard_map/all_to_all | solution.py:22
  159.0 0.1 slice.68
  159.1 0.0 copy-done.4
  159.1 1.3 fusion.8
  160.4 0.0 copy-start
  160.5 0.8 broadcast_in_dim.29
  161.3 6.6 %all-to-all-start.3 = ((bf16[16,24,512]{2,1,0:T(8,128)(2,1)}), bf16[16,24,512]{2,1,0:T(8,128)(2,1)S(1)}, u32[]{:S(2)}, u32[]{:S(2)}) async-start(bf16[16,24,512]{2,1,0:T(8,128)(2,1)} %broadcast_in_dim.29), calls=%async_computation.3 | async-start | bytes 786432 | tf_op jit(solution)/shard_map/all_to_all | solution.py:22
  167.9 2.6 %reduce_sum.25 = bf16[128,512]{1,0:T(8,128)(2,1)} reduce(bf16[16,128,512]{2,1,0:T(8,128)(2,1)} %all-to-all-done.1, bf16[]{:T(256)} %constant.110.clone.1), dimensions={0}, to_apply=%region_1.2 | reduce | flops 983040 | bytes 2228226 | tf_op jit(solution)/shard_map/reduce_sum | solution.py:399
  170.5 0.0 copy-done
  170.5 2.8 %shard_map.124 = bf16[16,128,512]{2,1,0:T(8,128)(2,1)} custom-call(bf16[64,128]{1,0:T(8,128)(2,1)S(1)} %copy-done, bf16[16,72,512]{2,1,0:T(8,128)(2,1)S(1)} %all_to_all.20.sums), custom_call_target="tpu_custom_call" | custom-call | flops 134217728 | bytes 8388608 | tf_op jit(solution)/shard_map/pallas_call | solution.py:412
  173.3 11.2 %all-to-all-done.3.own = bf16[16,24,512]{2,1,0:T(8,128)(2,1)S(1)} async-done(((bf16[16,24,512]{2,1,0:T(8,128)(2,1)}), bf16[16,24,512]{2,1,0:T(8,128)(2,1)S(1)}, u32[]{:S(2)}, u32[]{:S(2)}) %all-to-all-start.3) | async-done | bytes 393248 | tf_op jit(solution)/shard_map/all_to_all | solution.py:22
  184.4 9.7 %collective-permute-start.14 = (bf16[16,24,512]{2,1,0:T(8,128)(2,1)S(1)}, bf16[16,24,512]{2,1,0:T(8,128)(2,1)S(1)}, u32[]{:S(2)}, u32[]{:S(2)}) collective-permute-start(bf16[16,24,512]{2,1,0:T(8,128)(2,1)S(1)} %all-to-all-done.3.own), channel_id=1, source_target_pairs={{0,16},{16,0},{1,17},{17,1},{2,18},{18,2},{3,19},{19,3},{4,20},{20... | collective-permute-start | bytes 1179656 | tf_op jit(solution)/shard_map/ppermute | solution.py:47
  194.1 1.3 collective-permute-done.14.other
  195.4 0.0 copy-done.1
  195.4 1.4 shard_map.125
  (18 shorter events, 0.3 us)
Async XLA Ops:
  4.5 33.1 %collective-permute-start.2 = (bf16[64,512]{1,0:T(8,128)(2,1)}, bf16[64,512]{1,0:T(8,128)(2,1)S(1)}, u32[]{:S(2)}, u32[]{:S(2)}) collective-permute-start(bf16[64,512]{1,0:T(8,128)(2,1)} %get-tuple-element.30), channel_id=1, source_target_pairs={{0,384},{32,416},{64,448},{96,480},{128,0},{160,32},{192,64},{224,... | collective-permute-start | bytes 196616 | tf_op jit(solution)/shard_map/ppermute | solution.py:43
  17.8 19.8 %collective-permute-start.1 = (bf16[64,512]{1,0:T(8,128)(2,1)}, bf16[64,512]{1,0:T(8,128)(2,1)S(1)}, u32[]{:S(2)}, u32[]{:S(2)}) collective-permute-start(bf16[64,512]{1,0:T(8,128)(2,1)} %get-tuple-element.30), channel_id=1, source_target_pairs={{0,256},{32,288},{64,320},{96,352},{128,384},{160,416},{192,448},{... | collective-permute-start | bytes 196616 | tf_op jit(solution)/shard_map/ppermute | solution.py:43
  22.7 14.9 %collective-permute-start = (bf16[64,512]{1,0:T(8,128)(2,1)}, bf16[64,512]{1,0:T(8,128)(2,1)}, u32[]{:S(2)}, u32[]{:S(2)}) collective-permute-start(bf16[64,512]{1,0:T(8,128)(2,1)} %get-tuple-element.30), channel_id=1, source_target_pairs={{0,128},{32,160},{64,192},{96,224},{128,256},{160,288},{192,320},{... | collective-permute-start | bytes 196616 | tf_op jit(solution)/shard_map/ppermute | solution.py:43
  29.9 38.7 %all-to-all-start = ((bf16[16,144,512]{2,1,0:T(8,128)(2,1)}), bf16[16,144,512]{2,1,0:T(8,128)(2,1)S(1)}, u32[]{:S(2)}, u32[]{:S(2)}) async-start(bf16[16,144,512]{2,1,0:T(8,128)(2,1)} %get-tuple-element.27), calls=%async_computation | async-start | bytes 4718592 | tf_op jit(solution)/shard_map/all_to_all | solution.py:22
  36.7 31.9 %copy-start.2 = (f32[1,64]{1,0:T(1,128)S(1)}, f32[1,64]{1,0:T(1,128)}, u32[]{:S(2)}) copy-start(f32[1,64]{1,0:T(1,128)} %get-tuple-element.26.slot_of) | copy-start | bytes 772
  38.5 21.7 %collective-permute-start.5 = (bf16[4,64,512]{2,1,0:T(8,128)(2,1)S(1)}, bf16[4,64,512]{2,1,0:T(8,128)(2,1)S(1)}, u32[]{:S(2)}, u32[]{:S(2)}) collective-permute-start(bf16[4,64,512]{2,1,0:T(8,128)(2,1)S(1)} %pad_maximum_fusion), channel_id=1, source_target_pairs={{0,480},{16,496},{32,0},{48,16},{64,32},{80,48},{96,64},{112,80},{... | collective-permute-start | bytes 786440 | tf_op jit(solution)/shard_map/ppermute | solution.py:39
  44.9 15.3 %collective-permute-start.4 = (bf16[4,64,512]{2,1,0:T(8,128)(2,1)S(1)}, bf16[4,64,512]{2,1,0:T(8,128)(2,1)S(1)}, u32[]{:S(2)}, u32[]{:S(2)}) collective-permute-start(bf16[4,64,512]{2,1,0:T(8,128)(2,1)S(1)} %pad_maximum_fusion), channel_id=1, source_target_pairs={{0,64},{16,464},{32,96},{48,496},{64,128},{80,16},{96,160},{112,48... | collective-permute-start | bytes 786440 | tf_op jit(solution)/shard_map/ppermute | solution.py:39
  46.9 13.3 %collective-permute-start.3 = (bf16[4,64,512]{2,1,0:T(8,128)(2,1)S(1)}, bf16[4,64,512]{2,1,0:T(8,128)(2,1)S(1)}, u32[]{:S(2)}, u32[]{:S(2)}) collective-permute-start(bf16[4,64,512]{2,1,0:T(8,128)(2,1)S(1)} %pad_maximum_fusion), channel_id=1, source_target_pairs={{0,32},{16,48},{32,64},{48,80},{64,96},{80,112},{96,128},{112,144}... | collective-permute-start | bytes 786440 | tf_op jit(solution)/shard_map/ppermute | solution.py:39
  60.3 10.1 %collective-permute-start.6 = (bf16[16,64,512]{2,1,0:T(8,128)(2,1)S(1)}, bf16[16,64,512]{2,1,0:T(8,128)(2,1)}, u32[]{:S(2)}, u32[]{:S(2)}) collective-permute-start(bf16[16,64,512]{2,1,0:T(8,128)(2,1)S(1)} %constant_dynamic-update-slice_fusion.half), channel_id=1, source_target_pairs={{0,16},{16,0},{1,17},{17,1},{2,18},{18,2},{3,19},{19,3},{4,20},{20... | collective-permute-start | bytes 3145736 | tf_op jit(solution)/shard_map/ppermute | solution.py:47
  68.6 1.8 copy-start.3
  75.9 8.2 %collective-permute-start.7 = (bf16[4,288,512]{2,1,0:T(8,128)(2,1)S(1)}, bf16[4,288,512]{2,1,0:T(8,128)(2,1)S(1)}, u32[]{:S(2)}, u32[]{:S(2)}) collective-permute-start(bf16[4,288,512]{2,1,0:T(8,128)(2,1)S(1)} %get-tuple-element.32), channel_id=1, source_target_pairs={{0,16},{16,0},{1,17},{17,1},{2,18},{18,2},{3,19},{19,3},{4,20},{20... | collective-permute-start | bytes 3538952 | tf_op jit(solution)/shard_map/ppermute | solution.py:47
  84.1 49.5 %all-to-all-start.1 = ((bf16[16,128,512]{2,1,0:T(8,128)(2,1)}), bf16[16,128,512]{2,1,0:T(8,128)(2,1)}, u32[]{:S(2)}, u32[]{:S(2)}) async-start(bf16[16,128,512]{2,1,0:T(8,128)(2,1)} %shard_map.123), calls=%async_computation.1 | async-start | bytes 4194304 | tf_op jit(solution)/shard_map/all_to_all | solution.py:22
  89.0 11.8 %collective-permute-start.8 = (bf16[288,512]{1,0:T(8,128)(2,1)S(1)}, bf16[288,512]{1,0:T(8,128)(2,1)S(1)}, u32[]{:S(2)}, u32[]{:S(2)}) collective-permute-start(bf16[288,512]{1,0:T(8,128)(2,1)S(1)} %get-tuple-element.48), channel_id=1, source_target_pairs={{0,32},{16,48},{32,64},{48,80},{64,96},{80,112},{96,128},{112,144}... | collective-permute-start | bytes 884744 | tf_op jit(solution)/shard_map/ppermute | solution.py:39
  91.6 10.3 %collective-permute-start.10 = (bf16[288,512]{1,0:T(8,128)(2,1)S(1)}, bf16[288,512]{1,0:T(8,128)(2,1)S(1)}, u32[]{:S(2)}, u32[]{:S(2)}) collective-permute-start(bf16[288,512]{1,0:T(8,128)(2,1)S(1)} %get-tuple-element.49), channel_id=1, source_target_pairs={{0,480},{16,496},{32,0},{48,16},{64,32},{80,48},{96,64},{112,80},{... | collective-permute-start | bytes 884744 | tf_op jit(solution)/shard_map/ppermute | solution.py:39
  95.5 13.9 %collective-permute-start.9 = (bf16[288,512]{1,0:T(8,128)(2,1)S(1)}, bf16[288,512]{1,0:T(8,128)(2,1)S(1)}, u32[]{:S(2)}, u32[]{:S(2)}) collective-permute-start(bf16[288,512]{1,0:T(8,128)(2,1)S(1)} %get-tuple-element.50), channel_id=1, source_target_pairs={{0,64},{16,464},{32,96},{48,496},{64,128},{80,16},{96,160},{112,48... | collective-permute-start | bytes 884744 | tf_op jit(solution)/shard_map/ppermute | solution.py:39
  109.6 13.5 %collective-permute-start.11 = (bf16[72,512]{1,0:T(8,128)(2,1)S(1)}, bf16[72,512]{1,0:T(8,128)(2,1)S(1)}, u32[]{:S(2)}, u32[]{:S(2)}) collective-permute-start(bf16[72,512]{1,0:T(8,128)(2,1)S(1)} %pad_maximum_fusion.1), channel_id=1, source_target_pairs={{0,128},{32,160},{64,192},{96,224},{128,256},{160,288},{192,320},{... | collective-permute-start | bytes 221192 | tf_op jit(solution)/shard_map/ppermute | solution.py:43
  113.7 14.2 %collective-permute-start.12 = (bf16[72,512]{1,0:T(8,128)(2,1)S(1)}, bf16[72,512]{1,0:T(8,128)(2,1)S(1)}, u32[]{:S(2)}, u32[]{:S(2)}) collective-permute-start(bf16[72,512]{1,0:T(8,128)(2,1)S(1)} %pad_maximum_fusion.2), channel_id=1, source_target_pairs={{0,256},{32,288},{64,320},{96,352},{128,384},{160,416},{192,448},{... | collective-permute-start | bytes 221192 | tf_op jit(solution)/shard_map/ppermute | solution.py:43
  119.1 14.4 %collective-permute-start.13 = (bf16[72,512]{1,0:T(8,128)(2,1)S(1)}, bf16[72,512]{1,0:T(8,128)(2,1)S(1)}, u32[]{:S(2)}, u32[]{:S(2)}) collective-permute-start(bf16[72,512]{1,0:T(8,128)(2,1)S(1)} %pad_maximum_fusion.3), channel_id=1, source_target_pairs={{0,384},{32,416},{64,448},{96,480},{128,0},{160,32},{192,64},{224,... | collective-permute-start | bytes 221192 | tf_op jit(solution)/shard_map/ppermute | solution.py:43
  133.6 25.5 %copy-start.4 = (bf16[16,128,512]{2,1,0:T(8,128)(2,1)S(1)}, bf16[16,128,512]{2,1,0:T(8,128)(2,1)}, u32[]{:S(2)}) copy-start(bf16[16,128,512]{2,1,0:T(8,128)(2,1)} %core.1) | copy-start | bytes 6291460
  160.4 10.1 %copy-start = (bf16[64,128]{1,0:T(8,128)(2,1)S(1)}, bf16[64,128]{1,0:T(8,128)(2,1)}, u32[]{:S(2)}) copy-start(bf16[64,128]{1,0:T(8,128)(2,1)} %get-tuple-element.40.ordered) | copy-start | bytes 49156
  161.3 23.2 %all-to-all-start.3 = ((bf16[16,24,512]{2,1,0:T(8,128)(2,1)}), bf16[16,24,512]{2,1,0:T(8,128)(2,1)S(1)}, u32[]{:S(2)}, u32[]{:S(2)}) async-start(bf16[16,24,512]{2,1,0:T(8,128)(2,1)} %broadcast_in_dim.29), calls=%async_computation.3 | async-start | bytes 786432 | tf_op jit(solution)/shard_map/all_to_all | solution.py:22
  170.5 25.0 %copy-start.1 = (bf16[4,16,64]{2,1,0:T(8,128)(2,1)S(1)}, bf16[4,16,64]{2,1,0:T(8,128)(2,1)}, u32[]{:S(2)}) copy-start(bf16[4,16,64]{2,1,0:T(8,128)(2,1)} %get-tuple-element.44.order_sel) | copy-start | bytes 24580
  184.4 11.0 %collective-permute-start.14 = (bf16[16,24,512]{2,1,0:T(8,128)(2,1)S(1)}, bf16[16,24,512]{2,1,0:T(8,128)(2,1)S(1)}, u32[]{:S(2)}, u32[]{:S(2)}) collective-permute-start(bf16[16,24,512]{2,1,0:T(8,128)(2,1)S(1)} %all-to-all-done.3.own), channel_id=1, source_target_pairs={{0,16},{16,0},{1,17},{17,1},{2,18},{18,2},{3,19},{19,3},{4,20},{20... | collective-permute-start | bytes 1179656 | tf_op jit(solution)/shard_map/ppermute | solution.py:47

commit v9 on v8

--- a/solution.py
+++ b/solution.py
@@ -13,7 +13,7 @@
 REP = ("y", "x")
 LINE = ("zh", "zl")
 STEPS = (0, 1, 2, 3)
-EXTRA = 16
+EXTRA = 8
 F32 = jnp.float32
 BF16 = jnp.bfloat16
 
@@ -104,8 +104,7 @@
             limit = jnp.where(lane >= at, fill[0, (row * 128 + at) // cap], limit)
         limits.append(limit)
     numbers = [head_ids[...], tail_ids[...], rel_ids[...], jnp.concatenate(limits, axis=0)]
-    numbers = jnp.concatenate([a.astype(F32) for a in numbers], axis=1)
-    numbers = jnp.concatenate([numbers, jnp.zeros_like(numbers)], axis=0).astype(BF16)
+    numbers = jnp.concatenate([a.astype(F32) for a in numbers], axis=1).astype(BF16)
     for s in range(out.shape[0]):
         out[s, :ent_rows, :] = ents[...]
         out[s, ent_rows:, :] = numbers

time: 198 us -> 197 us (level)
  no operation moved by 1% of the time
where the time goes in v9:
time: 197 us; the launch traced here: 196 us
  starting transfers between devices  94.7 us (48%)
  waiting for transfers between devices  47.4 us (24%)
  blocking collectives  25.6 us (13%)
  Pallas kernels  18.3 us (9%)
  other arithmetic  4.65 us (2%)
  local copies, waits for them, and re-layouts  2.88 us (1%)
    ppermute x6, starting transfers between devices, far_move(): lax.ppermute(block, LINE, [(z, (z + 4 * step) % Z) for z in range(Z)])  38.9 us
    all_to_all x1, blocking collectives, exchange(): return lax.all_to_all(blocks, axis, split_axis=0, concat_axis=0, tiled=True)  25.6 us
    ppermute x6, starting transfers between devices, near_move(): return lax.ppermute(block, REL, pairs)  20.4 us
    ppermute x6, waiting for transfers between devices, near_move(): return lax.ppermute(block, REL, pairs)  20.2 us
    ppermute x3, starting transfers between devices, swap_core(): return lax.ppermute(block, 'core', [(0, 1), (1, 0)])  18.5 us
    all_to_all x3, starting transfers between devices, exchange(): return lax.all_to_all(blocks, axis, split_axis=0, concat_axis=0, tiled=True)  16.9 us
    all_to_all x3, waiting for transfers between devices, exchange(): return lax.all_to_all(blocks, axis, split_axis=0, concat_axis=0, tiled=True)  15.2 us
    ppermute x6, waiting for transfers between devices, far_move(): lax.ppermute(block, LINE, [(z, (z + 4 * step) % Z) for z in range(Z)])  10.7 us
  transfers between devices with their start and end apart: 18, of which 9 were waited for; matrix products, arithmetic and copies ran while one was open for 3% of the time, Pallas kernels for 4%

profile of v9, /device:TPU:1, one launch (start us, length us, event | category | flops | bytes accessed | tf_op | source)
XLA Modules:
  0.0 196.1 jit_solution(12966657727246490406)
XLA Ops:
  0.6 3.8 %shard_map.120 = (bf16[64,512]{1,0:T(8,128)(2,1)}, bf16[64,128]{1,0:T(8,128)(2,1)}, bf16[4,16,64]{2,1,0:T(8,128)(2,1)}, f32[1,64]{1,0:T(1,128)}, bf16[16,136,512]{2,1,0:T(8,128)(2,1)}) custom-call(s32[1,32]{1,0:T(1,128)} %fill.1, s32[1,64]{1,0:T(1,128)} %bitcast.56, bf16[64,128]{1,0:T(8,128)(2,1)} %rel_emb.1, bf16[16,128,512]{2,1,0:T(8,128)(2,1)} %core.1, ...), custom_call_target="tpu_custom_call" | custom-call | flops 33554432 | bytes 2097152 | tf_op jit(solution)/shard_map/pallas_call | solution.py:302
  4.4 13.3 %collective-permute-start.2 = (bf16[64,512]{1,0:T(8,128)(2,1)}, bf16[64,512]{1,0:T(8,128)(2,1)S(1)}, u32[]{:S(2)}, u32[]{:S(2)}) collective-permute-start(bf16[64,512]{1,0:T(8,128)(2,1)} %get-tuple-element.30), channel_id=1, source_target_pairs={{0,384},{32,416},{64,448},{96,480},{128,0},{160,32},{192,64},{224,... | collective-permute-start | bytes 196616 | tf_op jit(solution)/shard_map/ppermute | solution.py:43
  17.7 4.9 %collective-permute-start.1 = (bf16[64,512]{1,0:T(8,128)(2,1)}, bf16[64,512]{1,0:T(8,128)(2,1)S(1)}, u32[]{:S(2)}, u32[]{:S(2)}) collective-permute-start(bf16[64,512]{1,0:T(8,128)(2,1)} %get-tuple-element.30), channel_id=1, source_target_pairs={{0,256},{32,288},{64,320},{96,352},{128,384},{160,416},{192,448},{... | collective-permute-start | bytes 196616 | tf_op jit(solution)/shard_map/ppermute | solution.py:43
  22.6 7.3 %collective-permute-start = (bf16[64,512]{1,0:T(8,128)(2,1)}, bf16[64,512]{1,0:T(8,128)(2,1)S(1)}, u32[]{:S(2)}, u32[]{:S(2)}) collective-permute-start(bf16[64,512]{1,0:T(8,128)(2,1)} %get-tuple-element.30), channel_id=1, source_target_pairs={{0,128},{32,160},{64,192},{96,224},{128,256},{160,288},{192,320},{... | collective-permute-start | bytes 196616 | tf_op jit(solution)/shard_map/ppermute | solution.py:43
  29.9 0.0 copy-start.7
  29.9 6.9 %all-to-all-start = ((bf16[16,136,512]{2,1,0:T(8,128)(2,1)}), bf16[16,136,512]{2,1,0:T(8,128)(2,1)S(1)}, u32[]{:S(2)}, u32[]{:S(2)}) async-start(bf16[16,136,512]{2,1,0:T(8,128)(2,1)} %get-tuple-element.27), calls=%async_computation | async-start | bytes 4456448 | tf_op jit(solution)/shard_map/all_to_all | solution.py:22
  36.8 0.0 collective-permute-done.2
  36.9 0.0 copy-start.5
  36.9 0.0 collective-permute-done.1
  36.9 0.0 copy-start.6
  36.9 0.0 collective-permute-done
  37.0 6.9 %collective-permute-start.5 = (bf16[4,64,512]{2,1,0:T(8,128)(2,1)S(1)}, bf16[4,64,512]{2,1,0:T(8,128)(2,1)S(1)}, u32[]{:S(2)}, u32[]{:S(2)}) collective-permute-start(bf16[4,64,512]{2,1,0:T(8,128)(2,1)S(1)} %pad_maximum_fusion), channel_id=1, source_target_pairs={{0,480},{16,496},{32,0},{48,16},{64,32},{80,48},{96,64},{112,80},{... | collective-permute-start | bytes 786440 | tf_op jit(solution)/shard_map/ppermute | solution.py:39
  43.9 1.9 collective-permute-start.4
  45.8 3.1 %collective-permute-start.3 = (bf16[4,64,512]{2,1,0:T(8,128)(2,1)S(1)}, bf16[4,64,512]{2,1,0:T(8,128)(2,1)S(1)}, u32[]{:S(2)}, u32[]{:S(2)}) collective-permute-start(bf16[4,64,512]{2,1,0:T(8,128)(2,1)S(1)} %pad_maximum_fusion), channel_id=1, source_target_pairs={{0,32},{16,48},{32,64},{48,80},{64,96},{80,112},{96,128},{112,144}... | collective-permute-start | bytes 786440 | tf_op jit(solution)/shard_map/ppermute | solution.py:39
  48.9 0.0 copy-done.5
  48.9 0.0 copy-done.6
  49.0 0.0 copy-start.3
  49.0 0.9 constant_dynamic-update-slice_fusion.4
  49.9 0.8 constant_dynamic-update-slice_fusion.3
  50.7 8.2 %collective-permute-done.3 = bf16[4,64,512]{2,1,0:T(8,128)(2,1)S(1)} collective-permute-done((bf16[4,64,512]{2,1,0:T(8,128)(2,1)S(1)}, bf16[4,64,512]{2,1,0:T(8,128)(2,1)S(1)}, u32[]{:S(2)}, u32[]{:S(2)}) %collective-permute-start.3) | collective-permute-done | bytes 262176 | tf_op jit(solution)/shard_map/ppermute | solution.py:39
  58.9 0.0 collective-permute-done.4
  59.0 0.0 collective-permute-done.5
  59.0 3.5 %collective-permute-start.6 = (bf16[16,64,512]{2,1,0:T(8,128)(2,1)S(1)}, bf16[16,64,512]{2,1,0:T(8,128)(2,1)}, u32[]{:S(2)}, u32[]{:S(2)}) collective-permute-start(bf16[16,64,512]{2,1,0:T(8,128)(2,1)S(1)} %constant_dynamic-update-slice_fusion.half), channel_id=1, source_target_pairs={{0,16},{16,0},{1,17},{17,1},{2,18},{18,2},{3,19},{19,3},{4,20},{20... | collective-permute-start | bytes 3145736 | tf_op jit(solution)/shard_map/ppermute | solution.py:47
  62.5 0.1 pad_add_fusion.1.where
  62.6 4.0 %all-to-all-done.table = bf16[16,136,512]{2,1,0:T(8,128)(2,1)S(1)} async-done(((bf16[16,136,512]{2,1,0:T(8,128)(2,1)}), bf16[16,136,512]{2,1,0:T(8,128)(2,1)S(1)}, u32[]{:S(2)}, u32[]{:S(2)}) %all-to-all-start) | async-done | bytes 2228256 | tf_op jit(solution)/shard_map/all_to_all | solution.py:22
  66.7 1.7 shard_map.121
  68.4 0.0 collective-permute-done.6.other
  68.4 0.0 copy-done.3
  68.4 5.5 %shard_map.122 = (bf16[4,512,512]{2,1,0:T(8,128)(2,1)S(1)}, bf16[2,512,512]{2,1,0:T(8,128)(2,1)S(1)}, bf16[2,512,512]{2,1,0:T(8,128)(2,1)S(1)}, bf16[4,288,512]{2,1,0:T(8,128)(2,1)S(1)}, bf16[4,288,512]{2,1,0:T(8,128)(2,1)S(1)}) custom-call(s32[4,16]{1,0:T(4,128)S(1)} %pad_add_fusion.starts, bf16[4,512,512]{2,1,0:T(8,128)(2,1)S(1)} %get-tuple-element.28.heads, ...), custom_call_target="tpu_custom_call" | custom-call | flops 2952790016 | bytes 8388608 | tf_op jit(solution)/shard_map/pallas_call | solution.py:355
  73.9 5.4 %collective-permute-start.7 = (bf16[4,288,512]{2,1,0:T(8,128)(2,1)S(1)}, bf16[4,288,512]{2,1,0:T(8,128)(2,1)}, u32[]{:S(2)}, u32[]{:S(2)}) collective-permute-start(bf16[4,288,512]{2,1,0:T(8,128)(2,1)S(1)} %get-tuple-element.32), channel_id=1, source_target_pairs={{0,16},{16,0},{1,17},{17,1},{2,18},{18,2},{3,19},{19,3},{4,20},{20... | collective-permute-start | bytes 3538952 | tf_op jit(solution)/shard_map/ppermute | solution.py:47
  79.3 3.2 %shard_map.123 = bf16[16,128,512]{2,1,0:T(8,128)(2,1)} custom-call(f32[16,256]{1,0:T(8,128)S(1)} %get-tuple-element.33.ids, bf16[2,512,512]{2,1,0:T(8,128)(2,1)S(1)} %get-tuple-element.34.dquery, bf16[2,512,512]{2,1,0:T(8,128)(2,1)S(1)} %get-tuple-element.35.dtail, bf16[4,512,512]{2,1,0:T(8,128)(2,1)S(1)} %get-tuple-element.36.mats), custom_call_target="tpu_custom_call" | custom-call | flops 1476395008 | bytes 8388608 | tf_op jit(solution)/shard_map/pallas_call | solution.py:369
  82.5 0.0 collective-permute-done.7
  82.5 4.4 %all-to-all-start.1 = ((bf16[16,128,512]{2,1,0:T(8,128)(2,1)}), bf16[16,128,512]{2,1,0:T(8,128)(2,1)}, u32[]{:S(2)}, u32[]{:S(2)}) async-start(bf16[16,128,512]{2,1,0:T(8,128)(2,1)} %shard_map.123), calls=%async_computation.1 | async-start | bytes 4194304 | tf_op jit(solution)/shard_map/all_to_all | solution.py:22
  86.9 1.7 add_convert_fusion
  88.6 0.1 slice_bitcast_fusion.2
  88.7 2.6 %collective-permute-start.8 = (bf16[288,512]{1,0:T(8,128)(2,1)S(1)}, bf16[288,512]{1,0:T(8,128)(2,1)S(1)}, u32[]{:S(2)}, u32[]{:S(2)}) collective-permute-start(bf16[288,512]{1,0:T(8,128)(2,1)S(1)} %get-tuple-element.48), channel_id=1, source_target_pairs={{0,32},{16,48},{32,64},{48,80},{64,96},{80,112},{96,128},{112,144}... | collective-permute-start | bytes 884744 | tf_op jit(solution)/shard_map/ppermute | solution.py:39
  91.3 3.8 %collective-permute-start.10 = (bf16[288,512]{1,0:T(8,128)(2,1)S(1)}, bf16[288,512]{1,0:T(8,128)(2,1)S(1)}, u32[]{:S(2)}, u32[]{:S(2)}) collective-permute-start(bf16[288,512]{1,0:T(8,128)(2,1)S(1)} %get-tuple-element.49), channel_id=1, source_target_pairs={{0,480},{16,496},{32,0},{48,16},{64,32},{80,48},{96,64},{112,80},{... | collective-permute-start | bytes 884744 | tf_op jit(solution)/shard_map/ppermute | solution.py:39
  95.2 1.9 collective-permute-start.9
  97.1 3.3 %collective-permute-done.8 = bf16[288,512]{1,0:T(8,128)(2,1)S(1)} collective-permute-done((bf16[288,512]{1,0:T(8,128)(2,1)S(1)}, bf16[288,512]{1,0:T(8,128)(2,1)S(1)}, u32[]{:S(2)}, u32[]{:S(2)}) %collective-permute-start.8) | collective-permute-done | bytes 294944 | tf_op jit(solution)/shard_map/ppermute | solution.py:39
  100.4 1.2 collective-permute-done.10
  101.6 7.5 %collective-permute-done.9 = bf16[288,512]{1,0:T(8,128)(2,1)S(1)} collective-permute-done((bf16[288,512]{1,0:T(8,128)(2,1)S(1)}, bf16[288,512]{1,0:T(8,128)(2,1)S(1)}, u32[]{:S(2)}, u32[]{:S(2)}) %collective-permute-start.9) | collective-permute-done | bytes 294944 | tf_op jit(solution)/shard_map/ppermute | solution.py:39
  109.1 0.2 fusion.14
  109.3 4.0 %collective-permute-start.11 = (bf16[72,512]{1,0:T(8,128)(2,1)S(1)}, bf16[72,512]{1,0:T(8,128)(2,1)S(1)}, u32[]{:S(2)}, u32[]{:S(2)}) collective-permute-start(bf16[72,512]{1,0:T(8,128)(2,1)S(1)} %pad_maximum_fusion.1), channel_id=1, source_target_pairs={{0,128},{32,160},{64,192},{96,224},{128,256},{160,288},{192,320},{... | collective-permute-start | bytes 221192 | tf_op jit(solution)/shard_map/ppermute | solution.py:43
  113.4 5.4 %collective-permute-start.12 = (bf16[72,512]{1,0:T(8,128)(2,1)S(1)}, bf16[72,512]{1,0:T(8,128)(2,1)S(1)}, u32[]{:S(2)}, u32[]{:S(2)}) collective-permute-start(bf16[72,512]{1,0:T(8,128)(2,1)S(1)} %pad_maximum_fusion.2), channel_id=1, source_target_pairs={{0,256},{32,288},{64,320},{96,352},{128,384},{160,416},{192,448},{... | collective-permute-start | bytes 221192 | tf_op jit(solution)/shard_map/ppermute | solution.py:43
  118.8 4.1 %collective-permute-start.13 = (bf16[72,512]{1,0:T(8,128)(2,1)S(1)}, bf16[72,512]{1,0:T(8,128)(2,1)S(1)}, u32[]{:S(2)}, u32[]{:S(2)}) collective-permute-start(bf16[72,512]{1,0:T(8,128)(2,1)S(1)} %pad_maximum_fusion.3), channel_id=1, source_target_pairs={{0,384},{32,416},{64,448},{96,480},{128,0},{160,32},{192,64},{224,... | collective-permute-start | bytes 221192 | tf_op jit(solution)/shard_map/ppermute | solution.py:43
  122.9 0.0 collective-permute-done.11
  122.9 4.7 %collective-permute-done.12 = bf16[72,512]{1,0:T(8,128)(2,1)S(1)} collective-permute-done((bf16[72,512]{1,0:T(8,128)(2,1)S(1)}, bf16[72,512]{1,0:T(8,128)(2,1)S(1)}, u32[]{:S(2)}, u32[]{:S(2)}) %collective-permute-start.12) | collective-permute-done | bytes 73760 | tf_op jit(solution)/shard_map/ppermute | solution.py:43
  127.6 6.0 %collective-permute-done.13 = bf16[72,512]{1,0:T(8,128)(2,1)S(1)} collective-permute-done((bf16[72,512]{1,0:T(8,128)(2,1)S(1)}, bf16[72,512]{1,0:T(8,128)(2,1)S(1)}, u32[]{:S(2)}, u32[]{:S(2)}) %collective-permute-start.13) | collective-permute-done | bytes 73760 | tf_op jit(solution)/shard_map/ppermute | solution.py:43
  133.6 0.0 all-to-all-done.1
  133.6 0.1 broadcast_in_dim.28
  133.7 0.0 copy-start.4
  133.7 25.6 %all_to_all.20.sums = bf16[16,72,512]{2,1,0:T(8,128)(2,1)S(1)} all-to-all(bf16[16,72,512]{2,1,0:T(8,128)(2,1)S(1)} %broadcast_in_dim.28), channel_id=1, replica_groups=mesh['zh'=4,'zl'=4,'core'=2,'y'=4,'x'=4] {'y','x'}, dimensions={0} | all-to-all | bytes 2359296 | tf_op jit(solution)/shard_map/all_to_all | solution.py:22
  159.3 0.1 slice.68
  159.4 1.3 fusion.8
  160.8 0.0 copy-start
  160.8 0.8 broadcast_in_dim.29
  161.6 5.5 %all-to-all-start.3 = ((bf16[16,24,512]{2,1,0:T(8,128)(2,1)}), bf16[16,24,512]{2,1,0:T(8,128)(2,1)S(1)}, u32[]{:S(2)}, u32[]{:S(2)}) async-start(bf16[16,24,512]{2,1,0:T(8,128)(2,1)} %broadcast_in_dim.29), calls=%async_computation.3 | async-start | bytes 786432 | tf_op jit(solution)/shard_map/all_to_all | solution.py:22
  167.1 2.6 %reduce_sum.25 = bf16[128,512]{1,0:T(8,128)(2,1)} reduce(bf16[16,128,512]{2,1,0:T(8,128)(2,1)} %all-to-all-done.1, bf16[]{:T(256)} %constant.110.clone.1), dimensions={0}, to_apply=%region_1.2 | reduce | flops 983040 | bytes 2228226 | tf_op jit(solution)/shard_map/reduce_sum | solution.py:398
  169.7 0.0 copy-done
  169.7 2.8 %shard_map.124 = bf16[16,128,512]{2,1,0:T(8,128)(2,1)} custom-call(bf16[64,128]{1,0:T(8,128)(2,1)S(1)} %copy-done, bf16[16,72,512]{2,1,0:T(8,128)(2,1)S(1)} %all_to_all.20.sums), custom_call_target="tpu_custom_call" | custom-call | flops 134217728 | bytes 8388608 | tf_op jit(solution)/shard_map/pallas_call | solution.py:411
  172.5 11.2 %all-to-all-done.3.own = bf16[16,24,512]{2,1,0:T(8,128)(2,1)S(1)} async-done(((bf16[16,24,512]{2,1,0:T(8,128)(2,1)}), bf16[16,24,512]{2,1,0:T(8,128)(2,1)S(1)}, u32[]{:S(2)}, u32[]{:S(2)}) %all-to-all-start.3) | async-done | bytes 393248 | tf_op jit(solution)/shard_map/all_to_all | solution.py:22
  183.7 9.7 %collective-permute-start.14 = (bf16[16,24,512]{2,1,0:T(8,128)(2,1)S(1)}, bf16[16,24,512]{2,1,0:T(8,128)(2,1)S(1)}, u32[]{:S(2)}, u32[]{:S(2)}) collective-permute-start(bf16[16,24,512]{2,1,0:T(8,128)(2,1)S(1)} %all-to-all-done.3.own), channel_id=1, source_target_pairs={{0,16},{16,0},{1,17},{17,1},{2,18},{18,2},{3,19},{19,3},{4,20},{20... | collective-permute-start | bytes 1179656 | tf_op jit(solution)/shard_map/ppermute | solution.py:47
  193.4 1.3 collective-permute-done.14.other
  194.7 1.4 shard_map.125
  (24 shorter events, 0.3 us)
Async XLA Ops:
  4.4 32.4 %collective-permute-start.2 = (bf16[64,512]{1,0:T(8,128)(2,1)}, bf16[64,512]{1,0:T(8,128)(2,1)S(1)}, u32[]{:S(2)}, u32[]{:S(2)}) collective-permute-start(bf16[64,512]{1,0:T(8,128)(2,1)} %get-tuple-element.30), channel_id=1, source_target_pairs={{0,384},{32,416},{64,448},{96,480},{128,0},{160,32},{192,64},{224,... | collective-permute-start | bytes 196616 | tf_op jit(solution)/shard_map/ppermute | solution.py:43
  17.7 19.2 %collective-permute-start.1 = (bf16[64,512]{1,0:T(8,128)(2,1)}, bf16[64,512]{1,0:T(8,128)(2,1)S(1)}, u32[]{:S(2)}, u32[]{:S(2)}) collective-permute-start(bf16[64,512]{1,0:T(8,128)(2,1)} %get-tuple-element.30), channel_id=1, source_target_pairs={{0,256},{32,288},{64,320},{96,352},{128,384},{160,416},{192,448},{... | collective-permute-start | bytes 196616 | tf_op jit(solution)/shard_map/ppermute | solution.py:43
  22.6 14.3 %collective-permute-start = (bf16[64,512]{1,0:T(8,128)(2,1)}, bf16[64,512]{1,0:T(8,128)(2,1)S(1)}, u32[]{:S(2)}, u32[]{:S(2)}) collective-permute-start(bf16[64,512]{1,0:T(8,128)(2,1)} %get-tuple-element.30), channel_id=1, source_target_pairs={{0,128},{32,160},{64,192},{96,224},{128,256},{160,288},{192,320},{... | collective-permute-start | bytes 196616 | tf_op jit(solution)/shard_map/ppermute | solution.py:43
  29.9 6.9 %copy-start.7 = (bf16[64,512]{1,0:T(8,128)(2,1)S(1)}, bf16[64,512]{1,0:T(8,128)(2,1)}, u32[]{:S(2)}) copy-start(bf16[64,512]{1,0:T(8,128)(2,1)} %get-tuple-element.30) | copy-start | bytes 196612
  29.9 36.8 %all-to-all-start = ((bf16[16,136,512]{2,1,0:T(8,128)(2,1)}), bf16[16,136,512]{2,1,0:T(8,128)(2,1)S(1)}, u32[]{:S(2)}, u32[]{:S(2)}) async-start(bf16[16,136,512]{2,1,0:T(8,128)(2,1)} %get-tuple-element.27), calls=%async_computation | async-start | bytes 4456448 | tf_op jit(solution)/shard_map/all_to_all | solution.py:22
  36.8 29.9 %copy-start.2 = (f32[1,64]{1,0:T(1,128)S(1)}, f32[1,64]{1,0:T(1,128)}, u32[]{:S(2)}) copy-start(f32[1,64]{1,0:T(1,128)} %get-tuple-element.26.slot_of) | copy-start | bytes 772
  36.9 12.1 %copy-start.5 = (bf16[64,512]{1,0:T(8,128)(2,1)}, bf16[64,512]{1,0:T(8,128)(2,1)S(1)}, u32[]{:S(2)}) copy-start(bf16[64,512]{1,0:T(8,128)(2,1)S(1)} %collective-permute-done.2) | copy-start | bytes 196612
  36.9 12.1 %copy-start.6 = (bf16[64,512]{1,0:T(8,128)(2,1)}, bf16[64,512]{1,0:T(8,128)(2,1)S(1)}, u32[]{:S(2)}) copy-start(bf16[64,512]{1,0:T(8,128)(2,1)S(1)} %collective-permute-done.1) | copy-start | bytes 196612
  37.0 22.0 %collective-permute-start.5 = (bf16[4,64,512]{2,1,0:T(8,128)(2,1)S(1)}, bf16[4,64,512]{2,1,0:T(8,128)(2,1)S(1)}, u32[]{:S(2)}, u32[]{:S(2)}) collective-permute-start(bf16[4,64,512]{2,1,0:T(8,128)(2,1)S(1)} %pad_maximum_fusion), channel_id=1, source_target_pairs={{0,480},{16,496},{32,0},{48,16},{64,32},{80,48},{96,64},{112,80},{... | collective-permute-start | bytes 786440 | tf_op jit(solution)/shard_map/ppermute | solution.py:39
  43.9 15.0 %collective-permute-start.4 = (bf16[4,64,512]{2,1,0:T(8,128)(2,1)S(1)}, bf16[4,64,512]{2,1,0:T(8,128)(2,1)S(1)}, u32[]{:S(2)}, u32[]{:S(2)}) collective-permute-start(bf16[4,64,512]{2,1,0:T(8,128)(2,1)S(1)} %pad_maximum_fusion), channel_id=1, source_target_pairs={{0,64},{16,464},{32,96},{48,496},{64,128},{80,16},{96,160},{112,48... | collective-permute-start | bytes 786440 | tf_op jit(solution)/shard_map/ppermute | solution.py:39
  45.8 13.1 %collective-permute-start.3 = (bf16[4,64,512]{2,1,0:T(8,128)(2,1)S(1)}, bf16[4,64,512]{2,1,0:T(8,128)(2,1)S(1)}, u32[]{:S(2)}, u32[]{:S(2)}) collective-permute-start(bf16[4,64,512]{2,1,0:T(8,128)(2,1)S(1)} %pad_maximum_fusion), channel_id=1, source_target_pairs={{0,32},{16,48},{32,64},{48,80},{64,96},{80,112},{96,128},{112,144}... | collective-permute-start | bytes 786440 | tf_op jit(solution)/shard_map/ppermute | solution.py:39
  49.0 19.5 %copy-start.3 = (bf16[256,512]{1,0:T(8,128)(2,1)S(1)}, bf16[256,512]{1,0:T(8,128)(2,1)}, u32[]{:S(2)}) copy-start(bf16[256,512]{1,0:T(8,128)(2,1)} %pool.1) | copy-start | bytes 786436
  59.0 9.4 %collective-permute-start.6 = (bf16[16,64,512]{2,1,0:T(8,128)(2,1)S(1)}, bf16[16,64,512]{2,1,0:T(8,128)(2,1)}, u32[]{:S(2)}, u32[]{:S(2)}) collective-permute-start(bf16[16,64,512]{2,1,0:T(8,128)(2,1)S(1)} %constant_dynamic-update-slice_fusion.half), channel_id=1, source_target_pairs={{0,16},{16,0},{1,17},{17,1},{2,18},{18,2},{3,19},{19,3},{4,20},{20... | collective-permute-start | bytes 3145736 | tf_op jit(solution)/shard_map/ppermute | solution.py:47
  73.9 8.6 %collective-permute-start.7 = (bf16[4,288,512]{2,1,0:T(8,128)(2,1)S(1)}, bf16[4,288,512]{2,1,0:T(8,128)(2,1)}, u32[]{:S(2)}, u32[]{:S(2)}) collective-permute-start(bf16[4,288,512]{2,1,0:T(8,128)(2,1)S(1)} %get-tuple-element.32), channel_id=1, source_target_pairs={{0,16},{16,0},{1,17},{17,1},{2,18},{18,2},{3,19},{19,3},{4,20},{20... | collective-permute-start | bytes 3538952 | tf_op jit(solution)/shard_map/ppermute | solution.py:47
  82.5 51.1 %all-to-all-start.1 = ((bf16[16,128,512]{2,1,0:T(8,128)(2,1)}), bf16[16,128,512]{2,1,0:T(8,128)(2,1)}, u32[]{:S(2)}, u32[]{:S(2)}) async-start(bf16[16,128,512]{2,1,0:T(8,128)(2,1)} %shard_map.123), calls=%async_computation.1 | async-start | bytes 4194304 | tf_op jit(solution)/shard_map/all_to_all | solution.py:22
  88.7 11.7 %collective-permute-start.8 = (bf16[288,512]{1,0:T(8,128)(2,1)S(1)}, bf16[288,512]{1,0:T(8,128)(2,1)S(1)}, u32[]{:S(2)}, u32[]{:S(2)}) collective-permute-start(bf16[288,512]{1,0:T(8,128)(2,1)S(1)} %get-tuple-element.48), channel_id=1, source_target_pairs={{0,32},{16,48},{32,64},{48,80},{64,96},{80,112},{96,128},{112,144}... | collective-permute-start | bytes 884744 | tf_op jit(solution)/shard_map/ppermute | solution.py:39
  91.3 10.3 %collective-permute-start.10 = (bf16[288,512]{1,0:T(8,128)(2,1)S(1)}, bf16[288,512]{1,0:T(8,128)(2,1)S(1)}, u32[]{:S(2)}, u32[]{:S(2)}) collective-permute-start(bf16[288,512]{1,0:T(8,128)(2,1)S(1)} %get-tuple-element.49), channel_id=1, source_target_pairs={{0,480},{16,496},{32,0},{48,16},{64,32},{80,48},{96,64},{112,80},{... | collective-permute-start | bytes 884744 | tf_op jit(solution)/shard_map/ppermute | solution.py:39
  95.2 13.9 %collective-permute-start.9 = (bf16[288,512]{1,0:T(8,128)(2,1)S(1)}, bf16[288,512]{1,0:T(8,128)(2,1)S(1)}, u32[]{:S(2)}, u32[]{:S(2)}) collective-permute-start(bf16[288,512]{1,0:T(8,128)(2,1)S(1)} %get-tuple-element.50), channel_id=1, source_target_pairs={{0,64},{16,464},{32,96},{48,496},{64,128},{80,16},{96,160},{112,48... | collective-permute-start | bytes 884744 | tf_op jit(solution)/shard_map/ppermute | solution.py:39
  109.3 13.5 %collective-permute-start.11 = (bf16[72,512]{1,0:T(8,128)(2,1)S(1)}, bf16[72,512]{1,0:T(8,128)(2,1)S(1)}, u32[]{:S(2)}, u32[]{:S(2)}) collective-permute-start(bf16[72,512]{1,0:T(8,128)(2,1)S(1)} %pad_maximum_fusion.1), channel_id=1, source_target_pairs={{0,128},{32,160},{64,192},{96,224},{128,256},{160,288},{192,320},{... | collective-permute-start | bytes 221192 | tf_op jit(solution)/shard_map/ppermute | solution.py:43
  113.4 14.2 %collective-permute-start.12 = (bf16[72,512]{1,0:T(8,128)(2,1)S(1)}, bf16[72,512]{1,0:T(8,128)(2,1)S(1)}, u32[]{:S(2)}, u32[]{:S(2)}) collective-permute-start(bf16[72,512]{1,0:T(8,128)(2,1)S(1)} %pad_maximum_fusion.2), channel_id=1, source_target_pairs={{0,256},{32,288},{64,320},{96,352},{128,384},{160,416},{192,448},{... | collective-permute-start | bytes 221192 | tf_op jit(solution)/shard_map/ppermute | solution.py:43
  118.8 14.8 %collective-permute-start.13 = (bf16[72,512]{1,0:T(8,128)(2,1)S(1)}, bf16[72,512]{1,0:T(8,128)(2,1)S(1)}, u32[]{:S(2)}, u32[]{:S(2)}) collective-permute-start(bf16[72,512]{1,0:T(8,128)(2,1)S(1)} %pad_maximum_fusion.3), channel_id=1, source_target_pairs={{0,384},{32,416},{64,448},{96,480},{128,0},{160,32},{192,64},{224,... | collective-permute-start | bytes 221192 | tf_op jit(solution)/shard_map/ppermute | solution.py:43
  133.7 25.7 %copy-start.4 = (bf16[16,128,512]{2,1,0:T(8,128)(2,1)S(1)}, bf16[16,128,512]{2,1,0:T(8,128)(2,1)}, u32[]{:S(2)}) copy-start(bf16[16,128,512]{2,1,0:T(8,128)(2,1)} %core.1) | copy-start | bytes 6291460
  160.8 9.0 %copy-start = (bf16[64,128]{1,0:T(8,128)(2,1)S(1)}, bf16[64,128]{1,0:T(8,128)(2,1)}, u32[]{:S(2)}) copy-start(bf16[64,128]{1,0:T(8,128)(2,1)} %get-tuple-element.40.ordered) | copy-start | bytes 49156
  161.6 22.1 %all-to-all-start.3 = ((bf16[16,24,512]{2,1,0:T(8,128)(2,1)}), bf16[16,24,512]{2,1,0:T(8,128)(2,1)S(1)}, u32[]{:S(2)}, u32[]{:S(2)}) async-start(bf16[16,24,512]{2,1,0:T(8,128)(2,1)} %broadcast_in_dim.29), calls=%async_computation.3 | async-start | bytes 786432 | tf_op jit(solution)/shard_map/all_to_all | solution.py:22
  169.7 25.0 %copy-start.1 = (bf16[4,16,64]{2,1,0:T(8,128)(2,1)S(1)}, bf16[4,16,64]{2,1,0:T(8,128)(2,1)}, u32[]{:S(2)}) copy-start(bf16[4,16,64]{2,1,0:T(8,128)(2,1)} %get-tuple-element.44.order_sel) | copy-start | bytes 24580
  183.7 11.0 %collective-permute-start.14 = (bf16[16,24,512]{2,1,0:T(8,128)(2,1)S(1)}, bf16[16,24,512]{2,1,0:T(8,128)(2,1)S(1)}, u32[]{:S(2)}, u32[]{:S(2)}) collective-permute-start(bf16[16,24,512]{2,1,0:T(8,128)(2,1)S(1)} %all-to-all-done.3.own), channel_id=1, source_target_pairs={{0,16},{16,0},{1,17},{17,1},{2,18},{18,2},{3,19},{19,3},{4,20},{20... | collective-permute-start | bytes 1179656 | tf_op jit(solution)/shard_map/ppermute | solution.py:47

commit v10 on v8

--- a/solution.py
+++ b/solution.py
@@ -375,7 +375,7 @@
         (pltpu.VMEM((mine, slots, feats), BF16),),
     )(ids, dquery, dtail, mats)
 
-    given, sent = lax.optimization_barrier((swap_core(given), sent))
+    given = swap_core(given)
     back = exchange(sent, REP)
     pair = (kept.astype(F32) + given.astype(F32)).astype(BF16)
     total = pair[0].astype(F32)

time: 198 us -> 199 us (level)
  transfers between devices with their start and end apart: 18 -> 18, of which waited for: 9 -> 9; matrix products, arithmetic and copies ran while one was open for 3% -> 4% of each run, Pallas kernels for 4% -> 4%
where the time goes in v10:
time: 199 us; the launch traced here: 198 us
  starting transfers between devices  94.6 us (48%)
  waiting for transfers between devices  49 us (25%)
  blocking collectives  25.3 us (13%)
  Pallas kernels  18.4 us (9%)
  other arithmetic  5.52 us (3%)
  local copies, waits for them, and re-layouts  2.83 us (1%)
    ppermute x6, starting transfers between devices, far_move(): lax.ppermute(block, LINE, [(z, (z + 4 * step) % Z) for z in range(Z)])  38.9 us
    all_to_all x1, blocking collectives, exchange(): return lax.all_to_all(blocks, axis, split_axis=0, concat_axis=0, tiled=True)  25.3 us
    ppermute x6, waiting for transfers between devices, near_move(): return lax.ppermute(block, REL, pairs)  21.4 us
    ppermute x6, starting transfers between devices, near_move(): return lax.ppermute(block, REL, pairs)  19.8 us
    ppermute x3, starting transfers between devices, swap_core(): return lax.ppermute(block, 'core', [(0, 1), (1, 0)])  18 us
    all_to_all x3, starting transfers between devices, exchange(): return lax.all_to_all(blocks, axis, split_axis=0, concat_axis=0, tiled=True)  17.8 us
    all_to_all x3, waiting for transfers between devices, exchange(): return lax.all_to_all(blocks, axis, split_axis=0, concat_axis=0, tiled=True)  16 us
    ppermute x6, waiting for transfers between devices, far_move(): lax.ppermute(block, LINE, [(z, (z + 4 * step) % Z) for z in range(Z)])  10.3 us
  transfers between devices with their start and end apart: 18, of which 9 were waited for; matrix products, arithmetic and copies ran while one was open for 4% of the time, Pallas kernels for 4%

profile of v10, /device:TPU:1, one launch (start us, length us, event | category | flops | bytes accessed | tf_op | source)
XLA Modules:
  0.0 198.1 jit_solution(5623152759931737137)
XLA Ops:
  0.6 3.8 %shard_map.120 = (bf16[64,512]{1,0:T(8,128)(2,1)}, bf16[64,128]{1,0:T(8,128)(2,1)}, bf16[4,16,64]{2,1,0:T(8,128)(2,1)}, f32[1,64]{1,0:T(1,128)}, bf16[16,144,512]{2,1,0:T(8,128)(2,1)}) custom-call(s32[1,32]{1,0:T(1,128)} %fill.1, s32[1,64]{1,0:T(1,128)} %bitcast.55, bf16[64,128]{1,0:T(8,128)(2,1)} %rel_emb.1, bf16[16,128,512]{2,1,0:T(8,128)(2,1)} %core.1, ...), custom_call_target="tpu_custom_call" | custom-call | flops 33554432 | bytes 2097152 | tf_op jit(solution)/shard_map/pallas_call | solution.py:303
  4.5 13.3 %collective-permute-start.2 = (bf16[64,512]{1,0:T(8,128)(2,1)}, bf16[64,512]{1,0:T(8,128)(2,1)S(1)}, u32[]{:S(2)}, u32[]{:S(2)}) collective-permute-start(bf16[64,512]{1,0:T(8,128)(2,1)} %get-tuple-element.28), channel_id=1, source_target_pairs={{0,384},{32,416},{64,448},{96,480},{128,0},{160,32},{192,64},{224,... | collective-permute-start | bytes 196616 | tf_op jit(solution)/shard_map/ppermute | solution.py:43
  17.8 4.9 %collective-permute-start.1 = (bf16[64,512]{1,0:T(8,128)(2,1)}, bf16[64,512]{1,0:T(8,128)(2,1)S(1)}, u32[]{:S(2)}, u32[]{:S(2)}) collective-permute-start(bf16[64,512]{1,0:T(8,128)(2,1)} %get-tuple-element.28), channel_id=1, source_target_pairs={{0,256},{32,288},{64,320},{96,352},{128,384},{160,416},{192,448},{... | collective-permute-start | bytes 196616 | tf_op jit(solution)/shard_map/ppermute | solution.py:43
  22.7 7.3 %collective-permute-start = (bf16[64,512]{1,0:T(8,128)(2,1)}, bf16[64,512]{1,0:T(8,128)(2,1)}, u32[]{:S(2)}, u32[]{:S(2)}) collective-permute-start(bf16[64,512]{1,0:T(8,128)(2,1)} %get-tuple-element.28), channel_id=1, source_target_pairs={{0,128},{32,160},{64,192},{96,224},{128,256},{160,288},{192,320},{... | collective-permute-start | bytes 196616 | tf_op jit(solution)/shard_map/ppermute | solution.py:43
  29.9 6.8 %all-to-all-start = ((bf16[16,144,512]{2,1,0:T(8,128)(2,1)}), bf16[16,144,512]{2,1,0:T(8,128)(2,1)S(1)}, u32[]{:S(2)}, u32[]{:S(2)}) async-start(bf16[16,144,512]{2,1,0:T(8,128)(2,1)} %get-tuple-element.25), calls=%async_computation | async-start | bytes 4718592 | tf_op jit(solution)/shard_map/all_to_all | solution.py:22
  36.7 0.0 copy-start.2
  36.7 0.9 constant_dynamic-update-slice_fusion.6
  37.6 0.0 collective-permute-done.2
  37.6 0.0 collective-permute-done.1
  37.6 0.0 collective-permute-done
  37.6 0.9 pad_maximum_fusion
  38.5 6.4 %collective-permute-start.5 = (bf16[4,64,512]{2,1,0:T(8,128)(2,1)S(1)}, bf16[4,64,512]{2,1,0:T(8,128)(2,1)S(1)}, u32[]{:S(2)}, u32[]{:S(2)}) collective-permute-start(bf16[4,64,512]{2,1,0:T(8,128)(2,1)S(1)} %pad_maximum_fusion), channel_id=1, source_target_pairs={{0,480},{16,496},{32,0},{48,16},{64,32},{80,48},{96,64},{112,80},{... | collective-permute-start | bytes 786440 | tf_op jit(solution)/shard_map/ppermute | solution.py:39
  44.9 1.9 collective-permute-start.4
  46.9 3.1 %collective-permute-start.3 = (bf16[4,64,512]{2,1,0:T(8,128)(2,1)S(1)}, bf16[4,64,512]{2,1,0:T(8,128)(2,1)S(1)}, u32[]{:S(2)}, u32[]{:S(2)}) collective-permute-start(bf16[4,64,512]{2,1,0:T(8,128)(2,1)S(1)} %pad_maximum_fusion), channel_id=1, source_target_pairs={{0,32},{16,48},{32,64},{48,80},{64,96},{80,112},{96,128},{112,144}... | collective-permute-start | bytes 786440 | tf_op jit(solution)/shard_map/ppermute | solution.py:39
  50.0 0.8 constant_dynamic-update-slice_fusion.5
  50.8 9.4 %collective-permute-done.3 = bf16[4,64,512]{2,1,0:T(8,128)(2,1)S(1)} collective-permute-done((bf16[4,64,512]{2,1,0:T(8,128)(2,1)S(1)}, bf16[4,64,512]{2,1,0:T(8,128)(2,1)S(1)}, u32[]{:S(2)}, u32[]{:S(2)}) %collective-permute-start.3) | collective-permute-done | bytes 262176 | tf_op jit(solution)/shard_map/ppermute | solution.py:39
  60.2 0.0 collective-permute-done.4
  60.3 0.0 collective-permute-done.5
  60.3 3.3 %collective-permute-start.6 = (bf16[16,64,512]{2,1,0:T(8,128)(2,1)S(1)}, bf16[16,64,512]{2,1,0:T(8,128)(2,1)}, u32[]{:S(2)}, u32[]{:S(2)}) collective-permute-start(bf16[16,64,512]{2,1,0:T(8,128)(2,1)S(1)} %constant_dynamic-update-slice_fusion.half), channel_id=1, source_target_pairs={{0,16},{16,0},{1,17},{17,1},{2,18},{18,2},{3,19},{19,3},{4,20},{20... | collective-permute-start | bytes 3145736 | tf_op jit(solution)/shard_map/ppermute | solution.py:47
  63.7 0.1 pad_add_fusion.1.where
  63.8 4.8 %all-to-all-done.table = bf16[16,144,512]{2,1,0:T(8,128)(2,1)S(1)} async-done(((bf16[16,144,512]{2,1,0:T(8,128)(2,1)}), bf16[16,144,512]{2,1,0:T(8,128)(2,1)S(1)}, u32[]{:S(2)}, u32[]{:S(2)}) %all-to-all-start) | async-done | bytes 2359328 | tf_op jit(solution)/shard_map/all_to_all | solution.py:22
  68.6 0.0 copy-start.3
  68.6 0.0 copy-done.2
  68.6 1.8 shard_map.121
  70.4 0.0 collective-permute-done.6.other
  70.4 0.0 copy-done.3
  70.4 5.5 %shard_map.122 = (bf16[4,512,512]{2,1,0:T(8,128)(2,1)S(1)}, bf16[2,512,512]{2,1,0:T(8,128)(2,1)S(1)}, bf16[2,512,512]{2,1,0:T(8,128)(2,1)S(1)}, bf16[4,288,512]{2,1,0:T(8,128)(2,1)S(1)}, bf16[4,288,512]{2,1,0:T(8,128)(2,1)S(1)}) custom-call(s32[4,16]{1,0:T(4,128)S(1)} %pad_add_fusion.starts, bf16[4,512,512]{2,1,0:T(8,128)(2,1)S(1)} %get-tuple-element.26.heads, ...), custom_call_target="tpu_custom_call" | custom-call | flops 2952790016 | bytes 8388608 | tf_op jit(solution)/shard_map/pallas_call | solution.py:356
  75.9 5.0 %collective-permute-start.7 = (bf16[4,288,512]{2,1,0:T(8,128)(2,1)S(1)}, bf16[4,288,512]{2,1,0:T(8,128)(2,1)}, u32[]{:S(2)}, u32[]{:S(2)}) collective-permute-start(bf16[4,288,512]{2,1,0:T(8,128)(2,1)S(1)} %get-tuple-element.30), channel_id=1, source_target_pairs={{0,16},{16,0},{1,17},{17,1},{2,18},{18,2},{3,19},{19,3},{4,20},{20... | collective-permute-start | bytes 3538952 | tf_op jit(solution)/shard_map/ppermute | solution.py:47
  80.9 3.2 %shard_map.123 = bf16[16,128,512]{2,1,0:T(8,128)(2,1)} custom-call(f32[16,256]{1,0:T(8,128)S(1)} %get-tuple-element.31.ids, bf16[2,512,512]{2,1,0:T(8,128)(2,1)S(1)} %get-tuple-element.32.dquery, bf16[2,512,512]{2,1,0:T(8,128)(2,1)S(1)} %get-tuple-element.33.dtail, bf16[4,512,512]{2,1,0:T(8,128)(2,1)S(1)} %get-tuple-element.34.mats), custom_call_target="tpu_custom_call" | custom-call | flops 1476395008 | bytes 8388608 | tf_op jit(solution)/shard_map/pallas_call | solution.py:370
  84.1 4.4 %all-to-all-start.1 = ((bf16[16,128,512]{2,1,0:T(8,128)(2,1)}), bf16[16,128,512]{2,1,0:T(8,128)(2,1)}, u32[]{:S(2)}, u32[]{:S(2)}) async-start(bf16[16,128,512]{2,1,0:T(8,128)(2,1)} %shard_map.123), calls=%async_computation.1 | async-start | bytes 4194304 | tf_op jit(solution)/shard_map/all_to_all | solution.py:22
  88.5 0.0 collective-permute-done.7
  88.5 1.7 add_convert_fusion
  90.2 0.1 slice_bitcast_fusion.2
  90.3 2.6 %collective-permute-start.8 = (bf16[288,512]{1,0:T(8,128)(2,1)S(1)}, bf16[288,512]{1,0:T(8,128)(2,1)S(1)}, u32[]{:S(2)}, u32[]{:S(2)}) collective-permute-start(bf16[288,512]{1,0:T(8,128)(2,1)S(1)} %get-tuple-element.44), channel_id=1, source_target_pairs={{0,32},{16,48},{32,64},{48,80},{64,96},{80,112},{96,128},{112,144}... | collective-permute-start | bytes 884744 | tf_op jit(solution)/shard_map/ppermute | solution.py:39
  92.9 3.8 %collective-permute-start.10 = (bf16[288,512]{1,0:T(8,128)(2,1)S(1)}, bf16[288,512]{1,0:T(8,128)(2,1)S(1)}, u32[]{:S(2)}, u32[]{:S(2)}) collective-permute-start(bf16[288,512]{1,0:T(8,128)(2,1)S(1)} %get-tuple-element.45), channel_id=1, source_target_pairs={{0,480},{16,496},{32,0},{48,16},{64,32},{80,48},{96,64},{112,80},{... | collective-permute-start | bytes 884744 | tf_op jit(solution)/shard_map/ppermute | solution.py:39
  96.8 1.9 collective-permute-start.9
  98.7 3.3 %collective-permute-done.8 = bf16[288,512]{1,0:T(8,128)(2,1)S(1)} collective-permute-done((bf16[288,512]{1,0:T(8,128)(2,1)S(1)}, bf16[288,512]{1,0:T(8,128)(2,1)S(1)}, u32[]{:S(2)}, u32[]{:S(2)}) %collective-permute-start.8) | collective-permute-done | bytes 294944 | tf_op jit(solution)/shard_map/ppermute | solution.py:39
  102.0 1.2 collective-permute-done.10
  103.2 7.5 %collective-permute-done.9 = bf16[288,512]{1,0:T(8,128)(2,1)S(1)} collective-permute-done((bf16[288,512]{1,0:T(8,128)(2,1)S(1)}, bf16[288,512]{1,0:T(8,128)(2,1)S(1)}, u32[]{:S(2)}, u32[]{:S(2)}) %collective-permute-start.9) | collective-permute-done | bytes 294944 | tf_op jit(solution)/shard_map/ppermute | solution.py:39
  110.7 0.2 fusion.14
  110.9 4.0 %collective-permute-start.11 = (bf16[72,512]{1,0:T(8,128)(2,1)S(1)}, bf16[72,512]{1,0:T(8,128)(2,1)S(1)}, u32[]{:S(2)}, u32[]{:S(2)}) collective-permute-start(bf16[72,512]{1,0:T(8,128)(2,1)S(1)} %pad_maximum_fusion.1), channel_id=1, source_target_pairs={{0,128},{32,160},{64,192},{96,224},{128,256},{160,288},{192,320},{... | collective-permute-start | bytes 221192 | tf_op jit(solution)/shard_map/ppermute | solution.py:43
  115.0 5.4 %collective-permute-start.12 = (bf16[72,512]{1,0:T(8,128)(2,1)S(1)}, bf16[72,512]{1,0:T(8,128)(2,1)S(1)}, u32[]{:S(2)}, u32[]{:S(2)}) collective-permute-start(bf16[72,512]{1,0:T(8,128)(2,1)S(1)} %pad_maximum_fusion.2), channel_id=1, source_target_pairs={{0,256},{32,288},{64,320},{96,352},{128,384},{160,416},{192,448},{... | collective-permute-start | bytes 221192 | tf_op jit(solution)/shard_map/ppermute | solution.py:43
  120.4 4.1 %collective-permute-start.13 = (bf16[72,512]{1,0:T(8,128)(2,1)S(1)}, bf16[72,512]{1,0:T(8,128)(2,1)S(1)}, u32[]{:S(2)}, u32[]{:S(2)}) collective-permute-start(bf16[72,512]{1,0:T(8,128)(2,1)S(1)} %pad_maximum_fusion.3), channel_id=1, source_target_pairs={{0,384},{32,416},{64,448},{96,480},{128,0},{160,32},{192,64},{224,... | collective-permute-start | bytes 221192 | tf_op jit(solution)/shard_map/ppermute | solution.py:43
  124.5 0.0 collective-permute-done.11
  124.5 4.7 %collective-permute-done.12 = bf16[72,512]{1,0:T(8,128)(2,1)S(1)} collective-permute-done((bf16[72,512]{1,0:T(8,128)(2,1)S(1)}, bf16[72,512]{1,0:T(8,128)(2,1)S(1)}, u32[]{:S(2)}, u32[]{:S(2)}) %collective-permute-start.12) | collective-permute-done | bytes 73760 | tf_op jit(solution)/shard_map/ppermute | solution.py:43
  129.1 5.6 %collective-permute-done.13 = bf16[72,512]{1,0:T(8,128)(2,1)S(1)} collective-permute-done((bf16[72,512]{1,0:T(8,128)(2,1)S(1)}, bf16[72,512]{1,0:T(8,128)(2,1)S(1)}, u32[]{:S(2)}, u32[]{:S(2)}) %collective-permute-start.13) | collective-permute-done | bytes 73760 | tf_op jit(solution)/shard_map/ppermute | solution.py:43
  134.8 0.0 all-to-all-done.1
  134.8 0.1 broadcast_in_dim.28
  134.9 0.0 copy-start.4
  134.9 25.3 %all_to_all.20.sums = bf16[16,72,512]{2,1,0:T(8,128)(2,1)S(1)} all-to-all(bf16[16,72,512]{2,1,0:T(8,128)(2,1)S(1)} %broadcast_in_dim.28), channel_id=1, replica_groups=mesh['zh'=4,'zl'=4,'core'=2,'y'=4,'x'=4] {'y','x'}, dimensions={0} | all-to-all | bytes 2359296 | tf_op jit(solution)/shard_map/all_to_all | solution.py:22
  160.3 0.1 slice.68
  160.4 0.0 copy-done.4
  160.4 1.3 fusion.8
  161.7 0.0 copy-start
  161.8 0.8 broadcast_in_dim.29
  162.6 6.6 %all-to-all-start.3 = ((bf16[16,24,512]{2,1,0:T(8,128)(2,1)}), bf16[16,24,512]{2,1,0:T(8,128)(2,1)S(1)}, u32[]{:S(2)}, u32[]{:S(2)}) async-start(bf16[16,24,512]{2,1,0:T(8,128)(2,1)} %broadcast_in_dim.29), calls=%async_computation.3 | async-start | bytes 786432 | tf_op jit(solution)/shard_map/all_to_all | solution.py:22
  169.2 2.6 %reduce_sum.25 = bf16[128,512]{1,0:T(8,128)(2,1)} reduce(bf16[16,128,512]{2,1,0:T(8,128)(2,1)} %all-to-all-done.1, bf16[]{:T(256)} %constant.110.clone.1), dimensions={0}, to_apply=%region_1.2 | reduce | flops 983040 | bytes 2228226 | tf_op jit(solution)/shard_map/reduce_sum | solution.py:399
  171.8 0.0 copy-done
  171.8 2.8 %shard_map.124 = bf16[16,128,512]{2,1,0:T(8,128)(2,1)} custom-call(bf16[64,128]{1,0:T(8,128)(2,1)S(1)} %copy-done, bf16[16,72,512]{2,1,0:T(8,128)(2,1)S(1)} %all_to_all.20.sums), custom_call_target="tpu_custom_call" | custom-call | flops 134217728 | bytes 8388608 | tf_op jit(solution)/shard_map/pallas_call | solution.py:412
  174.6 11.2 %all-to-all-done.3.own = bf16[16,24,512]{2,1,0:T(8,128)(2,1)S(1)} async-done(((bf16[16,24,512]{2,1,0:T(8,128)(2,1)}), bf16[16,24,512]{2,1,0:T(8,128)(2,1)S(1)}, u32[]{:S(2)}, u32[]{:S(2)}) %all-to-all-start.3) | async-done | bytes 393248 | tf_op jit(solution)/shard_map/all_to_all | solution.py:22
  185.7 9.7 %collective-permute-start.14 = (bf16[16,24,512]{2,1,0:T(8,128)(2,1)S(1)}, bf16[16,24,512]{2,1,0:T(8,128)(2,1)S(1)}, u32[]{:S(2)}, u32[]{:S(2)}) collective-permute-start(bf16[16,24,512]{2,1,0:T(8,128)(2,1)S(1)} %all-to-all-done.3.own), channel_id=1, source_target_pairs={{0,16},{16,0},{1,17},{17,1},{2,18},{18,2},{3,19},{19,3},{4,20},{20... | collective-permute-start | bytes 1179656 | tf_op jit(solution)/shard_map/ppermute | solution.py:47
  195.4 1.3 collective-permute-done.14.other
  196.7 0.0 copy-done.1
  196.7 1.4 shard_map.125
  (18 shorter events, 0.3 us)
Async XLA Ops:
  4.5 33.1 %collective-permute-start.2 = (bf16[64,512]{1,0:T(8,128)(2,1)}, bf16[64,512]{1,0:T(8,128)(2,1)S(1)}, u32[]{:S(2)}, u32[]{:S(2)}) collective-permute-start(bf16[64,512]{1,0:T(8,128)(2,1)} %get-tuple-element.28), channel_id=1, source_target_pairs={{0,384},{32,416},{64,448},{96,480},{128,0},{160,32},{192,64},{224,... | collective-permute-start | bytes 196616 | tf_op jit(solution)/shard_map/ppermute | solution.py:43
  17.8 19.8 %collective-permute-start.1 = (bf16[64,512]{1,0:T(8,128)(2,1)}, bf16[64,512]{1,0:T(8,128)(2,1)S(1)}, u32[]{:S(2)}, u32[]{:S(2)}) collective-permute-start(bf16[64,512]{1,0:T(8,128)(2,1)} %get-tuple-element.28), channel_id=1, source_target_pairs={{0,256},{32,288},{64,320},{96,352},{128,384},{160,416},{192,448},{... | collective-permute-start | bytes 196616 | tf_op jit(solution)/shard_map/ppermute | solution.py:43
  22.7 14.9 %collective-permute-start = (bf16[64,512]{1,0:T(8,128)(2,1)}, bf16[64,512]{1,0:T(8,128)(2,1)}, u32[]{:S(2)}, u32[]{:S(2)}) collective-permute-start(bf16[64,512]{1,0:T(8,128)(2,1)} %get-tuple-element.28), channel_id=1, source_target_pairs={{0,128},{32,160},{64,192},{96,224},{128,256},{160,288},{192,320},{... | collective-permute-start | bytes 196616 | tf_op jit(solution)/shard_map/ppermute | solution.py:43
  29.9 38.7 %all-to-all-start = ((bf16[16,144,512]{2,1,0:T(8,128)(2,1)}), bf16[16,144,512]{2,1,0:T(8,128)(2,1)S(1)}, u32[]{:S(2)}, u32[]{:S(2)}) async-start(bf16[16,144,512]{2,1,0:T(8,128)(2,1)} %get-tuple-element.25), calls=%async_computation | async-start | bytes 4718592 | tf_op jit(solution)/shard_map/all_to_all | solution.py:22
  36.7 31.9 %copy-start.2 = (f32[1,64]{1,0:T(1,128)S(1)}, f32[1,64]{1,0:T(1,128)}, u32[]{:S(2)}) copy-start(f32[1,64]{1,0:T(1,128)} %get-tuple-element.24.slot_of) | copy-start | bytes 772
  38.5 21.7 %collective-permute-start.5 = (bf16[4,64,512]{2,1,0:T(8,128)(2,1)S(1)}, bf16[4,64,512]{2,1,0:T(8,128)(2,1)S(1)}, u32[]{:S(2)}, u32[]{:S(2)}) collective-permute-start(bf16[4,64,512]{2,1,0:T(8,128)(2,1)S(1)} %pad_maximum_fusion), channel_id=1, source_target_pairs={{0,480},{16,496},{32,0},{48,16},{64,32},{80,48},{96,64},{112,80},{... | collective-permute-start | bytes 786440 | tf_op jit(solution)/shard_map/ppermute | solution.py:39
  44.9 15.3 %collective-permute-start.4 = (bf16[4,64,512]{2,1,0:T(8,128)(2,1)S(1)}, bf16[4,64,512]{2,1,0:T(8,128)(2,1)S(1)}, u32[]{:S(2)}, u32[]{:S(2)}) collective-permute-start(bf16[4,64,512]{2,1,0:T(8,128)(2,1)S(1)} %pad_maximum_fusion), channel_id=1, source_target_pairs={{0,64},{16,464},{32,96},{48,496},{64,128},{80,16},{96,160},{112,48... | collective-permute-start | bytes 786440 | tf_op jit(solution)/shard_map/ppermute | solution.py:39
  46.9 13.3 %collective-permute-start.3 = (bf16[4,64,512]{2,1,0:T(8,128)(2,1)S(1)}, bf16[4,64,512]{2,1,0:T(8,128)(2,1)S(1)}, u32[]{:S(2)}, u32[]{:S(2)}) collective-permute-start(bf16[4,64,512]{2,1,0:T(8,128)(2,1)S(1)} %pad_maximum_fusion), channel_id=1, source_target_pairs={{0,32},{16,48},{32,64},{48,80},{64,96},{80,112},{96,128},{112,144}... | collective-permute-start | bytes 786440 | tf_op jit(solution)/shard_map/ppermute | solution.py:39
  60.3 10.1 %collective-permute-start.6 = (bf16[16,64,512]{2,1,0:T(8,128)(2,1)S(1)}, bf16[16,64,512]{2,1,0:T(8,128)(2,1)}, u32[]{:S(2)}, u32[]{:S(2)}) collective-permute-start(bf16[16,64,512]{2,1,0:T(8,128)(2,1)S(1)} %constant_dynamic-update-slice_fusion.half), channel_id=1, source_target_pairs={{0,16},{16,0},{1,17},{17,1},{2,18},{18,2},{3,19},{19,3},{4,20},{20... | collective-permute-start | bytes 3145736 | tf_op jit(solution)/shard_map/ppermute | solution.py:47
  68.6 1.8 copy-start.3
  75.9 12.7 %collective-permute-start.7 = (bf16[4,288,512]{2,1,0:T(8,128)(2,1)S(1)}, bf16[4,288,512]{2,1,0:T(8,128)(2,1)}, u32[]{:S(2)}, u32[]{:S(2)}) collective-permute-start(bf16[4,288,512]{2,1,0:T(8,128)(2,1)S(1)} %get-tuple-element.30), channel_id=1, source_target_pairs={{0,16},{16,0},{1,17},{17,1},{2,18},{18,2},{3,19},{19,3},{4,20},{20... | collective-permute-start | bytes 3538952 | tf_op jit(solution)/shard_map/ppermute | solution.py:47
  84.1 50.7 %all-to-all-start.1 = ((bf16[16,128,512]{2,1,0:T(8,128)(2,1)}), bf16[16,128,512]{2,1,0:T(8,128)(2,1)}, u32[]{:S(2)}, u32[]{:S(2)}) async-start(bf16[16,128,512]{2,1,0:T(8,128)(2,1)} %shard_map.123), calls=%async_computation.1 | async-start | bytes 4194304 | tf_op jit(solution)/shard_map/all_to_all | solution.py:22
  90.3 11.7 %collective-permute-start.8 = (bf16[288,512]{1,0:T(8,128)(2,1)S(1)}, bf16[288,512]{1,0:T(8,128)(2,1)S(1)}, u32[]{:S(2)}, u32[]{:S(2)}) collective-permute-start(bf16[288,512]{1,0:T(8,128)(2,1)S(1)} %get-tuple-element.44), channel_id=1, source_target_pairs={{0,32},{16,48},{32,64},{48,80},{64,96},{80,112},{96,128},{112,144}... | collective-permute-start | bytes 884744 | tf_op jit(solution)/shard_map/ppermute | solution.py:39
  92.9 10.3 %collective-permute-start.10 = (bf16[288,512]{1,0:T(8,128)(2,1)S(1)}, bf16[288,512]{1,0:T(8,128)(2,1)S(1)}, u32[]{:S(2)}, u32[]{:S(2)}) collective-permute-start(bf16[288,512]{1,0:T(8,128)(2,1)S(1)} %get-tuple-element.45), channel_id=1, source_target_pairs={{0,480},{16,496},{32,0},{48,16},{64,32},{80,48},{96,64},{112,80},{... | collective-permute-start | bytes 884744 | tf_op jit(solution)/shard_map/ppermute | solution.py:39
  96.8 13.9 %collective-permute-start.9 = (bf16[288,512]{1,0:T(8,128)(2,1)S(1)}, bf16[288,512]{1,0:T(8,128)(2,1)S(1)}, u32[]{:S(2)}, u32[]{:S(2)}) collective-permute-start(bf16[288,512]{1,0:T(8,128)(2,1)S(1)} %get-tuple-element.46), channel_id=1, source_target_pairs={{0,64},{16,464},{32,96},{48,496},{64,128},{80,16},{96,160},{112,48... | collective-permute-start | bytes 884744 | tf_op jit(solution)/shard_map/ppermute | solution.py:39
  110.9 13.5 %collective-permute-start.11 = (bf16[72,512]{1,0:T(8,128)(2,1)S(1)}, bf16[72,512]{1,0:T(8,128)(2,1)S(1)}, u32[]{:S(2)}, u32[]{:S(2)}) collective-permute-start(bf16[72,512]{1,0:T(8,128)(2,1)S(1)} %pad_maximum_fusion.1), channel_id=1, source_target_pairs={{0,128},{32,160},{64,192},{96,224},{128,256},{160,288},{192,320},{... | collective-permute-start | bytes 221192 | tf_op jit(solution)/shard_map/ppermute | solution.py:43
  115.0 14.2 %collective-permute-start.12 = (bf16[72,512]{1,0:T(8,128)(2,1)S(1)}, bf16[72,512]{1,0:T(8,128)(2,1)S(1)}, u32[]{:S(2)}, u32[]{:S(2)}) collective-permute-start(bf16[72,512]{1,0:T(8,128)(2,1)S(1)} %pad_maximum_fusion.2), channel_id=1, source_target_pairs={{0,256},{32,288},{64,320},{96,352},{128,384},{160,416},{192,448},{... | collective-permute-start | bytes 221192 | tf_op jit(solution)/shard_map/ppermute | solution.py:43
  120.4 14.4 %collective-permute-start.13 = (bf16[72,512]{1,0:T(8,128)(2,1)S(1)}, bf16[72,512]{1,0:T(8,128)(2,1)S(1)}, u32[]{:S(2)}, u32[]{:S(2)}) collective-permute-start(bf16[72,512]{1,0:T(8,128)(2,1)S(1)} %pad_maximum_fusion.3), channel_id=1, source_target_pairs={{0,384},{32,416},{64,448},{96,480},{128,0},{160,32},{192,64},{224,... | collective-permute-start | bytes 221192 | tf_op jit(solution)/shard_map/ppermute | solution.py:43
  134.9 25.5 %copy-start.4 = (bf16[16,128,512]{2,1,0:T(8,128)(2,1)S(1)}, bf16[16,128,512]{2,1,0:T(8,128)(2,1)}, u32[]{:S(2)}) copy-start(bf16[16,128,512]{2,1,0:T(8,128)(2,1)} %core.1) | copy-start | bytes 6291460
  161.7 10.1 %copy-start = (bf16[64,128]{1,0:T(8,128)(2,1)S(1)}, bf16[64,128]{1,0:T(8,128)(2,1)}, u32[]{:S(2)}) copy-start(bf16[64,128]{1,0:T(8,128)(2,1)} %get-tuple-element.36.ordered) | copy-start | bytes 49156
  162.6 23.2 %all-to-all-start.3 = ((bf16[16,24,512]{2,1,0:T(8,128)(2,1)}), bf16[16,24,512]{2,1,0:T(8,128)(2,1)S(1)}, u32[]{:S(2)}, u32[]{:S(2)}) async-start(bf16[16,24,512]{2,1,0:T(8,128)(2,1)} %broadcast_in_dim.29), calls=%async_computation.3 | async-start | bytes 786432 | tf_op jit(solution)/shard_map/all_to_all | solution.py:22
  171.8 25.0 %copy-start.1 = (bf16[4,16,64]{2,1,0:T(8,128)(2,1)S(1)}, bf16[4,16,64]{2,1,0:T(8,128)(2,1)}, u32[]{:S(2)}) copy-start(bf16[4,16,64]{2,1,0:T(8,128)(2,1)} %get-tuple-element.40.order_sel) | copy-start | bytes 24580
  185.7 11.0 %collective-permute-start.14 = (bf16[16,24,512]{2,1,0:T(8,128)(2,1)S(1)}, bf16[16,24,512]{2,1,0:T(8,128)(2,1)S(1)}, u32[]{:S(2)}, u32[]{:S(2)}) collective-permute-start(bf16[16,24,512]{2,1,0:T(8,128)(2,1)S(1)} %all-to-all-done.3.own), channel_id=1, source_target_pairs={{0,16},{16,0},{1,17},{17,1},{2,18},{18,2},{3,19},{19,3},{4,20},{20... | collective-permute-start | bytes 1179656 | tf_op jit(solution)/shard_map/ppermute | solution.py:47
